TPU v7x, 32 devices: a whole 2x2x4 slice. The times are simulated.
32 devices in a mesh: grp: 2 (over y), col: 4 (over z), row: 2 (over x), gz: 2 (over core).
Axes of the slice: x: 2, y: 2, z: 4, core: 2. Of those that a mesh axis runs over, the one named last changes fastest.
Arguments:
- electric: float32 [3, 64, 16, 1024], P(None, 'gz', 'row', ('grp', 'col')), parts along dimension 3, may hold values from -6 to 6
- magnetic: float32 [3, 64, 16, 1024], P(None, 'gz', 'row', ('grp', 'col')), parts along dimension 3, may hold values from -6 to 6
- material: int32 [64, 16, 1024], P('gz', 'row', ('grp', 'col')), parts along dimension 2, may hold values from 0 to 7
- eps_table: float32 [8], replicated, may hold values from 1.5 to 12
- mode_table: float32 [8, 64, 64], P(None, 'gz'), may hold values from -0.09375 to 0.09375
- port_row: int32 [4, 4, 4], P(('grp', 'row'), 'col'), parts along dimension 0, may hold values from 0 to 7
- port_col: int32 [4, 4, 4], P(('grp', 'row'), 'col'), parts along dimension 0, may hold values from 0 to 64
- port_mode: int32 [4, 4, 4], P(('grp', 'row'), 'col'), parts along dimension 0, may hold values from 0 to 7
- port_ids: int32 [4, 4, 4], P(('grp', 'row'), 'col'), parts along dimension 0, may hold values from 0 to 31, as said below
Outputs:
- electric_out: float32 [3, 64, 16, 1024], P(None, 'gz', 'row', ('grp', 'col')), parts along dimension 3
- magnetic_out: float32 [3, 64, 16, 1024], P(None, 'gz', 'row', ('grp', 'col')), parts along dimension 3
- intersections: float32 [64, 16], P(('grp', 'col', 'row', 'gz')), parts along dimension 0
There are 2 independent parts, one for each index of `grp`. A program takes and returns all parts, laid end to end along the dimension named above; an argument that names none is the same for every part. Nothing has to cross between parts.
Inputs may be any that keep to these rules, and one draw needn't show every extreme that they name: port_ids names every port number exactly once.
All inputs are finite; a program needn't handle non-finite values.
Results may differ from a plain program's by a relative error of at most 0.0003.
Values sent between devices are 32-bit elements; how exact they have to be, the bound alone decides.
No kernel may reach another device: no remote copies, remote signals or barrier semaphores. Data moves between devices by JAX's collectives and lax.ppermute only.
A program may use at most 64 MiB of HBM per device.

v0:
```python
import jax
import jax.numpy as jnp
from jax import lax
from jax.sharding import PartitionSpec as P

STEPS = 4
FREQ = 8
MATS = 8
PLEN = 64
PORT_TILE = 4


time_step = 0.5


def from_behind(block, axis, distance):
    devices = range(lax.axis_size(axis))
    route = [(i - distance, i) for i in devices if i - distance in devices]
    return lax.ppermute(block, axis, route)


def dft_basis():
    times = (jnp.arange(STEPS, dtype=jnp.float32) + 1.0) * time_step
    omegas = jnp.pi * (jnp.arange(FREQ, dtype=jnp.float32) + 1.0) / FREQ
    angle = times[:, None] * omegas[None, :]
    return jnp.concatenate([jnp.cos(angle), -jnp.sin(angle)], axis=1)


def port_samples(elec_z, rows_pos, cols_pos, modes_pos, mode_table, offset, layers):
    start = jnp.full((), offset, jnp.int32)

    def single(row_at, col_at, mode_at):
        strip = lax.dynamic_slice(
            elec_z, (start, row_at + offset, col_at + offset), (layers, 1, PLEN)
        )[:, 0, :]
        return jnp.sum(strip * mode_table[mode_at])

    return jax.vmap(single)(rows_pos, cols_pos, modes_pos)


def forward_parts(elec_x, elec_y, elec_z):
    paired = jnp.stack([elec_z, elec_x])
    beyond = from_behind(paired[:, :, :, :1], "col", -1)
    diff_y = jnp.diff(jnp.concatenate([paired, beyond], axis=3), axis=3)
    paired = jnp.stack([elec_y, elec_x])
    beyond = from_behind(paired[:, :1], "gz", -1)
    diff_z = jnp.diff(jnp.concatenate([paired, beyond], axis=1), axis=1)
    paired = jnp.stack([elec_z, elec_y])
    beyond = from_behind(paired[:, :, :1], "row", -1)
    diff_x = jnp.diff(jnp.concatenate([paired, beyond], axis=2), axis=2)
    return (diff_x, diff_y, diff_z)


def backward_parts(magn_x, magn_y, magn_z):
    paired = jnp.stack([magn_z, magn_x])
    before = from_behind(paired[:, :, :, -1:], "col", 1)
    diff_y = jnp.diff(jnp.concatenate([before, paired], axis=3), axis=3)
    paired = jnp.stack([magn_y, magn_x])
    before = from_behind(paired[:, -1:], "gz", 1)
    diff_z = jnp.diff(jnp.concatenate([before, paired], axis=1), axis=1)
    paired = jnp.stack([magn_z, magn_y])
    before = from_behind(paired[:, :, -1:], "row", 1)
    diff_x = jnp.diff(jnp.concatenate([before, paired], axis=2), axis=2)
    return (diff_x, diff_y, diff_z)


def per_device(
    electric, magnetic, material, eps_table, mode_table, port_row, port_col, port_mode, port_ids
):
    layers, rows_dev, cols_dev = material.shape
    inverse = 1.0 / eps_table
    lookup = jnp.zeros(material.shape, jnp.float32)
    for which in range(MATS):
        lookup = lookup + jnp.where(material == which, inverse[which], 0.0)
    coefficient = time_step * lookup
    rows_pos = port_row.reshape(-1)
    cols_pos = port_col.reshape(-1)
    modes_pos = port_mode.reshape(-1)
    samples = []
    elec_x, elec_y, elec_z = (electric[0], electric[1], electric[2])
    magn_x, magn_y, magn_z = (magnetic[0], magnetic[1], magnetic[2])
    for counter in range(STEPS):
        diff_x, diff_y, diff_z = forward_parts(elec_x, elec_y, elec_z)
        magn_x = magn_x - time_step * (diff_y[0] - diff_z[0])
        magn_y = magn_y - time_step * (diff_z[1] - diff_x[0])
        magn_z = magn_z - time_step * (diff_x[1] - diff_y[1])
        diff_x, diff_y, diff_z = backward_parts(magn_x, magn_y, magn_z)
        elec_x = elec_x + coefficient * (diff_y[0] - diff_z[0])
        elec_y = elec_y + coefficient * (diff_z[1] - diff_x[0])
        elec_z = elec_z + coefficient * (diff_x[1] - diff_y[1])
        samples.append(port_samples(elec_z, rows_pos, cols_pos, modes_pos, mode_table, 0, layers))
    electric_out = jnp.stack([elec_x, elec_y, elec_z])
    magnetic_out = jnp.stack([magn_x, magn_y, magn_z])
    sampled = jnp.stack(samples)
    transform = jnp.dot(sampled.T, dft_basis(), precision=lax.Precision.HIGHEST)
    total_ports = PORT_TILE * lax.axis_size("col") * lax.axis_size("row")
    onehot = (
        port_ids.reshape(-1)[:, None] == jnp.arange(total_ports, dtype=jnp.int32)[None, :]
    ).astype(jnp.float32)
    term = jnp.dot(onehot.T, transform, precision=lax.Precision.HIGHEST)
    intersections = lax.psum_scatter(term, ("col", "row", "gz"), scatter_dimension=0, tiled=True)
    return (electric_out, magnetic_out, intersections)


def solution(mesh):
    in_specs = (
        P(None, "gz", "row", ("grp", "col")),
        P(None, "gz", "row", ("grp", "col")),
        P("gz", "row", ("grp", "col")),
        P(),
        P(None, "gz", None),
        P(("grp", "row"), "col", None),
        P(("grp", "row"), "col", None),
        P(("grp", "row"), "col", None),
        P(("grp", "row"), "col", None),
    )
    out_specs = (
        P(None, "gz", "row", ("grp", "col")),
        P(None, "gz", "row", ("grp", "col")),
        P(("grp", "col", "row", "gz"), None),
    )
    return jax.shard_map(
        per_device, mesh=mesh, in_specs=in_specs, out_specs=out_specs, check_vma=False
    )
```

profile of v0, /device:TPU:0, one launch (start us, length us, event | category | flops | bytes accessed | tf_op | source)
XLA Modules:
  0.0 254.8 jit_solution(11291879808571491265)
XLA Ops:
  15.9 5.7 %collective-permute-start.3 = (f32[2,32,8,1]{1,2,3,0:T(8,128)S(1)}, f32[2,32,8,1]{1,2,3,0:T(8,128)S(1)}, u32[]{:S(2)}, u32[]{:S(2)}) collective-permute-start(f32[2,32,8,1]{1,2,3,0:T(8,128)S(1)} %fusion.108), channel_id=1, source_target_pairs={{0,4},{4,8},{8,12},{1,5},{5,9},{9,13},{2,6},{6,10},{10,14},{3,7},{... | collective-permute-start | bytes 6152 | tf_op jit(solution)/shard_map/ppermute | solution.py:19
  21.6 5.2 %collective-permute-start.5 = (f32[2,32,1,128]{1,2,3,0:T(1,128)S(1)}, f32[2,32,1,128]{1,2,3,0:T(1,128)}, u32[]{:S(2)}, u32[]{:S(2)}) collective-permute-start(f32[2,32,1,128]{1,2,3,0:T(1,128)S(1)} %fusion.100), channel_id=1, source_target_pairs={{0,2},{1,3},{4,6},{5,7},{8,10},{9,11},{12,14},{13,15},{16,18},{17,... | collective-permute-start | bytes 98312 | tf_op jit(solution)/shard_map/ppermute | solution.py:19
  26.8 2.2 copy.314
  28.9 3.0 %collective-permute-start.4 = (f32[2,1,8,128]{3,2,1,0:T(8,128)}, f32[2,1,8,128]{3,2,1,0:T(8,128)}, u32[]{:S(2)}, u32[]{:S(2)}) collective-permute-start(f32[2,1,8,128]{3,2,1,0:T(8,128)} %copy.314), channel_id=1, source_target_pairs={{0,1},{2,3},{4,5},{6,7},{8,9},{10,11},{12,13},{14,15},{16,17},{18,... | collective-permute-start | bytes 24584 | tf_op jit(solution)/shard_map/ppermute | solution.py:19
  34.9 2.3 fusion.28
  37.2 5.6 %fusion.135 = (f32[1,32,8,128]{1,2,3,0:T(8,128)S(1)}, f32[1,32,8,128]{1,2,3,0:T(8,128)S(1)}, f32[32,8,128]{0,1,2:T(8,128)S(1)}) fusion(f32[2,32,8,128]{1,2,3,0:T(8,128)S(1)} %get-tuple-element.50, f32[2,32,8,128]{1,2,3,0:T(8,128)S(1)} %get-tuple-element.49, f32[1,32,8,128]{1,2,3,0:T(8,128)S(1)} %copy.341, f32[]{:T(128)} %bitcast.8, ...), kind=kLoop, calls=%fused_computation.301 | loop fusion | flops 1081344 | bytes 1703968 | tf_op jit(solution)/shard_map/stack | solution.py:48
  47.5 2.2 copy.316
  55.1 2.7 %fusion.24 = (f32[2,32,8,128]{1,2,3,0:T(8,128)S(1)}, f32[2,32,8,128]{1,2,3,0:T(8,128)S(1)}, f32[2,32,8,128]{1,2,3,0:T(8,128)S(1)}) fusion(f32[1,32,8,128]{1,2,3,0:T(8,128)S(1)} %copy-done.30, f32[1,32,8,128]{1,2,3,0:T(8,128)S(1)} %bitcast.161, f32[2,32,1,128]{1,2,3,0:T(1,128)S(1)} %collective-permute-done.6, f32[1,32,8,128]{1,2,3,0:T(8,128)} %copy-done.31, ...), kind=kLoop, calls=%fused_computation.101 | loop fusion | flops 786432 | bytes 1222656 | tf_op jit(solution)/shard_map/jit(diff)/sub | solution.py:50
  60.4 4.7 %collective-permute-start.9 = (f32[2,32,8,1]{1,2,3,0:T(8,128)S(1)}, f32[2,32,8,1]{1,2,3,0:T(8,128)S(1)}, u32[]{:S(2)}, u32[]{:S(2)}) collective-permute-start(f32[2,32,8,1]{1,2,3,0:T(8,128)S(1)} %fusion.106), channel_id=1, source_target_pairs={{0,4},{4,8},{8,12},{1,5},{5,9},{9,13},{2,6},{6,10},{10,14},{3,7},{... | collective-permute-start | bytes 6152 | tf_op jit(solution)/shard_map/ppermute | solution.py:19
  65.1 4.6 %collective-permute-start.11 = (f32[2,32,1,128]{1,2,3,0:T(1,128)S(1)}, f32[2,32,1,128]{1,2,3,0:T(1,128)S(1)}, u32[]{:S(2)}, u32[]{:S(2)}) collective-permute-start(f32[2,32,1,128]{1,2,3,0:T(1,128)S(1)} %fusion.98), channel_id=1, source_target_pairs={{0,2},{1,3},{4,6},{5,7},{8,10},{9,11},{12,14},{13,15},{16,18},{17,... | collective-permute-start | bytes 98312 | tf_op jit(solution)/shard_map/ppermute | solution.py:19
  69.7 2.2 copy.318
  71.8 2.1 collective-permute-start.10
  74.7 2.1 copy.319
  76.8 2.3 fusion.22
  79.2 5.6 %fusion.69 = f32[32,8,128]{0,1,2:T(8,128)S(1)} fusion(f32[32,8,128]{0,1,2:T(8,128)S(1)} %get-tuple-element.18, f32[2,32,8,128]{1,2,3,0:T(8,128)S(1)} %get-tuple-element.45, f32[2,32,8,128]{1,2,3,0:T(8,128)S(1)} %get-tuple-element.44, f32[]{:T(128)} %bitcast.8, s32[32,8,128]{0,1,2:T(8,128)S(1)} %copy.299, f32[]{:T(128)} %bitcast.7, f32[]{:T(128)} %bitcast.6, ...), kind=kLoop, calls=%fused_computation.208 | loop fusion | flops 884736 | bytes 655392 | tf_op jit(solution)/shard_map/add | solution.py:90
  84.8 5.6 %fusion.66 = (f32[32,8,128]{0,1,2:T(8,128)S(1)}, f32[32,8,128]{0,1,2:T(8,128)S(1)}) fusion(f32[2,32,8,128]{1,2,3,0:T(8,128)S(1)} %get-tuple-element.44, f32[2,32,8,128]{1,2,3,0:T(8,128)S(1)} %get-tuple-element.43, f32[2,32,8,128]{1,2,3,0:T(8,128)S(1)} %copy-done.37, f32[2,32,8,128]{1,2,3,0:T(8,128)S(1)} %copy-done.26, f32[1,32,8,128]{1,2,3,0:T(8,128)S(1)} %copy.341, ...), kind=kLoop, calls=%fused_computation.204 | loop fusion | flops 1179648 | bytes 1703968 | tf_op jit(solution)/shard_map/add | solution.py:89
  100.0 2.1 fusion.18
  104.8 4.7 %collective-permute-start.15 = (f32[2,32,8,1]{1,2,3,0:T(8,128)S(1)}, f32[2,32,8,1]{1,2,3,0:T(8,128)S(1)}, u32[]{:S(2)}, u32[]{:S(2)}) collective-permute-start(f32[2,32,8,1]{1,2,3,0:T(8,128)S(1)} %fusion.104), channel_id=1, source_target_pairs={{0,4},{4,8},{8,12},{1,5},{5,9},{9,13},{2,6},{6,10},{10,14},{3,7},{... | collective-permute-start | bytes 6152 | tf_op jit(solution)/shard_map/ppermute | solution.py:19
  109.4 4.8 %collective-permute-start.17 = (f32[2,32,1,128]{1,2,3,0:T(1,128)}, f32[2,32,1,128]{1,2,3,0:T(1,128)}, u32[]{:S(2)}, u32[]{:S(2)}) collective-permute-start(f32[2,32,1,128]{1,2,3,0:T(1,128)} %fusion.96), channel_id=1, source_target_pairs={{0,2},{1,3},{4,6},{5,7},{8,10},{9,11},{12,14},{13,15},{16,18},{17,... | collective-permute-start | bytes 98312 | tf_op jit(solution)/shard_map/ppermute | solution.py:19
  122.8 2.3 fusion.16
  125.2 5.6 %fusion.137 = (f32[1,32,8,128]{1,2,3,0:T(8,128)S(1)}, f32[1,32,8,128]{1,2,3,0:T(8,128)S(1)}, f32[32,8,128]{0,1,2:T(8,128)S(1)}) fusion(f32[32,8,128]{0,1,2:T(8,128)S(1)} %get-tuple-element.11, f32[2,32,8,128]{1,2,3,0:T(8,128)S(1)} %get-tuple-element.38, f32[2,32,8,128]{1,2,3,0:T(8,128)S(1)} %get-tuple-element.37, f32[]{:T(128)} %bitcast.8, ...), kind=kLoop, calls=%fused_computation.303 | loop fusion | flops 1081344 | bytes 1703968 | tf_op jit(solution)/shard_map/stack | solution.py:48
  136.0 2.1 copy.324
  145.1 3.4 %fusion.12 = (f32[2,32,8,128]{1,2,3,0:T(8,128)S(1)}, f32[2,32,8,128]{1,2,3,0:T(8,128)S(1)}, f32[2,32,8,128]{1,2,3,0:T(8,128)S(1)}) fusion(f32[1,32,8,128]{1,2,3,0:T(8,128)} %copy-done.27, f32[1,32,8,128]{1,2,3,0:T(8,128)S(1)} %bitcast.167, f32[2,32,1,128]{1,2,3,0:T(1,128)} %collective-permute-done.18, f32[1,32,8,128]{1,2,3,0:T(8,128)} %copy-done.28, ...), kind=kLoop, calls=%fused_computation.89 | loop fusion | flops 786432 | bytes 1222656 | tf_op jit(solution)/shard_map/jit(diff)/sub | solution.py:50
  157.8 4.5 %collective-permute-start.21 = (f32[2,32,8,1]{1,2,3,0:T(8,128)}, f32[2,32,8,1]{1,2,3,0:T(8,128)S(1)}, u32[]{:S(2)}, u32[]{:S(2)}) collective-permute-start(f32[2,32,8,1]{1,2,3,0:T(8,128)} %fusion.102), channel_id=1, source_target_pairs={{0,4},{4,8},{8,12},{1,5},{5,9},{9,13},{2,6},{6,10},{10,14},{3,7},{... | collective-permute-start | bytes 6152 | tf_op jit(solution)/shard_map/ppermute | solution.py:19
  162.4 5.8 %collective-permute-start.23 = (f32[2,32,1,128]{1,2,3,0:T(1,128)}, f32[2,32,1,128]{1,2,3,0:T(1,128)}, u32[]{:S(2)}, u32[]{:S(2)}) collective-permute-start(f32[2,32,1,128]{1,2,3,0:T(1,128)} %fusion.94), channel_id=1, source_target_pairs={{0,2},{1,3},{4,6},{5,7},{8,10},{9,11},{12,14},{13,15},{16,18},{17,... | collective-permute-start | bytes 98312 | tf_op jit(solution)/shard_map/ppermute | solution.py:19
  168.2 2.1 copy.326
  170.4 3.6 %collective-permute-start.22 = (f32[2,1,8,128]{3,2,1,0:T(8,128)}, f32[2,1,8,128]{3,2,1,0:T(8,128)}, u32[]{:S(2)}, u32[]{:S(2)}) collective-permute-start(f32[2,1,8,128]{3,2,1,0:T(8,128)} %copy.326), channel_id=1, source_target_pairs={{0,1},{2,3},{4,5},{6,7},{8,9},{10,11},{12,13},{14,15},{16,17},{18,... | collective-permute-start | bytes 24584 | tf_op jit(solution)/shard_map/ppermute | solution.py:19
  175.7 2.1 copy.327
  177.8 2.4 fusion.10
  180.2 5.6 %fusion.34 = f32[32,8,128]{0,1,2:T(8,128)S(1)} fusion(f32[32,8,128]{0,1,2:T(8,128)S(1)} %get-tuple-element.15, f32[2,32,8,128]{1,2,3,0:T(8,128)S(1)} %get-tuple-element.33, f32[2,32,8,128]{1,2,3,0:T(8,128)S(1)} %get-tuple-element.32, f32[]{:T(128)} %bitcast.8, s32[32,8,128]{0,1,2:T(8,128)S(1)} %copy.299, f32[]{:T(128)} %bitcast.7, f32[]{:T(128)} %bitcast.6, ...), kind=kLoop, calls=%fused_computation.160 | loop fusion | flops 884736 | bytes 655392 | tf_op jit(solution)/shard_map/add | solution.py:90
  185.9 5.7 %fusion.42 = (f32[1,32,8,128]{1,2,3,0:T(8,128)S(1)}, f32[1,32,8,128]{1,2,3,0:T(8,128)S(1)}) fusion(f32[2,32,8,128]{1,2,3,0:T(8,128)S(1)} %get-tuple-element.31, f32[2,32,8,128]{1,2,3,0:T(8,128)S(1)} %get-tuple-element.33, f32[32,8,128]{0,1,2:T(8,128)S(1)} %get-tuple-element.12, f32[2,32,8,128]{1,2,3,0:T(8,128)S(1)} %copy-done.24, ...), kind=kLoop, calls=%fused_computation.170 | loop fusion | flops 1179648 | bytes 1703968 | tf_op jit(solution)/shard_map/stack | solution.py:92
  195.4 57.6 %all-reduce.1 = f32[32,16]{1,0:T(8,128)S(1)} all-reduce(f32[32,16]{1,0:T(8,128)S(1)} %fusion.122), channel_id=2, replica_groups=mesh['grp'=2,'col'=4,'row'=2,'gz'=2] {'col','row','gz'}, use_global_device_ids=true, to_apply=%region_4.5.clone | all-reduce | flops 512 | bytes 4096
  (222 shorter events, 79.9 us)
Async XLA Ops:
  0.6 116.7 %copy-start = (f32[8,32,64]{2,1,0:T(8,128)S(1)}, f32[8,32,64]{2,1,0:T(8,128)}, u32[]{:S(2)}) copy-start(f32[8,32,64]{2,1,0:T(8,128)} %param.13) | copy-start | bytes 196612
  2.3 10.0 %collective-permute-start.1 = (f32[2,32,8,1]{1,2,3,0:T(8,128)S(1)}, f32[2,32,8,1]{1,2,3,0:T(8,128)S(1)}, u32[]{:S(2)}, u32[]{:S(2)}) collective-permute-start(f32[2,32,8,1]{1,2,3,0:T(8,128)S(1)} %fusion.109), channel_id=1, source_target_pairs={{4,0},{8,4},{12,8},{5,1},{9,5},{13,9},{6,2},{10,6},{14,10},{7,3},{... | collective-permute-start | bytes 6152 | tf_op jit(solution)/shard_map/ppermute | solution.py:19
  3.9 8.3 %collective-permute-start = (f32[2,32,1,128]{1,2,3,0:T(1,128)S(1)}, f32[2,32,1,128]{1,2,3,0:T(1,128)S(1)}, u32[]{:S(2)}, u32[]{:S(2)}) collective-permute-start(f32[2,32,1,128]{1,2,3,0:T(1,128)S(1)} %fusion.101), channel_id=1, source_target_pairs={{2,0},{3,1},{6,4},{7,5},{10,8},{11,9},{14,12},{15,13},{18,16},{19,... | collective-permute-start | bytes 98312 | tf_op jit(solution)/shard_map/ppermute | solution.py:19
  5.7 6.1 %collective-permute-start.2 = (f32[2,1,8,128]{3,2,1,0:T(8,128)S(1)}, f32[2,1,8,128]{3,2,1,0:T(8,128)S(1)}, u32[]{:S(2)}, u32[]{:S(2)}) collective-permute-start(f32[2,1,8,128]{3,2,1,0:T(8,128)S(1)} %copy.311), channel_id=1, source_target_pairs={{1,0},{3,2},{5,4},{7,6},{9,8},{11,10},{13,12},{15,14},{17,16},{19,... | collective-permute-start | bytes 24584 | tf_op jit(solution)/shard_map/ppermute | solution.py:19
  13.8 21.1 %copy-start.16 = (f32[1,32,8,128]{1,2,3,0:T(8,128)}, f32[1,32,8,128]{1,2,3,0:T(8,128)S(1)}, u32[]{:S(2)}) copy-start(f32[1,32,8,128]{1,2,3,0:T(8,128)S(1)} %get-tuple-element.28) | copy-start | bytes 393220
  15.9 16.7 %copy-start.44 = (s32[32,8,128]{2,1,0:T(8,128)S(1)}, s32[32,8,128]{2,1,0:T(8,128)}, u32[]{:S(2)}) copy-start(s32[32,8,128]{2,1,0:T(8,128)} %param.11) | copy-start | bytes 393220
  15.9 19.0 %collective-permute-start.3 = (f32[2,32,8,1]{1,2,3,0:T(8,128)S(1)}, f32[2,32,8,1]{1,2,3,0:T(8,128)S(1)}, u32[]{:S(2)}, u32[]{:S(2)}) collective-permute-start(f32[2,32,8,1]{1,2,3,0:T(8,128)S(1)} %fusion.108), channel_id=1, source_target_pairs={{0,4},{4,8},{8,12},{1,5},{5,9},{9,13},{2,6},{6,10},{10,14},{3,7},{... | collective-permute-start | bytes 6152 | tf_op jit(solution)/shard_map/ppermute | solution.py:19
  21.6 13.3 %collective-permute-start.5 = (f32[2,32,1,128]{1,2,3,0:T(1,128)S(1)}, f32[2,32,1,128]{1,2,3,0:T(1,128)}, u32[]{:S(2)}, u32[]{:S(2)}) collective-permute-start(f32[2,32,1,128]{1,2,3,0:T(1,128)S(1)} %fusion.100), channel_id=1, source_target_pairs={{0,2},{1,3},{4,6},{5,7},{8,10},{9,11},{12,14},{13,15},{16,18},{17,... | collective-permute-start | bytes 98312 | tf_op jit(solution)/shard_map/ppermute | solution.py:19
  28.9 3.9 %collective-permute-start.4 = (f32[2,1,8,128]{3,2,1,0:T(8,128)}, f32[2,1,8,128]{3,2,1,0:T(8,128)}, u32[]{:S(2)}, u32[]{:S(2)}) collective-permute-start(f32[2,1,8,128]{3,2,1,0:T(8,128)} %copy.314), channel_id=1, source_target_pairs={{0,1},{2,3},{4,5},{6,7},{8,9},{10,11},{12,13},{14,15},{16,17},{18,... | collective-permute-start | bytes 24584 | tf_op jit(solution)/shard_map/ppermute | solution.py:19
  44.9 10.2 %collective-permute-start.7 = (f32[2,32,8,1]{1,2,3,0:T(8,128)S(1)}, f32[2,32,8,1]{1,2,3,0:T(8,128)S(1)}, u32[]{:S(2)}, u32[]{:S(2)}) collective-permute-start(f32[2,32,8,1]{1,2,3,0:T(8,128)S(1)} %fusion.107), channel_id=1, source_target_pairs={{4,0},{8,4},{12,8},{5,1},{9,5},{13,9},{6,2},{10,6},{14,10},{7,3},{... | collective-permute-start | bytes 6152 | tf_op jit(solution)/shard_map/ppermute | solution.py:19
  46.2 8.9 %collective-permute-start.6 = (f32[2,32,1,128]{1,2,3,0:T(1,128)S(1)}, f32[2,32,1,128]{1,2,3,0:T(1,128)S(1)}, u32[]{:S(2)}, u32[]{:S(2)}) collective-permute-start(f32[2,32,1,128]{1,2,3,0:T(1,128)S(1)} %fusion.99), channel_id=1, source_target_pairs={{2,0},{3,1},{6,4},{7,5},{10,8},{11,9},{14,12},{15,13},{18,16},{19,... | collective-permute-start | bytes 98312 | tf_op jit(solution)/shard_map/ppermute | solution.py:19
  49.7 3.4 %collective-permute-start.8 = (f32[2,1,8,128]{3,2,1,0:T(8,128)}, f32[2,1,8,128]{3,2,1,0:T(8,128)}, u32[]{:S(2)}, u32[]{:S(2)}) collective-permute-start(f32[2,1,8,128]{3,2,1,0:T(8,128)} %copy.316), channel_id=1, source_target_pairs={{1,0},{3,2},{5,4},{7,6},{9,8},{11,10},{13,12},{15,14},{17,16},{19,... | collective-permute-start | bytes 24584 | tf_op jit(solution)/shard_map/ppermute | solution.py:19
  58.1 18.7 %copy-start.5 = (f32[1,32,8,128]{1,2,3,0:T(8,128)}, f32[1,32,8,128]{1,2,3,0:T(8,128)S(1)}, u32[]{:S(2)}) copy-start(f32[1,32,8,128]{1,2,3,0:T(8,128)S(1)} %get-tuple-element.27) | copy-start | bytes 393220
  60.4 13.5 %copy-start.47 = (f32[4]{0:T(128)S(1)}, f32[4]{0:T(128)}, u32[]{:S(2)}) copy-start(f32[4]{0:T(128)} %add_multiply_fusion.2) | copy-start | bytes 52
  60.4 13.5 %copy-start.48 = (f32[8]{0:T(128)S(1)}, f32[8]{0:T(128)}, u32[]{:S(2)}) copy-start(f32[8]{0:T(128)} %add_multiply_fusion.1) | copy-start | bytes 100
  60.4 16.4 %collective-permute-start.9 = (f32[2,32,8,1]{1,2,3,0:T(8,128)S(1)}, f32[2,32,8,1]{1,2,3,0:T(8,128)S(1)}, u32[]{:S(2)}, u32[]{:S(2)}) collective-permute-start(f32[2,32,8,1]{1,2,3,0:T(8,128)S(1)} %fusion.106), channel_id=1, source_target_pairs={{0,4},{4,8},{8,12},{1,5},{5,9},{9,13},{2,6},{6,10},{10,14},{3,7},{... | collective-permute-start | bytes 6152 | tf_op jit(solution)/shard_map/ppermute | solution.py:19
  65.1 11.7 %collective-permute-start.11 = (f32[2,32,1,128]{1,2,3,0:T(1,128)S(1)}, f32[2,32,1,128]{1,2,3,0:T(1,128)S(1)}, u32[]{:S(2)}, u32[]{:S(2)}) collective-permute-start(f32[2,32,1,128]{1,2,3,0:T(1,128)S(1)} %fusion.98), channel_id=1, source_target_pairs={{0,2},{1,3},{4,6},{5,7},{8,10},{9,11},{12,14},{13,15},{16,18},{17,... | collective-permute-start | bytes 98312 | tf_op jit(solution)/shard_map/ppermute | solution.py:19
  71.8 2.8 %collective-permute-start.10 = (f32[2,1,8,128]{3,2,1,0:T(8,128)}, f32[2,1,8,128]{3,2,1,0:T(8,128)}, u32[]{:S(2)}, u32[]{:S(2)}) collective-permute-start(f32[2,1,8,128]{3,2,1,0:T(8,128)} %copy.318), channel_id=1, source_target_pairs={{0,1},{2,3},{4,5},{6,7},{8,9},{10,11},{12,13},{14,15},{16,17},{18,... | collective-permute-start | bytes 24584 | tf_op jit(solution)/shard_map/ppermute | solution.py:19
  91.3 8.2 %collective-permute-start.13 = (f32[2,32,8,1]{1,2,3,0:T(8,128)}, f32[2,32,8,1]{1,2,3,0:T(8,128)S(1)}, u32[]{:S(2)}, u32[]{:S(2)}) collective-permute-start(f32[2,32,8,1]{1,2,3,0:T(8,128)} %fusion.105), channel_id=1, source_target_pairs={{4,0},{8,4},{12,8},{5,1},{9,5},{13,9},{6,2},{10,6},{14,10},{7,3},{... | collective-permute-start | bytes 6152 | tf_op jit(solution)/shard_map/ppermute | solution.py:19
  92.6 7.5 %collective-permute-start.12 = (f32[2,32,1,128]{1,2,3,0:T(1,128)S(1)}, f32[2,32,1,128]{1,2,3,0:T(1,128)S(1)}, u32[]{:S(2)}, u32[]{:S(2)}) collective-permute-start(f32[2,32,1,128]{1,2,3,0:T(1,128)S(1)} %fusion.97), channel_id=1, source_target_pairs={{2,0},{3,1},{6,4},{7,5},{10,8},{11,9},{14,12},{15,13},{18,16},{19,... | collective-permute-start | bytes 98312 | tf_op jit(solution)/shard_map/ppermute | solution.py:19
  94.8 3.3 %collective-permute-start.14 = (f32[2,1,8,128]{3,2,1,0:T(8,128)}, f32[2,1,8,128]{3,2,1,0:T(8,128)S(1)}, u32[]{:S(2)}, u32[]{:S(2)}) collective-permute-start(f32[2,1,8,128]{3,2,1,0:T(8,128)} %copy.320), channel_id=1, source_target_pairs={{1,0},{3,2},{5,4},{7,6},{9,8},{11,10},{13,12},{15,14},{17,16},{19,... | collective-permute-start | bytes 24584 | tf_op jit(solution)/shard_map/ppermute | solution.py:19
  102.4 20.4 %copy-start.3 = (f32[1,32,8,128]{1,2,3,0:T(8,128)}, f32[1,32,8,128]{1,2,3,0:T(8,128)S(1)}, u32[]{:S(2)}) copy-start(f32[1,32,8,128]{1,2,3,0:T(8,128)S(1)} %get-tuple-element.24) | copy-start | bytes 393220
  104.8 12.5 %copy-start.51 = (s32[1,1,4]{2,1,0:T(1,128)S(1)}, s32[1,1,4]{2,1,0:T(1,128)}, u32[]{:S(2)}) copy-start(s32[1,1,4]{2,1,0:T(1,128)} %param.16) | copy-start | bytes 52
  104.8 18.0 %collective-permute-start.15 = (f32[2,32,8,1]{1,2,3,0:T(8,128)S(1)}, f32[2,32,8,1]{1,2,3,0:T(8,128)S(1)}, u32[]{:S(2)}, u32[]{:S(2)}) collective-permute-start(f32[2,32,8,1]{1,2,3,0:T(8,128)S(1)} %fusion.104), channel_id=1, source_target_pairs={{0,4},{4,8},{8,12},{1,5},{5,9},{9,13},{2,6},{6,10},{10,14},{3,7},{... | collective-permute-start | bytes 6152 | tf_op jit(solution)/shard_map/ppermute | solution.py:19
  109.4 13.3 %collective-permute-start.17 = (f32[2,32,1,128]{1,2,3,0:T(1,128)}, f32[2,32,1,128]{1,2,3,0:T(1,128)}, u32[]{:S(2)}, u32[]{:S(2)}) collective-permute-start(f32[2,32,1,128]{1,2,3,0:T(1,128)} %fusion.96), channel_id=1, source_target_pairs={{0,2},{1,3},{4,6},{5,7},{8,10},{9,11},{12,14},{13,15},{16,18},{17,... | collective-permute-start | bytes 98312 | tf_op jit(solution)/shard_map/ppermute | solution.py:19
  115.8 5.7 %collective-permute-start.16 = (f32[2,1,8,128]{3,2,1,0:T(8,128)S(1)}, f32[2,1,8,128]{3,2,1,0:T(8,128)S(1)}, u32[]{:S(2)}, u32[]{:S(2)}) collective-permute-start(f32[2,1,8,128]{3,2,1,0:T(8,128)S(1)} %copy.322), channel_id=1, source_target_pairs={{0,1},{2,3},{4,5},{6,7},{8,9},{10,11},{12,13},{14,15},{16,17},{18,... | collective-permute-start | bytes 24584 | tf_op jit(solution)/shard_map/ppermute | solution.py:19
  133.4 11.7 %collective-permute-start.19 = (f32[2,32,8,1]{1,2,3,0:T(8,128)}, f32[2,32,8,1]{1,2,3,0:T(8,128)S(1)}, u32[]{:S(2)}, u32[]{:S(2)}) collective-permute-start(f32[2,32,8,1]{1,2,3,0:T(8,128)} %fusion.103), channel_id=1, source_target_pairs={{4,0},{8,4},{12,8},{5,1},{9,5},{13,9},{6,2},{10,6},{14,10},{7,3},{... | collective-permute-start | bytes 6152 | tf_op jit(solution)/shard_map/ppermute | solution.py:19
  134.7 10.4 %collective-permute-start.18 = (f32[2,32,1,128]{1,2,3,0:T(1,128)}, f32[2,32,1,128]{1,2,3,0:T(1,128)}, u32[]{:S(2)}, u32[]{:S(2)}) collective-permute-start(f32[2,32,1,128]{1,2,3,0:T(1,128)} %fusion.95), channel_id=1, source_target_pairs={{2,0},{3,1},{6,4},{7,5},{10,8},{11,9},{14,12},{15,13},{18,16},{19,... | collective-permute-start | bytes 98312 | tf_op jit(solution)/shard_map/ppermute | solution.py:19
  138.1 4.9 %collective-permute-start.20 = (f32[2,1,8,128]{3,2,1,0:T(8,128)}, f32[2,1,8,128]{3,2,1,0:T(8,128)}, u32[]{:S(2)}, u32[]{:S(2)}) collective-permute-start(f32[2,1,8,128]{3,2,1,0:T(8,128)} %copy.324), channel_id=1, source_target_pairs={{1,0},{3,2},{5,4},{7,6},{9,8},{11,10},{13,12},{15,14},{17,16},{19,... | collective-permute-start | bytes 24584 | tf_op jit(solution)/shard_map/ppermute | solution.py:19
  157.8 20.0 %collective-permute-start.21 = (f32[2,32,8,1]{1,2,3,0:T(8,128)}, f32[2,32,8,1]{1,2,3,0:T(8,128)S(1)}, u32[]{:S(2)}, u32[]{:S(2)}) collective-permute-start(f32[2,32,8,1]{1,2,3,0:T(8,128)} %fusion.102), channel_id=1, source_target_pairs={{0,4},{4,8},{8,12},{1,5},{5,9},{9,13},{2,6},{6,10},{10,14},{3,7},{... | collective-permute-start | bytes 6152 | tf_op jit(solution)/shard_map/ppermute | solution.py:19
  162.4 15.4 %collective-permute-start.23 = (f32[2,32,1,128]{1,2,3,0:T(1,128)}, f32[2,32,1,128]{1,2,3,0:T(1,128)}, u32[]{:S(2)}, u32[]{:S(2)}) collective-permute-start(f32[2,32,1,128]{1,2,3,0:T(1,128)} %fusion.94), channel_id=1, source_target_pairs={{0,2},{1,3},{4,6},{5,7},{8,10},{9,11},{12,14},{13,15},{16,18},{17,... | collective-permute-start | bytes 98312 | tf_op jit(solution)/shard_map/ppermute | solution.py:19
  170.4 5.4 %collective-permute-start.22 = (f32[2,1,8,128]{3,2,1,0:T(8,128)}, f32[2,1,8,128]{3,2,1,0:T(8,128)}, u32[]{:S(2)}, u32[]{:S(2)}) collective-permute-start(f32[2,1,8,128]{3,2,1,0:T(8,128)} %copy.326), channel_id=1, source_target_pairs={{0,1},{2,3},{4,5},{6,7},{8,9},{10,11},{12,13},{14,15},{16,17},{18,... | collective-permute-start | bytes 24584 | tf_op jit(solution)/shard_map/ppermute | solution.py:19
  (46 other events, 139.1 us)
where the time goes:
time: 257 us; the launch traced here: 255 us
  other arithmetic  74.1 us (29%)
  starting transfers between devices  65.9 us (26%)
  blocking collectives  57.6 us (22%)
  local copies, waits for them, and re-layouts  51 us (20%)
  waiting for transfers between devices  3.35 us (1%)
    ppermute x24, starting transfers between devices, from_behind(): return lax.ppermute(block, axis, route)  65.9 us
    unnamed x1, blocking collectives  57.6 us
    ppermute x8, local copies, waits for them, and re-layouts, from_behind(): return lax.ppermute(block, axis, route)  13.4 us
    another operation x6, other arithmetic, forward_parts(): paired = jnp.stack([elec_z, elec_y])  12.4 us
    add x2, other arithmetic, per_device(): elec_z = elec_z + coefficient * (diff_x[1] - diff_y[1])  11.2 us
    unnamed x117, local copies, waits for them, and re-layouts  10.8 us
    sub x4, other arithmetic, backward_parts(): diff_z = jnp.diff(jnp.concatenate([before, paired], axis=1), axis=1)  9.4 us
    sub x4, other arithmetic, forward_parts(): diff_x = jnp.diff(jnp.concatenate([paired, beyond], axis=2), axis=2)  9.01 us
  transfers between devices with their start and end apart: 24, of which 3 were waited for; matrix products, arithmetic and copies ran while one was open for 17% of the time, Pallas kernels for 0%

commit v1 on v0

v1 whole, which is shorter than its diff:
```python
import functools

import jax
import jax.numpy as jnp
import numpy as np
from jax import lax
from jax.experimental import pallas as pl
from jax.experimental.pallas import tpu as pltpu
from jax.sharding import PartitionSpec as P

STEPS = 4
FREQ = 8
MATS = 8
PLEN = 64
PORT_TILE = 4
FIELDS = 7
DEPTH = STEPS

time_step = 0.5

VMEM = pl.BlockSpec(memory_space=pltpu.VMEM)
SMEM = pl.BlockSpec(memory_space=pltpu.SMEM)
PARAMS = pltpu.CompilerParams(vmem_limit_bytes=48 * 1024 * 1024)


def dft_basis():
    times = (np.arange(STEPS) + 1.0) * time_step
    omegas = np.pi * (np.arange(FREQ) + 1.0) / FREQ
    angle = times[:, None] * omegas[None, :]
    basis = np.zeros((8, 128), np.float32)
    basis[:STEPS, : 2 * FREQ] = np.concatenate([np.cos(angle), -np.sin(angle)], axis=1)
    return basis


def iota(shape, axis):
    return lax.broadcasted_iota(jnp.int32, shape, axis)


def pack_pair(first, second, up):
    low = iota((8, 128), 0) < DEPTH
    if up:
        return jnp.where(low, pltpu.roll(first, DEPTH, 0), second)
    return jnp.where(low, first, pltpu.roll(second, DEPTH, 0))


def pack_rows(pairs, row_size, out_refs):
    if row_size == 2:
        row = lax.axis_index("row")
        for up in (True, False):

            @pl.when(row == (0 if up else 1))
            def _(up=up):
                for i, (first, second) in enumerate(pairs):
                    out_refs[0][i] = pack_pair(first(), second(), up)
    else:
        for i, (first, second) in enumerate(pairs):
            out_refs[0][i] = pack_pair(first(), second(), True)
            out_refs[1][i] = pack_pair(first(), second(), False)


def unpack_pair(refs, i, row_size):
    low = iota((8, 128), 0) < DEPTH
    if row_size == 2:
        row = lax.axis_index("row")
        packed = refs[0][i]
        mine = (iota((8, 128), 0) < DEPTH) == (row == 0)
        turned = pltpu.roll(packed, DEPTH, 0)
        first = jnp.where(row == 0, packed, turned)
        second = jnp.where(row == 0, turned, packed)
        zero = jnp.zeros_like(packed)
        return jnp.where(mine, first, zero), jnp.where(mine, second, zero)
    below, above = refs[0][i], refs[1][i]
    first = jnp.where(low, above, pltpu.roll(below, DEPTH, 0))
    second = jnp.where(low, pltpu.roll(above, DEPTH, 0), below)
    return first, second


def pack_kernel(row_size, eps_ref, elec_ref, magn_ref, mat_ref, coef_ref, z_ref, up_ref, down_ref, *x_refs):
    layers = elec_ref.shape[1]
    gz = lax.axis_index("gz")
    for z in range(layers):
        material = mat_ref[z]
        eps = jnp.full((8, 128), eps_ref[0], jnp.float32)
        for which in range(1, MATS):
            eps = jnp.where(material == which, eps_ref[which], eps)
        coef_ref[z] = time_step * (1.0 / eps)

    def tile(field, z):
        if field < 3:
            return elec_ref[field, z]
        if field < 6:
            return magn_ref[field - 3, z]
        return coef_ref[z]

    start = jnp.where(gz == 0, layers - DEPTH, 0)
    for field in range(FIELDS):
        for k in range(DEPTH):
            z_ref[field * DEPTH + k] = tile(field, start + k)
    group = iota((8, 128), 1) // DEPTH
    for field in range(FIELDS):
        up = jnp.zeros((8, 128), jnp.float32)
        down = jnp.zeros((8, 128), jnp.float32)
        for z in range(layers):
            turned = pltpu.roll(tile(field, z), (DEPTH * (z + 1)) % 128, 1)
            up = jnp.where(group == z, turned, up)
            down = jnp.where(group == (z + 1) % layers, turned, down)
        up_ref[field] = up
        down_ref[field] = pltpu.roll(down, 128 - DEPTH, 1)
    pairs = [
        (functools.partial(tile, c, z), functools.partial(tile, c + 3, z))
        for c in range(3)
        for z in range(layers)
    ]
    pairs += [(functools.partial(tile, 6, z), functools.partial(tile, 6, z + layers // 2)) for z in range(layers // 2)]
    pack_rows(pairs, row_size, x_refs)


def corner_kernel(row_size, z_ref, y_ref, yz_ref, *x_refs):
    half = FIELDS * 2
    pairs = []
    for i in range(FIELDS * DEPTH):
        other = (y_ref, i) if i < half else (yz_ref, i - half)
        pairs.append((functools.partial(z_ref.__getitem__, i), functools.partial(other[0].__getitem__, other[1])))
    pack_rows(pairs, row_size, x_refs)


def fwd_y(main, side):
    last = iota((8, 128), 1) == 127
    a, b = pltpu.roll(main, 127, 1), pltpu.roll(side, 127, 1)
    return jnp.where(last, b, a) - main, jnp.where(last, a, b) - side


def bwd_y(main, side):
    first = iota((8, 128), 1) == 0
    a, b = pltpu.roll(main, 1, 1), pltpu.roll(side, 1, 1)
    return main - jnp.where(first, b, a), side - jnp.where(first, a, b)


def fwd_x(main, side):
    last = iota((8, 128), 0) == 7
    a, b = pltpu.roll(main, 7, 0), pltpu.roll(side, 7, 0)
    return jnp.where(last, b, a) - main, jnp.where(last, a, b) - side


def bwd_x(main, side):
    first = iota((8, 128), 0) == 0
    a, b = pltpu.roll(main, 1, 0), pltpu.roll(side, 1, 0)
    return main - jnp.where(first, b, a), side - jnp.where(first, a, b)


TILES = ((0, 0), (0, 1), (1, 0), (1, 1))


def diff(kind, tiles):
    out = {}
    if kind in (fwd_y, bwd_y):
        for r in range(2):
            out[r, 0], out[r, 1] = kind(tiles[r, 0], tiles[r, 1])
    else:
        for c in range(2):
            out[0, c], out[1, c] = kind(tiles[0, c], tiles[1, c])
    return out


def step_kernel(
    row_size, mode_ref, basis_ref, prow_ref, pcol_ref, pmode_ref, pid_ref,
    elec_ref, magn_ref, coef_ref, z_ref, y_ref, yz_ref, *rest,
):
    n_x = 1 if row_size == 2 else 2
    x_refs, corner_refs = rest[:n_x], rest[n_x : 2 * n_x]
    eout_ref, hout_ref, term_ref, field_ref, weight_ref, strip_ref, sum_ref = rest[2 * n_x :]
    layers = elec_ref.shape[1]
    extended = layers + DEPTH
    gz, row, col = (lax.axis_index(name) for name in ("gz", "row", "col"))
    lane, sub = iota((8, 128), 1), iota((8, 128), 0)

    def put(field, r, c, where, value):
        field_ref[field, where, 8 * r : 8 * r + 8, 128 * c : 128 * c + 128] = value

    def get(field, r, c, where):
        return field_ref[field, where, 8 * r : 8 * r + 8, 128 * c : 128 * c + 128]

    def assemble(gz_is):
        base = 1 + DEPTH * gz_is
        halo = 1 + layers * (1 - gz_is)
        far = 0 if gz_is == 0 else layers - DEPTH

        def side(low_tile, high_tile, z):
            low = pltpu.roll(low_tile, (128 - DEPTH - DEPTH * z) % 128, 1)
            high = pltpu.roll(high_tile, (128 - DEPTH * z) % 128, 1)
            return jnp.where(lane < 64, high, low)

        corner = {}
        for i in range(FIELDS * DEPTH):
            first, second = unpack_pair(corner_refs, i, row_size)
            corner["z", i] = first
            corner["y" if i < 2 * FIELDS else "yz", i % (2 * FIELDS)] = second
        for field in range(FIELDS):
            for c in (0, 1):
                put(field, 0, c, 0, jnp.zeros((8, 128), jnp.float32))
                put(field, 1, c, 0, jnp.zeros((8, 128), jnp.float32))
                put(field, 0, c, extended + 1, jnp.zeros((8, 128), jnp.float32))
                put(field, 1, c, extended + 1, jnp.zeros((8, 128), jnp.float32))
            for z in range(layers):
                if field < 3:
                    main = elec_ref[field, z]
                elif field < 6:
                    main = magn_ref[field - 3, z]
                else:
                    main = coef_ref[z]
                put(field, 0, 0, base + z, main)
                put(field, 0, 1, base + z, side(y_ref[field], y_ref[FIELDS + field], z))
                put(field, 1, 1, base + z, side(corner["y", field], corner["y", FIELDS + field], z))
            for k in range(DEPTH):
                i = field * DEPTH + k
                put(field, 0, 0, halo + k, z_ref[i])
                put(field, 0, 1, halo + k, side(yz_ref[field], yz_ref[FIELDS + field], far + k))
                put(field, 1, 0, halo + k, corner["z", i])
                put(field, 1, 1, halo + k, side(corner["yz", field], corner["yz", FIELDS + field], far + k))
        for c in range(3):
            for z in range(layers):
                first, second = unpack_pair(x_refs, c * layers + z, row_size)
                put(c, 1, 0, base + z, first)
                put(c + 3, 1, 0, base + z, second)
        for z in range(layers // 2):
            first, second = unpack_pair(x_refs, 3 * layers + z, row_size)
            put(6, 1, 0, base + z, first)
            put(6, 1, 0, base + z + layers // 2, second)
        for k in range(PORT_TILE):
            weight_ref[k] = jnp.zeros(weight_ref.shape[1:], jnp.float32)
            strip_ref[...] = jnp.zeros(strip_ref.shape, jnp.float32)
            strip_ref[:, :PLEN] = mode_ref[pmode_ref[0, 0, k]]
            moved = pltpu.roll(strip_ref[...], pcol_ref[0, 0, k], 1)
            weight_ref[k, DEPTH * gz_is : DEPTH * gz_is + layers, :] = moved

    for gz_is in (0, 1):
        pl.when(gz == gz_is)(functools.partial(assemble, gz_is))

    half = jnp.full((8, 128), time_step, jnp.float32)
    below = jnp.where((sub >= 4) & (row == 0), 0.0, half)
    before = jnp.where((lane >= 64) & (col == 0), 0.0, half)
    ch = {(0, 0): half, (0, 1): before, (1, 0): below, (1, 1): jnp.minimum(below, before)}

    def step(n, carry):
        hx_prev = {t: jnp.zeros((8, 128), jnp.float32) for t in TILES}
        hy_prev = dict(hx_prev)
        ex = {t: get(0, *t, 1) for t in TILES}
        ey = {t: get(1, *t, 1) for t in TILES}
        acc = [jnp.zeros((8, 128), jnp.float32) for _ in range(PORT_TILE)]
        for j in range(extended):
            at = j + 1
            ez = {t: get(2, *t, at) for t in TILES}
            ex_next = {t: get(0, *t, at + 1) for t in TILES}
            ey_next = {t: get(1, *t, at + 1) for t in TILES}
            dy_ez, dx_ez = diff(fwd_y, ez), diff(fwd_x, ez)
            dx_ey, dy_ex = diff(fwd_x, ey), diff(fwd_y, ex)
            hx, hy, hz = {}, {}, {}
            for t in TILES:
                hx[t] = get(3, *t, at) - ch[t] * (dy_ez[t] - (ey_next[t] - ey[t]))
                hy[t] = get(4, *t, at) - ch[t] * ((ex_next[t] - ex[t]) - dx_ez[t])
                hz[t] = get(5, *t, at) - ch[t] * (dx_ey[t] - dy_ex[t])
                put(3, *t, at, hx[t])
                put(4, *t, at, hy[t])
                put(5, *t, at, hz[t])
            dy_hz, dx_hz = diff(bwd_y, hz), diff(bwd_x, hz)
            dx_hy, dy_hx = diff(bwd_x, hy), diff(bwd_y, hx)
            for t in TILES:
                ce = get(6, *t, at)
                put(0, *t, at, ex[t] + ce * (dy_hz[t] - (hy[t] - hy_prev[t])))
                put(1, *t, at, ey[t] + ce * ((hx[t] - hx_prev[t]) - dx_hz[t]))
                new = ez[t] + ce * (dx_hy[t] - dy_hx[t])
                put(2, *t, at, new)
                if t == (0, 0):
                    acc = [acc[k] + new * weight_ref[k, j : j + 1, :] for k in range(PORT_TILE)]
            hx_prev, hy_prev, ex, ey = hx, hy, ex_next, ey_next
        for k in range(PORT_TILE):
            chosen = jnp.where(sub == prow_ref[0, 0, k], acc[k], 0.0)
            sum_ref[n, k : k + 1, :] = jnp.sum(chosen, axis=0, keepdims=True)
        return carry

    lax.fori_loop(0, STEPS, step, 0)

    transform = jnp.zeros((8, 128), jnp.float32)
    for n in range(STEPS):
        sampled = jnp.sum(sum_ref[n], axis=1, keepdims=True)
        transform = transform + sampled * basis_ref[n : n + 1, :]
    per_row = 128 // (2 * FREQ)
    place = iota(term_ref.shape, 0)
    term = jnp.zeros(term_ref.shape, jnp.float32)
    for k in range(PORT_TILE):
        port = pid_ref[0, 0, k]
        spread = jnp.broadcast_to(transform[k : k + 1, :], (8, 128))
        spread = pltpu.roll(spread, (port % per_row) * (2 * FREQ), 1)
        spread = jnp.concatenate([spread] * (term_ref.shape[0] // 8), axis=0)
        term = term + jnp.where(place == port // per_row, spread, 0.0)
    term_ref[...] = term

    for gz_is in (0, 1):

        @pl.when(gz == gz_is)
        def _(gz_is=gz_is):
            base = 1 + DEPTH * gz_is
            for c in range(3):
                eout_ref[c] = field_ref[c, base : base + layers, 0:8, 0:128]
                hout_ref[c] = field_ref[c + 3, base : base + layers, 0:8, 0:128]


def shifted(block, axis, size, distance):
    route = [(i - distance, i) for i in range(size) if 0 <= i - distance < size]
    return lax.ppermute(block, axis, route)


def swapped(block, axis, size, bit=1):
    return lax.ppermute(block, axis, [(i, i ^ bit) for i in range(size)])


def solution(mesh):
    sizes = dict(mesh.shape)
    row_size, col_size, gz_size = sizes["row"], sizes["col"], sizes["gz"]

    def across_rows(blocks):
        if row_size == 2:
            return (swapped(blocks[0], "row", 2),)
        return (shifted(blocks[0], "row", row_size, 1), shifted(blocks[1], "row", row_size, -1))

    def per_device(
        electric, magnetic, material, eps_table, mode_table, port_row, port_col, port_mode, port_ids
    ):
        layers, rows_dev, cols_dev = material.shape
        f32 = jnp.float32
        n_x = 1 if row_size == 2 else 2
        n_pairs = 3 * layers + layers // 2
        n_corner = FIELDS * DEPTH
        packed = pl.pallas_call(
            functools.partial(pack_kernel, row_size),
            out_shape=[
                jax.ShapeDtypeStruct(material.shape, f32),
                jax.ShapeDtypeStruct((FIELDS * DEPTH, 8, 128), f32),
                jax.ShapeDtypeStruct((FIELDS, 8, 128), f32),
                jax.ShapeDtypeStruct((FIELDS, 8, 128), f32),
            ]
            + [jax.ShapeDtypeStruct((n_pairs, 8, 128), f32)] * n_x,
            in_specs=[SMEM, VMEM, VMEM, VMEM],
            out_specs=[VMEM] * (4 + n_x),
            compiler_params=PARAMS,
            name="pack",
        )(eps_table, electric, magnetic, material)
        coef, z_send, up_send, down_send = packed[:4]
        x_halo = across_rows(packed[4:])
        low = shifted(up_send, "col", col_size, 1)
        high = shifted(down_send, "col", col_size, -1)
        z_halo = swapped(z_send, "gz", gz_size)
        y_halo = jnp.concatenate([low, high])
        yz_halo = swapped(y_halo, "gz", gz_size)
        corner_send = pl.pallas_call(
            functools.partial(corner_kernel, row_size),
            out_shape=[jax.ShapeDtypeStruct((n_corner, 8, 128), f32)] * n_x,
            in_specs=[VMEM] * 3,
            out_specs=[VMEM] * n_x,
            compiler_params=PARAMS,
            name="corners",
        )(z_halo, y_halo, yz_halo)
        corner = across_rows(corner_send)
        total_ports = PORT_TILE * col_size * row_size
        term_rows = max(8, total_ports * 2 * FREQ // 128)
        electric_out, magnetic_out, term = pl.pallas_call(
            functools.partial(step_kernel, row_size),
            out_shape=[
                jax.ShapeDtypeStruct(electric.shape, f32),
                jax.ShapeDtypeStruct(magnetic.shape, f32),
                jax.ShapeDtypeStruct((term_rows, 128), f32),
            ],
            in_specs=[VMEM] * 2 + [SMEM] * 4 + [VMEM] * (6 + 2 * n_x),
            out_specs=[VMEM] * 3,
            scratch_shapes=[
                pltpu.VMEM((FIELDS, layers + DEPTH + 2, 16, 256), f32),
                pltpu.VMEM((PORT_TILE, layers + 8, 128), f32),
                pltpu.VMEM((layers, 128), f32),
                pltpu.VMEM((STEPS, 8, 128), f32),
            ],
            compiler_params=PARAMS,
            name="steps",
        )(
            mode_table, jnp.asarray(dft_basis()), port_row, port_col, port_mode, port_ids,
            electric, magnetic, coef, z_halo, y_halo, yz_halo, *x_halo, *corner,
        )
        for axis in ("gz", "row", "col"):
            bit = 1
            while bit < sizes[axis]:
                term = term + swapped(term, axis, sizes[axis], bit)
                bit *= 2
        mine = (lax.axis_index("col") * row_size + lax.axis_index("row")) * gz_size + lax.axis_index("gz")
        own = total_ports // (col_size * row_size * gz_size)
        per_row = 128 // (own * 2 * FREQ)
        cut = lax.dynamic_slice(
            term, (mine // per_row, (mine % per_row) * own * 2 * FREQ), (1, own * 2 * FREQ)
        )
        return (electric_out, magnetic_out, cut.reshape(own, 2 * FREQ))

    in_specs = (
        P(None, "gz", "row", ("grp", "col")),
        P(None, "gz", "row", ("grp", "col")),
        P("gz", "row", ("grp", "col")),
        P(),
        P(None, "gz", None),
        P(("grp", "row"), "col", None),
        P(("grp", "row"), "col", None),
        P(("grp", "row"), "col", None),
        P(("grp", "row"), "col", None),
    )
    out_specs = (
        P(None, "gz", "row", ("grp", "col")),
        P(None, "gz", "row", ("grp", "col")),
        P(("grp", "col", "row", "gz"), None),
    )
    return jax.shard_map(
        per_device, mesh=mesh, in_specs=in_specs, out_specs=out_specs, check_vma=False
    )
```

time: 257 us -> 51.7 us (0.20)
  other arithmetic: 74.1 us -> 0.01 us
  blocking collectives: 57.6 us -> 0 us
  starting transfers between devices: 65.9 us -> 13.1 us
  local copies, waits for them, and re-layouts: 51 us -> 4.33 us
  waiting for transfers between devices: 3.35 us -> 18.5 us
  Pallas kernels: 0 us -> 14.6 us
    unnamed x1 -> x0, blocking collectives: 57.6 us -> none
    ppermute x24 -> x10, starting transfers between devices: 65.9 us -> 13.1 us  [the longest x8 8.36 us: swapped(): return lax.ppermute(block, axis, [(i, i ^ bit) for i in range(size)])]
    another operation x29 -> x0, other arithmetic: 33.1 us -> none  [the longest x6 12.4 us: forward_parts(): paired = jnp.stack([elec_z, elec_y])]
    sub x12 -> x0, other arithmetic: 20.5 us -> none  [the longest x4 9.4 us: backward_parts(): diff_z = jnp.diff(jnp.concatenate([before, paired], axis=1), axis=1)]
    add x3 -> x4, other arithmetic: 16.8 us -> 0.01 us  [per_device(): term = term + swapped(term, axis, sizes[axis], bit)]
    slice x11 -> x0, local copies, waits for them, and re-layouts: 16.4 us -> none  [the longest x4 8 us: backward_parts(): before = from_behind(paired[:, -1:], 'gz', 1)]
    ppermute x24 -> x10, waiting for transfers between devices: 3.35 us -> 18.5 us  [the longest x8 14.1 us: swapped(): return lax.ppermute(block, axis, [(i, i ^ bit) for i in range(size)])]
    pallas_call x0 -> x3, Pallas kernels: none -> 14.6 us  [the longest x1 13.5 us: per_device(): pl.pallas_call(functools.partial(step_kernel, row_size), out_shape=[jax.S...]
  transfers between devices with their start and end apart: 24 -> 10, of which waited for: 3 -> 8; matrix products, arithmetic and copies ran while one was open for 17% -> 0% of each run, Pallas kernels for 0% -> 0%
where the time goes in v1:
time: 51.7 us; the launch traced here: 51.4 us
  waiting for transfers between devices  18.5 us (36%)
  Pallas kernels  14.6 us (28%)
  starting transfers between devices  13.1 us (25%)
  local copies, waits for them, and re-layouts  4.33 us (8%)
  between operations  0.78 us (2%)
    ppermute x8, waiting for transfers between devices, swapped(): return lax.ppermute(block, axis, [(i, i ^ bit) for i in range(size)])  14.1 us
    pallas_call x1, Pallas kernels, per_device(): pl.pallas_call(functools.partial(step_kernel, row_size), out_shape=[jax.S...  13.5 us
    ppermute x8, starting transfers between devices, swapped(): return lax.ppermute(block, axis, [(i, i ^ bit) for i in range(size)])  8.36 us
    ppermute x2, starting transfers between devices, shifted(): return lax.ppermute(block, axis, route)  4.76 us
    ppermute x2, waiting for transfers between devices, shifted(): return lax.ppermute(block, axis, route)  4.38 us
    unnamed x25, local copies, waits for them, and re-layouts  3.59 us
    pallas_call x1, Pallas kernels, per_device(): pl.pallas_call(functools.partial(pack_kernel, row_size), out_shape=[jax.S...  1.12 us
  transfers between devices with their start and end apart: 10, of which 8 were waited for; matrix products, arithmetic and copies ran while one was open for 0% of the time, Pallas kernels for 0%

profile of v1, /device:TPU:0, one launch (start us, length us, event | category | flops | bytes accessed | tf_op | source)
XLA Modules:
  0.0 51.4 jit_solution(14390700071763668399)
XLA Ops:
  0.6 0.0 copy-start
  0.6 1.0 %copy-done = f32[3,32,8,128]{3,2,1,0:T(8,128)S(1)} copy-done((f32[3,32,8,128]{3,2,1,0:T(8,128)S(1)}, f32[3,32,8,128]{3,2,1,0:T(8,128)}, u32[]{:S(2)}) %copy-start) | copy-done | bytes 393240
  1.6 1.0 %copy-done.2 = f32[3,32,8,128]{3,2,1,0:T(8,128)S(1)} copy-done((f32[3,32,8,128]{3,2,1,0:T(8,128)S(1)}, f32[3,32,8,128]{3,2,1,0:T(8,128)}, u32[]{:S(2)}) %copy-start.2) | copy-done | bytes 393240
  2.6 0.9 %copy-done.4 = s32[32,8,128]{2,1,0:T(8,128)S(1)} copy-done((s32[32,8,128]{2,1,0:T(8,128)S(1)}, s32[32,8,128]{2,1,0:T(8,128)}, u32[]{:S(2)}) %copy-start.4) | copy-done | bytes 131096
  3.5 0.7 %copy-done.7 = f32[8]{0:T(128)S(1)} copy-done((f32[8]{0:T(128)S(1)}, f32[8]{0:T(128)}, u32[]{:S(2)}) %copy-start.7) | copy-done | bytes 56
  4.2 1.1 %pack.1 = (f32[32,8,128]{2,1,0:T(8,128)S(1)}, f32[28,8,128]{2,1,0:T(8,128)S(1)}, f32[7,8,128]{2,1,0:T(8,128)S(1)}, f32[7,8,128]{2,1,0:T(8,128)S(1)}, f32[112,8,128]{2,1,0:T(8,128)S(1)}) custom-call(f32[8]{0:T(128)S(1)} %copy-done.7, f32[3,32,8,128]{3,2,1,0:T(8,128)S(1)} %copy-done, f32[3,32,8,128]{3,2,1,0:T(8,128)S(1)} %copy-done.2, s32[32,8,128]{2,1,0:T(8,128)S(1)} %copy-done.4), custom_call_target="tpu_custom_call" | custom-call | tf_op jit(solution)/shard_map/pack/pallas_call | solution.py:334
  5.3 0.0 copy-start.1
  5.3 3.0 %collective-permute-start.4 = (f32[112,8,128]{2,1,0:T(8,128)S(1)}, f32[112,8,128]{2,1,0:T(8,128)S(1)}, u32[]{:S(2)}, u32[]{:S(2)}) collective-permute-start(f32[112,8,128]{2,1,0:T(8,128)S(1)} %get-tuple-element.15), channel_id=1, source_target_pairs={{0,2},{2,0},{1,3},{3,1},{4,6},{6,4},{5,7},{7,5},{8,10},{10,8},{9,1... | collective-permute-start | bytes 1376264 | tf_op jit(solution)/shard_map/ppermute | solution.py:314
  8.4 3.5 %collective-permute-start.1 = (f32[7,8,128]{2,1,0:T(8,128)S(1)}, f32[7,8,128]{2,1,0:T(8,128)S(1)}, u32[]{:S(2)}, u32[]{:S(2)}) collective-permute-start(f32[7,8,128]{2,1,0:T(8,128)S(1)} %get-tuple-element.13), channel_id=1, source_target_pairs={{0,4},{4,8},{8,12},{1,5},{5,9},{9,13},{2,6},{6,10},{10,14},{3,7},{... | collective-permute-start | bytes 86024 | tf_op jit(solution)/shard_map/ppermute | solution.py:310
  11.8 1.3 %collective-permute-start.2 = (f32[7,8,128]{2,1,0:T(8,128)S(1)}, f32[7,8,128]{2,1,0:T(8,128)S(1)}, u32[]{:S(2)}, u32[]{:S(2)}) collective-permute-start(f32[7,8,128]{2,1,0:T(8,128)S(1)} %get-tuple-element.14), channel_id=1, source_target_pairs={{4,0},{8,4},{12,8},{5,1},{9,5},{13,9},{6,2},{10,6},{14,10},{7,3},{... | collective-permute-start | bytes 86024 | tf_op jit(solution)/shard_map/ppermute | solution.py:310
  13.1 0.1 collective-permute-start
  13.2 0.2 collective-permute-done.1
  13.4 4.2 %collective-permute-done.2 = f32[7,8,128]{2,1,0:T(8,128)S(1)} collective-permute-done((f32[7,8,128]{2,1,0:T(8,128)S(1)}, f32[7,8,128]{2,1,0:T(8,128)S(1)}, u32[]{:S(2)}, u32[]{:S(2)}) %collective-permute-start.2) | collective-permute-done | bytes 28704 | tf_op jit(solution)/shard_map/ppermute | solution.py:310
  17.6 0.0 collective-permute-start.3
  17.6 1.2 %collective-permute-done.3.yz_ref = f32[14,8,128]{2,1,0:T(8,128)S(1)} collective-permute-done((f32[14,8,128]{2,1,0:T(8,128)S(1)}, f32[14,8,128]{2,1,0:T(8,128)S(1)}, u32[]{:S(2)}, u32[]{:S(2)}) %collective-permute-start.3) | collective-permute-done | bytes 57376 | tf_op jit(solution)/shard_map/ppermute | solution.py:314
  18.8 0.0 collective-permute-done.z_ref
  18.9 0.0 copy-start.8
  18.9 0.0 copy-start.9
  18.9 0.0 copy-start.10
  18.9 0.6 %collective-permute-start.5 = (f32[28,8,128]{2,1,0:T(8,128)S(1)}, f32[28,8,128]{2,1,0:T(8,128)S(1)}, u32[]{:S(2)}, u32[]{:S(2)}) collective-permute-start(f32[28,8,128]{2,1,0:T(8,128)S(1)} %corners.1), channel_id=1, source_target_pairs={{0,2},{2,0},{1,3},{3,1},{4,6},{6,4},{5,7},{7,5},{8,10},{10,8},{9,1... | collective-permute-start | bytes 344072 | tf_op jit(solution)/shard_map/ppermute | solution.py:314
  19.5 4.7 %collective-permute-done.5.rest_1_ = f32[28,8,128]{2,1,0:T(8,128)S(1)} collective-permute-done((f32[28,8,128]{2,1,0:T(8,128)S(1)}, f32[28,8,128]{2,1,0:T(8,128)S(1)}, u32[]{:S(2)}, u32[]{:S(2)}) %collective-permute-start.5) | collective-permute-done | bytes 114720 | tf_op jit(solution)/shard_map/ppermute | solution.py:314
  24.2 0.0 collective-permute-done.4.rest_0_
  24.3 13.5 %steps.1 = (f32[3,32,8,128]{3,2,1,0:T(8,128)}, f32[3,32,8,128]{3,2,1,0:T(8,128)}, f32[8,128]{1,0:T(8,128)S(1)}) custom-call(f32[8,32,64]{2,1,0:T(8,128)S(1)} %copy-done.5, f32[8,128]{1,0:T(8,128)S(1)} %copy-done.6, s32[1,1,4]{2,1,0:T(1,128)S(1)} %copy-done.8, s32[1,1,4]{2,1,0:T(1,128)S(1)} %copy-done.9, s32[1,1,4]{2,1,0:T(1,128)S(1)} %copy-done.10, ...), custom_call_target="tpu_custom_call" | custom-call | tf_op jit(solution)/shard_map/steps/pallas_call | solution.py:366
  37.7 1.2 %collective-permute-done.6 = f32[8,128]{1,0:T(8,128)S(1)} collective-permute-done((f32[8,128]{1,0:T(8,128)S(1)}, f32[8,128]{1,0:T(8,128)S(1)}, u32[]{:S(2)}, u32[]{:S(2)}) %collective-permute-start.6) | collective-permute-done | bytes 4128 | tf_op jit(solution)/shard_map/ppermute | solution.py:314
  38.9 0.5 collective-permute-start.7
  39.4 3.1 %collective-permute-done.7 = f32[8,128]{1,0:T(8,128)S(1)} collective-permute-done((f32[8,128]{1,0:T(8,128)S(1)}, f32[8,128]{1,0:T(8,128)S(1)}, u32[]{:S(2)}, u32[]{:S(2)}) %collective-permute-start.7) | collective-permute-done | bytes 4128 | tf_op jit(solution)/shard_map/ppermute | solution.py:314
  42.5 1.6 %collective-permute-start.8 = (f32[8,128]{1,0:T(8,128)S(1)}, f32[8,128]{1,0:T(8,128)S(1)}, u32[]{:S(2)}, u32[]{:S(2)}) collective-permute-start(f32[8,128]{1,0:T(8,128)S(1)} %add.30), channel_id=1, source_target_pairs={{0,4},{4,0},{8,12},{12,8},{1,5},{5,1},{9,13},{13,9},{2,6},{6,2},{1... | collective-permute-start | bytes 12296 | tf_op jit(solution)/shard_map/ppermute | solution.py:314
  44.1 2.0 %collective-permute-done.8 = f32[8,128]{1,0:T(8,128)S(1)} collective-permute-done((f32[8,128]{1,0:T(8,128)S(1)}, f32[8,128]{1,0:T(8,128)S(1)}, u32[]{:S(2)}, u32[]{:S(2)}) %collective-permute-start.8) | collective-permute-done | bytes 4128 | tf_op jit(solution)/shard_map/ppermute | solution.py:314
  46.1 2.6 %collective-permute-start.9 = (f32[8,128]{1,0:T(8,128)S(1)}, f32[8,128]{1,0:T(8,128)S(1)}, u32[]{:S(2)}, u32[]{:S(2)}) collective-permute-start(f32[8,128]{1,0:T(8,128)S(1)} %add.31), channel_id=1, source_target_pairs={{0,8},{4,12},{8,0},{12,4},{1,9},{5,13},{9,1},{13,5},{2,10},{6,14},... | collective-permute-start | bytes 12296 | tf_op jit(solution)/shard_map/ppermute | solution.py:314
  48.7 1.9 %collective-permute-done.9 = f32[8,128]{1,0:T(8,128)S(1)} collective-permute-done((f32[8,128]{1,0:T(8,128)S(1)}, f32[8,128]{1,0:T(8,128)S(1)}, u32[]{:S(2)}, u32[]{:S(2)}) %collective-permute-start.9) | collective-permute-done | bytes 4128 | tf_op jit(solution)/shard_map/ppermute | solution.py:314
  50.6 0.1 dynamic-slice_reduce_fusion
  50.7 0.6 %reshape.9 = f32[2,16]{1,0:T(2,128)} reshape(f32[32]{0:T(128)S(1)} %dynamic-slice_reduce_fusion) | data formatting | bytes 256 | tf_op jit(solution)/shard_map/reshape | solution.py:398
  (23 shorter events, 0.1 us)
Async XLA Ops:
  0.6 1.0 %copy-start = (f32[3,32,8,128]{3,2,1,0:T(8,128)S(1)}, f32[3,32,8,128]{3,2,1,0:T(8,128)}, u32[]{:S(2)}) copy-start(f32[3,32,8,128]{3,2,1,0:T(8,128)} %elec_ref.3) | copy-start | bytes 1179652
  1.6 1.0 %copy-start.2 = (f32[3,32,8,128]{3,2,1,0:T(8,128)S(1)}, f32[3,32,8,128]{3,2,1,0:T(8,128)}, u32[]{:S(2)}) copy-start(f32[3,32,8,128]{3,2,1,0:T(8,128)} %magn_ref.3) | copy-start | bytes 1179652
  2.6 0.9 %copy-start.4 = (s32[32,8,128]{2,1,0:T(8,128)S(1)}, s32[32,8,128]{2,1,0:T(8,128)}, u32[]{:S(2)}) copy-start(s32[32,8,128]{2,1,0:T(8,128)} %mat_ref.1) | copy-start | bytes 393220
  3.5 0.7 %copy-start.7 = (f32[8]{0:T(128)S(1)}, f32[8]{0:T(128)}, u32[]{:S(2)}) copy-start(f32[8]{0:T(128)} %eps_ref.1) | copy-start | bytes 100
  4.2 20.0 %copy-start.3 = (f32[3,32,8,128]{3,2,1,0:T(8,128)S(1)}, f32[3,32,8,128]{3,2,1,0:T(8,128)}, u32[]{:S(2)}) copy-start(f32[3,32,8,128]{3,2,1,0:T(8,128)} %magn_ref.3) | copy-start | bytes 1179652
  4.2 20.0 %copy-start.5 = (f32[8,32,64]{2,1,0:T(8,128)S(1)}, f32[8,32,64]{2,1,0:T(8,128)}, u32[]{:S(2)}) copy-start(f32[8,32,64]{2,1,0:T(8,128)} %mode_ref.1) | copy-start | bytes 196612
  5.3 18.9 %copy-start.1 = (f32[3,32,8,128]{3,2,1,0:T(8,128)S(1)}, f32[3,32,8,128]{3,2,1,0:T(8,128)}, u32[]{:S(2)}) copy-start(f32[3,32,8,128]{3,2,1,0:T(8,128)} %elec_ref.3) | copy-start | bytes 1179652
  5.3 18.9 %collective-permute-start.4 = (f32[112,8,128]{2,1,0:T(8,128)S(1)}, f32[112,8,128]{2,1,0:T(8,128)S(1)}, u32[]{:S(2)}, u32[]{:S(2)}) collective-permute-start(f32[112,8,128]{2,1,0:T(8,128)S(1)} %get-tuple-element.15), channel_id=1, source_target_pairs={{0,2},{2,0},{1,3},{3,1},{4,6},{6,4},{5,7},{7,5},{8,10},{10,8},{9,1... | collective-permute-start | bytes 1376264 | tf_op jit(solution)/shard_map/ppermute | solution.py:314
  8.4 5.0 %collective-permute-start.1 = (f32[7,8,128]{2,1,0:T(8,128)S(1)}, f32[7,8,128]{2,1,0:T(8,128)S(1)}, u32[]{:S(2)}, u32[]{:S(2)}) collective-permute-start(f32[7,8,128]{2,1,0:T(8,128)S(1)} %get-tuple-element.13), channel_id=1, source_target_pairs={{0,4},{4,8},{8,12},{1,5},{5,9},{9,13},{2,6},{6,10},{10,14},{3,7},{... | collective-permute-start | bytes 86024 | tf_op jit(solution)/shard_map/ppermute | solution.py:310
  11.8 5.8 %collective-permute-start.2 = (f32[7,8,128]{2,1,0:T(8,128)S(1)}, f32[7,8,128]{2,1,0:T(8,128)S(1)}, u32[]{:S(2)}, u32[]{:S(2)}) collective-permute-start(f32[7,8,128]{2,1,0:T(8,128)S(1)} %get-tuple-element.14), channel_id=1, source_target_pairs={{4,0},{8,4},{12,8},{5,1},{9,5},{13,9},{6,2},{10,6},{14,10},{7,3},{... | collective-permute-start | bytes 86024 | tf_op jit(solution)/shard_map/ppermute | solution.py:310
  13.1 5.7 %collective-permute-start = (f32[28,8,128]{2,1,0:T(8,128)S(1)}, f32[28,8,128]{2,1,0:T(8,128)S(1)}, u32[]{:S(2)}, u32[]{:S(2)}) collective-permute-start(f32[28,8,128]{2,1,0:T(8,128)S(1)} %get-tuple-element.12), channel_id=1, source_target_pairs={{0,1},{1,0},{2,3},{3,2},{4,5},{5,4},{6,7},{7,6},{8,9},{9,8},{10,11... | collective-permute-start | bytes 344072 | tf_op jit(solution)/shard_map/ppermute | solution.py:314
  17.6 1.2 %collective-permute-start.3 = (f32[14,8,128]{2,1,0:T(8,128)S(1)}, f32[14,8,128]{2,1,0:T(8,128)S(1)}, u32[]{:S(2)}, u32[]{:S(2)}) collective-permute-start(f32[14,8,128]{2,1,0:T(8,128)S(1)} %constant_dynamic-update-slice_fusion.y_ref), channel_id=1, source_target_pairs={{0,1},{1,0},{2,3},{3,2},{4,5},{5,4},{6,7},{7,6},{8,9},{9,8},{10,11... | collective-permute-start | bytes 172040 | tf_op jit(solution)/shard_map/ppermute | solution.py:314
  18.8 5.4 %copy-start.6 = (f32[8,128]{1,0:T(8,128)S(1)}, f32[8,128]{1,0:T(8,128)}, u32[]{:S(2)}) copy-start(f32[8,128]{1,0:T(8,128)} %constant.48.clone.basis_ref) | copy-start | bytes 12292
  18.8 5.4 %copy-start.11 = (s32[1,1,4]{2,1,0:T(1,128)S(1)}, s32[1,1,4]{2,1,0:T(1,128)}, u32[]{:S(2)}) copy-start(s32[1,1,4]{2,1,0:T(1,128)} %pid_ref.1) | copy-start | bytes 52
  18.9 5.3 %copy-start.8 = (s32[1,1,4]{2,1,0:T(1,128)S(1)}, s32[1,1,4]{2,1,0:T(1,128)}, u32[]{:S(2)}) copy-start(s32[1,1,4]{2,1,0:T(1,128)} %prow_ref.1) | copy-start | bytes 52
  18.9 5.3 %copy-start.9 = (s32[1,1,4]{2,1,0:T(1,128)S(1)}, s32[1,1,4]{2,1,0:T(1,128)}, u32[]{:S(2)}) copy-start(s32[1,1,4]{2,1,0:T(1,128)} %pcol_ref.1) | copy-start | bytes 52
  18.9 5.3 %copy-start.10 = (s32[1,1,4]{2,1,0:T(1,128)S(1)}, s32[1,1,4]{2,1,0:T(1,128)}, u32[]{:S(2)}) copy-start(s32[1,1,4]{2,1,0:T(1,128)} %pmode_ref.1) | copy-start | bytes 52
  18.9 5.3 %collective-permute-start.5 = (f32[28,8,128]{2,1,0:T(8,128)S(1)}, f32[28,8,128]{2,1,0:T(8,128)S(1)}, u32[]{:S(2)}, u32[]{:S(2)}) collective-permute-start(f32[28,8,128]{2,1,0:T(8,128)S(1)} %corners.1), channel_id=1, source_target_pairs={{0,2},{2,0},{1,3},{3,1},{4,6},{6,4},{5,7},{7,5},{8,10},{10,8},{9,1... | collective-permute-start | bytes 344072 | tf_op jit(solution)/shard_map/ppermute | solution.py:314
  37.7 1.2 %collective-permute-start.6 = (f32[8,128]{1,0:T(8,128)S(1)}, f32[8,128]{1,0:T(8,128)S(1)}, u32[]{:S(2)}, u32[]{:S(2)}) collective-permute-start(f32[8,128]{1,0:T(8,128)S(1)} %get-tuple-element.18), channel_id=1, source_target_pairs={{0,1},{1,0},{2,3},{3,2},{4,5},{5,4},{6,7},{7,6},{8,9},{9,8},{10,11... | collective-permute-start | bytes 12296 | tf_op jit(solution)/shard_map/ppermute | solution.py:314
  38.9 3.6 %collective-permute-start.7 = (f32[8,128]{1,0:T(8,128)S(1)}, f32[8,128]{1,0:T(8,128)S(1)}, u32[]{:S(2)}, u32[]{:S(2)}) collective-permute-start(f32[8,128]{1,0:T(8,128)S(1)} %add.29), channel_id=1, source_target_pairs={{0,2},{2,0},{1,3},{3,1},{4,6},{6,4},{5,7},{7,5},{8,10},{10,8},{9,1... | collective-permute-start | bytes 12296 | tf_op jit(solution)/shard_map/ppermute | solution.py:314
  42.5 3.6 %collective-permute-start.8 = (f32[8,128]{1,0:T(8,128)S(1)}, f32[8,128]{1,0:T(8,128)S(1)}, u32[]{:S(2)}, u32[]{:S(2)}) collective-permute-start(f32[8,128]{1,0:T(8,128)S(1)} %add.30), channel_id=1, source_target_pairs={{0,4},{4,0},{8,12},{12,8},{1,5},{5,1},{9,13},{13,9},{2,6},{6,2},{1... | collective-permute-start | bytes 12296 | tf_op jit(solution)/shard_map/ppermute | solution.py:314
  46.1 4.5 %collective-permute-start.9 = (f32[8,128]{1,0:T(8,128)S(1)}, f32[8,128]{1,0:T(8,128)S(1)}, u32[]{:S(2)}, u32[]{:S(2)}) collective-permute-start(f32[8,128]{1,0:T(8,128)S(1)} %add.31), channel_id=1, source_target_pairs={{0,8},{4,12},{8,0},{12,4},{1,9},{5,13},{9,1},{13,5},{2,10},{6,14},... | collective-permute-start | bytes 12296 | tf_op jit(solution)/shard_map/ppermute | solution.py:314

commit v2 on v1

--- a/solution.py
+++ b/solution.py
@@ -75,7 +75,15 @@
     return first, second
 
 
-def pack_kernel(row_size, eps_ref, elec_ref, magn_ref, mat_ref, coef_ref, z_ref, up_ref, down_ref, *x_refs):
+def pack_kernel(row_size, *refs):
+    inputs, outputs, (scratch, sems) = refs[:4], refs[4:-5], (refs[-5:-1], refs[-1])
+    coef_ref, z_ref, up_ref, down_ref, *x_refs = outputs
+    copies = [pltpu.make_async_copy(inputs[i], scratch[i], sems.at[i]) for i in range(4)]
+    for copy in copies:
+        copy.start()
+    for copy in copies:
+        copy.wait()
+    eps_ref, elec_ref, magn_ref, mat_ref = scratch
     layers = elec_ref.shape[1]
     gz = lax.axis_index("gz")
     for z in range(layers):
@@ -163,7 +171,7 @@
 
 
 def step_kernel(
-    row_size, mode_ref, basis_ref, prow_ref, pcol_ref, pmode_ref, pid_ref,
+    row_size, ports_each, mode_ref, basis_ref, prow_ref, pcol_ref, pmode_ref, pid_ref,
     elec_ref, magn_ref, coef_ref, z_ref, y_ref, yz_ref, *rest,
 ):
     n_x = 1 if row_size == 2 else 2
@@ -284,15 +292,14 @@
     for n in range(STEPS):
         sampled = jnp.sum(sum_ref[n], axis=1, keepdims=True)
         transform = transform + sampled * basis_ref[n : n + 1, :]
-    per_row = 128 // (2 * FREQ)
     place = iota(term_ref.shape, 0)
     term = jnp.zeros(term_ref.shape, jnp.float32)
     for k in range(PORT_TILE):
         port = pid_ref[0, 0, k]
         spread = jnp.broadcast_to(transform[k : k + 1, :], (8, 128))
-        spread = pltpu.roll(spread, (port % per_row) * (2 * FREQ), 1)
+        spread = pltpu.roll(spread, (port % ports_each) * (2 * FREQ), 1)
         spread = jnp.concatenate([spread] * (term_ref.shape[0] // 8), axis=0)
-        term = term + jnp.where(place == port // per_row, spread, 0.0)
+        term = term + jnp.where(place == port // ports_each, spread, 0.0)
     term_ref[...] = term
 
     for gz_is in (0, 1):
@@ -340,8 +347,15 @@
                 jax.ShapeDtypeStruct((FIELDS, 8, 128), f32),
             ]
             + [jax.ShapeDtypeStruct((n_pairs, 8, 128), f32)] * n_x,
-            in_specs=[SMEM, VMEM, VMEM, VMEM],
+            in_specs=[pl.BlockSpec(memory_space=pl.ANY)] * 4,
             out_specs=[VMEM] * (4 + n_x),
+            scratch_shapes=[
+                pltpu.SMEM(eps_table.shape, f32),
+                pltpu.VMEM(electric.shape, f32),
+                pltpu.VMEM(magnetic.shape, f32),
+                pltpu.VMEM(material.shape, jnp.int32),
+                pltpu.SemaphoreType.DMA((4,)),
+            ],
             compiler_params=PARAMS,
             name="pack",
         )(eps_table, electric, magnetic, material)
@@ -361,14 +375,14 @@
             name="corners",
         )(z_halo, y_halo, yz_halo)
         corner = across_rows(corner_send)
-        total_ports = PORT_TILE * col_size * row_size
-        term_rows = max(8, total_ports * 2 * FREQ // 128)
+        devices = col_size * row_size * gz_size
+        ports_each = PORT_TILE * col_size * row_size // devices
         electric_out, magnetic_out, term = pl.pallas_call(
-            functools.partial(step_kernel, row_size),
+            functools.partial(step_kernel, row_size, ports_each),
             out_shape=[
                 jax.ShapeDtypeStruct(electric.shape, f32),
                 jax.ShapeDtypeStruct(magnetic.shape, f32),
-                jax.ShapeDtypeStruct((term_rows, 128), f32),
+                jax.ShapeDtypeStruct((devices, 128), f32),
             ],
             in_specs=[VMEM] * 2 + [SMEM] * 4 + [VMEM] * (6 + 2 * n_x),
             out_specs=[VMEM] * 3,
@@ -384,18 +398,9 @@
             mode_table, jnp.asarray(dft_basis()), port_row, port_col, port_mode, port_ids,
             electric, magnetic, coef, z_halo, y_halo, yz_halo, *x_halo, *corner,
         )
-        for axis in ("gz", "row", "col"):
-            bit = 1
-            while bit < sizes[axis]:
-                term = term + swapped(term, axis, sizes[axis], bit)
-                bit *= 2
-        mine = (lax.axis_index("col") * row_size + lax.axis_index("row")) * gz_size + lax.axis_index("gz")
-        own = total_ports // (col_size * row_size * gz_size)
-        per_row = 128 // (own * 2 * FREQ)
-        cut = lax.dynamic_slice(
-            term, (mine // per_row, (mine % per_row) * own * 2 * FREQ), (1, own * 2 * FREQ)
-        )
-        return (electric_out, magnetic_out, cut.reshape(own, 2 * FREQ))
+        terms = lax.all_to_all(term, ("col", "row", "gz"), 0, 0, tiled=True)
+        mine = jnp.sum(terms, axis=0)[: ports_each * 2 * FREQ]
+        return (electric_out, magnetic_out, mine.reshape(ports_each, 2 * FREQ))
 
     in_specs = (
         P(None, "gz", "row", ("grp", "col")),

time: 51.7 us -> 48.9 us (0.946)
  blocking collectives: 0 us -> 10.2 us
  waiting for transfers between devices: 18.5 us -> 10.3 us
  starting transfers between devices: 13.1 us -> 8.44 us
    all_to_all x0 -> x1, blocking collectives: none -> 10.2 us  [per_device(): terms = lax.all_to_all(term, ('col', 'row', 'gz'), 0, 0, tiled=True)]
    ppermute x8 -> x4, waiting for transfers between devices: 14.1 us -> 5.93 us  [swapped(): return lax.ppermute(block, axis, [(i, i ^ bit) for i in range(size)])]
    ppermute x8 -> x4, starting transfers between devices: 8.36 us -> 3.68 us  [swapped(): return lax.ppermute(block, axis, [(i, i ^ bit) for i in range(size)])]
  transfers between devices with their start and end apart: 10 -> 6, of which waited for: 8 -> 4; matrix products, arithmetic and copies ran while one was open for 0% -> 0% of each run, Pallas kernels for 0% -> 0%
where the time goes in v2:
time: 48.9 us; the launch traced here: 48.7 us
  Pallas kernels  14.7 us (30%)
  waiting for transfers between devices  10.3 us (21%)
  blocking collectives  10.2 us (21%)
  starting transfers between devices  8.44 us (17%)
  local copies, waits for them, and re-layouts  4.24 us (9%)
  between operations  0.77 us (2%)
    pallas_call x1, Pallas kernels, per_device(): pl.pallas_call(functools.partial(step_kernel, row_size, ports_each), out_...  13.5 us
    all_to_all x1, blocking collectives, per_device(): terms = lax.all_to_all(term, ('col', 'row', 'gz'), 0, 0, tiled=True)  10.2 us
    ppermute x4, waiting for transfers between devices, swapped(): return lax.ppermute(block, axis, [(i, i ^ bit) for i in range(size)])  5.93 us
    ppermute x2, starting transfers between devices, shifted(): return lax.ppermute(block, axis, route)  4.76 us
    ppermute x2, waiting for transfers between devices, shifted(): return lax.ppermute(block, axis, route)  4.38 us
    ppermute x4, starting transfers between devices, swapped(): return lax.ppermute(block, axis, [(i, i ^ bit) for i in range(size)])  3.68 us
    unnamed x25, local copies, waits for them, and re-layouts  3.59 us
    pallas_call x1, Pallas kernels, per_device(): pl.pallas_call(functools.partial(pack_kernel, row_size), out_shape=[jax.S...  1.16 us
  transfers between devices with their start and end apart: 6, of which 4 were waited for; matrix products, arithmetic and copies ran while one was open for 0% of the time, Pallas kernels for 0%

profile of v2, /device:TPU:0, one launch (start us, length us, event | category | flops | bytes accessed | tf_op | source)
XLA Modules:
  0.0 48.7 jit_solution(5015780389265086732)
XLA Ops:
  0.6 0.0 copy-start
  0.6 1.0 %copy-done = f32[3,32,8,128]{3,2,1,0:T(8,128)S(1)} copy-done((f32[3,32,8,128]{3,2,1,0:T(8,128)S(1)}, f32[3,32,8,128]{3,2,1,0:T(8,128)}, u32[]{:S(2)}) %copy-start) | copy-done | bytes 393240
  1.6 1.0 %copy-done.2 = f32[3,32,8,128]{3,2,1,0:T(8,128)S(1)} copy-done((f32[3,32,8,128]{3,2,1,0:T(8,128)S(1)}, f32[3,32,8,128]{3,2,1,0:T(8,128)}, u32[]{:S(2)}) %copy-start.2) | copy-done | bytes 393240
  2.6 0.9 %copy-done.4 = s32[32,8,128]{2,1,0:T(8,128)S(1)} copy-done((s32[32,8,128]{2,1,0:T(8,128)S(1)}, s32[32,8,128]{2,1,0:T(8,128)}, u32[]{:S(2)}) %copy-start.4) | copy-done | bytes 131096
  3.5 0.7 %copy-done.7 = f32[8]{0:T(128)S(1)} copy-done((f32[8]{0:T(128)S(1)}, f32[8]{0:T(128)}, u32[]{:S(2)}) %copy-start.7) | copy-done | bytes 56
  4.2 1.2 %pack.1 = (f32[32,8,128]{2,1,0:T(8,128)S(1)}, f32[28,8,128]{2,1,0:T(8,128)S(1)}, f32[7,8,128]{2,1,0:T(8,128)S(1)}, f32[7,8,128]{2,1,0:T(8,128)S(1)}, f32[112,8,128]{2,1,0:T(8,128)S(1)}) custom-call(f32[8]{0:T(128)S(1)} %copy-done.7, f32[3,32,8,128]{3,2,1,0:T(8,128)S(1)} %copy-done, f32[3,32,8,128]{3,2,1,0:T(8,128)S(1)} %copy-done.2, s32[32,8,128]{2,1,0:T(8,128)S(1)} %copy-done.4), custom_call_target="tpu_custom_call" | custom-call | tf_op jit(solution)/shard_map/pack/pallas_call | solution.py:341
  5.4 0.0 copy-start.1
  5.4 3.0 %collective-permute-start.4 = (f32[112,8,128]{2,1,0:T(8,128)S(1)}, f32[112,8,128]{2,1,0:T(8,128)S(1)}, u32[]{:S(2)}, u32[]{:S(2)}) collective-permute-start(f32[112,8,128]{2,1,0:T(8,128)S(1)} %get-tuple-element.15), channel_id=1, source_target_pairs={{0,2},{2,0},{1,3},{3,1},{4,6},{6,4},{5,7},{7,5},{8,10},{10,8},{9,1... | collective-permute-start | bytes 1376264 | tf_op jit(solution)/shard_map/ppermute | solution.py:321
  8.4 3.5 %collective-permute-start.1 = (f32[7,8,128]{2,1,0:T(8,128)S(1)}, f32[7,8,128]{2,1,0:T(8,128)S(1)}, u32[]{:S(2)}, u32[]{:S(2)}) collective-permute-start(f32[7,8,128]{2,1,0:T(8,128)S(1)} %get-tuple-element.13), channel_id=1, source_target_pairs={{0,4},{4,8},{8,12},{1,5},{5,9},{9,13},{2,6},{6,10},{10,14},{3,7},{... | collective-permute-start | bytes 86024 | tf_op jit(solution)/shard_map/ppermute | solution.py:317
  11.9 1.3 %collective-permute-start.2 = (f32[7,8,128]{2,1,0:T(8,128)S(1)}, f32[7,8,128]{2,1,0:T(8,128)S(1)}, u32[]{:S(2)}, u32[]{:S(2)}) collective-permute-start(f32[7,8,128]{2,1,0:T(8,128)S(1)} %get-tuple-element.14), channel_id=1, source_target_pairs={{4,0},{8,4},{12,8},{5,1},{9,5},{13,9},{6,2},{10,6},{14,10},{7,3},{... | collective-permute-start | bytes 86024 | tf_op jit(solution)/shard_map/ppermute | solution.py:317
  13.2 0.1 collective-permute-start
  13.3 0.2 collective-permute-done.1
  13.4 4.2 %collective-permute-done.2 = f32[7,8,128]{2,1,0:T(8,128)S(1)} collective-permute-done((f32[7,8,128]{2,1,0:T(8,128)S(1)}, f32[7,8,128]{2,1,0:T(8,128)S(1)}, u32[]{:S(2)}, u32[]{:S(2)}) %collective-permute-start.2) | collective-permute-done | bytes 28704 | tf_op jit(solution)/shard_map/ppermute | solution.py:317
  17.6 0.0 collective-permute-start.3
  17.6 1.2 %collective-permute-done.3.yz_ref = f32[14,8,128]{2,1,0:T(8,128)S(1)} collective-permute-done((f32[14,8,128]{2,1,0:T(8,128)S(1)}, f32[14,8,128]{2,1,0:T(8,128)S(1)}, u32[]{:S(2)}, u32[]{:S(2)}) %collective-permute-start.3) | collective-permute-done | bytes 57376 | tf_op jit(solution)/shard_map/ppermute | solution.py:321
  18.9 0.0 collective-permute-done.z_ref
  18.9 0.0 copy-start.8
  18.9 0.0 copy-start.9
  18.9 0.0 copy-start.10
  19.0 0.6 %collective-permute-start.5 = (f32[28,8,128]{2,1,0:T(8,128)S(1)}, f32[28,8,128]{2,1,0:T(8,128)S(1)}, u32[]{:S(2)}, u32[]{:S(2)}) collective-permute-start(f32[28,8,128]{2,1,0:T(8,128)S(1)} %corners.1), channel_id=1, source_target_pairs={{0,2},{2,0},{1,3},{3,1},{4,6},{6,4},{5,7},{7,5},{8,10},{10,8},{9,1... | collective-permute-start | bytes 344072 | tf_op jit(solution)/shard_map/ppermute | solution.py:321
  19.5 4.7 %collective-permute-done.5.rest_1_ = f32[28,8,128]{2,1,0:T(8,128)S(1)} collective-permute-done((f32[28,8,128]{2,1,0:T(8,128)S(1)}, f32[28,8,128]{2,1,0:T(8,128)S(1)}, u32[]{:S(2)}, u32[]{:S(2)}) %collective-permute-start.5) | collective-permute-done | bytes 114720 | tf_op jit(solution)/shard_map/ppermute | solution.py:321
  24.2 0.0 collective-permute-done.4.rest_0_
  24.2 0.0 copy-done.3
  24.2 0.0 copy-done.1
  24.2 0.0 copy-done.6
  24.3 0.0 copy-done.11
  24.3 0.0 copy-done.8
  24.3 0.0 copy-done.9
  24.3 0.0 copy-done.10
  24.3 13.5 %steps.1 = (f32[3,32,8,128]{3,2,1,0:T(8,128)}, f32[3,32,8,128]{3,2,1,0:T(8,128)}, f32[16,128]{1,0:T(8,128)S(1)}) custom-call(f32[8,32,64]{2,1,0:T(8,128)S(1)} %copy-done.5, f32[8,128]{1,0:T(8,128)S(1)} %copy-done.6, s32[1,1,4]{2,1,0:T(1,128)S(1)} %copy-done.8, s32[1,1,4]{2,1,0:T(1,128)S(1)} %copy-done.9, s32[1,1,4]{2,1,0:T(1,128)S(1)} %copy-done.10, ...), custom_call_target="tpu_custom_call" | custom-call | tf_op jit(solution)/shard_map/steps/pallas_call | solution.py:380
  37.8 10.2 %all_to_all.9 = f32[16,1,128]{2,1,0:T(1,128)S(1)} all-to-all(f32[16,1,128]{2,1,0:T(1,128)S(1)} %bitcast.4), channel_id=1, replica_groups=mesh['grp'=2,'col'=4,'row'=2,'gz'=2] {'col','row','gz'}, dimensions={0} | all-to-all | bytes 16384 | tf_op jit(solution)/shard_map/all_to_all | solution.py:401
  48.0 0.6 %reshape.19 = f32[2,16]{1,0:T(2,128)} reshape(f32[32]{0:T(128)S(1)} %bitcast.5) | data formatting | bytes 256 | tf_op jit(solution)/shard_map/reshape | solution.py:403
  (12 shorter events, 0.1 us)
Async XLA Ops:
  0.6 1.0 %copy-start = (f32[3,32,8,128]{3,2,1,0:T(8,128)S(1)}, f32[3,32,8,128]{3,2,1,0:T(8,128)}, u32[]{:S(2)}) copy-start(f32[3,32,8,128]{3,2,1,0:T(8,128)} %elec_ref.1) | copy-start | bytes 1179652
  1.6 1.0 %copy-start.2 = (f32[3,32,8,128]{3,2,1,0:T(8,128)S(1)}, f32[3,32,8,128]{3,2,1,0:T(8,128)}, u32[]{:S(2)}) copy-start(f32[3,32,8,128]{3,2,1,0:T(8,128)} %magn_ref.1) | copy-start | bytes 1179652
  2.6 0.9 %copy-start.4 = (s32[32,8,128]{2,1,0:T(8,128)S(1)}, s32[32,8,128]{2,1,0:T(8,128)}, u32[]{:S(2)}) copy-start(s32[32,8,128]{2,1,0:T(8,128)} %refs_3_.1) | copy-start | bytes 393220
  3.5 0.7 %copy-start.7 = (f32[8]{0:T(128)S(1)}, f32[8]{0:T(128)}, u32[]{:S(2)}) copy-start(f32[8]{0:T(128)} %refs_0_.1) | copy-start | bytes 100
  4.2 20.0 %copy-start.3 = (f32[3,32,8,128]{3,2,1,0:T(8,128)S(1)}, f32[3,32,8,128]{3,2,1,0:T(8,128)}, u32[]{:S(2)}) copy-start(f32[3,32,8,128]{3,2,1,0:T(8,128)} %magn_ref.1) | copy-start | bytes 1179652
  4.2 20.0 %copy-start.5 = (f32[8,32,64]{2,1,0:T(8,128)S(1)}, f32[8,32,64]{2,1,0:T(8,128)}, u32[]{:S(2)}) copy-start(f32[8,32,64]{2,1,0:T(8,128)} %mode_ref.1) | copy-start | bytes 196612
  5.4 18.9 %copy-start.1 = (f32[3,32,8,128]{3,2,1,0:T(8,128)S(1)}, f32[3,32,8,128]{3,2,1,0:T(8,128)}, u32[]{:S(2)}) copy-start(f32[3,32,8,128]{3,2,1,0:T(8,128)} %elec_ref.1) | copy-start | bytes 1179652
  5.4 18.9 %collective-permute-start.4 = (f32[112,8,128]{2,1,0:T(8,128)S(1)}, f32[112,8,128]{2,1,0:T(8,128)S(1)}, u32[]{:S(2)}, u32[]{:S(2)}) collective-permute-start(f32[112,8,128]{2,1,0:T(8,128)S(1)} %get-tuple-element.15), channel_id=1, source_target_pairs={{0,2},{2,0},{1,3},{3,1},{4,6},{6,4},{5,7},{7,5},{8,10},{10,8},{9,1... | collective-permute-start | bytes 1376264 | tf_op jit(solution)/shard_map/ppermute | solution.py:321
  8.4 5.0 %collective-permute-start.1 = (f32[7,8,128]{2,1,0:T(8,128)S(1)}, f32[7,8,128]{2,1,0:T(8,128)S(1)}, u32[]{:S(2)}, u32[]{:S(2)}) collective-permute-start(f32[7,8,128]{2,1,0:T(8,128)S(1)} %get-tuple-element.13), channel_id=1, source_target_pairs={{0,4},{4,8},{8,12},{1,5},{5,9},{9,13},{2,6},{6,10},{10,14},{3,7},{... | collective-permute-start | bytes 86024 | tf_op jit(solution)/shard_map/ppermute | solution.py:317
  11.9 5.8 %collective-permute-start.2 = (f32[7,8,128]{2,1,0:T(8,128)S(1)}, f32[7,8,128]{2,1,0:T(8,128)S(1)}, u32[]{:S(2)}, u32[]{:S(2)}) collective-permute-start(f32[7,8,128]{2,1,0:T(8,128)S(1)} %get-tuple-element.14), channel_id=1, source_target_pairs={{4,0},{8,4},{12,8},{5,1},{9,5},{13,9},{6,2},{10,6},{14,10},{7,3},{... | collective-permute-start | bytes 86024 | tf_op jit(solution)/shard_map/ppermute | solution.py:317
  13.2 5.7 %collective-permute-start = (f32[28,8,128]{2,1,0:T(8,128)S(1)}, f32[28,8,128]{2,1,0:T(8,128)S(1)}, u32[]{:S(2)}, u32[]{:S(2)}) collective-permute-start(f32[28,8,128]{2,1,0:T(8,128)S(1)} %get-tuple-element.12), channel_id=1, source_target_pairs={{0,1},{1,0},{2,3},{3,2},{4,5},{5,4},{6,7},{7,6},{8,9},{9,8},{10,11... | collective-permute-start | bytes 344072 | tf_op jit(solution)/shard_map/ppermute | solution.py:321
  17.6 1.2 %collective-permute-start.3 = (f32[14,8,128]{2,1,0:T(8,128)S(1)}, f32[14,8,128]{2,1,0:T(8,128)S(1)}, u32[]{:S(2)}, u32[]{:S(2)}) collective-permute-start(f32[14,8,128]{2,1,0:T(8,128)S(1)} %constant_dynamic-update-slice_fusion.y_ref), channel_id=1, source_target_pairs={{0,1},{1,0},{2,3},{3,2},{4,5},{5,4},{6,7},{7,6},{8,9},{9,8},{10,11... | collective-permute-start | bytes 172040 | tf_op jit(solution)/shard_map/ppermute | solution.py:321
  18.9 5.4 %copy-start.6 = (f32[8,128]{1,0:T(8,128)S(1)}, f32[8,128]{1,0:T(8,128)}, u32[]{:S(2)}) copy-start(f32[8,128]{1,0:T(8,128)} %constant.4.clone.basis_ref) | copy-start | bytes 12292
  18.9 5.4 %copy-start.11 = (s32[1,1,4]{2,1,0:T(1,128)S(1)}, s32[1,1,4]{2,1,0:T(1,128)}, u32[]{:S(2)}) copy-start(s32[1,1,4]{2,1,0:T(1,128)} %pid_ref.1) | copy-start | bytes 52
  18.9 5.3 %copy-start.8 = (s32[1,1,4]{2,1,0:T(1,128)S(1)}, s32[1,1,4]{2,1,0:T(1,128)}, u32[]{:S(2)}) copy-start(s32[1,1,4]{2,1,0:T(1,128)} %prow_ref.1) | copy-start | bytes 52
  18.9 5.3 %copy-start.9 = (s32[1,1,4]{2,1,0:T(1,128)S(1)}, s32[1,1,4]{2,1,0:T(1,128)}, u32[]{:S(2)}) copy-start(s32[1,1,4]{2,1,0:T(1,128)} %pcol_ref.1) | copy-start | bytes 52
  18.9 5.3 %copy-start.10 = (s32[1,1,4]{2,1,0:T(1,128)S(1)}, s32[1,1,4]{2,1,0:T(1,128)}, u32[]{:S(2)}) copy-start(s32[1,1,4]{2,1,0:T(1,128)} %pmode_ref.1) | copy-start | bytes 52
  19.0 5.3 %collective-permute-start.5 = (f32[28,8,128]{2,1,0:T(8,128)S(1)}, f32[28,8,128]{2,1,0:T(8,128)S(1)}, u32[]{:S(2)}, u32[]{:S(2)}) collective-permute-start(f32[28,8,128]{2,1,0:T(8,128)S(1)} %corners.1), channel_id=1, source_target_pairs={{0,2},{2,0},{1,3},{3,1},{4,6},{6,4},{5,7},{7,5},{8,10},{10,8},{9,1... | collective-permute-start | bytes 344072 | tf_op jit(solution)/shard_map/ppermute | solution.py:321

commit v3 on v0

v3 whole, which is shorter than its diff:
```python
import functools

import jax
import jax.numpy as jnp
import numpy as np
from jax import lax
from jax.experimental import pallas as pl
from jax.experimental.pallas import tpu as pltpu
from jax.sharding import PartitionSpec as P

STEPS = 4
FREQ = 8
MATS = 8
PLEN = 64
PORT_TILE = 4
FIELDS = 7
DEPTH = STEPS
ROWS = 8
LAYERS = 32
CHUNK = 5
GROUP = 32

time_step = 0.5

UP_PLANES = [(f, 4) for f in (0, 1, 2, 4, 5)] + [(f, x) for x in (5, 6, 7) for f in range(FIELDS)]
DOWN_PLANES = [(f, x) for x in (0, 1, 2) for f in range(FIELDS)] + [(1, 3), (2, 3)]
PLANES = max(len(UP_PLANES), len(DOWN_PLANES))
PAIRS = (PLANES + 1) // 2

VMEM = pl.BlockSpec(memory_space=pltpu.VMEM)
SMEM = pl.BlockSpec(memory_space=pltpu.SMEM)
HBM = pl.BlockSpec(memory_space=pltpu.HBM)


def dft_basis():
    times = (np.arange(STEPS) + 1.0) * time_step
    omegas = np.pi * (np.arange(FREQ) + 1.0) / FREQ
    angle = times[:, None] * omegas[None, :]
    basis = np.zeros((8, 128), np.float32)
    basis[:STEPS, : 2 * FREQ] = np.concatenate([np.cos(angle), -np.sin(angle)], axis=1)
    return basis


def iota(axis):
    return lax.broadcasted_iota(jnp.int32, (8, 128), axis)


def turn(tile, shift, axis):
    return pltpu.roll(tile, shift % tile.shape[axis], axis)


def directions(row_size, body):
    if row_size == 2:
        row = lax.axis_index("row")
        pl.when(row == 0)(functools.partial(body, True, 0))
        pl.when(row == 1)(functools.partial(body, False, 0))
    else:
        body(True, 0)
        body(False, 1)


def pack_kernel(row_size, eps_hbm, elec_hbm, magn_hbm, mat_hbm, main_ref, z_ref, *rest):
    x_refs, (eps_ref, mat_ref, sems) = rest[:-3], rest[-3:]
    block = LAYERS * ROWS
    copies = [pltpu.make_async_copy(eps_hbm, eps_ref, sems.at[0]), pltpu.make_async_copy(mat_hbm, mat_ref, sems.at[1])]
    copies.append(pltpu.make_async_copy(elec_hbm, main_ref.at[pl.ds(0, 3)], sems.at[2]))
    copies.append(pltpu.make_async_copy(magn_hbm, main_ref.at[pl.ds(3, 3)], sems.at[3]))
    for copy in copies:
        copy.start()
    copies[0].wait()
    copies[1].wait()
    for z in range(LAYERS):
        material = mat_ref[z]
        eps = jnp.full((8, 128), eps_ref[0], jnp.float32)
        for which in range(1, MATS):
            eps = jnp.where(material == which, eps_ref[which], eps)
        main_ref[6, z] = time_step * (1.0 / eps)
    copies[2].wait()
    copies[3].wait()
    flat = main_ref.reshape(FIELDS * block, 128)

    def send(up, slot):
        for i, (f, x) in enumerate(UP_PLANES if up else DOWN_PLANES):
            x_refs[slot][i] = flat[pl.ds(f * block + x, LAYERS, stride=ROWS), :]

    directions(row_size, send)
    start = jnp.where(lax.axis_index("gz") == 0, LAYERS - DEPTH, 0)
    for f in range(FIELDS):
        z_ref[f] = main_ref[f, pl.ds(start, DEPTH)]


def edge_kernel(main_ref, z_ref, mode_ref, prow_ref, pcol_ref, pmode_ref,
                state_ref, own_ref, up_ref, down_ref, ext_ref, weight_ref, stage_ref, strip_ref):
    lane = iota(1)
    group = lane // GROUP
    place = lane % GROUP
    gz = lax.axis_index("gz")
    block = LAYERS * ROWS
    for f in range(FIELDS):
        stage_ref[f, 0:block] = main_ref[f].reshape(block, 128)
        halo = z_ref[f].reshape(DEPTH * ROWS, 128)
        nothing = jnp.zeros_like(halo)
        stage_ref[f, block : block + DEPTH * ROWS] = jnp.where(gz == 0, halo, nothing)
        stage_ref[f, block + DEPTH * ROWS :] = jnp.where(gz == 0, nothing, halo)
        ext_ref[f] = stage_ref[f, block:]
    for b in range(2):
        for zz in range(CHUNK):
            up = jnp.zeros((8, 128), jnp.float32)
            down = jnp.zeros((8, 128), jnp.float32)
            for f in range(FIELDS):
                own = None
                for r in range(4):
                    x = 4 * b + r
                    tile = stage_ref[f, pl.ds(zz * ROWS + x, 8, stride=CHUNK * ROWS), :]
                    state_ref[f, x, zz] = tile
                    moved = turn(tile, GROUP * r + 8, 1)
                    own = moved if own is None else jnp.where(group == r, moved, own)
                own_ref[f, b, zz] = own
                up = jnp.where(place // DEPTH == f, turn(own, DEPTH * f - 4, 1), up)
                down = jnp.where(place // DEPTH == f, turn(own, DEPTH * f - 8, 1), down)
            up_ref[b, zz] = up
            down_ref[b, zz] = down
    for k in range(PORT_TILE):
        strip_ref[...] = jnp.zeros(strip_ref.shape, jnp.float32)
        strip_ref[0:LAYERS, 0:PLEN] = mode_ref[pmode_ref[0, 0, k]]
        strip_ref[...] = pltpu.roll(strip_ref[...], pcol_ref[0, 0, k], 1)
        at = lane - GROUP * (prow_ref[0, 0, k] % 4)
        for zz in range(CHUNK):
            tile = strip_ref[pl.ds(zz, 8, stride=CHUNK), :]
            weight_ref[k, 0, zz] = jnp.where((lane >= DEPTH) & (lane < 128 - DEPTH), tile, 0.0)
            own = pltpu.roll(tile, GROUP * (prow_ref[0, 0, k] % 4) + 8, 1)
            edge = jnp.where((at >= 4) & (at < 8), own, 0.0)
            weight_ref[k, 1, zz] = jnp.where((at >= 16) & (at < 20), turn(own, 8, 1), edge)


def corner_kernel(row_size, ext_ref, low_ref, high_ref, *x_refs):
    def send(up, slot):
        planes = UP_PLANES if up else DOWN_PLANES

        def tile(i):
            f, x = planes[i]
            return ext_ref[f, pl.ds(x, 8, stride=ROWS), :]

        for i in range(PAIRS):
            first = tile(i)
            if i + PAIRS < len(planes):
                first = first + turn(tile(i + PAIRS), 4, 0)
            x_refs[slot][i] = first
        b = 1 if up else 0
        for zz in range(CHUNK):
            x_refs[slot][PAIRS + zz] = low_ref[b, zz]
            x_refs[slot][PAIRS + CHUNK + zz] = high_ref[b, zz]

    directions(row_size, send)


def edge_tile(own, low, high, f):
    place = iota(1) % GROUP
    out = jnp.where(place < 16, turn(low, 12 - DEPTH * f, 1), turn(own, 8, 1))
    out = jnp.where(place < 12, turn(high, 8 - DEPTH * f, 1), out)
    return jnp.where(place < 8, own, out)


def step_kernel(row_size, ports_each, basis_ref, prow_ref, pid_ref, state_ref, own_ref, low_ref, high_ref, weight_ref, *rest):
    n_x = 1 if row_size == 2 else 2
    x_refs, corner_refs = rest[:n_x], rest[n_x : 2 * n_x]
    eout_hbm, hout_hbm, term_ref, main, edge, plane_ref, sum_ref, out_ref, sems = rest[2 * n_x :]
    gz, row, col = (lax.axis_index(name) for name in ("gz", "row", "col"))
    lane, sub = iota(1), iota(0)
    place, group = lane % GROUP, lane // GROUP
    zeros = jnp.zeros((8, 128), jnp.float32)
    last_group, first_group = group == 3, group == 0

    def run(has_below, has_above):
        for f in range(FIELDS):
            for x in range(ROWS):
                for zz in range(CHUNK):
                    main[f, DEPTH + x, zz] = state_ref[f, x, zz]
            for b in range(2):
                for zz in range(CHUNK):
                    edge[f, 1 + b, zz] = edge_tile(own_ref[f, b, zz], low_ref[b, zz], high_ref[b, zz], f)

        def halo_rows(planes, slot, offset, b):
            valid = (sub < 4) == (gz == 0)
            got = set(planes)
            for i, (f, x) in enumerate(planes):
                packed = corner_refs[slot][i % PAIRS]
                if i >= PAIRS:
                    packed = turn(packed, 4, 0)
                plane_ref[slot, i, 0:LAYERS] = x_refs[slot][i]
                plane_ref[slot, i, LAYERS:] = jnp.where(valid, packed, 0.0)
            for i, (f, x) in enumerate(planes):
                for zz in range(CHUNK):
                    main[f, DEPTH + x + offset, zz] = plane_ref[slot, i, pl.ds(zz, 8, stride=CHUNK), :]
            for f in range(FIELDS):
                for zz in range(CHUNK):
                    own = zeros
                    for r in range(4):
                        x = 4 * b + r
                        if (f, x - offset) in got:
                            own = jnp.where(group == r, turn(main[f, DEPTH + x, zz], GROUP * r + 8, 1), own)
                    low = corner_refs[slot][PAIRS + zz]
                    high = corner_refs[slot][PAIRS + CHUNK + zz]
                    edge[f, 1 + b, zz] = edge_tile(own, low, high, f)

        if has_below:
            halo_rows(UP_PLANES, 0, -ROWS, -1)
        if has_above:
            halo_rows(DOWN_PLANES, n_x - 1, ROWS, 2)

        below_layers = (sub == 7) & (gz == 0)
        half = [jnp.where(below_layers, 0.0, time_step) if zz else jnp.full((8, 128), time_step) for zz in range(CHUNK)]
        outside = (place >= 12) & (place < 16) & (col == 0)
        edge_half = [jnp.where(outside, 0.0, half[zz]) for zz in range(CHUNK)]
        lowest = jnp.where(row == 0, 0.0, 1.0) if row_size > 2 else None

        def above(tiles, zz):
            return tiles[zz + 1] if zz + 1 < CHUNK else turn(tiles[0], -1, 0)

        def beneath(tiles, zz):
            return tiles[zz - 1] if zz else turn(tiles[CHUNK - 1], 1, 0)

        def update(keep, i, h, with_e, with_hx, carry, next_x, prev_x):
            every = range(CHUNK)
            ex, ey, ez = ([keep[f, i, zz] for zz in every] for f in range(3))
            ey_up, ez_up = next_x(1, ey, i), next_x(2, ez, i)
            hx, hy, hz = [], [], []
            for zz in every:
                if with_hx:
                    curl = (turn(ez[zz], -1, 1) - ez[zz]) - (above(ey, zz) - ey[zz])
                    hx.append(keep[3, i, zz] - h[zz] * curl)
                    keep[3, i, zz] = hx[zz]
                curl = (above(ex, zz) - ex[zz]) - (ez_up[zz] - ez[zz])
                hy.append(keep[4, i, zz] - h[zz] * curl)
                keep[4, i, zz] = hy[zz]
                curl = (ey_up[zz] - ey[zz]) - (turn(ex[zz], -1, 1) - ex[zz])
                hz.append(keep[5, i, zz] - h[zz] * curl)
                keep[5, i, zz] = hz[zz]
            if with_e:
                hy_down, hz_down = prev_x(hy, carry and carry[0]), prev_x(hz, carry and carry[1])
                for zz in every:
                    c = keep[6, i, zz]
                    curl = (hz[zz] - turn(hz[zz], 1, 1)) - (hy[zz] - beneath(hy, zz))
                    keep[0, i, zz] = ex[zz] + c * curl
                    curl = (hx[zz] - beneath(hx, zz)) - (hz[zz] - hz_down[zz])
                    keep[1, i, zz] = ey[zz] + c * curl
                    curl = (hy[zz] - hy_down[zz]) - (hx[zz] - turn(hx[zz], 1, 1))
                    keep[2, i, zz] = ez[zz] + c * curl
            return hy, hz

        blank = [zeros] * CHUNK

        for n in range(1, STEPS + 1):
            first = n - 5 if has_below else 0
            last = 11 - n if has_above else 7
            final = DEPTH + 11 if has_above else DEPTH + 7

            def next_row(f, own, i):
                return [main[f, i + 1, zz] for zz in range(CHUNK)] if i < final else blank

            def prev_row(own, carry):
                return carry or blank

            carry = None
            for x in range(first, last + 1):
                h = half if lowest is None or x >= 0 else [v * lowest for v in half]
                with_e = not (has_below and x == first)
                carry = update(main, DEPTH + x, h, with_e, with_e, carry, next_row, prev_row)

            top = 3 if has_above else 2

            def next_block(f, own, i):
                turned = [turn(v, -GROUP, 1) for v in own]
                other = [turn(edge[f, i + 1, zz], -GROUP, 1) for zz in range(CHUNK)] if i < top else blank
                return [jnp.where(last_group, o, v) for o, v in zip(other, turned)]

            def prev_block(own, carry):
                turned = [turn(v, GROUP, 1) for v in own]
                other = [turn(v, GROUP, 1) for v in carry] if carry else blank
                return [jnp.where(first_group, o, v) for o, v in zip(other, turned)]

            carry = None
            for i in range(0 if has_below else 1, top + 1):
                h = edge_half if lowest is None or i else [v * lowest for v in edge_half]
                carry = update(edge, i, h, True, True, carry, next_block, prev_block)

            for k in range(PORT_TILE):
                at = prow_ref[0, 0, k]
                total = zeros
                for zz in range(CHUNK):
                    total = total + main[2, DEPTH + at, zz] * weight_ref[k, 0, zz]
                    total = total + edge[2, 1 + at // 4, zz] * weight_ref[k, 1, zz]
                sum_ref[n - 1, k : k + 1, :] = jnp.sum(total, axis=0, keepdims=True)

    if row_size == 2:
        pl.when(row == 0)(functools.partial(run, False, True))
        pl.when(row == 1)(functools.partial(run, True, False))
    else:
        run(True, True)

    copies = []
    for f in range(6):
        for b in range(2):
            for zz in range(CHUNK):
                tile = edge[f, 1 + b, zz]
                near = jnp.where(place < 8, tile, turn(tile, -8, 1))
                for r in range(4):
                    x = 4 * b + r
                    sides = turn(near, -(GROUP * r + 8), 1)
                    tile = jnp.where((lane < DEPTH) | (lane >= 128 - DEPTH), sides, main[f, DEPTH + x, zz])
                    out_ref[f, pl.ds(zz * ROWS + x, 8, stride=CHUNK * ROWS), :] = tile
        dest = eout_hbm if f < 3 else hout_hbm
        copies.append(pltpu.make_async_copy(out_ref.at[f, pl.ds(0, LAYERS * ROWS)], dest.at[f % 3], sems.at[f]))
        copies[-1].start()

    transform = zeros
    for n in range(STEPS):
        sampled = jnp.sum(sum_ref[n], axis=1, keepdims=True)
        transform = transform + sampled * basis_ref[n : n + 1, :]
    target = lax.broadcasted_iota(jnp.int32, term_ref.shape, 0)
    term = jnp.zeros(term_ref.shape, jnp.float32)
    for k in range(PORT_TILE):
        port = pid_ref[0, 0, k]
        spread = jnp.broadcast_to(transform[k : k + 1, :], (8, 128))
        spread = pltpu.roll(spread, (port % ports_each) * (2 * FREQ), 1)
        spread = jnp.concatenate([spread] * (term_ref.shape[0] // 8), axis=0)
        term = term + jnp.where(target == port // ports_each, spread, 0.0)
    term_ref[...] = term
    for copy in copies:
        copy.wait()


def shifted(block, axis, size, distance):
    route = [(i - distance, i) for i in range(size) if 0 <= i - distance < size]
    return lax.ppermute(block, axis, route)


def swapped(block, axis, size):
    return lax.ppermute(block, axis, [(i, i ^ 1) for i in range(size)])


def solution(mesh):
    sizes = dict(mesh.shape)
    row_size, col_size, gz_size = sizes["row"], sizes["col"], sizes["gz"]
    n_x = 1 if row_size == 2 else 2

    def across_rows(blocks):
        if row_size == 2:
            return (swapped(blocks[0], "row", 2),)
        return (shifted(blocks[0], "row", row_size, 1), shifted(blocks[1], "row", row_size, -1))

    def per_device(
        electric, magnetic, material, eps_table, mode_table, port_row, port_col, port_mode, port_ids
    ):
        f32 = jnp.float32

        def array(*shape):
            return jax.ShapeDtypeStruct(shape, f32)

        main, z_send, *x_send = pl.pallas_call(
            functools.partial(pack_kernel, row_size),
            out_shape=[array(FIELDS, LAYERS, ROWS, 128), array(FIELDS, DEPTH, ROWS, 128)]
            + [array(PLANES, LAYERS, 128)] * n_x,
            in_specs=[HBM] * 4,
            out_specs=[VMEM] * (2 + n_x),
            scratch_shapes=[
                pltpu.SMEM(eps_table.shape, f32),
                pltpu.VMEM(material.shape, jnp.int32),
                pltpu.SemaphoreType.DMA((4,)),
            ],
            name="pack",
        )(eps_table, electric, magnetic, material)
        x_halo = across_rows(x_send)
        z_halo = swapped(z_send, "gz", gz_size)
        state, own, up_send, down_send, ext, weights = pl.pallas_call(
            edge_kernel,
            out_shape=[
                array(FIELDS, ROWS, CHUNK, 8, 128),
                array(FIELDS, 2, CHUNK, 8, 128),
                array(2, CHUNK, 8, 128),
                array(2, CHUNK, 8, 128),
                array(FIELDS, 2 * DEPTH * ROWS, 128),
                array(PORT_TILE, 2, CHUNK, 8, 128),
            ],
            in_specs=[VMEM] * 3 + [SMEM] * 3,
            out_specs=[VMEM] * 6,
            scratch_shapes=[
                pltpu.VMEM((FIELDS, 8 * CHUNK * ROWS, 128), f32),
                pltpu.VMEM((8 * CHUNK, 128), f32),
            ],
            name="edges",
        )(main, z_halo, mode_table, port_row, port_col, port_mode)
        low = shifted(up_send, "col", col_size, 1)
        high = shifted(down_send, "col", col_size, -1)
        corner_send = pl.pallas_call(
            functools.partial(corner_kernel, row_size),
            out_shape=[array(PAIRS + 2 * CHUNK, 8, 128)] * n_x,
            in_specs=[VMEM] * 3,
            out_specs=[VMEM] * n_x,
            name="corners",
        )(ext, low, high)
        corner = across_rows(corner_send)
        devices = col_size * row_size * gz_size
        ports_each = PORT_TILE * col_size * row_size // devices
        electric_out, magnetic_out, term = pl.pallas_call(
            functools.partial(step_kernel, row_size, ports_each),
            out_shape=[array(3, LAYERS * ROWS, 128), array(3, LAYERS * ROWS, 128), array(devices, 128)],
            in_specs=[VMEM] + [SMEM] * 2 + [VMEM] * (5 + 2 * n_x),
            out_specs=[HBM, HBM, VMEM],
            scratch_shapes=[
                pltpu.VMEM((FIELDS, ROWS + 2 * DEPTH, CHUNK, 8, 128), f32),
                pltpu.VMEM((FIELDS, 4, CHUNK, 8, 128), f32),
                pltpu.VMEM((n_x, PLANES, 8 * CHUNK, 128), f32),
                pltpu.VMEM((STEPS, 8, 128), f32),
                pltpu.VMEM((6, 8 * CHUNK * ROWS, 128), f32),
                pltpu.SemaphoreType.DMA((6,)),
            ],
            name="steps",
        )(jnp.asarray(dft_basis()), port_row, port_ids, state, own, low, high, weights, *x_halo, *corner)
        terms = lax.all_to_all(term, ("col", "row", "gz"), 0, 0, tiled=True)
        mine = jnp.sum(terms, axis=0)[: ports_each * 2 * FREQ]
        return (
            electric_out.reshape(electric.shape),
            magnetic_out.reshape(magnetic.shape),
            mine.reshape(ports_each, 2 * FREQ),
        )

    in_specs = (
        P(None, "gz", "row", ("grp", "col")),
        P(None, "gz", "row", ("grp", "col")),
        P("gz", "row", ("grp", "col")),
        P(),
        P(None, "gz", None),
        P(("grp", "row"), "col", None),
        P(("grp", "row"), "col", None),
        P(("grp", "row"), "col", None),
        P(("grp", "row"), "col", None),
    )
    out_specs = (
        P(None, "gz", "row", ("grp", "col")),
        P(None, "gz", "row", ("grp", "col")),
        P(("grp", "col", "row", "gz"), None),
    )
    return jax.shard_map(
        per_device, mesh=mesh, in_specs=in_specs, out_specs=out_specs, check_vma=False
    )
```

time: 257 us -> 56.5 us (0.22)
  other arithmetic: 74.1 us -> 0.03 us
  starting transfers between devices: 65.9 us -> 8.3 us
  local copies, waits for them, and re-layouts: 51 us -> 2.73 us
  blocking collectives: 57.6 us -> 10.4 us
  Pallas kernels: 0 us -> 23.5 us
  waiting for transfers between devices: 3.35 us -> 10.6 us
    unnamed x1 -> x0, blocking collectives: 57.6 us -> none
    ppermute x24 -> x5, starting transfers between devices: 65.9 us -> 8.3 us  [the longest x2 4.76 us: shifted(): return lax.ppermute(block, axis, route)]
    another operation x29 -> x0, other arithmetic: 33.1 us -> none  [the longest x6 12.4 us: forward_parts(): paired = jnp.stack([elec_z, elec_y])]
    pallas_call x0 -> x4, Pallas kernels: none -> 23.5 us  [the longest x1 13 us: per_device(): pl.pallas_call(functools.partial(step_kernel, row_size, ports_each), out_...]
    sub x12 -> x0, other arithmetic: 20.5 us -> none  [the longest x4 9.4 us: backward_parts(): diff_z = jnp.diff(jnp.concatenate([before, paired], axis=1), axis=1)]
    add x3 -> x0, other arithmetic: 16.8 us -> none  [the longest x2 11.2 us: per_device(): elec_z = elec_z + coefficient * (diff_x[1] - diff_y[1])]
    slice x11 -> x0, local copies, waits for them, and re-layouts: 16.4 us -> none  [the longest x4 8 us: backward_parts(): before = from_behind(paired[:, -1:], 'gz', 1)]
    ppermute x8 -> x0, local copies, waits for them, and re-layouts: 13.4 us -> none  [from_behind(): return lax.ppermute(block, axis, route)]
  transfers between devices with their start and end apart: 24 -> 5, of which waited for: 3 -> 4; matrix products, arithmetic and copies ran while one was open for 17% -> 0% of each run, Pallas kernels for 0% -> 14%
where the time goes in v3:
time: 56.5 us; the launch traced here: 56.2 us
  Pallas kernels  23.5 us (42%)
  waiting for transfers between devices  10.6 us (19%)
  blocking collectives  10.4 us (18%)
  starting transfers between devices  8.3 us (15%)
  local copies, waits for them, and re-layouts  2.73 us (5%)
  between operations  0.67 us (1%)
    pallas_call x1, Pallas kernels, per_device(): pl.pallas_call(functools.partial(step_kernel, row_size, ports_each), out_...  13 us
    all_to_all x1, blocking collectives, per_device(): terms = lax.all_to_all(term, ('col', 'row', 'gz'), 0, 0, tiled=True)  10.4 us
    pallas_call x1, Pallas kernels, per_device(): pl.pallas_call(edge_kernel, out_shape=[array(FIELDS, ROWS, CHUNK, 8, 128)...  6.47 us
    ppermute x3, waiting for transfers between devices, swapped(): return lax.ppermute(block, axis, [(i, i ^ 1) for i in range(size)])  5.77 us
    ppermute x2, waiting for transfers between devices, shifted(): return lax.ppermute(block, axis, route)  4.8 us
    ppermute x2, starting transfers between devices, shifted(): return lax.ppermute(block, axis, route)  4.76 us
    ppermute x3, starting transfers between devices, swapped(): return lax.ppermute(block, axis, [(i, i ^ 1) for i in range(size)])  3.54 us
    pallas_call x1, Pallas kernels, per_device(): pl.pallas_call(functools.partial(pack_kernel, row_size), out_shape=[array...  2.4 us
  transfers between devices with their start and end apart: 5, of which 4 were waited for; matrix products, arithmetic and copies ran while one was open for 0% of the time, Pallas kernels for 14%

profile of v3, /device:TPU:0, one launch (start us, length us, event | category | flops | bytes accessed | tf_op | source)
XLA Modules:
  0.0 56.2 jit_solution(16919115521127424158)
XLA Ops:
  0.6 2.4 %pack.1 = (f32[7,32,8,128]{3,2,1,0:T(8,128)}, f32[7,4,8,128]{3,2,1,0:T(8,128)}, f32[26,32,128]{2,1,0:T(8,128)}) custom-call(f32[8]{0:T(128)} %eps_hbm.1, f32[3,32,8,128]{3,2,1,0:T(8,128)} %elec_hbm.1, f32[3,32,8,128]{3,2,1,0:T(8,128)} %magn_hbm.1, s32[32,8,128]{2,1,0:T(8,128)} %mat_hbm.1), custom_call_target="tpu_custom_call" | custom-call | tf_op jit(solution)/shard_map/pack/pallas_call | solution.py:360
  3.0 3.0 %collective-permute-start.3 = (f32[26,32,128]{2,1,0:T(8,128)}, f32[26,32,128]{2,1,0:T(8,128)S(1)}, u32[]{:S(2)}, u32[]{:S(2)}) collective-permute-start(f32[26,32,128]{2,1,0:T(8,128)} %get-tuple-element.22), channel_id=1, source_target_pairs={{0,2},{2,0},{1,3},{3,1},{4,6},{6,4},{5,7},{7,5},{8,10},{10,8},{9,1... | collective-permute-start | bytes 1277960 | tf_op jit(solution)/shard_map/ppermute | solution.py:339
  6.0 0.0 collective-permute-start
  6.0 1.5 %collective-permute-done.z_ref = f32[7,4,8,128]{3,2,1,0:T(8,128)S(1)} collective-permute-done((f32[7,4,8,128]{3,2,1,0:T(8,128)}, f32[7,4,8,128]{3,2,1,0:T(8,128)S(1)}, u32[]{:S(2)}, u32[]{:S(2)}) %collective-permute-start) | collective-permute-done | bytes 114720 | tf_op jit(solution)/shard_map/ppermute | solution.py:339
  7.6 0.0 copy-start.3
  7.6 0.6 %copy-done.3 = f32[7,4,8,128]{3,2,1,0:T(8,128)} copy-done((f32[7,4,8,128]{3,2,1,0:T(8,128)}, f32[7,4,8,128]{3,2,1,0:T(8,128)S(1)}, u32[]{:S(2)}) %copy-start.3) | copy-done | bytes 114712
  8.2 6.5 %edges.1 = (f32[7,8,5,8,128]{4,3,2,1,0:T(8,128)}, f32[7,2,5,8,128]{4,3,2,1,0:T(8,128)}, f32[2,5,8,128]{3,2,1,0:T(8,128)}, f32[2,5,8,128]{3,2,1,0:T(8,128)}, f32[...) custom-call(f32[7,32,8,128]{3,2,1,0:T(8,128)} %get-tuple-element.15.main_ref, f32[7,4,8,128]{3,2,1,0:T(8,128)} %copy-done.3, ...), custom_call_target="tpu_custom_call" | custom-call | tf_op jit(solution)/shard_map/edges/pallas_call | solution.py:375
  14.7 3.5 %collective-permute-start.1 = (f32[2,5,8,128]{3,2,1,0:T(8,128)}, f32[2,5,8,128]{3,2,1,0:T(8,128)S(1)}, u32[]{:S(2)}, u32[]{:S(2)}) collective-permute-start(f32[2,5,8,128]{3,2,1,0:T(8,128)} %get-tuple-element.19), channel_id=1, source_target_pairs={{0,4},{4,8},{8,12},{1,5},{5,9},{9,13},{2,6},{6,10},{10,14},{3,7},{... | collective-permute-start | bytes 122888 | tf_op jit(solution)/shard_map/ppermute | solution.py:335
  18.2 1.3 %collective-permute-start.2 = (f32[2,5,8,128]{3,2,1,0:T(8,128)}, f32[2,5,8,128]{3,2,1,0:T(8,128)S(1)}, u32[]{:S(2)}, u32[]{:S(2)}) collective-permute-start(f32[2,5,8,128]{3,2,1,0:T(8,128)} %get-tuple-element.20), channel_id=1, source_target_pairs={{4,0},{8,4},{12,8},{5,1},{9,5},{13,9},{6,2},{10,6},{14,10},{7,3},{... | collective-permute-start | bytes 122888 | tf_op jit(solution)/shard_map/ppermute | solution.py:335
  19.5 0.7 %collective-permute-done.1.low_ref = f32[2,5,8,128]{3,2,1,0:T(8,128)S(1)} collective-permute-done((f32[2,5,8,128]{3,2,1,0:T(8,128)}, f32[2,5,8,128]{3,2,1,0:T(8,128)S(1)}, u32[]{:S(2)}, u32[]{:S(2)}) %collective-permute-start.1) | collective-permute-done | bytes 40992 | tf_op jit(solution)/shard_map/ppermute | solution.py:335
  20.1 0.0 copy-start.1
  20.1 4.1 %collective-permute-done.2.high_ref = f32[2,5,8,128]{3,2,1,0:T(8,128)S(1)} collective-permute-done((f32[2,5,8,128]{3,2,1,0:T(8,128)}, f32[2,5,8,128]{3,2,1,0:T(8,128)S(1)}, u32[]{:S(2)}, u32[]{:S(2)}) %collective-permute-start.2) | collective-permute-done | bytes 40992 | tf_op jit(solution)/shard_map/ppermute | solution.py:335
  24.3 0.0 copy-start.2
  24.3 0.0 copy-done.1
  24.3 0.6 %copy-done.2 = f32[2,5,8,128]{3,2,1,0:T(8,128)} copy-done((f32[2,5,8,128]{3,2,1,0:T(8,128)}, f32[2,5,8,128]{3,2,1,0:T(8,128)S(1)}, u32[]{:S(2)}) %copy-start.2) | copy-done | bytes 40984
  24.9 1.6 %corners.1 = f32[23,8,128]{2,1,0:T(8,128)} custom-call(f32[7,64,128]{2,1,0:T(8,128)} %get-tuple-element.23.ext_ref, f32[2,5,8,128]{3,2,1,0:T(8,128)} %copy-done.1, f32[2,5,8,128]{3,2,1,0:T(8,128)} %copy-done.2), custom_call_target="tpu_custom_call" | custom-call | tf_op jit(solution)/shard_map/corners/pallas_call | solution.py:395
  26.5 0.5 collective-permute-start.4
  27.1 4.2 %collective-permute-done.4.rest_1_ = f32[23,8,128]{2,1,0:T(8,128)S(1)} collective-permute-done((f32[23,8,128]{2,1,0:T(8,128)}, f32[23,8,128]{2,1,0:T(8,128)S(1)}, u32[]{:S(2)}, u32[]{:S(2)}) %collective-permute-start.4) | collective-permute-done | bytes 94240 | tf_op jit(solution)/shard_map/ppermute | solution.py:339
  31.3 0.0 copy-start.4
  31.3 0.0 collective-permute-done.3.rest_0_
  31.3 0.0 copy-start
  31.3 0.6 %copy-done.4 = f32[23,8,128]{2,1,0:T(8,128)} copy-done((f32[23,8,128]{2,1,0:T(8,128)}, f32[23,8,128]{2,1,0:T(8,128)S(1)}, u32[]{:S(2)}) %copy-start.4) | copy-done | bytes 94232
  32.0 0.2 copy-done
  32.1 13.0 %steps.1 = (f32[3,256,128]{2,1,0:T(8,128)}, f32[3,256,128]{2,1,0:T(8,128)}, f32[16,128]{1,0:T(8,128)}) custom-call(f32[8,128]{1,0:T(8,128)} %constant.4.clone.basis_ref, s32[1,1,4]{2,1,0:T(1,128)} %prow_ref.3, s32[1,1,4]{2,1,0:T(1,128)} %pid_ref.1, f32[7,8,5,8,128]{4,3,2,1,0:T(8,128)} %get-tuple-element.17.state_ref, ...), custom_call_target="tpu_custom_call" | custom-call | tf_op jit(solution)/shard_map/steps/pallas_call | solution.py:405
  45.1 10.4 %all_to_all.9 = f32[16,1,128]{2,1,0:T(1,128)S(1)} all-to-all(f32[16,1,128]{2,1,0:T(1,128)} %bitcast.6), channel_id=1, replica_groups=mesh['grp'=2,'col'=4,'row'=2,'gz'=2] {'col','row','gz'}, dimensions={0} | all-to-all | bytes 16384 | tf_op jit(solution)/shard_map/all_to_all | solution.py:420
  55.6 0.6 %reshape.27 = f32[2,16]{1,0:T(2,128)} reshape(f32[32]{0:T(128)S(1)} %bitcast.7) | data formatting | bytes 256 | tf_op jit(solution)/shard_map/reshape | solution.py:425
  (1 shorter events, 0.0 us)
Async XLA Ops:
  3.0 28.3 %collective-permute-start.3 = (f32[26,32,128]{2,1,0:T(8,128)}, f32[26,32,128]{2,1,0:T(8,128)S(1)}, u32[]{:S(2)}, u32[]{:S(2)}) collective-permute-start(f32[26,32,128]{2,1,0:T(8,128)} %get-tuple-element.22), channel_id=1, source_target_pairs={{0,2},{2,0},{1,3},{3,1},{4,6},{6,4},{5,7},{7,5},{8,10},{10,8},{9,1... | collective-permute-start | bytes 1277960 | tf_op jit(solution)/shard_map/ppermute | solution.py:339
  6.0 1.5 %collective-permute-start = (f32[7,4,8,128]{3,2,1,0:T(8,128)}, f32[7,4,8,128]{3,2,1,0:T(8,128)S(1)}, u32[]{:S(2)}, u32[]{:S(2)}) collective-permute-start(f32[7,4,8,128]{3,2,1,0:T(8,128)} %get-tuple-element.16), channel_id=1, source_target_pairs={{0,1},{1,0},{2,3},{3,2},{4,5},{5,4},{6,7},{7,6},{8,9},{9,8},{10,11... | collective-permute-start | bytes 344072 | tf_op jit(solution)/shard_map/ppermute | solution.py:339
  7.6 0.6 %copy-start.3 = (f32[7,4,8,128]{3,2,1,0:T(8,128)}, f32[7,4,8,128]{3,2,1,0:T(8,128)S(1)}, u32[]{:S(2)}) copy-start(f32[7,4,8,128]{3,2,1,0:T(8,128)S(1)} %collective-permute-done.z_ref) | copy-start | bytes 344068
  14.7 5.4 %collective-permute-start.1 = (f32[2,5,8,128]{3,2,1,0:T(8,128)}, f32[2,5,8,128]{3,2,1,0:T(8,128)S(1)}, u32[]{:S(2)}, u32[]{:S(2)}) collective-permute-start(f32[2,5,8,128]{3,2,1,0:T(8,128)} %get-tuple-element.19), channel_id=1, source_target_pairs={{0,4},{4,8},{8,12},{1,5},{5,9},{9,13},{2,6},{6,10},{10,14},{3,7},{... | collective-permute-start | bytes 122888 | tf_op jit(solution)/shard_map/ppermute | solution.py:335
  18.2 6.1 %collective-permute-start.2 = (f32[2,5,8,128]{3,2,1,0:T(8,128)}, f32[2,5,8,128]{3,2,1,0:T(8,128)S(1)}, u32[]{:S(2)}, u32[]{:S(2)}) collective-permute-start(f32[2,5,8,128]{3,2,1,0:T(8,128)} %get-tuple-element.20), channel_id=1, source_target_pairs={{4,0},{8,4},{12,8},{5,1},{9,5},{13,9},{6,2},{10,6},{14,10},{7,3},{... | collective-permute-start | bytes 122888 | tf_op jit(solution)/shard_map/ppermute | solution.py:335
  20.1 4.1 %copy-start.1 = (f32[2,5,8,128]{3,2,1,0:T(8,128)}, f32[2,5,8,128]{3,2,1,0:T(8,128)S(1)}, u32[]{:S(2)}) copy-start(f32[2,5,8,128]{3,2,1,0:T(8,128)S(1)} %collective-permute-done.1.low_ref) | copy-start | bytes 122884
  24.3 0.6 %copy-start.2 = (f32[2,5,8,128]{3,2,1,0:T(8,128)}, f32[2,5,8,128]{3,2,1,0:T(8,128)S(1)}, u32[]{:S(2)}) copy-start(f32[2,5,8,128]{3,2,1,0:T(8,128)S(1)} %collective-permute-done.2.high_ref) | copy-start | bytes 122884
  26.5 4.8 %collective-permute-start.4 = (f32[23,8,128]{2,1,0:T(8,128)}, f32[23,8,128]{2,1,0:T(8,128)S(1)}, u32[]{:S(2)}, u32[]{:S(2)}) collective-permute-start(f32[23,8,128]{2,1,0:T(8,128)} %corners.1), channel_id=1, source_target_pairs={{0,2},{2,0},{1,3},{3,1},{4,6},{6,4},{5,7},{7,5},{8,10},{10,8},{9,1... | collective-permute-start | bytes 282632 | tf_op jit(solution)/shard_map/ppermute | solution.py:339
  31.3 0.7 %copy-start.4 = (f32[23,8,128]{2,1,0:T(8,128)}, f32[23,8,128]{2,1,0:T(8,128)S(1)}, u32[]{:S(2)}) copy-start(f32[23,8,128]{2,1,0:T(8,128)S(1)} %collective-permute-done.4.rest_1_) | copy-start | bytes 282628
  31.3 0.8 %copy-start = (f32[26,32,128]{2,1,0:T(8,128)}, f32[26,32,128]{2,1,0:T(8,128)S(1)}, u32[]{:S(2)}) copy-start(f32[26,32,128]{2,1,0:T(8,128)S(1)} %collective-permute-done.3.rest_0_) | copy-start | bytes 1277956

commit v4 on v3

--- a/solution.py
+++ b/solution.py
@@ -30,6 +30,7 @@
 VMEM = pl.BlockSpec(memory_space=pltpu.VMEM)
 SMEM = pl.BlockSpec(memory_space=pltpu.SMEM)
 HBM = pl.BlockSpec(memory_space=pltpu.HBM)
+PARAMS = pltpu.CompilerParams(vmem_limit_bytes=16 * 1024 * 1024)
 
 
 def dft_basis():
@@ -105,19 +106,24 @@
         ext_ref[f] = stage_ref[f, block:]
     for b in range(2):
         for zz in range(CHUNK):
+            tiles = [
+                [stage_ref[f, pl.ds(zz * ROWS + 4 * b + r, 8, stride=CHUNK * ROWS), :] for r in range(4)]
+                for f in range(FIELDS)
+            ]
             up = jnp.zeros((8, 128), jnp.float32)
             down = jnp.zeros((8, 128), jnp.float32)
+            owns = []
             for f in range(FIELDS):
-                own = None
-                for r in range(4):
-                    x = 4 * b + r
-                    tile = stage_ref[f, pl.ds(zz * ROWS + x, 8, stride=CHUNK * ROWS), :]
-                    state_ref[f, x, zz] = tile
-                    moved = turn(tile, GROUP * r + 8, 1)
-                    own = moved if own is None else jnp.where(group == r, moved, own)
-                own_ref[f, b, zz] = own
+                own = turn(tiles[f][0], 8, 1)
+                for r in range(1, 4):
+                    own = jnp.where(group == r, turn(tiles[f][r], GROUP * r + 8, 1), own)
                 up = jnp.where(place // DEPTH == f, turn(own, DEPTH * f - 4, 1), up)
                 down = jnp.where(place // DEPTH == f, turn(own, DEPTH * f - 8, 1), down)
+                owns.append(own)
+            for f in range(FIELDS):
+                for r in range(4):
+                    state_ref[f, 4 * b + r, zz] = tiles[f][r]
+                own_ref[f, b, zz] = owns[f]
             up_ref[b, zz] = up
             down_ref[b, zz] = down
     for k in range(PORT_TILE):
@@ -161,25 +167,48 @@
     return jnp.where(place < 8, own, out)
 
 
-def step_kernel(row_size, ports_each, basis_ref, prow_ref, pid_ref, state_ref, own_ref, low_ref, high_ref, weight_ref, *rest):
+def join_kernel(own_ref, low_ref, high_ref, edge_ref):
+    for b in range(2):
+        for zz in range(CHUNK):
+            low, high = low_ref[b, zz], high_ref[b, zz]
+            tiles = [edge_tile(own_ref[f, b, zz], low, high, f) for f in range(FIELDS)]
+            for f in range(FIELDS):
+                edge_ref[f, b, zz] = tiles[f]
+
+
+def step_kernel(row_size, ports_each, basis_ref, prow_ref, pid_ref, state_ref, joined_ref, weight_ref, *rest):
     n_x = 1 if row_size == 2 else 2
     x_refs, corner_refs = rest[:n_x], rest[n_x : 2 * n_x]
-    eout_hbm, hout_hbm, term_ref, main, edge, plane_ref, sum_ref, out_ref, sems = rest[2 * n_x :]
+    eout_hbm, hout_hbm, keep_ref, send_ref, main_e, main_h, main_c, edge_e, edge_h, edge_c, plane_ref, sum_ref, out_ref, sems = rest[2 * n_x :]
     gz, row, col = (lax.axis_index(name) for name in ("gz", "row", "col"))
     lane, sub = iota(1), iota(0)
     place, group = lane % GROUP, lane // GROUP
     zeros = jnp.zeros((8, 128), jnp.float32)
     last_group, first_group = group == 3, group == 0
 
+    def at_main(f, i, zz, n):
+        if DEPTH <= i < DEPTH + ROWS and (n == 1 or f == 6):
+            return state_ref[f, i - DEPTH, zz]
+        if f == 6:
+            return main_c[i, zz]
+        return main_e[f, i, zz] if f < 3 else main_h[f - 3, i, zz]
+
+    def at_edge(f, i, zz, n):
+        if 1 <= i < 3 and (n == 1 or f == 6):
+            return joined_ref[f, i - 1, zz]
+        if f == 6:
+            return edge_c[i, zz]
+        return edge_e[f, i, zz] if f < 3 else edge_h[f - 3, i, zz]
+
+    def put(e, h, c, f, i, zz, tile):
+        if f == 6:
+            c[i, zz] = tile
+        elif f < 3:
+            e[f, i, zz] = tile
+        else:
+            h[f - 3, i, zz] = tile
+
     def run(has_below, has_above):
-        for f in range(FIELDS):
-            for x in range(ROWS):
-                for zz in range(CHUNK):
-                    main[f, DEPTH + x, zz] = state_ref[f, x, zz]
-            for b in range(2):
-                for zz in range(CHUNK):
-                    edge[f, 1 + b, zz] = edge_tile(own_ref[f, b, zz], low_ref[b, zz], high_ref[b, zz], f)
-
         def halo_rows(planes, slot, offset, b):
             valid = (sub < 4) == (gz == 0)
             got = set(planes)
@@ -189,19 +218,26 @@
                     packed = turn(packed, 4, 0)
                 plane_ref[slot, i, 0:LAYERS] = x_refs[slot][i]
                 plane_ref[slot, i, LAYERS:] = jnp.where(valid, packed, 0.0)
+            rows = {}
             for i, (f, x) in enumerate(planes):
                 for zz in range(CHUNK):
-                    main[f, DEPTH + x + offset, zz] = plane_ref[slot, i, pl.ds(zz, 8, stride=CHUNK), :]
-            for f in range(FIELDS):
+                    rows[f, x, zz] = plane_ref[slot, i, pl.ds(zz, 8, stride=CHUNK), :]
                 for zz in range(CHUNK):
+                    put(main_e, main_h, main_c, f, DEPTH + x + offset, zz, rows[f, x, zz])
+            for zz in range(CHUNK):
+                low = corner_refs[slot][PAIRS + zz]
+                high = corner_refs[slot][PAIRS + CHUNK + zz]
+                tiles = []
+                for f in range(FIELDS):
                     own = zeros
                     for r in range(4):
-                        x = 4 * b + r
-                        if (f, x - offset) in got:
-                            own = jnp.where(group == r, turn(main[f, DEPTH + x, zz], GROUP * r + 8, 1), own)
-                    low = corner_refs[slot][PAIRS + zz]
-                    high = corner_refs[slot][PAIRS + CHUNK + zz]
-                    edge[f, 1 + b, zz] = edge_tile(own, low, high, f)
+                        x = 4 * b + r - offset
+                        if (f, x) in got:
+                            tile = at_main(f, DEPTH + x + offset, zz, 0)
+                            own = jnp.where(group == r, turn(tile, GROUP * r + 8, 1), own)
+                    tiles.append(edge_tile(own, low, high, f))
+                for f in range(FIELDS):
+                    put(edge_e, edge_h, edge_c, f, 1 + b, zz, tiles[f])
 
         if has_below:
             halo_rows(UP_PLANES, 0, -ROWS, -1)
@@ -220,76 +256,116 @@
         def beneath(tiles, zz):
             return tiles[zz - 1] if zz else turn(tiles[CHUNK - 1], 1, 0)
 
-        def update(keep, i, h, with_e, with_hx, carry, next_x, prev_x):
-            every = range(CHUNK)
-            ex, ey, ez = ([keep[f, i, zz] for zz in every] for f in range(3))
-            ey_up, ez_up = next_x(1, ey, i), next_x(2, ez, i)
-            hx, hy, hz = [], [], []
-            for zz in every:
-                if with_hx:
-                    curl = (turn(ez[zz], -1, 1) - ez[zz]) - (above(ey, zz) - ey[zz])
-                    hx.append(keep[3, i, zz] - h[zz] * curl)
-                    keep[3, i, zz] = hx[zz]
-                curl = (above(ex, zz) - ex[zz]) - (ez_up[zz] - ez[zz])
-                hy.append(keep[4, i, zz] - h[zz] * curl)
-                keep[4, i, zz] = hy[zz]
-                curl = (ey_up[zz] - ey[zz]) - (turn(ex[zz], -1, 1) - ex[zz])
-                hz.append(keep[5, i, zz] - h[zz] * curl)
-                keep[5, i, zz] = hz[zz]
-            if with_e:
-                hy_down, hz_down = prev_x(hy, carry and carry[0]), prev_x(hz, carry and carry[1])
+        blank = [zeros] * CHUNK
+        every = range(CHUNK)
+
+        def sweep(items, load, work):
+            loaded = {items[0]: load(items[0])}
+            for i in items:
+                if i + 1 in items:
+                    loaded[i + 1] = load(i + 1)
+                work(i, loaded)
+
+        def phases(n, items, final, at, keep_e, keep_h, across, half_of, only_h):
+            def load_e(i):
+                ex, ey, ez = ([at(f, i, zz, n) for zz in every] for f in range(3))
+                return ex, ey, ez, [turn(v, -1, 1) for v in ex], [turn(v, -1, 1) for v in ez], across(ey, -1), across(ez, -1)
+
+            def work_h(i, loaded):
+                ex, ey, ez, ex_right, ez_right, ey_own, ez_own = loaded[i]
+                old = [[at(f, i, zz, n) for zz in every] for f in (3, 4, 5)]
+                h = half_of(i)
+                if i + 1 in loaded:
+                    after = loaded[i + 1]
+                elif i < final:
+                    after = load_e(i + 1)
+                else:
+                    after = [blank] * 7
+                ey_up, ez_up = across.pick(ey_own, after[5]), across.pick(ez_own, after[6])
+                new = []
                 for zz in every:
-                    c = keep[6, i, zz]
-                    curl = (hz[zz] - turn(hz[zz], 1, 1)) - (hy[zz] - beneath(hy, zz))
-                    keep[0, i, zz] = ex[zz] + c * curl
-                    curl = (hx[zz] - beneath(hx, zz)) - (hz[zz] - hz_down[zz])
-                    keep[1, i, zz] = ey[zz] + c * curl
-                    curl = (hy[zz] - hy_down[zz]) - (hx[zz] - turn(hx[zz], 1, 1))
-                    keep[2, i, zz] = ez[zz] + c * curl
-            return hy, hz
-
-        blank = [zeros] * CHUNK
+                    hx = (ez_right[zz] - ez[zz]) - (above(ey, zz) - ey[zz])
+                    hy = (above(ex, zz) - ex[zz]) - (ez_up[zz] - ez[zz])
+                    hz = (ey_up[zz] - ey[zz]) - (ex_right[zz] - ex[zz])
+                    new.append([old[c][zz] - h[zz] * v for c, v in enumerate((hx, hy, hz))])
+                for zz in every:
+                    for c in range(3):
+                        if c or i not in only_h:
+                            keep_h[c, i, zz] = new[zz][c]
+
+            def load_h(i):
+                hy, hz = ([keep_h[c, i, zz] for zz in every] for c in (1, 2))
+                shifted_h = across(hy, 1), across(hz, 1)
+                if i in only_h:
+                    return None, hy, hz, None, None, *shifted_h
+                hx = [keep_h[0, i, zz] for zz in every]
+                return hx, hy, hz, [turn(v, 1, 1) for v in hx], [turn(v, 1, 1) for v in hz], *shifted_h
+
+            def work_e(i, loaded):
+                if i in only_h:
+                    return
+                hx, hy, hz, hx_left, hz_left, hy_own, hz_own = loaded[i]
+                old = [[at(f, i, zz, n) for zz in every] for f in range(3)]
+                coef = [at(6, i, zz, n) for zz in every]
+                before = loaded.get(i - 1, [blank] * 7)
+                hy_down, hz_down = across.pick(hy_own, before[5]), across.pick(hz_own, before[6])
+                new = []
+                for zz in every:
+                    ex = (hz[zz] - hz_left[zz]) - (hy[zz] - beneath(hy, zz))
+                    ey = (hx[zz] - beneath(hx, zz)) - (hz[zz] - hz_down[zz])
+                    ez = (hy[zz] - hy_down[zz]) - (hx[zz] - hx_left[zz])
+                    new.append([old[c][zz] + coef[zz] * v for c, v in enumerate((ex, ey, ez))])
+                for zz in every:
+                    for c in range(3):
+                        keep_e[c, i, zz] = new[zz][c]
+
+            sweep(items, load_e, work_h)
+            yield
+            sweep(items, load_h, work_e)
+
+        class RowAcross:
+            def __call__(self, tiles, way):
+                return tiles
+
+            def pick(self, own, other):
+                return other
+
+        class BlockAcross:
+            def __call__(self, tiles, way):
+                self.edge = last_group if way < 0 else first_group
+                return [turn(v, way * GROUP, 1) for v in tiles]
+
+            def pick(self, own, other):
+                return [jnp.where(self.edge, o, v) for o, v in zip(other, own)]
 
         for n in range(1, STEPS + 1):
             first = n - 5 if has_below else 0
             last = 11 - n if has_above else 7
             final = DEPTH + 11 if has_above else DEPTH + 7
-
-            def next_row(f, own, i):
-                return [main[f, i + 1, zz] for zz in range(CHUNK)] if i < final else blank
-
-            def prev_row(own, carry):
-                return carry or blank
-
-            carry = None
-            for x in range(first, last + 1):
-                h = half if lowest is None or x >= 0 else [v * lowest for v in half]
-                with_e = not (has_below and x == first)
-                carry = update(main, DEPTH + x, h, with_e, with_e, carry, next_row, prev_row)
-
             top = 3 if has_above else 2
 
-            def next_block(f, own, i):
-                turned = [turn(v, -GROUP, 1) for v in own]
-                other = [turn(edge[f, i + 1, zz], -GROUP, 1) for zz in range(CHUNK)] if i < top else blank
-                return [jnp.where(last_group, o, v) for o, v in zip(other, turned)]
-
-            def prev_block(own, carry):
-                turned = [turn(v, GROUP, 1) for v in own]
-                other = [turn(v, GROUP, 1) for v in carry] if carry else blank
-                return [jnp.where(first_group, o, v) for o, v in zip(other, turned)]
-
-            carry = None
-            for i in range(0 if has_below else 1, top + 1):
-                h = edge_half if lowest is None or i else [v * lowest for v in edge_half]
-                carry = update(edge, i, h, True, True, carry, next_block, prev_block)
+            def half_of(i, limit, values):
+                return values if lowest is None or i >= limit else [v * lowest for v in values]
+
+            rows = phases(
+                n, list(range(DEPTH + first, DEPTH + last + 1)), final, at_main, main_e, main_h, RowAcross(),
+                lambda i: half_of(i, DEPTH, half), [DEPTH + first] if has_below else [],
+            )
+            blocks = phases(
+                n, list(range(0 if has_below else 1, top + 1)), top, at_edge, edge_e, edge_h, BlockAcross(),
+                lambda i: half_of(i, 1, edge_half), [],
+            )
+            for part in (rows, blocks):
+                next(part)
+            for part in (rows, blocks):
+                next(part, None)
 
             for k in range(PORT_TILE):
                 at = prow_ref[0, 0, k]
                 total = zeros
                 for zz in range(CHUNK):
-                    total = total + main[2, DEPTH + at, zz] * weight_ref[k, 0, zz]
-                    total = total + edge[2, 1 + at // 4, zz] * weight_ref[k, 1, zz]
+                    total = total + main_e[2, DEPTH + at, zz] * weight_ref[k, 0, zz]
+                    total = total + edge_e[2, 1 + at // 4, zz] * weight_ref[k, 1, zz]
                 sum_ref[n - 1, k : k + 1, :] = jnp.sum(total, axis=0, keepdims=True)
 
     if row_size == 2:
@@ -300,15 +376,18 @@
 
     copies = []
     for f in range(6):
+        main, edge = (main_e, edge_e) if f < 3 else (main_h, edge_h)
         for b in range(2):
-            for zz in range(CHUNK):
-                tile = edge[f, 1 + b, zz]
-                near = jnp.where(place < 8, tile, turn(tile, -8, 1))
-                for r in range(4):
-                    x = 4 * b + r
-                    sides = turn(near, -(GROUP * r + 8), 1)
-                    tile = jnp.where((lane < DEPTH) | (lane >= 128 - DEPTH), sides, main[f, DEPTH + x, zz])
-                    out_ref[f, pl.ds(zz * ROWS + x, 8, stride=CHUNK * ROWS), :] = tile
+            tiles = [edge[f % 3, 1 + b, zz] for zz in range(CHUNK)]
+            near = [jnp.where(place < 8, tile, turn(tile, -8, 1)) for tile in tiles]
+            done = {}
+            for r in range(4):
+                for zz in range(CHUNK):
+                    sides = turn(near[zz], -(GROUP * r + 8), 1)
+                    own = main[f % 3, DEPTH + 4 * b + r, zz]
+                    done[r, zz] = jnp.where((lane < DEPTH) | (lane >= 128 - DEPTH), sides, own)
+            for (r, zz), tile in done.items():
+                out_ref[f, pl.ds(zz * ROWS + 4 * b + r, 8, stride=CHUNK * ROWS), :] = tile
         dest = eout_hbm if f < 3 else hout_hbm
         copies.append(pltpu.make_async_copy(out_ref.at[f, pl.ds(0, LAYERS * ROWS)], dest.at[f % 3], sems.at[f]))
         copies[-1].start()
@@ -317,15 +396,17 @@
     for n in range(STEPS):
         sampled = jnp.sum(sum_ref[n], axis=1, keepdims=True)
         transform = transform + sampled * basis_ref[n : n + 1, :]
-    target = lax.broadcasted_iota(jnp.int32, term_ref.shape, 0)
-    term = jnp.zeros(term_ref.shape, jnp.float32)
+    keep_ref[...] = jnp.zeros(keep_ref.shape, jnp.float32)
+    send_ref[...] = jnp.zeros(send_ref.shape, jnp.float32)
     for k in range(PORT_TILE):
         port = pid_ref[0, 0, k]
-        spread = jnp.broadcast_to(transform[k : k + 1, :], (8, 128))
-        spread = pltpu.roll(spread, (port % ports_each) * (2 * FREQ), 1)
-        spread = jnp.concatenate([spread] * (term_ref.shape[0] // 8), axis=0)
-        term = term + jnp.where(target == port // ports_each, spread, 0.0)
-    term_ref[...] = term
+        device = port // ports_each
+
+        def place_in(ref, k=k, port=port, device=device):
+            ref[device // 2, pl.ds(port % ports_each, 1), :] = transform[k : k + 1, : 2 * FREQ]
+
+        pl.when(device % 2 == gz)(functools.partial(place_in, keep_ref))
+        pl.when(device % 2 != gz)(functools.partial(place_in, send_ref))
     for copy in copies:
         copy.wait()
 
@@ -368,6 +449,7 @@
                 pltpu.VMEM(material.shape, jnp.int32),
                 pltpu.SemaphoreType.DMA((4,)),
             ],
+            compiler_params=PARAMS,
             name="pack",
         )(eps_table, electric, magnetic, material)
         x_halo = across_rows(x_send)
@@ -388,6 +470,7 @@
                 pltpu.VMEM((FIELDS, 8 * CHUNK * ROWS, 128), f32),
                 pltpu.VMEM((8 * CHUNK, 128), f32),
             ],
+            compiler_params=PARAMS,
             name="edges",
         )(main, z_halo, mode_table, port_row, port_col, port_mode)
         low = shifted(up_send, "col", col_size, 1)
@@ -397,32 +480,47 @@
             out_shape=[array(PAIRS + 2 * CHUNK, 8, 128)] * n_x,
             in_specs=[VMEM] * 3,
             out_specs=[VMEM] * n_x,
+            compiler_params=PARAMS,
             name="corners",
         )(ext, low, high)
         corner = across_rows(corner_send)
         devices = col_size * row_size * gz_size
         ports_each = PORT_TILE * col_size * row_size // devices
-        electric_out, magnetic_out, term = pl.pallas_call(
+        edges = pl.pallas_call(
+            join_kernel,
+            out_shape=array(FIELDS, 2, CHUNK, 8, 128),
+            in_specs=[VMEM] * 3,
+            out_specs=VMEM,
+            compiler_params=PARAMS,
+            name="joins",
+        )(own, low, high)
+        electric_out, magnetic_out, keep, send = pl.pallas_call(
             functools.partial(step_kernel, row_size, ports_each),
-            out_shape=[array(3, LAYERS * ROWS, 128), array(3, LAYERS * ROWS, 128), array(devices, 128)],
-            in_specs=[VMEM] + [SMEM] * 2 + [VMEM] * (5 + 2 * n_x),
-            out_specs=[HBM, HBM, VMEM],
+            out_shape=[array(3, LAYERS * ROWS, 128)] * 2 + [array(devices // 2, ports_each, 2 * FREQ)] * 2,
+            in_specs=[VMEM] + [SMEM] * 2 + [VMEM] * (3 + 2 * n_x),
+            out_specs=[HBM, HBM, VMEM, VMEM],
             scratch_shapes=[
-                pltpu.VMEM((FIELDS, ROWS + 2 * DEPTH, CHUNK, 8, 128), f32),
-                pltpu.VMEM((FIELDS, 4, CHUNK, 8, 128), f32),
+                pltpu.VMEM((3, ROWS + 2 * DEPTH, CHUNK, 8, 128), f32),
+                pltpu.VMEM((3, ROWS + 2 * DEPTH, CHUNK, 8, 128), f32),
+                pltpu.VMEM((ROWS + 2 * DEPTH, CHUNK, 8, 128), f32),
+                pltpu.VMEM((3, 4, CHUNK, 8, 128), f32),
+                pltpu.VMEM((3, 4, CHUNK, 8, 128), f32),
+                pltpu.VMEM((4, CHUNK, 8, 128), f32),
                 pltpu.VMEM((n_x, PLANES, 8 * CHUNK, 128), f32),
                 pltpu.VMEM((STEPS, 8, 128), f32),
                 pltpu.VMEM((6, 8 * CHUNK * ROWS, 128), f32),
                 pltpu.SemaphoreType.DMA((6,)),
             ],
+            compiler_params=PARAMS,
             name="steps",
-        )(jnp.asarray(dft_basis()), port_row, port_ids, state, own, low, high, weights, *x_halo, *corner)
-        terms = lax.all_to_all(term, ("col", "row", "gz"), 0, 0, tiled=True)
-        mine = jnp.sum(terms, axis=0)[: ports_each * 2 * FREQ]
+        )(jnp.asarray(dft_basis()), port_row, port_ids, state, edges, weights, *x_halo, *corner)
+        terms = keep + swapped(send, "gz", gz_size)
+        terms = lax.all_to_all(terms, ("col", "row"), 0, 0, tiled=True)
+        mine = jnp.sum(terms, axis=0)
         return (
             electric_out.reshape(electric.shape),
             magnetic_out.reshape(magnetic.shape),
-            mine.reshape(ports_each, 2 * FREQ),
+            mine,
         )
 
     in_specs = (

time: 56.5 us -> 49 us (0.87)
  Pallas kernels: 23.5 us -> 11.3 us
  local copies, waits for them, and re-layouts: 2.73 us -> 6.42 us
    pallas_call x1, Pallas kernels: 13 us -> 5.67 us  [per_device(): pl.pallas_call(functools.partial(step_kernel, row_size, ports_each), out_...]
    unnamed x10 -> x20, local copies, waits for them, and re-layouts: 2.08 us -> 6.42 us
    pallas_call x1, Pallas kernels: 6.47 us -> 4.62 us  [per_device(): pl.pallas_call(edge_kernel, out_shape=[array(FIELDS, ROWS, CHUNK, 8, 128)...]
    pallas_call x1, Pallas kernels: 2.4 us -> 0.76 us  [per_device(): pl.pallas_call(functools.partial(pack_kernel, row_size), out_shape=[array...]
    pallas_call x1, Pallas kernels: 1.63 us -> 0.03 us  [per_device(): pl.pallas_call(functools.partial(corner_kernel, row_size), out_shape=[arr...]
    reshape x1 -> x0, local copies, waits for them, and re-layouts: 0.65 us -> none  [per_device(): mine.reshape(ports_each, 2 * FREQ)]
    ppermute x3 -> x4, waiting for transfers between devices: 5.77 us -> 6.24 us  [swapped(): return lax.ppermute(block, axis, [(i, i ^ 1) for i in range(size)])]
    ppermute x3 -> x4, starting transfers between devices: 3.54 us -> 3.67 us  [swapped(): return lax.ppermute(block, axis, [(i, i ^ 1) for i in range(size)])]
  transfers between devices with their start and end apart: 5 -> 6, of which waited for: 4 -> 5; matrix products, arithmetic and copies ran while one was open for 0% -> 0% of each run, Pallas kernels for 14% -> 10%
where the time goes in v4:
time: 49 us; the launch traced here: 48.7 us
  Pallas kernels  11.3 us (23%)
  waiting for transfers between devices  10.8 us (22%)
  blocking collectives  10.3 us (21%)
  starting transfers between devices  8.44 us (17%)
  local copies, waits for them, and re-layouts  6.42 us (13%)
  between operations  0.73 us (1%)
  other arithmetic  0.59 us (1%)
    all_to_all x1, blocking collectives, per_device(): terms = lax.all_to_all(terms, ('col', 'row'), 0, 0, tiled=True)  10.3 us
    unnamed x20, local copies, waits for them, and re-layouts  6.42 us
    ppermute x4, waiting for transfers between devices, swapped(): return lax.ppermute(block, axis, [(i, i ^ 1) for i in range(size)])  6.24 us
    pallas_call x1, Pallas kernels, per_device(): pl.pallas_call(functools.partial(step_kernel, row_size, ports_each), out_...  5.67 us
    ppermute x2, starting transfers between devices, shifted(): return lax.ppermute(block, axis, route)  4.77 us
    pallas_call x1, Pallas kernels, per_device(): pl.pallas_call(edge_kernel, out_shape=[array(FIELDS, ROWS, CHUNK, 8, 128)...  4.62 us
    ppermute x2, waiting for transfers between devices, shifted(): return lax.ppermute(block, axis, route)  4.6 us
    ppermute x4, starting transfers between devices, swapped(): return lax.ppermute(block, axis, [(i, i ^ 1) for i in range(size)])  3.67 us
  transfers between devices with their start and end apart: 6, of which 5 were waited for; matrix products, arithmetic and copies ran while one was open for 0% of the time, Pallas kernels for 10%

profile of v4, /device:TPU:0, one launch (start us, length us, event | category | flops | bytes accessed | tf_op | source)
XLA Modules:
  0.0 48.7 jit_solution(8201446013008849605)
XLA Ops:
  0.6 0.0 copy-start
  0.6 1.0 %copy-done = f32[3,32,8,128]{3,2,1,0:T(8,128)S(1)} copy-done((f32[3,32,8,128]{3,2,1,0:T(8,128)S(1)}, f32[3,32,8,128]{3,2,1,0:T(8,128)}, u32[]{:S(2)}) %copy-start) | copy-done | bytes 393240
  1.6 0.0 copy-start.1
  1.6 1.0 %copy-done.1 = f32[3,32,8,128]{3,2,1,0:T(8,128)S(1)} copy-done((f32[3,32,8,128]{3,2,1,0:T(8,128)S(1)}, f32[3,32,8,128]{3,2,1,0:T(8,128)}, u32[]{:S(2)}) %copy-start.1) | copy-done | bytes 393240
  2.6 0.9 %copy-done.2 = s32[32,8,128]{2,1,0:T(8,128)S(1)} copy-done((s32[32,8,128]{2,1,0:T(8,128)S(1)}, s32[32,8,128]{2,1,0:T(8,128)}, u32[]{:S(2)}) %copy-start.2) | copy-done | bytes 131096
  3.5 0.7 %copy-done.8 = f32[8]{0:T(128)S(1)} copy-done((f32[8]{0:T(128)S(1)}, f32[8]{0:T(128)}, u32[]{:S(2)}) %copy-start.8) | copy-done | bytes 56
  4.2 0.8 %pack.1 = (f32[7,32,8,128]{3,2,1,0:T(8,128)S(1)}, f32[7,4,8,128]{3,2,1,0:T(8,128)S(1)}, f32[26,32,128]{2,1,0:T(8,128)S(1)}) custom-call(f32[8]{0:T(128)S(1)} %copy-done.8, f32[3,32,8,128]{3,2,1,0:T(8,128)S(1)} %copy-done, f32[3,32,8,128]{3,2,1,0:T(8,128)S(1)} %copy-done.1, s32[32,8,128]{2,1,0:T(8,128)S(1)} %copy-done.2), custom_call_target="tpu_custom_call" | custom-call | tf_op jit(solution)/shard_map/pack/pallas_call | solution.py:441
  5.0 0.0 copy-start.4
  5.0 0.0 copy-start.9
  5.0 3.0 %collective-permute-start.3 = (f32[26,32,128]{2,1,0:T(8,128)S(1)}, f32[26,32,128]{2,1,0:T(8,128)S(1)}, u32[]{:S(2)}, u32[]{:S(2)}) collective-permute-start(f32[26,32,128]{2,1,0:T(8,128)S(1)} %get-tuple-element.23), channel_id=1, source_target_pairs={{0,2},{2,0},{1,3},{3,1},{4,6},{6,4},{5,7},{7,5},{8,10},{10,8},{9,1... | collective-permute-start | bytes 1277960 | tf_op jit(solution)/shard_map/ppermute | solution.py:420
  8.0 0.0 collective-permute-start
  8.0 1.3 %collective-permute-done.z_ref = f32[7,4,8,128]{3,2,1,0:T(8,128)S(1)} collective-permute-done((f32[7,4,8,128]{3,2,1,0:T(8,128)S(1)}, f32[7,4,8,128]{3,2,1,0:T(8,128)S(1)}, u32[]{:S(2)}, u32[]{:S(2)}) %collective-permute-start) | collective-permute-done | bytes 114720 | tf_op jit(solution)/shard_map/ppermute | solution.py:420
  9.3 0.9 %copy-done.3 = f32[8,32,64]{2,1,0:T(8,128)S(1)} copy-done((f32[8,32,64]{2,1,0:T(8,128)S(1)}, f32[8,32,64]{2,1,0:T(8,128)}, u32[]{:S(2)}) %copy-start.3) | copy-done | bytes 65560
  10.2 0.7 %copy-done.5 = s32[1,1,4]{2,1,0:T(1,128)S(1)} copy-done((s32[1,1,4]{2,1,0:T(1,128)S(1)}, s32[1,1,4]{2,1,0:T(1,128)}, u32[]{:S(2)}) %copy-start.5) | copy-done | bytes 40
  10.9 0.7 %copy-done.6 = s32[1,1,4]{2,1,0:T(1,128)S(1)} copy-done((s32[1,1,4]{2,1,0:T(1,128)S(1)}, s32[1,1,4]{2,1,0:T(1,128)}, u32[]{:S(2)}) %copy-start.6) | copy-done | bytes 40
  11.5 0.7 %copy-done.7 = s32[1,1,4]{2,1,0:T(1,128)S(1)} copy-done((s32[1,1,4]{2,1,0:T(1,128)S(1)}, s32[1,1,4]{2,1,0:T(1,128)}, u32[]{:S(2)}) %copy-start.7) | copy-done | bytes 40
  12.2 4.6 %edges.1 = (f32[7,8,5,8,128]{4,3,2,1,0:T(8,128)S(1)}, f32[7,2,5,8,128]{4,3,2,1,0:T(8,128)S(1)}, f32[2,5,8,128]{3,2,1,0:T(8,128)S(1)}, f32[2,5,8,128]{3,2,1,0:T(8...) custom-call(f32[7,32,8,128]{3,2,1,0:T(8,128)S(1)} %get-tuple-element.16.main_ref, ...), custom_call_target="tpu_custom_call" | custom-call | tf_op jit(solution)/shard_map/edges/pallas_call | solution.py:457
  16.8 3.5 %collective-permute-start.1 = (f32[2,5,8,128]{3,2,1,0:T(8,128)S(1)}, f32[2,5,8,128]{3,2,1,0:T(8,128)S(1)}, u32[]{:S(2)}, u32[]{:S(2)}) collective-permute-start(f32[2,5,8,128]{3,2,1,0:T(8,128)S(1)} %get-tuple-element.20), channel_id=1, source_target_pairs={{0,4},{4,8},{8,12},{1,5},{5,9},{9,13},{2,6},{6,10},{10,14},{3,7},{... | collective-permute-start | bytes 122888 | tf_op jit(solution)/shard_map/ppermute | solution.py:416
  20.3 1.3 %collective-permute-start.2 = (f32[2,5,8,128]{3,2,1,0:T(8,128)S(1)}, f32[2,5,8,128]{3,2,1,0:T(8,128)S(1)}, u32[]{:S(2)}, u32[]{:S(2)}) collective-permute-start(f32[2,5,8,128]{3,2,1,0:T(8,128)S(1)} %get-tuple-element.21), channel_id=1, source_target_pairs={{4,0},{8,4},{12,8},{5,1},{9,5},{13,9},{6,2},{10,6},{14,10},{7,3},{... | collective-permute-start | bytes 122888 | tf_op jit(solution)/shard_map/ppermute | solution.py:416
  21.6 0.4 collective-permute-done.1.low_ref
  21.9 4.2 %collective-permute-done.2.high_ref = f32[2,5,8,128]{3,2,1,0:T(8,128)S(1)} collective-permute-done((f32[2,5,8,128]{3,2,1,0:T(8,128)S(1)}, f32[2,5,8,128]{3,2,1,0:T(8,128)S(1)}, u32[]{:S(2)}, u32[]{:S(2)}) %collective-permute-start.2) | collective-permute-done | bytes 40992 | tf_op jit(solution)/shard_map/ppermute | solution.py:416
  26.2 0.6 %collective-permute-start.4 = (f32[23,8,128]{2,1,0:T(8,128)S(1)}, f32[23,8,128]{2,1,0:T(8,128)S(1)}, u32[]{:S(2)}, u32[]{:S(2)}) collective-permute-start(f32[23,8,128]{2,1,0:T(8,128)S(1)} %corners.1), channel_id=1, source_target_pairs={{0,2},{2,0},{1,3},{3,1},{4,6},{6,4},{5,7},{7,5},{8,10},{10,8},{9,1... | collective-permute-start | bytes 282632 | tf_op jit(solution)/shard_map/ppermute | solution.py:420
  26.8 0.3 joins.1.joined_ref
  27.1 3.8 %collective-permute-done.4.rest_1_ = f32[23,8,128]{2,1,0:T(8,128)S(1)} collective-permute-done((f32[23,8,128]{2,1,0:T(8,128)S(1)}, f32[23,8,128]{2,1,0:T(8,128)S(1)}, u32[]{:S(2)}, u32[]{:S(2)}) %collective-permute-start.4) | collective-permute-done | bytes 94240 | tf_op jit(solution)/shard_map/ppermute | solution.py:420
  30.9 0.0 collective-permute-done.3.rest_0_
  30.9 0.0 copy-done.4
  30.9 0.0 copy-done.9
  30.9 5.7 %steps.1 = (f32[3,256,128]{2,1,0:T(8,128)}, f32[3,256,128]{2,1,0:T(8,128)}, f32[8,2,16]{2,1,0:T(2,128)S(1)}, f32[8,2,16]{2,1,0:T(2,128)S(1)}) custom-call(f32[8,128]{1,0:T(8,128)S(1)} %copy-done.4, s32[1,1,4]{2,1,0:T(1,128)S(1)} %copy-done.5, s32[1,1,4]{2,1,0:T(1,128)S(1)} %copy-done.9, f32[7,8,5,8,128]{4,3,2,1,0:T(8,128)S(1)} %get-tuple-element.18.state_ref, ...), custom_call_target="tpu_custom_call" | custom-call | tf_op jit(solution)/shard_map/steps/pallas_call | solution.py:497
  36.5 0.1 collective-permute-start.5
  36.6 1.2 %collective-permute-done.5 = f32[8,2,16]{2,1,0:T(2,128)S(1)} collective-permute-done((f32[8,2,16]{2,1,0:T(2,128)S(1)}, f32[8,2,16]{2,1,0:T(2,128)S(1)}, u32[]{:S(2)}, u32[]{:S(2)}) %collective-permute-start.5) | collective-permute-done | bytes 1056 | tf_op jit(solution)/shard_map/ppermute | solution.py:420
  37.8 10.3 %all_to_all.5 = f32[8,2,16]{2,1,0:T(2,128)S(1)} all-to-all(f32[8,2,16]{2,1,0:T(2,128)S(1)} %add.3), channel_id=1, replica_groups=mesh['grp'=2,'col'=4,'row'=2,'gz'=2] {'col','row'}, dimensions={0} | all-to-all | bytes 2048 | tf_op jit(solution)/shard_map/all_to_all | solution.py:518
  48.1 0.6 %reduce_sum.9 = f32[2,16]{1,0:T(2,128)} reduce(f32[8,2,16]{2,1,0:T(2,128)S(1)} %all_to_all.5, f32[]{:T(128)} %constant.1.clone.1), dimensions={0}, to_apply=%region_0.0 | reduce | flops 224 | bytes 1156 | tf_op jit(solution)/shard_map/reduce_sum | solution.py:519
  (8 shorter events, 0.0 us)
Async XLA Ops:
  0.6 1.0 %copy-start = (f32[3,32,8,128]{3,2,1,0:T(8,128)S(1)}, f32[3,32,8,128]{3,2,1,0:T(8,128)}, u32[]{:S(2)}) copy-start(f32[3,32,8,128]{3,2,1,0:T(8,128)} %elec_hbm.1) | copy-start | bytes 1179652
  1.6 1.0 %copy-start.1 = (f32[3,32,8,128]{3,2,1,0:T(8,128)S(1)}, f32[3,32,8,128]{3,2,1,0:T(8,128)}, u32[]{:S(2)}) copy-start(f32[3,32,8,128]{3,2,1,0:T(8,128)} %magn_hbm.1) | copy-start | bytes 1179652
  2.6 0.9 %copy-start.2 = (s32[32,8,128]{2,1,0:T(8,128)S(1)}, s32[32,8,128]{2,1,0:T(8,128)}, u32[]{:S(2)}) copy-start(s32[32,8,128]{2,1,0:T(8,128)} %mat_hbm.1) | copy-start | bytes 393220
  3.5 0.7 %copy-start.8 = (f32[8]{0:T(128)S(1)}, f32[8]{0:T(128)}, u32[]{:S(2)}) copy-start(f32[8]{0:T(128)} %eps_hbm.1) | copy-start | bytes 100
  5.0 25.9 %copy-start.4 = (f32[8,128]{1,0:T(8,128)S(1)}, f32[8,128]{1,0:T(8,128)}, u32[]{:S(2)}) copy-start(f32[8,128]{1,0:T(8,128)} %constant.4.clone.basis_ref) | copy-start | bytes 12292
  5.0 25.9 %copy-start.9 = (s32[1,1,4]{2,1,0:T(1,128)S(1)}, s32[1,1,4]{2,1,0:T(1,128)}, u32[]{:S(2)}) copy-start(s32[1,1,4]{2,1,0:T(1,128)} %pid_ref.1) | copy-start | bytes 52
  5.0 25.9 %collective-permute-start.3 = (f32[26,32,128]{2,1,0:T(8,128)S(1)}, f32[26,32,128]{2,1,0:T(8,128)S(1)}, u32[]{:S(2)}, u32[]{:S(2)}) collective-permute-start(f32[26,32,128]{2,1,0:T(8,128)S(1)} %get-tuple-element.23), channel_id=1, source_target_pairs={{0,2},{2,0},{1,3},{3,1},{4,6},{6,4},{5,7},{7,5},{8,10},{10,8},{9,1... | collective-permute-start | bytes 1277960 | tf_op jit(solution)/shard_map/ppermute | solution.py:420
  8.0 1.3 %collective-permute-start = (f32[7,4,8,128]{3,2,1,0:T(8,128)S(1)}, f32[7,4,8,128]{3,2,1,0:T(8,128)S(1)}, u32[]{:S(2)}, u32[]{:S(2)}) collective-permute-start(f32[7,4,8,128]{3,2,1,0:T(8,128)S(1)} %get-tuple-element.17), channel_id=1, source_target_pairs={{0,1},{1,0},{2,3},{3,2},{4,5},{5,4},{6,7},{7,6},{8,9},{9,8},{10,11... | collective-permute-start | bytes 344072 | tf_op jit(solution)/shard_map/ppermute | solution.py:420
  9.3 0.9 %copy-start.3 = (f32[8,32,64]{2,1,0:T(8,128)S(1)}, f32[8,32,64]{2,1,0:T(8,128)}, u32[]{:S(2)}) copy-start(f32[8,32,64]{2,1,0:T(8,128)} %mode_ref.1) | copy-start | bytes 196612
  10.2 0.7 %copy-start.5 = (s32[1,1,4]{2,1,0:T(1,128)S(1)}, s32[1,1,4]{2,1,0:T(1,128)}, u32[]{:S(2)}) copy-start(s32[1,1,4]{2,1,0:T(1,128)} %prow_ref.3) | copy-start | bytes 52
  10.9 0.7 %copy-start.6 = (s32[1,1,4]{2,1,0:T(1,128)S(1)}, s32[1,1,4]{2,1,0:T(1,128)}, u32[]{:S(2)}) copy-start(s32[1,1,4]{2,1,0:T(1,128)} %pcol_ref.1) | copy-start | bytes 52
  11.5 0.7 %copy-start.7 = (s32[1,1,4]{2,1,0:T(1,128)S(1)}, s32[1,1,4]{2,1,0:T(1,128)}, u32[]{:S(2)}) copy-start(s32[1,1,4]{2,1,0:T(1,128)} %pmode_ref.1) | copy-start | bytes 52
  16.8 5.1 %collective-permute-start.1 = (f32[2,5,8,128]{3,2,1,0:T(8,128)S(1)}, f32[2,5,8,128]{3,2,1,0:T(8,128)S(1)}, u32[]{:S(2)}, u32[]{:S(2)}) collective-permute-start(f32[2,5,8,128]{3,2,1,0:T(8,128)S(1)} %get-tuple-element.20), channel_id=1, source_target_pairs={{0,4},{4,8},{8,12},{1,5},{5,9},{9,13},{2,6},{6,10},{10,14},{3,7},{... | collective-permute-start | bytes 122888 | tf_op jit(solution)/shard_map/ppermute | solution.py:416
  20.3 5.9 %collective-permute-start.2 = (f32[2,5,8,128]{3,2,1,0:T(8,128)S(1)}, f32[2,5,8,128]{3,2,1,0:T(8,128)S(1)}, u32[]{:S(2)}, u32[]{:S(2)}) collective-permute-start(f32[2,5,8,128]{3,2,1,0:T(8,128)S(1)} %get-tuple-element.21), channel_id=1, source_target_pairs={{4,0},{8,4},{12,8},{5,1},{9,5},{13,9},{6,2},{10,6},{14,10},{7,3},{... | collective-permute-start | bytes 122888 | tf_op jit(solution)/shard_map/ppermute | solution.py:416
  26.2 4.6 %collective-permute-start.4 = (f32[23,8,128]{2,1,0:T(8,128)S(1)}, f32[23,8,128]{2,1,0:T(8,128)S(1)}, u32[]{:S(2)}, u32[]{:S(2)}) collective-permute-start(f32[23,8,128]{2,1,0:T(8,128)S(1)} %corners.1), channel_id=1, source_target_pairs={{0,2},{2,0},{1,3},{3,1},{4,6},{6,4},{5,7},{7,5},{8,10},{10,8},{9,1... | collective-permute-start | bytes 282632 | tf_op jit(solution)/shard_map/ppermute | solution.py:420
  36.5 1.2 %collective-permute-start.5 = (f32[8,2,16]{2,1,0:T(2,128)S(1)}, f32[8,2,16]{2,1,0:T(2,128)S(1)}, u32[]{:S(2)}, u32[]{:S(2)}) collective-permute-start(f32[8,2,16]{2,1,0:T(2,128)S(1)} %get-tuple-element.28), channel_id=1, source_target_pairs={{0,1},{1,0},{2,3},{3,2},{4,5},{5,4},{6,7},{7,6},{8,9},{9,8},{10,11... | collective-permute-start | bytes 3080 | tf_op jit(solution)/shard_map/ppermute | solution.py:420

commit v5 on v4

--- a/solution.py
+++ b/solution.py
@@ -60,9 +60,7 @@
         body(False, 1)
 
 
-def pack_kernel(row_size, eps_hbm, elec_hbm, magn_hbm, mat_hbm, main_ref, z_ref, *rest):
-    x_refs, (eps_ref, mat_ref, sems) = rest[:-3], rest[-3:]
-    block = LAYERS * ROWS
+def pack_kernel(eps_hbm, elec_hbm, magn_hbm, mat_hbm, main_ref, z_ref, eps_ref, mat_ref, sems):
     copies = [pltpu.make_async_copy(eps_hbm, eps_ref, sems.at[0]), pltpu.make_async_copy(mat_hbm, mat_ref, sems.at[1])]
     copies.append(pltpu.make_async_copy(elec_hbm, main_ref.at[pl.ds(0, 3)], sems.at[2]))
     copies.append(pltpu.make_async_copy(magn_hbm, main_ref.at[pl.ds(3, 3)], sems.at[3]))
@@ -78,38 +76,31 @@
         main_ref[6, z] = time_step * (1.0 / eps)
     copies[2].wait()
     copies[3].wait()
-    flat = main_ref.reshape(FIELDS * block, 128)
-
-    def send(up, slot):
-        for i, (f, x) in enumerate(UP_PLANES if up else DOWN_PLANES):
-            x_refs[slot][i] = flat[pl.ds(f * block + x, LAYERS, stride=ROWS), :]
-
-    directions(row_size, send)
     start = jnp.where(lax.axis_index("gz") == 0, LAYERS - DEPTH, 0)
     for f in range(FIELDS):
         z_ref[f] = main_ref[f, pl.ds(start, DEPTH)]
 
 
-def edge_kernel(main_ref, z_ref, mode_ref, prow_ref, pcol_ref, pmode_ref,
-                state_ref, own_ref, up_ref, down_ref, ext_ref, weight_ref, stage_ref, strip_ref):
+def edge_kernel(main_ref, z_ref, state_ref, own_ref, up_ref, down_ref, ext_ref):
     lane = iota(1)
-    group = lane // GROUP
-    place = lane % GROUP
+    group, place = lane // GROUP, lane % GROUP
     gz = lax.axis_index("gz")
     block = LAYERS * ROWS
+    flat = main_ref.reshape(FIELDS * block, 128)
     for f in range(FIELDS):
-        stage_ref[f, 0:block] = main_ref[f].reshape(block, 128)
         halo = z_ref[f].reshape(DEPTH * ROWS, 128)
         nothing = jnp.zeros_like(halo)
-        stage_ref[f, block : block + DEPTH * ROWS] = jnp.where(gz == 0, halo, nothing)
-        stage_ref[f, block + DEPTH * ROWS :] = jnp.where(gz == 0, nothing, halo)
-        ext_ref[f] = stage_ref[f, block:]
+        ext_ref[f, : DEPTH * ROWS] = jnp.where(gz == 0, halo, nothing)
+        ext_ref[f, DEPTH * ROWS :] = jnp.where(gz == 0, nothing, halo)
+
+    def tile(f, x, zz):
+        if zz == CHUNK - 1:
+            return ext_ref[f, pl.ds(x, 8, stride=ROWS), :]
+        return flat[pl.ds(f * block + zz * 8 * ROWS + x, 8, stride=ROWS), :]
+
     for b in range(2):
         for zz in range(CHUNK):
-            tiles = [
-                [stage_ref[f, pl.ds(zz * ROWS + 4 * b + r, 8, stride=CHUNK * ROWS), :] for r in range(4)]
-                for f in range(FIELDS)
-            ]
+            tiles = [[tile(f, 4 * b + r, zz) for r in range(4)] for f in range(FIELDS)]
             up = jnp.zeros((8, 128), jnp.float32)
             down = jnp.zeros((8, 128), jnp.float32)
             owns = []
@@ -126,36 +117,31 @@
                 own_ref[f, b, zz] = owns[f]
             up_ref[b, zz] = up
             down_ref[b, zz] = down
-    for k in range(PORT_TILE):
-        strip_ref[...] = jnp.zeros(strip_ref.shape, jnp.float32)
-        strip_ref[0:LAYERS, 0:PLEN] = mode_ref[pmode_ref[0, 0, k]]
-        strip_ref[...] = pltpu.roll(strip_ref[...], pcol_ref[0, 0, k], 1)
-        at = lane - GROUP * (prow_ref[0, 0, k] % 4)
-        for zz in range(CHUNK):
-            tile = strip_ref[pl.ds(zz, 8, stride=CHUNK), :]
-            weight_ref[k, 0, zz] = jnp.where((lane >= DEPTH) & (lane < 128 - DEPTH), tile, 0.0)
-            own = pltpu.roll(tile, GROUP * (prow_ref[0, 0, k] % 4) + 8, 1)
-            edge = jnp.where((at >= 4) & (at < 8), own, 0.0)
-            weight_ref[k, 1, zz] = jnp.where((at >= 16) & (at < 20), turn(own, 8, 1), edge)
-
-
-def corner_kernel(row_size, ext_ref, low_ref, high_ref, *x_refs):
+
+
+def plane_kernel(row_size, state_ref, *x_refs):
     def send(up, slot):
         planes = UP_PLANES if up else DOWN_PLANES
-
-        def tile(i):
+        for i, (f, x) in enumerate(planes):
+            for zz in range(CHUNK - 1):
+                x_refs[slot][i * (CHUNK - 1) + zz] = state_ref[f, x, zz]
+        for i in range(PAIRS):
             f, x = planes[i]
-            return ext_ref[f, pl.ds(x, 8, stride=ROWS), :]
-
-        for i in range(PAIRS):
-            first = tile(i)
+            pair = state_ref[f, x, CHUNK - 1]
             if i + PAIRS < len(planes):
-                first = first + turn(tile(i + PAIRS), 4, 0)
-            x_refs[slot][i] = first
+                f, x = planes[i + PAIRS]
+                pair = pair + turn(state_ref[f, x, CHUNK - 1], 4, 0)
+            x_refs[slot][PLANES * (CHUNK - 1) + i] = pair
+
+    directions(row_size, send)
+
+
+def corner_kernel(row_size, low_ref, high_ref, *x_refs):
+    def send(up, slot):
         b = 1 if up else 0
         for zz in range(CHUNK):
-            x_refs[slot][PAIRS + zz] = low_ref[b, zz]
-            x_refs[slot][PAIRS + CHUNK + zz] = high_ref[b, zz]
+            x_refs[slot][zz] = low_ref[b, zz]
+            x_refs[slot][CHUNK + zz] = high_ref[b, zz]
 
     directions(row_size, send)
 
@@ -167,19 +153,31 @@
     return jnp.where(place < 8, own, out)
 
 
-def join_kernel(own_ref, low_ref, high_ref, edge_ref):
+def join_kernel(own_ref, low_ref, high_ref, mode_ref, prow_ref, pcol_ref, pmode_ref, edge_ref, weight_ref, strip_ref):
     for b in range(2):
         for zz in range(CHUNK):
             low, high = low_ref[b, zz], high_ref[b, zz]
             tiles = [edge_tile(own_ref[f, b, zz], low, high, f) for f in range(FIELDS)]
             for f in range(FIELDS):
                 edge_ref[f, b, zz] = tiles[f]
-
-
-def step_kernel(row_size, ports_each, basis_ref, prow_ref, pid_ref, state_ref, joined_ref, weight_ref, *rest):
+    lane = iota(1)
+    for k in range(PORT_TILE):
+        strip_ref[k] = jnp.zeros(strip_ref.shape[1:], jnp.float32)
+        strip_ref[k, :, 0:PLEN] = mode_ref[pmode_ref[0, 0, k]]
+        turned = GROUP * (prow_ref[0, 0, k] % 4)
+        at = lane - turned
+        for zz in range(CHUNK - 1):
+            tile = pltpu.roll(strip_ref[k, 8 * zz : 8 * zz + 8, :], pcol_ref[0, 0, k], 1)
+            weight_ref[k, 0, zz] = jnp.where((lane >= DEPTH) & (lane < 128 - DEPTH), tile, 0.0)
+            own = pltpu.roll(tile, turned + 8, 1)
+            edge = jnp.where((at >= 4) & (at < 8), own, 0.0)
+            weight_ref[k, 1, zz] = jnp.where((at >= 16) & (at < 20), turn(own, 8, 1), edge)
+
+
+def step_kernel(row_size, basis_ref, prow_ref, pid_ref, state_ref, joined_ref, weight_ref, *rest):
     n_x = 1 if row_size == 2 else 2
     x_refs, corner_refs = rest[:n_x], rest[n_x : 2 * n_x]
-    eout_hbm, hout_hbm, keep_ref, send_ref, main_e, main_h, main_c, edge_e, edge_h, edge_c, plane_ref, sum_ref, out_ref, sems = rest[2 * n_x :]
+    eout_hbm, hout_hbm, term_ref, main_e, main_h, main_c, edge_e, edge_h, edge_c, sum_ref, out_ref, sems = rest[2 * n_x :]
     gz, row, col = (lax.axis_index(name) for name in ("gz", "row", "col"))
     lane, sub = iota(1), iota(0)
     place, group = lane % GROUP, lane // GROUP
@@ -213,20 +211,16 @@
             valid = (sub < 4) == (gz == 0)
             got = set(planes)
             for i, (f, x) in enumerate(planes):
-                packed = corner_refs[slot][i % PAIRS]
+                rows = [x_refs[slot][i * (CHUNK - 1) + zz] for zz in range(CHUNK - 1)]
+                packed = x_refs[slot][PLANES * (CHUNK - 1) + i % PAIRS]
                 if i >= PAIRS:
                     packed = turn(packed, 4, 0)
-                plane_ref[slot, i, 0:LAYERS] = x_refs[slot][i]
-                plane_ref[slot, i, LAYERS:] = jnp.where(valid, packed, 0.0)
-            rows = {}
-            for i, (f, x) in enumerate(planes):
+                rows.append(jnp.where(valid, packed, 0.0))
                 for zz in range(CHUNK):
-                    rows[f, x, zz] = plane_ref[slot, i, pl.ds(zz, 8, stride=CHUNK), :]
-                for zz in range(CHUNK):
-                    put(main_e, main_h, main_c, f, DEPTH + x + offset, zz, rows[f, x, zz])
+                    put(main_e, main_h, main_c, f, DEPTH + x + offset, zz, rows[zz])
             for zz in range(CHUNK):
-                low = corner_refs[slot][PAIRS + zz]
-                high = corner_refs[slot][PAIRS + CHUNK + zz]
+                low = corner_refs[slot][zz]
+                high = corner_refs[slot][CHUNK + zz]
                 tiles = []
                 for f in range(FIELDS):
                     own = zeros
@@ -244,17 +238,19 @@
         if has_above:
             halo_rows(DOWN_PLANES, n_x - 1, ROWS, 2)
 
-        below_layers = (sub == 7) & (gz == 0)
-        half = [jnp.where(below_layers, 0.0, time_step) if zz else jnp.full((8, 128), time_step) for zz in range(CHUNK)]
+        half = [jnp.full((8, 128), time_step)] * (CHUNK - 1)
+        half.append(jnp.where((sub >= 4) & (gz == 0), 0.0, time_step))
         outside = (place >= 12) & (place < 16) & (col == 0)
         edge_half = [jnp.where(outside, 0.0, half[zz]) for zz in range(CHUNK)]
         lowest = jnp.where(row == 0, 0.0, 1.0) if row_size > 2 else None
 
-        def above(tiles, zz):
-            return tiles[zz + 1] if zz + 1 < CHUNK else turn(tiles[0], -1, 0)
-
-        def beneath(tiles, zz):
-            return tiles[zz - 1] if zz else turn(tiles[CHUNK - 1], 1, 0)
+        def above(tiles):
+            turned = [turn(v, -1, 0) for v in tiles]
+            return [jnp.where(sub == 7, turned[(zz + 1) % CHUNK], turned[zz]) for zz in range(CHUNK)]
+
+        def beneath(tiles):
+            turned = [turn(v, 1, 0) for v in tiles]
+            return [jnp.where(sub == 0, turned[zz - 1], turned[zz]) for zz in range(CHUNK)]
 
         blank = [zeros] * CHUNK
         every = range(CHUNK)
@@ -269,10 +265,10 @@
         def phases(n, items, final, at, keep_e, keep_h, across, half_of, only_h):
             def load_e(i):
                 ex, ey, ez = ([at(f, i, zz, n) for zz in every] for f in range(3))
-                return ex, ey, ez, [turn(v, -1, 1) for v in ex], [turn(v, -1, 1) for v in ez], across(ey, -1), across(ez, -1)
+                return ex, ey, ez, [turn(v, -1, 1) for v in ex], [turn(v, -1, 1) for v in ez], across(ey, -1), across(ez, -1), above(ex), above(ey)
 
             def work_h(i, loaded):
-                ex, ey, ez, ex_right, ez_right, ey_own, ez_own = loaded[i]
+                ex, ey, ez, ex_right, ez_right, ey_own, ez_own, ex_above, ey_above = loaded[i]
                 old = [[at(f, i, zz, n) for zz in every] for f in (3, 4, 5)]
                 h = half_of(i)
                 if i + 1 in loaded:
@@ -284,8 +280,8 @@
                 ey_up, ez_up = across.pick(ey_own, after[5]), across.pick(ez_own, after[6])
                 new = []
                 for zz in every:
-                    hx = (ez_right[zz] - ez[zz]) - (above(ey, zz) - ey[zz])
-                    hy = (above(ex, zz) - ex[zz]) - (ez_up[zz] - ez[zz])
+                    hx = (ez_right[zz] - ez[zz]) - (ey_above[zz] - ey[zz])
+                    hy = (ex_above[zz] - ex[zz]) - (ez_up[zz] - ez[zz])
                     hz = (ey_up[zz] - ey[zz]) - (ex_right[zz] - ex[zz])
                     new.append([old[c][zz] - h[zz] * v for c, v in enumerate((hx, hy, hz))])
                 for zz in every:
@@ -297,22 +293,22 @@
                 hy, hz = ([keep_h[c, i, zz] for zz in every] for c in (1, 2))
                 shifted_h = across(hy, 1), across(hz, 1)
                 if i in only_h:
-                    return None, hy, hz, None, None, *shifted_h
+                    return None, hy, hz, None, None, *shifted_h, None, None
                 hx = [keep_h[0, i, zz] for zz in every]
-                return hx, hy, hz, [turn(v, 1, 1) for v in hx], [turn(v, 1, 1) for v in hz], *shifted_h
+                return hx, hy, hz, [turn(v, 1, 1) for v in hx], [turn(v, 1, 1) for v in hz], *shifted_h, beneath(hx), beneath(hy)
 
             def work_e(i, loaded):
                 if i in only_h:
                     return
-                hx, hy, hz, hx_left, hz_left, hy_own, hz_own = loaded[i]
+                hx, hy, hz, hx_left, hz_left, hy_own, hz_own, hx_beneath, hy_beneath = loaded[i]
                 old = [[at(f, i, zz, n) for zz in every] for f in range(3)]
                 coef = [at(6, i, zz, n) for zz in every]
                 before = loaded.get(i - 1, [blank] * 7)
                 hy_down, hz_down = across.pick(hy_own, before[5]), across.pick(hz_own, before[6])
                 new = []
                 for zz in every:
-                    ex = (hz[zz] - hz_left[zz]) - (hy[zz] - beneath(hy, zz))
-                    ey = (hx[zz] - beneath(hx, zz)) - (hz[zz] - hz_down[zz])
+                    ex = (hz[zz] - hz_left[zz]) - (hy[zz] - hy_beneath[zz])
+                    ey = (hx[zz] - hx_beneath[zz]) - (hz[zz] - hz_down[zz])
                     ez = (hy[zz] - hy_down[zz]) - (hx[zz] - hx_left[zz])
                     new.append([old[c][zz] + coef[zz] * v for c, v in enumerate((ex, ey, ez))])
                 for zz in every:
@@ -363,7 +359,7 @@
             for k in range(PORT_TILE):
                 at = prow_ref[0, 0, k]
                 total = zeros
-                for zz in range(CHUNK):
+                for zz in range(CHUNK - 1):
                     total = total + main_e[2, DEPTH + at, zz] * weight_ref[k, 0, zz]
                     total = total + edge_e[2, 1 + at // 4, zz] * weight_ref[k, 1, zz]
                 sum_ref[n - 1, k : k + 1, :] = jnp.sum(total, axis=0, keepdims=True)
@@ -378,35 +374,28 @@
     for f in range(6):
         main, edge = (main_e, edge_e) if f < 3 else (main_h, edge_h)
         for b in range(2):
-            tiles = [edge[f % 3, 1 + b, zz] for zz in range(CHUNK)]
+            tiles = [edge[f % 3, 1 + b, zz] for zz in range(CHUNK - 1)]
             near = [jnp.where(place < 8, tile, turn(tile, -8, 1)) for tile in tiles]
             done = {}
             for r in range(4):
-                for zz in range(CHUNK):
+                for zz in range(CHUNK - 1):
                     sides = turn(near[zz], -(GROUP * r + 8), 1)
                     own = main[f % 3, DEPTH + 4 * b + r, zz]
                     done[r, zz] = jnp.where((lane < DEPTH) | (lane >= 128 - DEPTH), sides, own)
             for (r, zz), tile in done.items():
-                out_ref[f, pl.ds(zz * ROWS + 4 * b + r, 8, stride=CHUNK * ROWS), :] = tile
+                out_ref[f, pl.ds(zz * 8 * ROWS + 4 * b + r, 8, stride=ROWS), :] = tile
         dest = eout_hbm if f < 3 else hout_hbm
-        copies.append(pltpu.make_async_copy(out_ref.at[f, pl.ds(0, LAYERS * ROWS)], dest.at[f % 3], sems.at[f]))
+        copies.append(pltpu.make_async_copy(out_ref.at[f], dest.at[f % 3], sems.at[f]))
         copies[-1].start()
 
     transform = zeros
     for n in range(STEPS):
         sampled = jnp.sum(sum_ref[n], axis=1, keepdims=True)
         transform = transform + sampled * basis_ref[n : n + 1, :]
-    keep_ref[...] = jnp.zeros(keep_ref.shape, jnp.float32)
-    send_ref[...] = jnp.zeros(send_ref.shape, jnp.float32)
+    term_ref[...] = transform[:PORT_TILE, : 4 * FREQ]
     for k in range(PORT_TILE):
-        port = pid_ref[0, 0, k]
-        device = port // ports_each
-
-        def place_in(ref, k=k, port=port, device=device):
-            ref[device // 2, pl.ds(port % ports_each, 1), :] = transform[k : k + 1, : 2 * FREQ]
-
-        pl.when(device % 2 == gz)(functools.partial(place_in, keep_ref))
-        pl.when(device % 2 != gz)(functools.partial(place_in, send_ref))
+        port = jnp.full((1, 2 * FREQ), pid_ref[0, 0, k]).astype(jnp.float32)
+        term_ref[k : k + 1, 2 * FREQ :] = port
     for copy in copies:
         copy.wait()
 
@@ -438,67 +427,69 @@
         def array(*shape):
             return jax.ShapeDtypeStruct(shape, f32)
 
-        main, z_send, *x_send = pl.pallas_call(
-            functools.partial(pack_kernel, row_size),
-            out_shape=[array(FIELDS, LAYERS, ROWS, 128), array(FIELDS, DEPTH, ROWS, 128)]
-            + [array(PLANES, LAYERS, 128)] * n_x,
+        main, z_send = pl.pallas_call(
+            pack_kernel,
+            out_shape=[array(FIELDS, LAYERS, ROWS, 128), array(FIELDS, DEPTH, ROWS, 128)],
             in_specs=[HBM] * 4,
-            out_specs=[VMEM] * (2 + n_x),
+            out_specs=[VMEM] * 2,
             scratch_shapes=[
                 pltpu.SMEM(eps_table.shape, f32),
                 pltpu.VMEM(material.shape, jnp.int32),
                 pltpu.SemaphoreType.DMA((4,)),
             ],
-            compiler_params=PARAMS,
             name="pack",
         )(eps_table, electric, magnetic, material)
-        x_halo = across_rows(x_send)
         z_halo = swapped(z_send, "gz", gz_size)
-        state, own, up_send, down_send, ext, weights = pl.pallas_call(
+        state, own, up_send, down_send = pl.pallas_call(
             edge_kernel,
             out_shape=[
                 array(FIELDS, ROWS, CHUNK, 8, 128),
                 array(FIELDS, 2, CHUNK, 8, 128),
                 array(2, CHUNK, 8, 128),
                 array(2, CHUNK, 8, 128),
-                array(FIELDS, 2 * DEPTH * ROWS, 128),
-                array(PORT_TILE, 2, CHUNK, 8, 128),
             ],
-            in_specs=[VMEM] * 3 + [SMEM] * 3,
-            out_specs=[VMEM] * 6,
-            scratch_shapes=[
-                pltpu.VMEM((FIELDS, 8 * CHUNK * ROWS, 128), f32),
-                pltpu.VMEM((8 * CHUNK, 128), f32),
-            ],
+            in_specs=[VMEM] * 2,
+            out_specs=[VMEM] * 4,
+            scratch_shapes=[pltpu.VMEM((FIELDS, 8 * ROWS, 128), f32)],
             compiler_params=PARAMS,
             name="edges",
-        )(main, z_halo, mode_table, port_row, port_col, port_mode)
+        )(main, z_halo)
         low = shifted(up_send, "col", col_size, 1)
         high = shifted(down_send, "col", col_size, -1)
+        x_send = pl.pallas_call(
+            functools.partial(plane_kernel, row_size),
+            out_shape=[array(PLANES * (CHUNK - 1) + PAIRS, 8, 128)] * n_x,
+            in_specs=[VMEM],
+            out_specs=[VMEM] * n_x,
+            compiler_params=PARAMS,
+            name="planes",
+        )(state)
+        x_halo = across_rows(x_send)
         corner_send = pl.pallas_call(
             functools.partial(corner_kernel, row_size),
-            out_shape=[array(PAIRS + 2 * CHUNK, 8, 128)] * n_x,
-            in_specs=[VMEM] * 3,
+            out_shape=[array(2 * CHUNK, 8, 128)] * n_x,
+            in_specs=[VMEM] * 2,
             out_specs=[VMEM] * n_x,
             compiler_params=PARAMS,
             name="corners",
-        )(ext, low, high)
+        )(low, high)
         corner = across_rows(corner_send)
         devices = col_size * row_size * gz_size
         ports_each = PORT_TILE * col_size * row_size // devices
-        edges = pl.pallas_call(
+        edges, weights = pl.pallas_call(
             join_kernel,
-            out_shape=array(FIELDS, 2, CHUNK, 8, 128),
-            in_specs=[VMEM] * 3,
-            out_specs=VMEM,
+            out_shape=[array(FIELDS, 2, CHUNK, 8, 128), array(PORT_TILE, 2, CHUNK - 1, 8, 128)],
+            in_specs=[VMEM] * 4 + [SMEM] * 3,
+            out_specs=[VMEM] * 2,
+            scratch_shapes=[pltpu.VMEM((PORT_TILE, LAYERS, 128), f32)],
             compiler_params=PARAMS,
             name="joins",
-        )(own, low, high)
-        electric_out, magnetic_out, keep, send = pl.pallas_call(
-            functools.partial(step_kernel, row_size, ports_each),
-            out_shape=[array(3, LAYERS * ROWS, 128)] * 2 + [array(devices // 2, ports_each, 2 * FREQ)] * 2,
+        )(own, low, high, mode_table, port_row, port_col, port_mode)
+        electric_out, magnetic_out, term = pl.pallas_call(
+            functools.partial(step_kernel, row_size),
+            out_shape=[array(3, LAYERS * ROWS, 128)] * 2 + [array(PORT_TILE, 4 * FREQ)],
             in_specs=[VMEM] + [SMEM] * 2 + [VMEM] * (3 + 2 * n_x),
-            out_specs=[HBM, HBM, VMEM, VMEM],
+            out_specs=[HBM, HBM, VMEM],
             scratch_shapes=[
                 pltpu.VMEM((3, ROWS + 2 * DEPTH, CHUNK, 8, 128), f32),
                 pltpu.VMEM((3, ROWS + 2 * DEPTH, CHUNK, 8, 128), f32),
@@ -506,17 +497,22 @@
                 pltpu.VMEM((3, 4, CHUNK, 8, 128), f32),
                 pltpu.VMEM((3, 4, CHUNK, 8, 128), f32),
                 pltpu.VMEM((4, CHUNK, 8, 128), f32),
-                pltpu.VMEM((n_x, PLANES, 8 * CHUNK, 128), f32),
                 pltpu.VMEM((STEPS, 8, 128), f32),
-                pltpu.VMEM((6, 8 * CHUNK * ROWS, 128), f32),
+                pltpu.VMEM((6, LAYERS * ROWS, 128), f32),
                 pltpu.SemaphoreType.DMA((6,)),
             ],
             compiler_params=PARAMS,
             name="steps",
         )(jnp.asarray(dft_basis()), port_row, port_ids, state, edges, weights, *x_halo, *corner)
-        terms = keep + swapped(send, "gz", gz_size)
-        terms = lax.all_to_all(terms, ("col", "row"), 0, 0, tiled=True)
-        mine = jnp.sum(terms, axis=0)
+        names = ("col", "row", "gz")
+        terms = lax.all_gather(term, names, axis=0, tiled=True)
+        first = lax.axis_index(names) * ports_each
+        mine = jnp.stack(
+            [
+                jnp.sum(jnp.where(terms[:, 2 * FREQ :] == first + j, terms[:, : 2 * FREQ], 0.0), axis=0)
+                for j in range(ports_each)
+            ]
+        )
         return (
             electric_out.reshape(electric.shape),
             magnetic_out.reshape(magnetic.shape),

time: 49 us -> 52.9 us (1.080)
  blocking collectives: 10.3 us -> 20.8 us
  local copies, waits for them, and re-layouts: 6.42 us -> 1.21 us
  waiting for transfers between devices: 10.8 us -> 8.3 us
  Pallas kernels: 11.3 us -> 12.2 us
    all_gather x0 -> x1, blocking collectives: none -> 20.8 us  [per_device(): terms = lax.all_gather(term, names, axis=0, tiled=True)]
    all_to_all x1 -> x0, blocking collectives: 10.3 us -> none  [per_device(): terms = lax.all_to_all(terms, ('col', 'row'), 0, 0, tiled=True)]
    unnamed x20 -> x14, local copies, waits for them, and re-layouts: 6.42 us -> 1.21 us
    ppermute x4 -> x3, waiting for transfers between devices: 6.24 us -> 3.7 us  [swapped(): return lax.ppermute(block, axis, [(i, i ^ 1) for i in range(size)])]
    pallas_call x3 -> x4, Pallas kernels: 6.69 us -> 8.68 us  [the longest x1 5.54 us: per_device(): pl.pallas_call(functools.partial(step_kernel, row_size), out_shape=[array...]
    pallas_call x1, Pallas kernels: 4.62 us -> 3.56 us  [per_device(): pl.pallas_call(edge_kernel, out_shape=[array(FIELDS, ROWS, CHUNK, 8, 128)...]
    another operation x0 -> x1, other arithmetic: none -> 0.58 us  [per_device(): jnp.stack([jnp.sum(jnp.where(terms[:, 2 * FREQ:] == first + j, terms[:, :...]
    ppermute x4 -> x3, starting transfers between devices: 3.67 us -> 3.96 us  [swapped(): return lax.ppermute(block, axis, [(i, i ^ 1) for i in range(size)])]
  transfers between devices with their start and end apart: 6 -> 5, of which waited for: 5 -> 4; matrix products, arithmetic and copies ran while one was open for 0% -> 0% of each run, Pallas kernels for 10% -> 2%
where the time goes in v5:
time: 52.9 us; the launch traced here: 52.7 us
  blocking collectives  20.8 us (39%)
  Pallas kernels  12.2 us (23%)
  starting transfers between devices  8.73 us (17%)
  waiting for transfers between devices  8.3 us (16%)
  local copies, waits for them, and re-layouts  1.21 us (2%)
  between operations  0.74 us (1%)
  other arithmetic  0.67 us (1%)
    all_gather x1, blocking collectives, per_device(): terms = lax.all_gather(term, names, axis=0, tiled=True)  20.8 us
    pallas_call x1, Pallas kernels, per_device(): pl.pallas_call(functools.partial(step_kernel, row_size), out_shape=[array...  5.54 us
    ppermute x2, starting transfers between devices, shifted(): return lax.ppermute(block, axis, route)  4.76 us
    ppermute x2, waiting for transfers between devices, shifted(): return lax.ppermute(block, axis, route)  4.6 us
    ppermute x3, starting transfers between devices, swapped(): return lax.ppermute(block, axis, [(i, i ^ 1) for i in range(size)])  3.96 us
    ppermute x3, waiting for transfers between devices, swapped(): return lax.ppermute(block, axis, [(i, i ^ 1) for i in range(size)])  3.7 us
    pallas_call x1, Pallas kernels, per_device(): pl.pallas_call(edge_kernel, out_shape=[array(FIELDS, ROWS, CHUNK, 8, 128)...  3.56 us
    pallas_call x1, Pallas kernels, per_device(): pl.pallas_call(pack_kernel, out_shape=[array(FIELDS, LAYERS, ROWS, 128),...  2.17 us
  transfers between devices with their start and end apart: 5, of which 4 were waited for; matrix products, arithmetic and copies ran while one was open for 0% of the time, Pallas kernels for 2%

profile of v5, /device:TPU:0, one launch (start us, length us, event | category | flops | bytes accessed | tf_op | source)
XLA Modules:
  0.0 52.7 jit_solution(16604903544756287562)
XLA Ops:
  0.6 2.2 %pack.1 = (f32[7,32,8,128]{3,2,1,0:T(8,128)}, f32[7,4,8,128]{3,2,1,0:T(8,128)}) custom-call(f32[8]{0:T(128)} %eps_hbm.1, f32[3,32,8,128]{3,2,1,0:T(8,128)} %elec_hbm.1, f32[3,32,8,128]{3,2,1,0:T(8,128)} %magn_hbm.1, s32[32,8,128]{2,1,0:T(8,128)} %mat_hbm.1), custom_call_target="tpu_custom_call" | custom-call | tf_op jit(solution)/shard_map/pack/pallas_call | solution.py:430
  2.8 0.5 collective-permute-start
  3.3 1.2 %collective-permute-done.z_ref = f32[7,4,8,128]{3,2,1,0:T(8,128)S(1)} collective-permute-done((f32[7,4,8,128]{3,2,1,0:T(8,128)}, f32[7,4,8,128]{3,2,1,0:T(8,128)S(1)}, u32[]{:S(2)}, u32[]{:S(2)}) %collective-permute-start) | collective-permute-done | bytes 114720 | tf_op jit(solution)/shard_map/ppermute | solution.py:409
  4.5 0.0 copy-start
  4.5 1.2 %copy-done = f32[7,32,8,128]{3,2,1,0:T(8,128)S(1)} copy-done((f32[7,32,8,128]{3,2,1,0:T(8,128)S(1)}, f32[7,32,8,128]{3,2,1,0:T(8,128)}, u32[]{:S(2)}) %copy-start) | copy-done | bytes 917528
  5.7 3.6 %edges.1 = (f32[7,8,5,8,128]{4,3,2,1,0:T(8,128)S(1)}, f32[7,2,5,8,128]{4,3,2,1,0:T(8,128)S(1)}, f32[2,5,8,128]{3,2,1,0:T(8,128)S(1)}, f32[2,5,8,128]{3,2,1,0:T(8,128)S(1)}) custom-call(f32[7,32,8,128]{3,2,1,0:T(8,128)S(1)} %copy-done, f32[7,4,8,128]{3,2,1,0:T(8,128)S(1)} %collective-permute-done.z_ref), custom_call_target="tpu_custom_call" | custom-call | tf_op jit(solution)/shard_map/edges/pallas_call | solution.py:443
  9.2 0.0 copy-start.1
  9.3 0.0 copy-start.3
  9.3 0.0 copy-start.4
  9.3 0.0 copy-start.5
  9.3 0.0 copy-start.2
  9.3 0.0 copy-start.6
  9.3 0.1 planes.1
  9.4 2.9 %collective-permute-start.3 = (f32[117,8,128]{2,1,0:T(8,128)S(1)}, f32[117,8,128]{2,1,0:T(8,128)S(1)}, u32[]{:S(2)}, u32[]{:S(2)}) collective-permute-start(f32[117,8,128]{2,1,0:T(8,128)S(1)} %planes.1), channel_id=1, source_target_pairs={{0,2},{2,0},{1,3},{3,1},{4,6},{6,4},{5,7},{7,5},{8,10},{10,8},{9,1... | collective-permute-start | bytes 1437704 | tf_op jit(solution)/shard_map/ppermute | solution.py:409
  12.3 3.5 %collective-permute-start.1 = (f32[2,5,8,128]{3,2,1,0:T(8,128)S(1)}, f32[2,5,8,128]{3,2,1,0:T(8,128)S(1)}, u32[]{:S(2)}, u32[]{:S(2)}) collective-permute-start(f32[2,5,8,128]{3,2,1,0:T(8,128)S(1)} %get-tuple-element.18), channel_id=1, source_target_pairs={{0,4},{4,8},{8,12},{1,5},{5,9},{9,13},{2,6},{6,10},{10,14},{3,7},{... | collective-permute-start | bytes 122888 | tf_op jit(solution)/shard_map/ppermute | solution.py:405
  15.8 1.3 %collective-permute-start.2 = (f32[2,5,8,128]{3,2,1,0:T(8,128)S(1)}, f32[2,5,8,128]{3,2,1,0:T(8,128)S(1)}, u32[]{:S(2)}, u32[]{:S(2)}) collective-permute-start(f32[2,5,8,128]{3,2,1,0:T(8,128)S(1)} %get-tuple-element.19), channel_id=1, source_target_pairs={{4,0},{8,4},{12,8},{5,1},{9,5},{13,9},{6,2},{10,6},{14,10},{7,3},{... | collective-permute-start | bytes 122888 | tf_op jit(solution)/shard_map/ppermute | solution.py:405
  17.1 0.4 collective-permute-done.1.low_ref
  17.4 4.2 %collective-permute-done.2.high_ref = f32[2,5,8,128]{3,2,1,0:T(8,128)S(1)} collective-permute-done((f32[2,5,8,128]{3,2,1,0:T(8,128)S(1)}, f32[2,5,8,128]{3,2,1,0:T(8,128)S(1)}, u32[]{:S(2)}, u32[]{:S(2)}) %collective-permute-start.2) | collective-permute-done | bytes 40992 | tf_op jit(solution)/shard_map/ppermute | solution.py:405
  21.7 0.5 %collective-permute-start.4 = (f32[10,8,128]{2,1,0:T(8,128)S(1)}, f32[10,8,128]{2,1,0:T(8,128)S(1)}, u32[]{:S(2)}, u32[]{:S(2)}) collective-permute-start(f32[10,8,128]{2,1,0:T(8,128)S(1)} %corners.1), channel_id=1, source_target_pairs={{0,2},{2,0},{1,3},{3,1},{4,6},{6,4},{5,7},{7,5},{8,10},{10,8},{9,1... | collective-permute-start | bytes 122888 | tf_op jit(solution)/shard_map/ppermute | solution.py:409
  22.2 0.0 copy-done.1
  22.2 0.0 copy-done.3
  22.2 0.0 copy-done.4
  22.2 0.0 copy-done.5
  22.2 0.9 %joins.1 = (f32[7,2,5,8,128]{4,3,2,1,0:T(8,128)S(1)}, f32[4,2,4,8,128]{4,3,2,1,0:T(8,128)S(1)}) custom-call(f32[7,2,5,8,128]{4,3,2,1,0:T(8,128)S(1)} %get-tuple-element.17.own_ref, f32[2,5,8,128]{3,2,1,0:T(8,128)S(1)} %collective-permute-done.1.low_ref, f32[2,5,8,128]{3,2,1,0:T(8,128)S(1)} %collective-permute-done.2.high_ref, f32[8,32,64]{2,1,0:T(8,128)S(1)} %copy-done.1, ...), custom_call_target="tpu_custom_call" | custom-call | tf_op jit(solution)/shard_map/joins/pallas_call | solution.py:479
  23.1 2.5 %collective-permute-done.4.rest_1_ = f32[10,8,128]{2,1,0:T(8,128)S(1)} collective-permute-done((f32[10,8,128]{2,1,0:T(8,128)S(1)}, f32[10,8,128]{2,1,0:T(8,128)S(1)}, u32[]{:S(2)}, u32[]{:S(2)}) %collective-permute-start.4) | collective-permute-done | bytes 40992 | tf_op jit(solution)/shard_map/ppermute | solution.py:409
  25.7 0.0 collective-permute-done.3.rest_0_
  25.7 0.0 copy-done.2
  25.7 0.0 copy-done.6
  25.7 5.5 %steps.1 = (f32[3,256,128]{2,1,0:T(8,128)}, f32[3,256,128]{2,1,0:T(8,128)}, f32[4,32]{1,0:T(4,128)S(1)}) custom-call(f32[8,128]{1,0:T(8,128)S(1)} %copy-done.2, s32[1,1,4]{2,1,0:T(1,128)S(1)} %copy-done.3, s32[1,1,4]{2,1,0:T(1,128)S(1)} %copy-done.6, f32[7,8,5,8,128]{4,3,2,1,0:T(8,128)S(1)} %get-tuple-element.16.state_ref, ...), custom_call_target="tpu_custom_call" | custom-call | tf_op jit(solution)/shard_map/steps/pallas_call | solution.py:488
  31.2 20.8 %all-gather = f32[16,4,32]{2,1,0:T(4,128)S(1)} all-gather(f32[1,4,32]{2,1,0:T(4,128)S(1)} %bitcast.6), channel_id=1, replica_groups=mesh['grp'=2,'col'=4,'row'=2,'gz'=2] {'col','row','gz'}, dimensions={0}, use_global_device_ids=true | all-gather | bytes 8704 | tf_op jit(solution)/shard_map/all_gather | solution.py:508
  52.0 0.1 select_reduce_fusion.1
  52.1 0.6 %pad_maximum_fusion = f32[2,16]{1,0:T(2,128)} fusion(f32[1,16]{1,0:T(1,128)S(1)} %bitcast.9, f32[1,16]{1,0:T(1,128)S(1)} %bitcast.8), kind=kLoop, calls=%fused_computation.2 | loop fusion | flops 32 | bytes 256 | tf_op jit(solution)/shard_map/stack | solution.py:510
  (1 shorter events, 0.0 us)
Async XLA Ops:
  2.8 1.7 %collective-permute-start = (f32[7,4,8,128]{3,2,1,0:T(8,128)}, f32[7,4,8,128]{3,2,1,0:T(8,128)S(1)}, u32[]{:S(2)}, u32[]{:S(2)}) collective-permute-start(f32[7,4,8,128]{3,2,1,0:T(8,128)} %get-tuple-element.15), channel_id=1, source_target_pairs={{0,1},{1,0},{2,3},{3,2},{4,5},{5,4},{6,7},{7,6},{8,9},{9,8},{10,11... | collective-permute-start | bytes 344072 | tf_op jit(solution)/shard_map/ppermute | solution.py:409
  4.5 1.2 %copy-start = (f32[7,32,8,128]{3,2,1,0:T(8,128)S(1)}, f32[7,32,8,128]{3,2,1,0:T(8,128)}, u32[]{:S(2)}) copy-start(f32[7,32,8,128]{3,2,1,0:T(8,128)} %get-tuple-element.14.main_ref) | copy-start | bytes 2752516
  9.2 13.0 %copy-start.1 = (f32[8,32,64]{2,1,0:T(8,128)S(1)}, f32[8,32,64]{2,1,0:T(8,128)}, u32[]{:S(2)}) copy-start(f32[8,32,64]{2,1,0:T(8,128)} %mode_ref.1) | copy-start | bytes 196612
  9.3 13.0 %copy-start.3 = (s32[1,1,4]{2,1,0:T(1,128)S(1)}, s32[1,1,4]{2,1,0:T(1,128)}, u32[]{:S(2)}) copy-start(s32[1,1,4]{2,1,0:T(1,128)} %prow_ref.3) | copy-start | bytes 52
  9.3 12.9 %copy-start.4 = (s32[1,1,4]{2,1,0:T(1,128)S(1)}, s32[1,1,4]{2,1,0:T(1,128)}, u32[]{:S(2)}) copy-start(s32[1,1,4]{2,1,0:T(1,128)} %pcol_ref.1) | copy-start | bytes 52
  9.3 12.9 %copy-start.5 = (s32[1,1,4]{2,1,0:T(1,128)S(1)}, s32[1,1,4]{2,1,0:T(1,128)}, u32[]{:S(2)}) copy-start(s32[1,1,4]{2,1,0:T(1,128)} %pmode_ref.1) | copy-start | bytes 52
  9.3 16.4 %copy-start.2 = (f32[8,128]{1,0:T(8,128)S(1)}, f32[8,128]{1,0:T(8,128)}, u32[]{:S(2)}) copy-start(f32[8,128]{1,0:T(8,128)} %constant.21.clone.basis_ref) | copy-start | bytes 12292
  9.3 16.4 %copy-start.6 = (s32[1,1,4]{2,1,0:T(1,128)S(1)}, s32[1,1,4]{2,1,0:T(1,128)}, u32[]{:S(2)}) copy-start(s32[1,1,4]{2,1,0:T(1,128)} %pid_ref.1) | copy-start | bytes 52
  9.4 16.3 %collective-permute-start.3 = (f32[117,8,128]{2,1,0:T(8,128)S(1)}, f32[117,8,128]{2,1,0:T(8,128)S(1)}, u32[]{:S(2)}, u32[]{:S(2)}) collective-permute-start(f32[117,8,128]{2,1,0:T(8,128)S(1)} %planes.1), channel_id=1, source_target_pairs={{0,2},{2,0},{1,3},{3,1},{4,6},{6,4},{5,7},{7,5},{8,10},{10,8},{9,1... | collective-permute-start | bytes 1437704 | tf_op jit(solution)/shard_map/ppermute | solution.py:409
  12.3 5.1 %collective-permute-start.1 = (f32[2,5,8,128]{3,2,1,0:T(8,128)S(1)}, f32[2,5,8,128]{3,2,1,0:T(8,128)S(1)}, u32[]{:S(2)}, u32[]{:S(2)}) collective-permute-start(f32[2,5,8,128]{3,2,1,0:T(8,128)S(1)} %get-tuple-element.18), channel_id=1, source_target_pairs={{0,4},{4,8},{8,12},{1,5},{5,9},{9,13},{2,6},{6,10},{10,14},{3,7},{... | collective-permute-start | bytes 122888 | tf_op jit(solution)/shard_map/ppermute | solution.py:405
  15.8 5.9 %collective-permute-start.2 = (f32[2,5,8,128]{3,2,1,0:T(8,128)S(1)}, f32[2,5,8,128]{3,2,1,0:T(8,128)S(1)}, u32[]{:S(2)}, u32[]{:S(2)}) collective-permute-start(f32[2,5,8,128]{3,2,1,0:T(8,128)S(1)} %get-tuple-element.19), channel_id=1, source_target_pairs={{4,0},{8,4},{12,8},{5,1},{9,5},{13,9},{6,2},{10,6},{14,10},{7,3},{... | collective-permute-start | bytes 122888 | tf_op jit(solution)/shard_map/ppermute | solution.py:405
  21.7 4.0 %collective-permute-start.4 = (f32[10,8,128]{2,1,0:T(8,128)S(1)}, f32[10,8,128]{2,1,0:T(8,128)S(1)}, u32[]{:S(2)}, u32[]{:S(2)}) collective-permute-start(f32[10,8,128]{2,1,0:T(8,128)S(1)} %corners.1), channel_id=1, source_target_pairs={{0,2},{2,0},{1,3},{3,1},{4,6},{6,4},{5,7},{7,5},{8,10},{10,8},{9,1... | collective-permute-start | bytes 122888 | tf_op jit(solution)/shard_map/ppermute | solution.py:409

commit v6 on v3

v6 whole, which is shorter than its diff:
```python
import functools

import jax
import jax.numpy as jnp
import numpy as np
from jax import lax
from jax.experimental import pallas as pl
from jax.experimental.pallas import tpu as pltpu
from jax.sharding import PartitionSpec as P

STEPS = 4
FREQ = 8
MATS = 8
PLEN = 64
PORT_TILE = 4
FIELDS = 7
DEPTH = STEPS
ROWS = 8
LAYERS = 32
OWN = 4
CHUNK = 5
GROUP = 32

time_step = 0.5

UP_PLANES = [(f, 4) for f in (0, 1, 2, 4, 5)] + [(f, x) for x in (5, 6, 7) for f in range(FIELDS)]
DOWN_PLANES = [(f, x) for x in (0, 1, 2) for f in range(FIELDS)] + [(1, 3), (2, 3)]
PLANES = max(len(UP_PLANES), len(DOWN_PLANES))
PAIRS = (PLANES + 1) // 2

VMEM = pl.BlockSpec(memory_space=pltpu.VMEM)
SMEM = pl.BlockSpec(memory_space=pltpu.SMEM)
HBM = pl.BlockSpec(memory_space=pltpu.HBM)
PARAMS = pltpu.CompilerParams(vmem_limit_bytes=16 * 1024 * 1024)


def dft_basis():
    times = (np.arange(STEPS) + 1.0) * time_step
    omegas = np.pi * (np.arange(FREQ) + 1.0) / FREQ
    angle = times[:, None] * omegas[None, :]
    basis = np.zeros((8, 128), np.float32)
    basis[:STEPS, : 2 * FREQ] = np.concatenate([np.cos(angle), -np.sin(angle)], axis=1)
    return basis


def iota(axis):
    return lax.broadcasted_iota(jnp.int32, (8, 128), axis)


def turn(tile, shift, axis):
    return pltpu.roll(tile, shift % tile.shape[axis], axis)


def directions(row_size, body):
    if row_size == 2:
        row = lax.axis_index("row")
        pl.when(row == 0)(functools.partial(body, True, 0))
        pl.when(row == 1)(functools.partial(body, False, 0))
    else:
        body(True, 0)
        body(False, 1)


def pack_kernel(row_size, eps_hbm, elec_hbm, magn_hbm, mat_hbm, main_ref, z_ref, *rest):
    x_refs, (eps_ref, mat_ref, sems) = rest[:-3], rest[-3:]
    block = LAYERS * ROWS
    copies = [pltpu.make_async_copy(eps_hbm, eps_ref, sems.at[0]), pltpu.make_async_copy(mat_hbm, mat_ref, sems.at[1])]
    copies.append(pltpu.make_async_copy(elec_hbm, main_ref.at[pl.ds(0, 3)], sems.at[2]))
    copies.append(pltpu.make_async_copy(magn_hbm, main_ref.at[pl.ds(3, 3)], sems.at[3]))
    for copy in copies:
        copy.start()
    copies[0].wait()
    copies[1].wait()
    for z in range(LAYERS):
        material = mat_ref[z]
        eps = jnp.full((8, 128), eps_ref[0], jnp.float32)
        for which in range(1, MATS):
            eps = jnp.where(material == which, eps_ref[which], eps)
        main_ref[6, z] = time_step * (1.0 / eps)
    copies[2].wait()
    copies[3].wait()
    flat = main_ref.reshape(FIELDS * block, 128)

    def send(up, slot):
        for i, (f, x) in enumerate(UP_PLANES if up else DOWN_PLANES):
            x_refs[slot][i] = flat[pl.ds(f * block + x, LAYERS, stride=ROWS), :]

    directions(row_size, send)
    start = jnp.where(lax.axis_index("gz") == 0, LAYERS - DEPTH, 0)
    for f in range(FIELDS):
        z_ref[f] = main_ref[f, pl.ds(start, DEPTH)]


def gather_edges(tiles, groups):
    own = None
    for r, tile in enumerate(tiles):
        if tile is not None:
            moved = turn(tile, GROUP * r + 8, 1)
            own = moved if own is None else jnp.where(groups[r], moved, own)
    return own


def edge_kernel(main_ref, own_ref, up_ref, down_ref):
    lane = iota(1)
    groups = [(lane >> 5) == r for r in range(4)]
    slots = [((lane & (GROUP - 1)) >> 2) == f for f in range(FIELDS)]
    block = LAYERS * ROWS
    flat = main_ref.reshape(FIELDS * block, 128)
    for b in range(2):
        for zz in range(OWN):
            up = down = jnp.zeros((8, 128), jnp.float32)
            for f in range(FIELDS):
                at = f * block + zz * 8 * ROWS + 4 * b
                tiles = [flat[pl.ds(at + r, 8, stride=ROWS), :] for r in range(4)]
                own = gather_edges(tiles, groups)
                up = jnp.where(slots[f], turn(own, DEPTH * f - 4, 1), up)
                down = jnp.where(slots[f], turn(own, DEPTH * f - 8, 1), down)
                own_ref[f, b, zz] = own
            up_ref[b, zz] = up
            down_ref[b, zz] = down


def halo_layers(valid, gz, side_ref, b):
    return jnp.where(valid, jnp.where(gz == 0, side_ref[b, 0], side_ref[b, OWN - 1]), 0.0)


def spread_layers(gz, z_ref, ext_ref):
    for f in range(FIELDS):
        halo = z_ref[f].reshape(DEPTH * ROWS, 128)
        nothing = jnp.zeros_like(halo)
        ext_ref[f, : DEPTH * ROWS] = jnp.where(gz == 0, halo, nothing)
        ext_ref[f, DEPTH * ROWS :] = jnp.where(gz == 0, nothing, halo)


def corner_kernel(row_size, z_ref, low_ref, high_ref, low_z_ref, high_z_ref, *rest):
    x_refs, ext_ref = rest[:-1], rest[-1]
    gz = lax.axis_index("gz")
    valid = (iota(0) < 4) == (gz == 0)
    spread_layers(gz, z_ref, ext_ref)

    def send(up, slot):
        planes = UP_PLANES if up else DOWN_PLANES

        def tile(i):
            f, x = planes[i]
            return ext_ref[f, pl.ds(x, 8, stride=ROWS), :]

        for i in range(PAIRS):
            pair = tile(i)
            if i + PAIRS < len(planes):
                pair = pair + turn(tile(i + PAIRS), 4, 0)
            x_refs[slot][i] = pair
        b = 1 if up else 0
        for zz in range(OWN):
            x_refs[slot][PAIRS + zz] = low_ref[b, zz]
            x_refs[slot][PAIRS + CHUNK + zz] = high_ref[b, zz]
        x_refs[slot][PAIRS + OWN] = halo_layers(valid, gz, low_z_ref, b)
        x_refs[slot][PAIRS + CHUNK + OWN] = halo_layers(valid, gz, high_z_ref, b)

    directions(row_size, send)


def edge_tile(own, low, high, f, place):
    out = jnp.where(place < 16, turn(low, 12 - DEPTH * f, 1), turn(own, 8, 1))
    out = jnp.where(place < 12, turn(high, 8 - DEPTH * f, 1), out)
    return jnp.where(place < 8, own, out)


class Tiles:
    def __init__(self, first, e_ref, h_ref, shift):
        self.first, self.e_ref, self.h_ref, self.shift = first, e_ref, h_ref, shift
        self.written = set()

    def get(self, f, i, zz):
        if (f, i) not in self.written:
            return self.first(f, i, zz)
        return self.e_ref[f, i - self.shift, zz] if f < 3 else self.h_ref[f - 3, i - self.shift, zz]

    def put(self, f, i, zz, tile):
        if f < 3:
            self.e_ref[f, i - self.shift, zz] = tile
        else:
            self.h_ref[f - 3, i - self.shift, zz] = tile

    def keep(self, fields, i):
        self.written |= {(f, i) for f in fields}


def leapfrog(tiles, exists, h_rows, e_rows, across, h_of, c_of, h_layers, e_layers, skip_hx):
    sub = iota(0)
    every = range(CHUNK)
    blank = [jnp.zeros((8, 128), jnp.float32)] * CHUNK

    def above(values):
        turned = [turn(v, -1, 0) for v in values]
        return [jnp.where(sub == 7, turned[(zz + 1) % CHUNK], turned[zz]) for zz in every]

    def beneath(values):
        turned = [turn(v, 1, 0) for v in values]
        return [jnp.where(sub == 0, turned[zz - 1], turned[zz]) for zz in every]

    def row(f, i):
        return [tiles.get(f, i, zz) for zz in every]

    def load_e(i):
        ey, ez = row(1, i), row(2, i)
        out = dict(ey=ey, ez=ez, ey_x=across.turned(ey, -1), ez_x=across.turned(ez, -1))
        if i in h_rows:
            ex = row(0, i)
            out.update(ex=ex, ex_y=[turn(v, -1, 1) for v in ex], ex_z=above(ex))
            if i not in skip_hx:
                out.update(ez_y=[turn(v, -1, 1) for v in ez], ey_z=above(ey))
        return out

    def work_h(i, loaded):
        e, after, h = loaded[i], loaded.get(i + 1), h_of(i)
        ey_x = across.pick(e["ey_x"], after["ey_x"] if after else blank, -1)
        ez_x = across.pick(e["ez_x"], after["ez_x"] if after else blank, -1)
        new = {}
        for zz in h_layers:
            if i not in skip_hx:
                curl = (e["ez_y"][zz] - e["ez"][zz]) - (e["ey_z"][zz] - e["ey"][zz])
                new[3, zz] = tiles.get(3, i, zz) - h[zz] * curl
            curl = (e["ex_z"][zz] - e["ex"][zz]) - (ez_x[zz] - e["ez"][zz])
            new[4, zz] = tiles.get(4, i, zz) - h[zz] * curl
            curl = (ey_x[zz] - e["ey"][zz]) - (e["ex_y"][zz] - e["ex"][zz])
            new[5, zz] = tiles.get(5, i, zz) - h[zz] * curl
        for (f, zz), tile in new.items():
            tiles.put(f, i, zz, tile)
        tiles.keep((4, 5) if i in skip_hx else (3, 4, 5), i)

    def load_h(i):
        hy, hz = row(4, i), row(5, i)
        out = dict(hy=hy, hz=hz, hy_x=across.turned(hy, 1), hz_x=across.turned(hz, 1))
        if i in e_rows:
            hx = row(3, i)
            out.update(hx=hx, hx_y=[turn(v, 1, 1) for v in hx], hz_y=[turn(v, 1, 1) for v in hz])
            out.update(hx_z=beneath(hx), hy_z=beneath(hy))
        return out

    def work_e(i, loaded):
        h, before, c = loaded[i], loaded.get(i - 1), c_of(i)
        hy_x = across.pick(h["hy_x"], before["hy_x"] if before else blank, 1)
        hz_x = across.pick(h["hz_x"], before["hz_x"] if before else blank, 1)
        new = {}
        for zz in e_layers:
            curl = (h["hz"][zz] - h["hz_y"][zz]) - (h["hy"][zz] - h["hy_z"][zz])
            new[0, zz] = tiles.get(0, i, zz) + c[zz] * curl
            curl = (h["hx"][zz] - h["hx_z"][zz]) - (h["hz"][zz] - hz_x[zz])
            new[1, zz] = tiles.get(1, i, zz) + c[zz] * curl
            curl = (h["hy"][zz] - hy_x[zz]) - (h["hx"][zz] - h["hx_y"][zz])
            new[2, zz] = tiles.get(2, i, zz) + c[zz] * curl
        for (f, zz), tile in new.items():
            tiles.put(f, i, zz, tile)
        tiles.keep((0, 1, 2), i)

    def sweep(rows, load, work):
        loaded = {}

        def want(i):
            if i not in loaded and i in exists:
                loaded[i] = load(i)

        for i in rows:
            for j in (i - 1, i, i + 1):
                if j in rows or j == i + (1 if load is load_e else -1):
                    want(j)
            work(i, loaded)

    sweep(h_rows, load_e, work_h)
    yield
    sweep(e_rows, load_h, work_e)


class Rows:
    def turned(self, values, way):
        return values

    def pick(self, own, other, way):
        return other


class Blocks:
    def __init__(self, groups):
        self.groups = groups

    def turned(self, values, way):
        return [turn(v, way * GROUP, 1) for v in values]

    def pick(self, own, other, way):
        edge = self.groups[3] if way < 0 else self.groups[0]
        return [jnp.where(edge, o, v) for o, v in zip(other, own)]


def spans_inner(n, has_below, has_above):
    last = 7 - n if has_above else 7
    return (n - 1 if has_below else 0, last), (n if has_below else 0, last)


def spans_below(n):
    return (n - 5, n - 2), (n - 4, n - 1)


def spans_above(n):
    return (8 - n, 11 - n), (8 - n, 11 - n)


def advance(n, spans, main, edge, main_exists, edge_exists, values, skip_hx):
    row_size, gz, row, col = values
    lane, sub = iota(1), iota(0)
    place, group = lane & (GROUP - 1), lane >> 5
    groups = [group == r for r in range(4)]
    full = jnp.full((8, 128), time_step, jnp.float32)
    layer_half = [full] * OWN + [jnp.where((sub >= 4) & (gz == 0), 0.0, full)]
    outside = (place >= 12) & (place < 16) & (col == 0)
    edge_half = [jnp.where(outside, 0.0, v) for v in layer_half]
    lowest = jnp.where(row == 0, 0.0, 1.0) if row_size > 2 else None

    def cover(block, span):
        low, high = max(span[0] - 4 * block, 0), min(span[1] - 4 * block, 3)
        if low == 0 and high == 3:
            return None
        return (group >= low) & (group <= high)

    def blocks_of(span):
        return [b + 1 for b in range(-1, 3) if span[0] <= 4 * b + 3 and span[1] >= 4 * b]

    def main_h(i):
        return layer_half if lowest is None or i >= DEPTH else [v * lowest for v in layer_half]

    def main_c(i):
        return [main.get(6, i, zz) for zz in range(CHUNK)]

    def edge_h(i, span):
        h = edge_half if lowest is None or i else [v * lowest for v in edge_half]
        mask = cover(i - 1, span)
        return h if mask is None else [jnp.where(mask, v, 0.0) for v in h]

    def edge_c(i, span):
        c = [edge.get(6, i, zz) for zz in range(CHUNK)]
        mask = cover(i - 1, span)
        return c if mask is None else [jnp.where(mask, v, 0.0) for v in c]

    layers = range(CHUNK)
    last = range(OWN) if n == STEPS else layers
    parts = []
    for h_span, e_span in spans:
        h_rows = list(range(DEPTH + h_span[0], DEPTH + h_span[1] + 1))
        e_rows = list(range(DEPTH + e_span[0], DEPTH + e_span[1] + 1))
        skip = h_rows[:1] if skip_hx and h_span[0] < e_span[0] else []
        parts.append(leapfrog(main, main_exists, h_rows, e_rows, Rows(), main_h, main_c, layers, last, skip))
        h_of, c_of = functools.partial(edge_h, span=h_span), functools.partial(edge_c, span=e_span)
        parts.append(
            leapfrog(edge, edge_exists, blocks_of(h_span), blocks_of(e_span), Blocks(groups), h_of, c_of, layers, last, [])
        )
    for part in parts:
        next(part)
    for part in parts:
        next(part, None)


def port_sums(n, reached, prow_ref, weight_ref, e_ref, edge_ref, shift, edge_shift, sum_ref, add_ref):
    for k in range(PORT_TILE):
        at = prow_ref[0, 0, k]
        total = jnp.zeros((8, 128), jnp.float32)
        for zz in range(OWN):
            total = total + e_ref[2, at + shift, zz] * weight_ref[k, 0, zz]
            total = total + edge_ref[2, (at >> 2) + edge_shift, zz] * weight_ref[k, 1, zz]
        total = jnp.sum(jnp.where(reached(n, at), total, 0.0), axis=0, keepdims=True)
        if add_ref is not None:
            total = total + add_ref[n - 1, k : k + 1, :]
        sum_ref[n - 1, k : k + 1, :] = total


def finished(f, b, main, edge):
    lane = iota(1)
    place = lane & (GROUP - 1)
    sides = (lane < DEPTH) | (lane >= 128 - DEPTH)
    out = {}
    for zz in range(OWN):
        tile = edge.get(f, b + 1, zz)
        near = jnp.where(place < 8, tile, turn(tile, -8, 1))
        for r in range(4):
            own = main.get(f, DEPTH + 4 * b + r, zz)
            out[r, zz] = jnp.where(sides, turn(near, -(GROUP * r + 8), 1), own)
    return out


def inner_kernel(
    row_size, main_ref, z_ref, own_ref, low_ref, high_ref, low_z_ref, high_z_ref, mode_ref, prow_ref, pcol_ref, pmode_ref,
    e_ref, h_ref, c_ref, edge_e_ref, edge_h_ref, edge_c_ref, done_ref, weight_ref, sum_ref, ext_ref, strip_ref, joined_ref,
):
    gz, row, col = (lax.axis_index(name) for name in ("gz", "row", "col"))
    lane, sub = iota(1), iota(0)
    place = lane & (GROUP - 1)
    groups = [(lane >> 5) == r for r in range(4)]
    valid = (sub < 4) == (gz == 0)
    block = LAYERS * ROWS
    flat = main_ref.reshape(FIELDS * block, 128)
    spread_layers(gz, z_ref, ext_ref)

    def first(f, i, zz):
        x = i - DEPTH
        if zz == OWN:
            return ext_ref[f, pl.ds(x, 8, stride=ROWS), :]
        return flat[pl.ds(f * block + zz * 8 * ROWS + x, 8, stride=ROWS), :]

    for b in range(2):
        for zz in range(CHUNK):
            if zz < OWN:
                low, high = low_ref[b, zz], high_ref[b, zz]
            else:
                low, high = (halo_layers(valid, gz, ref, b) for ref in (low_z_ref, high_z_ref))
            for f in range(FIELDS):
                if zz < OWN:
                    own = own_ref[f, b, zz]
                else:
                    own = gather_edges([first(f, DEPTH + 4 * b + r, zz) for r in range(4)], groups)
                tile = edge_tile(own, low, high, f, place)
                joined_ref[f, b, zz] = tile
                if f == 6:
                    edge_c_ref[b, zz] = tile
    for k in range(PORT_TILE):
        strip_ref[k] = jnp.zeros(strip_ref.shape[1:], jnp.float32)
        strip_ref[k, :, 0:PLEN] = mode_ref[pmode_ref[0, 0, k]]
    for k in range(PORT_TILE):
        turned = GROUP * (prow_ref[0, 0, k] & 3)
        at = lane - turned
        for zz in range(OWN):
            tile = pltpu.roll(strip_ref[k, 8 * zz : 8 * zz + 8, :], pcol_ref[0, 0, k], 1)
            weight_ref[k, 0, zz] = jnp.where((lane >= DEPTH) & (lane < 128 - DEPTH), tile, 0.0)
            own = pltpu.roll(tile, turned + 8, 1)
            edge = jnp.where((at >= 4) & (at < 8), own, 0.0)
            weight_ref[k, 1, zz] = jnp.where((at >= 16) & (at < 20), turn(own, 8, 1), edge)
    sum_ref[...] = jnp.zeros(sum_ref.shape, jnp.float32)
    for x in range(ROWS):
        for zz in range(CHUNK):
            c_ref[x, zz] = first(6, DEPTH + x, zz)

    def run(has_below, has_above):
        main = Tiles(first, e_ref, h_ref, DEPTH)
        edge = Tiles(lambda f, i, zz: joined_ref[f, i - 1, zz], edge_e_ref, edge_h_ref, 1)

        def reached(n, at):
            low, high = spans_inner(n, has_below, has_above)[1]
            return (at >= low) & (at <= high)

        for n in range(1, STEPS + 1):
            spans = [spans_inner(n, has_below, has_above)]
            advance(n, spans, main, edge, range(4, 12), (1, 2), (row_size, gz, row, col), False)
            port_sums(n, reached, prow_ref, weight_ref, e_ref, edge_e_ref, 0, 0, sum_ref, None)
        for f in range(6):
            for i in range(4, 12):
                if (f, i) not in main.written:
                    for zz in range(CHUNK):
                        main.put(f, i, zz, main.get(f, i, zz))
            for i in (1, 2):
                if (f, i) not in edge.written:
                    for zz in range(CHUNK):
                        edge.put(f, i, zz, edge.get(f, i, zz))
        if has_below != has_above:
            for f in range(6):
                for (r, zz), tile in finished(f, 0 if has_above else 1, main, edge).items():
                    done_ref[f, r, zz] = tile

    if row_size == 2:
        pl.when(row == 0)(functools.partial(run, False, True))
        pl.when(row == 1)(functools.partial(run, True, False))
    else:
        run(True, True)


def outer_kernel(
    row_size, ports_each, basis_ref, prow_ref, pid_ref, e_in, h_in, c_in, edge_e_in, edge_h_in, edge_c_in, done_ref, weight_ref,
    sum_in, *rest,
):
    n_x = 1 if row_size == 2 else 2
    x_refs, corner_refs = rest[:n_x], rest[n_x : 2 * n_x]
    eout_hbm, hout_hbm, term_ref, e_ref, h_ref, c_ref, edge_e_ref, edge_h_ref, edge_c_ref, sum_ref, out_ref, sems = rest[2 * n_x :]
    gz, row, col = (lax.axis_index(name) for name in ("gz", "row", "col"))
    lane, sub = iota(1), iota(0)
    place = lane & (GROUP - 1)
    groups = [(lane >> 5) == r for r in range(4)]
    valid = (sub < 4) == (gz == 0)
    zeros = jnp.zeros((8, 128), jnp.float32)

    def first_main(f, i, zz):
        own = 4 <= i < 12
        if f == 6:
            return c_in[i - DEPTH, zz] if own else c_ref[i, zz]
        return e_in[f, i - DEPTH, zz] if f < 3 else h_in[f - 3, i - DEPTH, zz]

    def first_edge(f, i, zz):
        own = i in (1, 2)
        if f == 6:
            return edge_c_in[i - 1, zz] if own else edge_c_ref[i, zz]
        return edge_e_in[f, i - 1, zz] if f < 3 else edge_h_in[f - 3, i - 1, zz]

    def run(has_below, has_above):
        main = Tiles(first_main, e_ref, h_ref, 0)
        edge = Tiles(first_edge, edge_e_ref, edge_h_ref, 0)

        def halo_rows(planes, slot, offset, b):
            got = {}
            for i, (f, x) in enumerate(planes):
                packed = corner_refs[slot][i % PAIRS]
                if i >= PAIRS:
                    packed = turn(packed, 4, 0)
                tiles = [x_refs[slot][i, 8 * zz : 8 * zz + 8, :] for zz in range(OWN)]
                tiles.append(jnp.where(valid, packed, 0.0))
                for zz in range(CHUNK):
                    if f == 6:
                        c_ref[DEPTH + x + offset, zz] = tiles[zz]
                    else:
                        main.put(f, DEPTH + x + offset, zz, tiles[zz])
                    got[f, x + offset - 4 * b, zz] = tiles[zz]
                main.keep((f,), DEPTH + x + offset)
            main.written -= {(6, i) for i in range(16)}
            for zz in range(CHUNK):
                low = corner_refs[slot][PAIRS + zz]
                high = corner_refs[slot][PAIRS + CHUNK + zz]
                for f in range(FIELDS):
                    tiles = [got.get((f, r, zz)) for r in range(4)]
                    own = gather_edges(tiles, groups)
                    tile = edge_tile(zeros if own is None else own, low, high, f, place)
                    if f == 6:
                        edge_c_ref[1 + b, zz] = tile
                    else:
                        edge.put(f, 1 + b, zz, tile)
            edge.keep(range(6), 1 + b)

        if has_below:
            halo_rows(UP_PLANES, 0, -ROWS, -1)
        if has_above:
            halo_rows(DOWN_PLANES, n_x - 1, ROWS, 2)

        def reached(n, at):
            out = None
            for wanted, span in ((has_below, spans_below(n)[1]), (has_above, spans_above(n)[1])):
                if wanted:
                    part = (at >= span[0]) & (at <= span[1])
                    out = part if out is None else out | part
            return out

        rows = range(0 if has_below else 4, 16 if has_above else 12)
        blocks = range(0 if has_below else 1, 4 if has_above else 3)
        for n in range(1, STEPS + 1):
            spans = ([spans_below(n)] if has_below else []) + ([spans_above(n)] if has_above else [])
            advance(n, spans, main, edge, rows, blocks, (row_size, gz, row, col), True)
            port_sums(n, reached, prow_ref, weight_ref, e_ref, edge_e_ref, DEPTH, 1, sum_ref, sum_in)
        for f in range(6):
            for b in range(2):
                if has_below and has_above or b == (1 if has_above else 0):
                    tiles = finished(f, b, main, edge)
                else:
                    tiles = {(r, zz): done_ref[f, r, zz] for r in range(4) for zz in range(OWN)}
                for (r, zz), tile in tiles.items():
                    out_ref[f, pl.ds(zz * 8 * ROWS + 4 * b + r, 8, stride=ROWS), :] = tile

    if row_size == 2:
        pl.when(row == 0)(functools.partial(run, False, True))
        pl.when(row == 1)(functools.partial(run, True, False))
    else:
        run(True, True)

    copies = []
    for part, dest in ((0, eout_hbm), (1, hout_hbm)):
        copies.append(pltpu.make_async_copy(out_ref.at[pl.ds(3 * part, 3)], dest, sems.at[part]))
        copies[-1].start()
    transform = zeros
    for n in range(STEPS):
        sampled = jnp.sum(sum_ref[n], axis=1, keepdims=True)
        transform = transform + sampled * basis_ref[n : n + 1, :]
    term_ref[...] = jnp.zeros(term_ref.shape, jnp.float32)
    for k in range(PORT_TILE):
        port = pid_ref[0, 0, k]
        term_ref[port // ports_each, pl.ds(port % ports_each, 1), :] = transform[k : k + 1, : 2 * FREQ]
    for copy in copies:
        copy.wait()


def shifted(block, axis, size, distance):
    route = [(i - distance, i) for i in range(size) if 0 <= i - distance < size]
    return lax.ppermute(block, axis, route)


def swapped(block, axis, size):
    return lax.ppermute(block, axis, [(i, i ^ 1) for i in range(size)])


def solution(mesh):
    sizes = dict(mesh.shape)
    row_size, col_size, gz_size = sizes["row"], sizes["col"], sizes["gz"]
    n_x = 1 if row_size == 2 else 2

    def across_rows(blocks):
        if row_size == 2:
            return (swapped(blocks[0], "row", 2),)
        return (shifted(blocks[0], "row", row_size, 1), shifted(blocks[1], "row", row_size, -1))

    def per_device(
        electric, magnetic, material, eps_table, mode_table, port_row, port_col, port_mode, port_ids
    ):
        f32 = jnp.float32

        def array(*shape):
            return jax.ShapeDtypeStruct(shape, f32)

        def scratch(*shape):
            return pltpu.VMEM(shape, f32)

        main, z_send, *x_send = pl.pallas_call(
            functools.partial(pack_kernel, row_size),
            out_shape=[array(FIELDS, LAYERS, ROWS, 128), array(FIELDS, DEPTH, ROWS, 128)]
            + [array(PLANES, LAYERS, 128)] * n_x,
            in_specs=[HBM] * 4,
            out_specs=[VMEM] * (2 + n_x),
            scratch_shapes=[
                pltpu.SMEM(eps_table.shape, f32),
                pltpu.VMEM(material.shape, jnp.int32),
                pltpu.SemaphoreType.DMA((4,)),
            ],
            name="pack",
        )(eps_table, electric, magnetic, material)
        x_halo = across_rows(x_send)
        own, up_send, down_send = pl.pallas_call(
            edge_kernel,
            out_shape=[array(FIELDS, 2, OWN, 8, 128), array(2, OWN, 8, 128), array(2, OWN, 8, 128)],
            in_specs=[VMEM],
            out_specs=[VMEM] * 3,
            compiler_params=PARAMS,
            name="edges",
        )(main)
        low = shifted(up_send, "col", col_size, 1)
        high = shifted(down_send, "col", col_size, -1)
        z_halo = swapped(z_send, "gz", gz_size)
        low_z = swapped(low, "gz", gz_size)
        high_z = swapped(high, "gz", gz_size)
        corner_send = pl.pallas_call(
            functools.partial(corner_kernel, row_size),
            out_shape=[array(PAIRS + 2 * CHUNK, 8, 128)] * n_x,
            in_specs=[VMEM] * 5,
            out_specs=[VMEM] * n_x,
            scratch_shapes=[scratch(FIELDS, 8 * ROWS, 128)],
            compiler_params=PARAMS,
            name="corners",
        )(z_halo, low, high, low_z, high_z)
        corner = across_rows(corner_send)
        inner = pl.pallas_call(
            functools.partial(inner_kernel, row_size),
            out_shape=[
                array(3, ROWS, CHUNK, 8, 128),
                array(3, ROWS, CHUNK, 8, 128),
                array(ROWS, CHUNK, 8, 128),
                array(3, 2, CHUNK, 8, 128),
                array(3, 2, CHUNK, 8, 128),
                array(2, CHUNK, 8, 128),
                array(6, 4, OWN, 8, 128),
                array(PORT_TILE, 2, OWN, 8, 128),
                array(STEPS, 8, 128),
            ],
            in_specs=[VMEM] * 8 + [SMEM] * 3,
            out_specs=[VMEM] * 9,
            scratch_shapes=[
                scratch(FIELDS, 8 * ROWS, 128),
                scratch(PORT_TILE, LAYERS, 128),
                scratch(FIELDS, 2, CHUNK, 8, 128),
            ],
            compiler_params=PARAMS,
            name="inner",
        )(main, z_halo, own, low, high, low_z, high_z, mode_table, port_row, port_col, port_mode)
        devices = col_size * row_size * gz_size
        ports_each = PORT_TILE * col_size * row_size // devices
        electric_out, magnetic_out, term = pl.pallas_call(
            functools.partial(outer_kernel, row_size, ports_each),
            out_shape=[array(3, LAYERS * ROWS, 128)] * 2 + [array(devices, ports_each, 2 * FREQ)],
            in_specs=[VMEM] + [SMEM] * 2 + [VMEM] * (9 + 2 * n_x),
            out_specs=[HBM, HBM, VMEM],
            scratch_shapes=[
                scratch(3, 16, CHUNK, 8, 128),
                scratch(3, 16, CHUNK, 8, 128),
                scratch(16, CHUNK, 8, 128),
                scratch(3, 4, CHUNK, 8, 128),
                scratch(3, 4, CHUNK, 8, 128),
                scratch(4, CHUNK, 8, 128),
                scratch(STEPS, 8, 128),
                scratch(6, LAYERS * ROWS, 128),
                pltpu.SemaphoreType.DMA((2,)),
            ],
            compiler_params=PARAMS,
            name="outer",
        )(jnp.asarray(dft_basis()), port_row, port_ids, *inner, *x_halo, *corner)
        terms = lax.all_to_all(term, ("col", "row", "gz"), 0, 0, tiled=True)
        return (
            electric_out.reshape(electric.shape),
            magnetic_out.reshape(magnetic.shape),
            jnp.sum(terms, axis=0),
        )

    in_specs = (
        P(None, "gz", "row", ("grp", "col")),
        P(None, "gz", "row", ("grp", "col")),
        P("gz", "row", ("grp", "col")),
        P(),
        P(None, "gz", None),
        P(("grp", "row"), "col", None),
        P(("grp", "row"), "col", None),
        P(("grp", "row"), "col", None),
        P(("grp", "row"), "col", None),
    )
    out_specs = (
        P(None, "gz", "row", ("grp", "col")),
        P(None, "gz", "row", ("grp", "col")),
        P(("grp", "col", "row", "gz"), None),
    )
    return jax.shard_map(
        per_device, mesh=mesh, in_specs=in_specs, out_specs=out_specs, check_vma=False
    )
```

time: 56.5 us -> 43 us (0.76)
  Pallas kernels: 23.5 us -> 14 us
  waiting for transfers between devices: 10.6 us -> 5.97 us
  local copies, waits for them, and re-layouts: 2.73 us -> 1.93 us
    pallas_call x2 -> x3, Pallas kernels: 19.5 us -> 11.5 us  [the longest x1 5.22 us: per_device(): pl.pallas_call(functools.partial(outer_kernel, row_size, ports_each), out...]
    ppermute x3 -> x5, waiting for transfers between devices: 5.77 us -> 1.63 us  [swapped(): return lax.ppermute(block, axis, [(i, i ^ 1) for i in range(size)])]
    pallas_call x1, Pallas kernels: 1.63 us -> 0.05 us  [per_device(): pl.pallas_call(functools.partial(corner_kernel, row_size), out_shape=[arr...]
    reshape x1 -> x0, local copies, waits for them, and re-layouts: 0.65 us -> none  [per_device(): mine.reshape(ports_each, 2 * FREQ)]
    ppermute x3 -> x5, starting transfers between devices: 3.54 us -> 3.77 us  [swapped(): return lax.ppermute(block, axis, [(i, i ^ 1) for i in range(size)])]
    unnamed x10 -> x16, local copies, waits for them, and re-layouts: 2.08 us -> 1.93 us
  transfers between devices with their start and end apart: 5 -> 7, of which waited for: 4 -> 4; matrix products, arithmetic and copies ran while one was open for 0% -> 0% of each run, Pallas kernels for 14% -> 15%
where the time goes in v6:
time: 43 us; the launch traced here: 42.7 us
  Pallas kernels  14 us (33%)
  blocking collectives  10.8 us (25%)
  starting transfers between devices  8.68 us (20%)
  waiting for transfers between devices  5.97 us (14%)
  local copies, waits for them, and re-layouts  1.93 us (4%)
  between operations  0.72 us (2%)
  other arithmetic  0.59 us (1%)
    all_to_all x1, blocking collectives, per_device(): terms = lax.all_to_all(term, ('col', 'row', 'gz'), 0, 0, tiled=True)  10.8 us
    pallas_call x1, Pallas kernels, per_device(): pl.pallas_call(functools.partial(outer_kernel, row_size, ports_each), out...  5.22 us
    ppermute x2, starting transfers between devices, shifted(): return lax.ppermute(block, axis, route)  4.9 us
    ppermute x2, waiting for transfers between devices, shifted(): return lax.ppermute(block, axis, route)  4.34 us
    ppermute x5, starting transfers between devices, swapped(): return lax.ppermute(block, axis, [(i, i ^ 1) for i in range(size)])  3.77 us
    pallas_call x1, Pallas kernels, per_device(): pl.pallas_call(functools.partial(inner_kernel, row_size), out_shape=[arra...  3.75 us
    pallas_call x1, Pallas kernels, per_device(): pl.pallas_call(edge_kernel, out_shape=[array(FIELDS, 2, OWN, 8, 128), arr...  2.55 us
    pallas_call x1, Pallas kernels, per_device(): pl.pallas_call(functools.partial(pack_kernel, row_size), out_shape=[array...  2.41 us
  transfers between devices with their start and end apart: 7, of which 4 were waited for; matrix products, arithmetic and copies ran while one was open for 0% of the time, Pallas kernels for 15%

profile of v6, /device:TPU:0, one launch (start us, length us, event | category | flops | bytes accessed | tf_op | source)
XLA Modules:
  0.0 42.7 jit_solution(17628373664722351533)
XLA Ops:
  0.6 2.4 %pack.1 = (f32[7,32,8,128]{3,2,1,0:T(8,128)}, f32[7,4,8,128]{3,2,1,0:T(8,128)}, f32[26,32,128]{2,1,0:T(8,128)}) custom-call(f32[8]{0:T(128)} %eps_hbm.1, f32[3,32,8,128]{3,2,1,0:T(8,128)} %elec_hbm.1, f32[3,32,8,128]{3,2,1,0:T(8,128)} %magn_hbm.1, s32[32,8,128]{2,1,0:T(8,128)} %mat_hbm.1), custom_call_target="tpu_custom_call" | custom-call | tf_op jit(solution)/shard_map/pack/pallas_call | solution.py:612
  3.1 3.0 %collective-permute-start.5 = (f32[26,32,128]{2,1,0:T(8,128)}, f32[26,32,128]{2,1,0:T(8,128)S(1)}, u32[]{:S(2)}, u32[]{:S(2)}) collective-permute-start(f32[26,32,128]{2,1,0:T(8,128)} %get-tuple-element.35), channel_id=1, source_target_pairs={{0,2},{2,0},{1,3},{3,1},{4,6},{6,4},{5,7},{7,5},{8,10},{10,8},{9,1... | collective-permute-start | bytes 1277960 | tf_op jit(solution)/shard_map/ppermute | solution.py:588
  6.0 0.0 collective-permute-start
  6.0 1.2 %copy-done = f32[7,32,8,128]{3,2,1,0:T(8,128)S(1)} copy-done((f32[7,32,8,128]{3,2,1,0:T(8,128)S(1)}, f32[7,32,8,128]{3,2,1,0:T(8,128)}, u32[]{:S(2)}) %copy-start) | copy-done | bytes 917528
  7.2 2.5 %edges.1 = (f32[7,2,4,8,128]{4,3,2,1,0:T(8,128)S(1)}, f32[2,4,8,128]{3,2,1,0:T(8,128)S(1)}, f32[2,4,8,128]{3,2,1,0:T(8,128)S(1)}) custom-call(f32[7,32,8,128]{3,2,1,0:T(8,128)S(1)} %copy-done), custom_call_target="tpu_custom_call" | custom-call | tf_op jit(solution)/shard_map/edges/pallas_call | solution.py:626
  9.8 3.5 %collective-permute-start.1 = (f32[2,4,8,128]{3,2,1,0:T(8,128)S(1)}, f32[2,4,8,128]{3,2,1,0:T(8,128)S(1)}, u32[]{:S(2)}, u32[]{:S(2)}) collective-permute-start(f32[2,4,8,128]{3,2,1,0:T(8,128)S(1)} %get-tuple-element.24), channel_id=1, source_target_pairs={{0,4},{4,8},{8,12},{1,5},{5,9},{9,13},{2,6},{6,10},{10,14},{3,7},{... | collective-permute-start | bytes 98312 | tf_op jit(solution)/shard_map/ppermute | solution.py:584
  13.3 0.0 copy-start.2
  13.3 1.4 %collective-permute-start.2 = (f32[2,4,8,128]{3,2,1,0:T(8,128)S(1)}, f32[2,4,8,128]{3,2,1,0:T(8,128)S(1)}, u32[]{:S(2)}, u32[]{:S(2)}) collective-permute-start(f32[2,4,8,128]{3,2,1,0:T(8,128)S(1)} %get-tuple-element.25), channel_id=1, source_target_pairs={{4,0},{8,4},{12,8},{5,1},{9,5},{13,9},{6,2},{10,6},{14,10},{7,3},{... | collective-permute-start | bytes 98312 | tf_op jit(solution)/shard_map/ppermute | solution.py:584
  14.7 0.1 collective-permute-done.1.low_ref
  14.8 0.2 collective-permute-start.3
  15.0 4.2 %collective-permute-done.2.high_ref = f32[2,4,8,128]{3,2,1,0:T(8,128)S(1)} collective-permute-done((f32[2,4,8,128]{3,2,1,0:T(8,128)S(1)}, f32[2,4,8,128]{3,2,1,0:T(8,128)S(1)}, u32[]{:S(2)}, u32[]{:S(2)}) %collective-permute-start.2) | collective-permute-done | bytes 32800 | tf_op jit(solution)/shard_map/ppermute | solution.py:584
  19.2 0.0 collective-permute-start.4
  19.2 0.0 collective-permute-done.3.low_z_ref
  19.2 1.2 %collective-permute-done.4.high_z_ref = f32[2,4,8,128]{3,2,1,0:T(8,128)S(1)} collective-permute-done((f32[2,4,8,128]{3,2,1,0:T(8,128)S(1)}, f32[2,4,8,128]{3,2,1,0:T(8,128)S(1)}, u32[]{:S(2)}, u32[]{:S(2)}) %collective-permute-start.4) | collective-permute-done | bytes 32800 | tf_op jit(solution)/shard_map/ppermute | solution.py:588
  20.4 0.0 collective-permute-done.z_ref
  20.5 0.0 copy-start.4
  20.5 0.0 copy-start.5
  20.5 0.0 copy-start.6
  20.5 0.6 %collective-permute-start.6 = (f32[23,8,128]{2,1,0:T(8,128)S(1)}, f32[23,8,128]{2,1,0:T(8,128)S(1)}, u32[]{:S(2)}, u32[]{:S(2)}) collective-permute-start(f32[23,8,128]{2,1,0:T(8,128)S(1)} %corners.1), channel_id=1, source_target_pairs={{0,2},{2,0},{1,3},{3,1},{4,6},{6,4},{5,7},{7,5},{8,10},{10,8},{9,1... | collective-permute-start | bytes 282632 | tf_op jit(solution)/shard_map/ppermute | solution.py:588
  21.1 0.0 copy-done.1
  21.1 0.0 copy-done.2
  21.1 0.0 copy-done.4
  21.1 0.0 copy-done.5
  21.2 0.0 copy-done.6
  21.2 3.8 %inner.1 = (f32[3,8,5,8,128]{4,3,2,1,0:T(8,128)S(1)}, f32[3,8,5,8,128]{4,3,2,1,0:T(8,128)S(1)}, f32[8,5,8,128]{3,2,1,0:T(8,128)S(1)}, f32[3,2,5,8,128]{4,3,2,1,0...) custom-call(f32[7,32,8,128]{3,2,1,0:T(8,128)S(1)} %copy-done.1, ...), custom_call_target="tpu_custom_call" | custom-call | tf_op jit(solution)/shard_map/inner/pallas_call | solution.py:649
  24.9 0.4 collective-permute-done.6.rest_1_
  25.4 0.0 collective-permute-done.5.rest_0_
  25.4 0.7 %copy-done.3 = f32[8,128]{1,0:T(8,128)S(1)} copy-done((f32[8,128]{1,0:T(8,128)S(1)}, f32[8,128]{1,0:T(8,128)}, u32[]{:S(2)}) %copy-start.3) | copy-done | bytes 4120
  26.1 0.0 copy-done.7
  26.1 5.2 %outer.1 = (f32[3,256,128]{2,1,0:T(8,128)}, f32[3,256,128]{2,1,0:T(8,128)}, f32[16,2,16]{2,1,0:T(2,128)S(1)}) custom-call(f32[8,128]{1,0:T(8,128)S(1)} %copy-done.3, s32[1,1,4]{2,1,0:T(1,128)S(1)} %copy-done.4, s32[1,1,4]{2,1,0:T(1,128)S(1)} %copy-done.7, f32[3,8,5,8,128]{4,3,2,1,0:T(8,128)S(1)} %get-tuple-element.26.e_in, ...), custom_call_target="tpu_custom_call" | custom-call | tf_op jit(solution)/shard_map/outer/pallas_call | solution.py:674
  31.3 10.8 %all_to_all.5 = f32[16,2,16]{2,1,0:T(2,128)S(1)} all-to-all(f32[16,2,16]{2,1,0:T(2,128)S(1)} %get-tuple-element.38), channel_id=1, replica_groups=mesh['grp'=2,'col'=4,'row'=2,'gz'=2] {'col','row','gz'}, dimensions={0} | all-to-all | bytes 4096 | tf_op jit(solution)/shard_map/all_to_all | solution.py:693
  42.1 0.6 %reduce_sum.9 = f32[2,16]{1,0:T(2,128)} reduce(f32[16,2,16]{2,1,0:T(2,128)S(1)} %all_to_all.5, f32[]{:T(128)} %constant.1.clone.1), dimensions={0}, to_apply=%region_0.0 | reduce | flops 480 | bytes 2180 | tf_op jit(solution)/shard_map/reduce_sum | solution.py:697
  (5 shorter events, 0.1 us)
Async XLA Ops:
  3.1 22.3 %collective-permute-start.5 = (f32[26,32,128]{2,1,0:T(8,128)}, f32[26,32,128]{2,1,0:T(8,128)S(1)}, u32[]{:S(2)}, u32[]{:S(2)}) collective-permute-start(f32[26,32,128]{2,1,0:T(8,128)} %get-tuple-element.35), channel_id=1, source_target_pairs={{0,2},{2,0},{1,3},{3,1},{4,6},{6,4},{5,7},{7,5},{8,10},{10,8},{9,1... | collective-permute-start | bytes 1277960 | tf_op jit(solution)/shard_map/ppermute | solution.py:588
  6.0 14.4 %collective-permute-start = (f32[7,4,8,128]{3,2,1,0:T(8,128)}, f32[7,4,8,128]{3,2,1,0:T(8,128)S(1)}, u32[]{:S(2)}, u32[]{:S(2)}) collective-permute-start(f32[7,4,8,128]{3,2,1,0:T(8,128)} %get-tuple-element.22), channel_id=1, source_target_pairs={{0,1},{1,0},{2,3},{3,2},{4,5},{5,4},{6,7},{7,6},{8,9},{9,8},{10,11... | collective-permute-start | bytes 344072 | tf_op jit(solution)/shard_map/ppermute | solution.py:588
  6.0 1.2 %copy-start = (f32[7,32,8,128]{3,2,1,0:T(8,128)S(1)}, f32[7,32,8,128]{3,2,1,0:T(8,128)}, u32[]{:S(2)}) copy-start(f32[7,32,8,128]{3,2,1,0:T(8,128)} %get-tuple-element.21.main_ref) | copy-start | bytes 2752516
  7.2 13.9 %copy-start.1 = (f32[7,32,8,128]{3,2,1,0:T(8,128)S(1)}, f32[7,32,8,128]{3,2,1,0:T(8,128)}, u32[]{:S(2)}) copy-start(f32[7,32,8,128]{3,2,1,0:T(8,128)} %get-tuple-element.21.main_ref) | copy-start | bytes 2752516
  9.8 5.1 %collective-permute-start.1 = (f32[2,4,8,128]{3,2,1,0:T(8,128)S(1)}, f32[2,4,8,128]{3,2,1,0:T(8,128)S(1)}, u32[]{:S(2)}, u32[]{:S(2)}) collective-permute-start(f32[2,4,8,128]{3,2,1,0:T(8,128)S(1)} %get-tuple-element.24), channel_id=1, source_target_pairs={{0,4},{4,8},{8,12},{1,5},{5,9},{9,13},{2,6},{6,10},{10,14},{3,7},{... | collective-permute-start | bytes 98312 | tf_op jit(solution)/shard_map/ppermute | solution.py:584
  13.3 7.9 %copy-start.2 = (f32[8,32,64]{2,1,0:T(8,128)S(1)}, f32[8,32,64]{2,1,0:T(8,128)}, u32[]{:S(2)}) copy-start(f32[8,32,64]{2,1,0:T(8,128)} %mode_ref.1) | copy-start | bytes 196612
  13.3 5.9 %collective-permute-start.2 = (f32[2,4,8,128]{3,2,1,0:T(8,128)S(1)}, f32[2,4,8,128]{3,2,1,0:T(8,128)S(1)}, u32[]{:S(2)}, u32[]{:S(2)}) collective-permute-start(f32[2,4,8,128]{3,2,1,0:T(8,128)S(1)} %get-tuple-element.25), channel_id=1, source_target_pairs={{4,0},{8,4},{12,8},{5,1},{9,5},{13,9},{6,2},{10,6},{14,10},{7,3},{... | collective-permute-start | bytes 98312 | tf_op jit(solution)/shard_map/ppermute | solution.py:584
  14.8 4.4 %collective-permute-start.3 = (f32[2,4,8,128]{3,2,1,0:T(8,128)S(1)}, f32[2,4,8,128]{3,2,1,0:T(8,128)S(1)}, u32[]{:S(2)}, u32[]{:S(2)}) collective-permute-start(f32[2,4,8,128]{3,2,1,0:T(8,128)S(1)} %collective-permute-done.1.low_ref), channel_id=1, source_target_pairs={{0,1},{1,0},{2,3},{3,2},{4,5},{5,4},{6,7},{7,6},{8,9},{9,8},{10,11... | collective-permute-start | bytes 98312 | tf_op jit(solution)/shard_map/ppermute | solution.py:588
  19.2 1.2 %collective-permute-start.4 = (f32[2,4,8,128]{3,2,1,0:T(8,128)S(1)}, f32[2,4,8,128]{3,2,1,0:T(8,128)S(1)}, u32[]{:S(2)}, u32[]{:S(2)}) collective-permute-start(f32[2,4,8,128]{3,2,1,0:T(8,128)S(1)} %collective-permute-done.2.high_ref), channel_id=1, source_target_pairs={{0,1},{1,0},{2,3},{3,2},{4,5},{5,4},{6,7},{7,6},{8,9},{9,8},{10,11... | collective-permute-start | bytes 98312 | tf_op jit(solution)/shard_map/ppermute | solution.py:588
  20.5 0.7 %copy-start.4 = (s32[1,1,4]{2,1,0:T(1,128)S(1)}, s32[1,1,4]{2,1,0:T(1,128)}, u32[]{:S(2)}) copy-start(s32[1,1,4]{2,1,0:T(1,128)} %prow_ref.3) | copy-start | bytes 52
  20.5 0.7 %copy-start.5 = (s32[1,1,4]{2,1,0:T(1,128)S(1)}, s32[1,1,4]{2,1,0:T(1,128)}, u32[]{:S(2)}) copy-start(s32[1,1,4]{2,1,0:T(1,128)} %pcol_ref.1) | copy-start | bytes 52
  20.5 0.7 %copy-start.6 = (s32[1,1,4]{2,1,0:T(1,128)S(1)}, s32[1,1,4]{2,1,0:T(1,128)}, u32[]{:S(2)}) copy-start(s32[1,1,4]{2,1,0:T(1,128)} %pmode_ref.1) | copy-start | bytes 52
  20.5 4.8 %collective-permute-start.6 = (f32[23,8,128]{2,1,0:T(8,128)S(1)}, f32[23,8,128]{2,1,0:T(8,128)S(1)}, u32[]{:S(2)}, u32[]{:S(2)}) collective-permute-start(f32[23,8,128]{2,1,0:T(8,128)S(1)} %corners.1), channel_id=1, source_target_pairs={{0,2},{2,0},{1,3},{3,1},{4,6},{6,4},{5,7},{7,5},{8,10},{10,8},{9,1... | collective-permute-start | bytes 282632 | tf_op jit(solution)/shard_map/ppermute | solution.py:588
  25.4 0.7 %copy-start.3 = (f32[8,128]{1,0:T(8,128)S(1)}, f32[8,128]{1,0:T(8,128)}, u32[]{:S(2)}) copy-start(f32[8,128]{1,0:T(8,128)} %constant.4.clone.basis_ref) | copy-start | bytes 12292
  25.4 0.7 %copy-start.7 = (s32[1,1,4]{2,1,0:T(1,128)S(1)}, s32[1,1,4]{2,1,0:T(1,128)}, u32[]{:S(2)}) copy-start(s32[1,1,4]{2,1,0:T(1,128)} %pid_ref.1) | copy-start | bytes 52

commit v7 on v6

--- a/solution.py
+++ b/solution.py
@@ -38,9 +38,10 @@
     times = (np.arange(STEPS) + 1.0) * time_step
     omegas = np.pi * (np.arange(FREQ) + 1.0) / FREQ
     angle = times[:, None] * omegas[None, :]
-    basis = np.zeros((8, 128), np.float32)
-    basis[:STEPS, : 2 * FREQ] = np.concatenate([np.cos(angle), -np.sin(angle)], axis=1)
-    return basis
+    return np.concatenate([np.cos(angle), -np.sin(angle)], axis=1)
+
+
+BASIS = dft_basis()
 
 
 def iota(axis):
@@ -61,9 +62,7 @@
         body(False, 1)
 
 
-def pack_kernel(row_size, eps_hbm, elec_hbm, magn_hbm, mat_hbm, main_ref, z_ref, *rest):
-    x_refs, (eps_ref, mat_ref, sems) = rest[:-3], rest[-3:]
-    block = LAYERS * ROWS
+def pack_kernel(eps_hbm, elec_hbm, magn_hbm, mat_hbm, main_ref, z_ref, own_ref, up_ref, down_ref, eps_ref, mat_ref, sems):
     copies = [pltpu.make_async_copy(eps_hbm, eps_ref, sems.at[0]), pltpu.make_async_copy(mat_hbm, mat_ref, sems.at[1])]
     copies.append(pltpu.make_async_copy(elec_hbm, main_ref.at[pl.ds(0, 3)], sems.at[2]))
     copies.append(pltpu.make_async_copy(magn_hbm, main_ref.at[pl.ds(3, 3)], sems.at[3]))
@@ -79,16 +78,10 @@
         main_ref[6, z] = time_step * (1.0 / eps)
     copies[2].wait()
     copies[3].wait()
-    flat = main_ref.reshape(FIELDS * block, 128)
-
-    def send(up, slot):
-        for i, (f, x) in enumerate(UP_PLANES if up else DOWN_PLANES):
-            x_refs[slot][i] = flat[pl.ds(f * block + x, LAYERS, stride=ROWS), :]
-
-    directions(row_size, send)
     start = jnp.where(lax.axis_index("gz") == 0, LAYERS - DEPTH, 0)
     for f in range(FIELDS):
         z_ref[f] = main_ref[f, pl.ds(start, DEPTH)]
+    pack_edges(main_ref, own_ref, up_ref, down_ref)
 
 
 def gather_edges(tiles, groups):
@@ -100,24 +93,39 @@
     return own
 
 
-def edge_kernel(main_ref, own_ref, up_ref, down_ref):
+def pack_edges(main_ref, own_ref, up_ref, down_ref):
     lane = iota(1)
     groups = [(lane >> 5) == r for r in range(4)]
     slots = [((lane & (GROUP - 1)) >> 2) == f for f in range(FIELDS)]
     block = LAYERS * ROWS
     flat = main_ref.reshape(FIELDS * block, 128)
+    values = []
     for b in range(2):
         for zz in range(OWN):
             up = down = jnp.zeros((8, 128), jnp.float32)
             for f in range(FIELDS):
                 at = f * block + zz * 8 * ROWS + 4 * b
-                tiles = [flat[pl.ds(at + r, 8, stride=ROWS), :] for r in range(4)]
-                own = gather_edges(tiles, groups)
+                own = gather_edges([flat[pl.ds(at + r, 8, stride=ROWS), :] for r in range(4)], groups)
                 up = jnp.where(slots[f], turn(own, DEPTH * f - 4, 1), up)
                 down = jnp.where(slots[f], turn(own, DEPTH * f - 8, 1), down)
-                own_ref[f, b, zz] = own
-            up_ref[b, zz] = up
-            down_ref[b, zz] = down
+                values.append((own_ref, (f, b, zz), own))
+            values += [(up_ref, (b, zz), up), (down_ref, (b, zz), down)]
+    for ref, where, value in values:
+        ref[where] = value
+
+
+def plane_kernel(row_size, main_ref, low_ref, high_ref, *x_refs):
+    block = LAYERS * ROWS
+    flat = main_ref.reshape(FIELDS * block, 128)
+
+    def send(up, slot):
+        planes = UP_PLANES if up else DOWN_PLANES
+        for start in range(0, len(planes), 8):
+            part = [flat[pl.ds(f * block + x, LAYERS, stride=ROWS), :] for f, x in planes[start : start + 8]]
+            for i, plane in enumerate(part):
+                x_refs[slot][start + i] = plane
+
+    directions(row_size, send)
 
 
 def halo_layers(valid, gz, side_ref, b):
@@ -167,23 +175,19 @@
 
 
 class Tiles:
-    def __init__(self, first, e_ref, h_ref, shift):
-        self.first, self.e_ref, self.h_ref, self.shift = first, e_ref, h_ref, shift
-        self.written = set()
+    def __init__(self, first, ez_ref, shift):
+        self.first, self.ez_ref, self.shift = first, ez_ref, shift
+        self.values = {}
 
     def get(self, f, i, zz):
-        if (f, i) not in self.written:
-            return self.first(f, i, zz)
-        return self.e_ref[f, i - self.shift, zz] if f < 3 else self.h_ref[f - 3, i - self.shift, zz]
+        value = self.values.get((f, i, zz))
+        return self.first(f, i, zz) if value is None else value
 
     def put(self, f, i, zz, tile):
-        if f < 3:
-            self.e_ref[f, i - self.shift, zz] = tile
-        else:
-            self.h_ref[f - 3, i - self.shift, zz] = tile
-
-    def keep(self, fields, i):
-        self.written |= {(f, i) for f in fields}
+        self.values[f, i, zz] = tile
+        at = i - self.shift
+        if f == 2 and zz < OWN and 0 <= at < self.ez_ref.shape[0]:
+            self.ez_ref[at, zz] = tile
 
 
 def leapfrog(tiles, exists, h_rows, e_rows, across, h_of, c_of, h_layers, e_layers, skip_hx):
@@ -227,7 +231,6 @@
             new[5, zz] = tiles.get(5, i, zz) - h[zz] * curl
         for (f, zz), tile in new.items():
             tiles.put(f, i, zz, tile)
-        tiles.keep((4, 5) if i in skip_hx else (3, 4, 5), i)
 
     def load_h(i):
         hy, hz = row(4, i), row(5, i)
@@ -252,7 +255,6 @@
             new[2, zz] = tiles.get(2, i, zz) + c[zz] * curl
         for (f, zz), tile in new.items():
             tiles.put(f, i, zz, tile)
-        tiles.keep((0, 1, 2), i)
 
     def sweep(rows, load, work):
         loaded = {}
@@ -305,67 +307,73 @@
     return (8 - n, 11 - n), (8 - n, 11 - n)
 
 
-def advance(n, spans, main, edge, main_exists, edge_exists, values, skip_hx):
-    row_size, gz, row, col = values
-    lane, sub = iota(1), iota(0)
-    place, group = lane & (GROUP - 1), lane >> 5
-    groups = [group == r for r in range(4)]
-    full = jnp.full((8, 128), time_step, jnp.float32)
-    layer_half = [full] * OWN + [jnp.where((sub >= 4) & (gz == 0), 0.0, full)]
-    outside = (place >= 12) & (place < 16) & (col == 0)
-    edge_half = [jnp.where(outside, 0.0, v) for v in layer_half]
-    lowest = jnp.where(row == 0, 0.0, 1.0) if row_size > 2 else None
-
-    def cover(block, span):
+class Stepper:
+    def __init__(self, row_size, main, edge, main_exists, edge_exists, skip_hx):
+        gz, row, col = (lax.axis_index(name) for name in ("gz", "row", "col"))
+        lane, sub = iota(1), iota(0)
+        place, self.group = lane & (GROUP - 1), lane >> 5
+        full = jnp.full((8, 128), time_step, jnp.float32)
+        self.layer_half = [full] * OWN + [jnp.where((sub >= 4) & (gz == 0), 0.0, full)]
+        outside = (place >= 12) & (place < 16) & (col == 0)
+        self.edge_half = [jnp.where(outside, 0.0, v) for v in self.layer_half]
+        self.lowest = jnp.where(row == 0, 0.0, 1.0) if row_size > 2 else None
+        self.main, self.edge, self.skip_hx = main, edge, skip_hx
+        self.main_exists, self.edge_exists = main_exists, edge_exists
+        self.blocks = Blocks([self.group == r for r in range(4)])
+
+    def masked(self, values, block, span):
         low, high = max(span[0] - 4 * block, 0), min(span[1] - 4 * block, 3)
         if low == 0 and high == 3:
-            return None
-        return (group >= low) & (group <= high)
-
-    def blocks_of(span):
-        return [b + 1 for b in range(-1, 3) if span[0] <= 4 * b + 3 and span[1] >= 4 * b]
-
-    def main_h(i):
-        return layer_half if lowest is None or i >= DEPTH else [v * lowest for v in layer_half]
-
-    def main_c(i):
-        return [main.get(6, i, zz) for zz in range(CHUNK)]
-
-    def edge_h(i, span):
-        h = edge_half if lowest is None or i else [v * lowest for v in edge_half]
-        mask = cover(i - 1, span)
-        return h if mask is None else [jnp.where(mask, v, 0.0) for v in h]
-
-    def edge_c(i, span):
-        c = [edge.get(6, i, zz) for zz in range(CHUNK)]
-        mask = cover(i - 1, span)
-        return c if mask is None else [jnp.where(mask, v, 0.0) for v in c]
-
-    layers = range(CHUNK)
-    last = range(OWN) if n == STEPS else layers
-    parts = []
-    for h_span, e_span in spans:
-        h_rows = list(range(DEPTH + h_span[0], DEPTH + h_span[1] + 1))
-        e_rows = list(range(DEPTH + e_span[0], DEPTH + e_span[1] + 1))
-        skip = h_rows[:1] if skip_hx and h_span[0] < e_span[0] else []
-        parts.append(leapfrog(main, main_exists, h_rows, e_rows, Rows(), main_h, main_c, layers, last, skip))
-        h_of, c_of = functools.partial(edge_h, span=h_span), functools.partial(edge_c, span=e_span)
-        parts.append(
-            leapfrog(edge, edge_exists, blocks_of(h_span), blocks_of(e_span), Blocks(groups), h_of, c_of, layers, last, [])
-        )
-    for part in parts:
-        next(part)
-    for part in parts:
-        next(part, None)
-
-
-def port_sums(n, reached, prow_ref, weight_ref, e_ref, edge_ref, shift, edge_shift, sum_ref, add_ref):
+            return values
+        mask = (self.group >= low) & (self.group <= high)
+        return [jnp.where(mask, v, 0.0) for v in values]
+
+    def main_h(self, i):
+        return self.layer_half if self.lowest is None or i >= DEPTH else [v * self.lowest for v in self.layer_half]
+
+    def main_c(self, i):
+        return [self.main.get(6, i, zz) for zz in range(CHUNK)]
+
+    def edge_h(self, i, span):
+        h = self.edge_half if self.lowest is None or i else [v * self.lowest for v in self.edge_half]
+        return self.masked(h, i - 1, span)
+
+    def edge_c(self, i, span):
+        return self.masked([self.edge.get(6, i, zz) for zz in range(CHUNK)], i - 1, span)
+
+    def step(self, n, spans):
+        def blocks_of(span):
+            return [b + 1 for b in range(-1, 3) if span[0] <= 4 * b + 3 and span[1] >= 4 * b]
+
+        layers = range(CHUNK)
+        last = range(OWN) if n == STEPS else layers
+        parts = []
+        for h_span, e_span in spans:
+            h_rows = list(range(DEPTH + h_span[0], DEPTH + h_span[1] + 1))
+            e_rows = list(range(DEPTH + e_span[0], DEPTH + e_span[1] + 1))
+            skip = h_rows[:1] if self.skip_hx and h_span[0] < e_span[0] else []
+            parts.append(
+                leapfrog(self.main, self.main_exists, h_rows, e_rows, Rows(), self.main_h, self.main_c, layers, last, skip)
+            )
+            h_of, c_of = functools.partial(self.edge_h, span=h_span), functools.partial(self.edge_c, span=e_span)
+            parts.append(
+                leapfrog(
+                    self.edge, self.edge_exists, blocks_of(h_span), blocks_of(e_span), self.blocks, h_of, c_of, layers, last, []
+                )
+            )
+        for part in parts:
+            next(part)
+        for part in parts:
+            next(part, None)
+
+
+def port_sums(n, reached, prow_ref, weight_ref, ez_ref, edge_ref, sum_ref, add_ref):
     for k in range(PORT_TILE):
         at = prow_ref[0, 0, k]
         total = jnp.zeros((8, 128), jnp.float32)
         for zz in range(OWN):
-            total = total + e_ref[2, at + shift, zz] * weight_ref[k, 0, zz]
-            total = total + edge_ref[2, (at >> 2) + edge_shift, zz] * weight_ref[k, 1, zz]
+            total = total + ez_ref[at, zz] * weight_ref[k, 0, zz]
+            total = total + edge_ref[at >> 2, zz] * weight_ref[k, 1, zz]
         total = jnp.sum(jnp.where(reached(n, at), total, 0.0), axis=0, keepdims=True)
         if add_ref is not None:
             total = total + add_ref[n - 1, k : k + 1, :]
@@ -388,9 +396,9 @@
 
 def inner_kernel(
     row_size, main_ref, z_ref, own_ref, low_ref, high_ref, low_z_ref, high_z_ref, mode_ref, prow_ref, pcol_ref, pmode_ref,
-    e_ref, h_ref, c_ref, edge_e_ref, edge_h_ref, edge_c_ref, done_ref, weight_ref, sum_ref, ext_ref, strip_ref, joined_ref,
+    e_ref, h_ref, c_ref, edge_e_ref, edge_h_ref, edge_c_ref, done_ref, weight_ref, sum_ref, ext_ref, strip_ref, ez_ref, edge_ez_ref,
 ):
-    gz, row, col = (lax.axis_index(name) for name in ("gz", "row", "col"))
+    gz, row = lax.axis_index("gz"), lax.axis_index("row")
     lane, sub = iota(1), iota(0)
     place = lane & (GROUP - 1)
     groups = [(lane >> 5) == r for r in range(4)]
@@ -405,6 +413,7 @@
             return ext_ref[f, pl.ds(x, 8, stride=ROWS), :]
         return flat[pl.ds(f * block + zz * 8 * ROWS + x, 8, stride=ROWS), :]
 
+    joined = {}
     for b in range(2):
         for zz in range(CHUNK):
             if zz < OWN:
@@ -416,10 +425,7 @@
                     own = own_ref[f, b, zz]
                 else:
                     own = gather_edges([first(f, DEPTH + 4 * b + r, zz) for r in range(4)], groups)
-                tile = edge_tile(own, low, high, f, place)
-                joined_ref[f, b, zz] = tile
-                if f == 6:
-                    edge_c_ref[b, zz] = tile
+                joined[f, b + 1, zz] = edge_tile(own, low, high, f, place)
     for k in range(PORT_TILE):
         strip_ref[k] = jnp.zeros(strip_ref.shape[1:], jnp.float32)
         strip_ref[k, :, 0:PLEN] = mode_ref[pmode_ref[0, 0, k]]
@@ -432,32 +438,28 @@
             own = pltpu.roll(tile, turned + 8, 1)
             edge = jnp.where((at >= 4) & (at < 8), own, 0.0)
             weight_ref[k, 1, zz] = jnp.where((at >= 16) & (at < 20), turn(own, 8, 1), edge)
-    sum_ref[...] = jnp.zeros(sum_ref.shape, jnp.float32)
-    for x in range(ROWS):
-        for zz in range(CHUNK):
-            c_ref[x, zz] = first(6, DEPTH + x, zz)
 
     def run(has_below, has_above):
-        main = Tiles(first, e_ref, h_ref, DEPTH)
-        edge = Tiles(lambda f, i, zz: joined_ref[f, i - 1, zz], edge_e_ref, edge_h_ref, 1)
+        main = Tiles(first, ez_ref, DEPTH)
+        edge = Tiles(lambda f, i, zz: joined[f, i, zz], edge_ez_ref, 1)
+        stepper = Stepper(row_size, main, edge, range(4, 12), (1, 2), False)
 
         def reached(n, at):
             low, high = spans_inner(n, has_below, has_above)[1]
             return (at >= low) & (at <= high)
 
         for n in range(1, STEPS + 1):
-            spans = [spans_inner(n, has_below, has_above)]
-            advance(n, spans, main, edge, range(4, 12), (1, 2), (row_size, gz, row, col), False)
-            port_sums(n, reached, prow_ref, weight_ref, e_ref, edge_e_ref, 0, 0, sum_ref, None)
-        for f in range(6):
-            for i in range(4, 12):
-                if (f, i) not in main.written:
-                    for zz in range(CHUNK):
-                        main.put(f, i, zz, main.get(f, i, zz))
-            for i in (1, 2):
-                if (f, i) not in edge.written:
-                    for zz in range(CHUNK):
-                        edge.put(f, i, zz, edge.get(f, i, zz))
+            stepper.step(n, [spans_inner(n, has_below, has_above)])
+            port_sums(n, reached, prow_ref, weight_ref, ez_ref, edge_ez_ref, sum_ref, None)
+        for tiles, base, count, refs in (
+            (main, DEPTH, ROWS, (e_ref, h_ref, c_ref)),
+            (edge, 1, 2, (edge_e_ref, edge_h_ref, edge_c_ref)),
+        ):
+            for i in range(count):
+                for zz in range(CHUNK):
+                    for f in range(6):
+                        refs[f // 3][f % 3, i, zz] = tiles.get(f, base + i, zz)
+                    refs[2][i, zz] = tiles.get(6, base + i, zz)
         if has_below != has_above:
             for f in range(6):
                 for (r, zz), tile in finished(f, 0 if has_above else 1, main, edge).items():
@@ -471,13 +473,13 @@
 
 
 def outer_kernel(
-    row_size, ports_each, basis_ref, prow_ref, pid_ref, e_in, h_in, c_in, edge_e_in, edge_h_in, edge_c_in, done_ref, weight_ref,
+    row_size, ports_each, prow_ref, pid_ref, e_in, h_in, c_in, edge_e_in, edge_h_in, edge_c_in, done_ref, weight_ref,
     sum_in, *rest,
 ):
     n_x = 1 if row_size == 2 else 2
     x_refs, corner_refs = rest[:n_x], rest[n_x : 2 * n_x]
-    eout_hbm, hout_hbm, term_ref, e_ref, h_ref, c_ref, edge_e_ref, edge_h_ref, edge_c_ref, sum_ref, out_ref, sems = rest[2 * n_x :]
-    gz, row, col = (lax.axis_index(name) for name in ("gz", "row", "col"))
+    eout_hbm, hout_hbm, term_ref, ez_ref, edge_ez_ref, sum_ref, out_ref, sems = rest[2 * n_x :]
+    gz, row = lax.axis_index("gz"), lax.axis_index("row")
     lane, sub = iota(1), iota(0)
     place = lane & (GROUP - 1)
     groups = [(lane >> 5) == r for r in range(4)]
@@ -485,20 +487,18 @@
     zeros = jnp.zeros((8, 128), jnp.float32)
 
     def first_main(f, i, zz):
-        own = 4 <= i < 12
         if f == 6:
-            return c_in[i - DEPTH, zz] if own else c_ref[i, zz]
+            return c_in[i - DEPTH, zz]
         return e_in[f, i - DEPTH, zz] if f < 3 else h_in[f - 3, i - DEPTH, zz]
 
     def first_edge(f, i, zz):
-        own = i in (1, 2)
         if f == 6:
-            return edge_c_in[i - 1, zz] if own else edge_c_ref[i, zz]
+            return edge_c_in[i - 1, zz]
         return edge_e_in[f, i - 1, zz] if f < 3 else edge_h_in[f - 3, i - 1, zz]
 
     def run(has_below, has_above):
-        main = Tiles(first_main, e_ref, h_ref, 0)
-        edge = Tiles(first_edge, edge_e_ref, edge_h_ref, 0)
+        main = Tiles(first_main, ez_ref, DEPTH)
+        edge = Tiles(first_edge, edge_ez_ref, 1)
 
         def halo_rows(planes, slot, offset, b):
             got = {}
@@ -509,13 +509,8 @@
                 tiles = [x_refs[slot][i, 8 * zz : 8 * zz + 8, :] for zz in range(OWN)]
                 tiles.append(jnp.where(valid, packed, 0.0))
                 for zz in range(CHUNK):
-                    if f == 6:
-                        c_ref[DEPTH + x + offset, zz] = tiles[zz]
-                    else:
-                        main.put(f, DEPTH + x + offset, zz, tiles[zz])
+                    main.put(f, DEPTH + x + offset, zz, tiles[zz])
                     got[f, x + offset - 4 * b, zz] = tiles[zz]
-                main.keep((f,), DEPTH + x + offset)
-            main.written -= {(6, i) for i in range(16)}
             for zz in range(CHUNK):
                 low = corner_refs[slot][PAIRS + zz]
                 high = corner_refs[slot][PAIRS + CHUNK + zz]
@@ -523,11 +518,7 @@
                     tiles = [got.get((f, r, zz)) for r in range(4)]
                     own = gather_edges(tiles, groups)
                     tile = edge_tile(zeros if own is None else own, low, high, f, place)
-                    if f == 6:
-                        edge_c_ref[1 + b, zz] = tile
-                    else:
-                        edge.put(f, 1 + b, zz, tile)
-            edge.keep(range(6), 1 + b)
+                    edge.put(f, 1 + b, zz, tile)
 
         if has_below:
             halo_rows(UP_PLANES, 0, -ROWS, -1)
@@ -544,10 +535,11 @@
 
         rows = range(0 if has_below else 4, 16 if has_above else 12)
         blocks = range(0 if has_below else 1, 4 if has_above else 3)
+        stepper = Stepper(row_size, main, edge, rows, blocks, True)
         for n in range(1, STEPS + 1):
             spans = ([spans_below(n)] if has_below else []) + ([spans_above(n)] if has_above else [])
-            advance(n, spans, main, edge, rows, blocks, (row_size, gz, row, col), True)
-            port_sums(n, reached, prow_ref, weight_ref, e_ref, edge_e_ref, DEPTH, 1, sum_ref, sum_in)
+            stepper.step(n, spans)
+            port_sums(n, reached, prow_ref, weight_ref, ez_ref, edge_ez_ref, sum_ref, sum_in)
         for f in range(6):
             for b in range(2):
                 if has_below and has_above or b == (1 if has_above else 0):
@@ -567,10 +559,14 @@
     for part, dest in ((0, eout_hbm), (1, hout_hbm)):
         copies.append(pltpu.make_async_copy(out_ref.at[pl.ds(3 * part, 3)], dest, sems.at[part]))
         copies[-1].start()
+    basis = zeros
+    for n in range(STEPS):
+        for f in range(2 * FREQ):
+            basis = jnp.where((sub == n) & (lane == f), float(BASIS[n, f]), basis)
     transform = zeros
     for n in range(STEPS):
         sampled = jnp.sum(sum_ref[n], axis=1, keepdims=True)
-        transform = transform + sampled * basis_ref[n : n + 1, :]
+        transform = transform + sampled * basis[n : n + 1, :]
     term_ref[...] = jnp.zeros(term_ref.shape, jnp.float32)
     for k in range(PORT_TILE):
         port = pid_ref[0, 0, k]
@@ -609,12 +605,17 @@
         def scratch(*shape):
             return pltpu.VMEM(shape, f32)
 
-        main, z_send, *x_send = pl.pallas_call(
-            functools.partial(pack_kernel, row_size),
-            out_shape=[array(FIELDS, LAYERS, ROWS, 128), array(FIELDS, DEPTH, ROWS, 128)]
-            + [array(PLANES, LAYERS, 128)] * n_x,
+        main, z_send, own, up_send, down_send = pl.pallas_call(
+            pack_kernel,
+            out_shape=[
+                array(FIELDS, LAYERS, ROWS, 128),
+                array(FIELDS, DEPTH, ROWS, 128),
+                array(FIELDS, 2, OWN, 8, 128),
+                array(2, OWN, 8, 128),
+                array(2, OWN, 8, 128),
+            ],
             in_specs=[HBM] * 4,
-            out_specs=[VMEM] * (2 + n_x),
+            out_specs=[VMEM] * 5,
             scratch_shapes=[
                 pltpu.SMEM(eps_table.shape, f32),
                 pltpu.VMEM(material.shape, jnp.int32),
@@ -622,18 +623,18 @@
             ],
             name="pack",
         )(eps_table, electric, magnetic, material)
-        x_halo = across_rows(x_send)
-        own, up_send, down_send = pl.pallas_call(
-            edge_kernel,
-            out_shape=[array(FIELDS, 2, OWN, 8, 128), array(2, OWN, 8, 128), array(2, OWN, 8, 128)],
-            in_specs=[VMEM],
-            out_specs=[VMEM] * 3,
-            compiler_params=PARAMS,
-            name="edges",
-        )(main)
         low = shifted(up_send, "col", col_size, 1)
         high = shifted(down_send, "col", col_size, -1)
         z_halo = swapped(z_send, "gz", gz_size)
+        x_send = pl.pallas_call(
+            functools.partial(plane_kernel, row_size),
+            out_shape=[array(PLANES, LAYERS, 128)] * n_x,
+            in_specs=[VMEM] + [pl.BlockSpec(memory_space=pl.ANY)] * 2,
+            out_specs=[VMEM] * n_x,
+            compiler_params=PARAMS,
+            name="planes",
+        )(main, low, high)
+        x_halo = across_rows(x_send)
         low_z = swapped(low, "gz", gz_size)
         high_z = swapped(high, "gz", gz_size)
         corner_send = pl.pallas_call(
@@ -664,7 +665,8 @@
             scratch_shapes=[
                 scratch(FIELDS, 8 * ROWS, 128),
                 scratch(PORT_TILE, LAYERS, 128),
-                scratch(FIELDS, 2, CHUNK, 8, 128),
+                scratch(ROWS, OWN, 8, 128),
+                scratch(2, OWN, 8, 128),
             ],
             compiler_params=PARAMS,
             name="inner",
@@ -674,22 +676,18 @@
         electric_out, magnetic_out, term = pl.pallas_call(
             functools.partial(outer_kernel, row_size, ports_each),
             out_shape=[array(3, LAYERS * ROWS, 128)] * 2 + [array(devices, ports_each, 2 * FREQ)],
-            in_specs=[VMEM] + [SMEM] * 2 + [VMEM] * (9 + 2 * n_x),
+            in_specs=[SMEM] * 2 + [VMEM] * (9 + 2 * n_x),
             out_specs=[HBM, HBM, VMEM],
             scratch_shapes=[
-                scratch(3, 16, CHUNK, 8, 128),
-                scratch(3, 16, CHUNK, 8, 128),
-                scratch(16, CHUNK, 8, 128),
-                scratch(3, 4, CHUNK, 8, 128),
-                scratch(3, 4, CHUNK, 8, 128),
-                scratch(4, CHUNK, 8, 128),
+                scratch(ROWS, OWN, 8, 128),
+                scratch(2, OWN, 8, 128),
                 scratch(STEPS, 8, 128),
                 scratch(6, LAYERS * ROWS, 128),
                 pltpu.SemaphoreType.DMA((2,)),
             ],
             compiler_params=PARAMS,
             name="outer",
-        )(jnp.asarray(dft_basis()), port_row, port_ids, *inner, *x_halo, *corner)
+        )(port_row, port_ids, *inner, *x_halo, *corner)
         terms = lax.all_to_all(term, ("col", "row", "gz"), 0, 0, tiled=True)
         return (
             electric_out.reshape(electric.shape),

time: 43 us -> 47.6 us (1.11)
  waiting for transfers between devices: 5.97 us -> 10.3 us
    ppermute x5, waiting for transfers between devices: 1.63 us -> 5.55 us  [swapped(): return lax.ppermute(block, axis, [(i, i ^ 1) for i in range(size)])]
    ppermute x2, starting transfers between devices: 4.9 us -> 6.22 us  [shifted(): return lax.ppermute(block, axis, route)]
    ppermute x5, starting transfers between devices: 3.77 us -> 2.85 us  [swapped(): return lax.ppermute(block, axis, [(i, i ^ 1) for i in range(size)])]
    unnamed x16 -> x18, local copies, waits for them, and re-layouts: 1.93 us -> 1.87 us
  transfers between devices with their start and end apart: 7 -> 7, of which waited for: 4 -> 5; matrix products, arithmetic and copies ran while one was open for 0% -> 0% of each run, Pallas kernels for 15% -> 8%
where the time goes in v7:
time: 47.6 us; the launch traced here: 47.3 us
  Pallas kernels  13.6 us (29%)
  blocking collectives  11.2 us (24%)
  waiting for transfers between devices  10.3 us (22%)
  starting transfers between devices  9.08 us (19%)
  local copies, waits for them, and re-layouts  1.87 us (4%)
  between operations  0.75 us (2%)
  other arithmetic  0.59 us (1%)
    all_to_all x1, blocking collectives, per_device(): terms = lax.all_to_all(term, ('col', 'row', 'gz'), 0, 0, tiled=True)  11.2 us
    ppermute x2, starting transfers between devices, shifted(): return lax.ppermute(block, axis, route)  6.22 us
    ppermute x5, waiting for transfers between devices, swapped(): return lax.ppermute(block, axis, [(i, i ^ 1) for i in range(size)])  5.55 us
    pallas_call x1, Pallas kernels, per_device(): pl.pallas_call(functools.partial(outer_kernel, row_size, ports_each), out...  5.19 us
    ppermute x2, waiting for transfers between devices, shifted(): return lax.ppermute(block, axis, route)  4.72 us
    pallas_call x1, Pallas kernels, per_device(): pl.pallas_call(pack_kernel, out_shape=[array(FIELDS, LAYERS, ROWS, 128),...  4.62 us
    pallas_call x1, Pallas kernels, per_device(): pl.pallas_call(functools.partial(inner_kernel, row_size), out_shape=[arra...  3.66 us
    ppermute x5, starting transfers between devices, swapped(): return lax.ppermute(block, axis, [(i, i ^ 1) for i in range(size)])  2.85 us
  transfers between devices with their start and end apart: 7, of which 5 were waited for; matrix products, arithmetic and copies ran while one was open for 0% of the time, Pallas kernels for 8%

profile of v7, /device:TPU:0, one launch (start us, length us, event | category | flops | bytes accessed | tf_op | source)
XLA Modules:
  0.0 47.3 jit_solution(13641436791067204888)
XLA Ops:
  0.6 4.6 %pack.1 = (f32[7,32,8,128]{3,2,1,0:T(8,128)}, f32[7,4,8,128]{3,2,1,0:T(8,128)}, f32[7,2,4,8,128]{4,3,2,1,0:T(8,128)}, f32[2,4,8,128]{3,2,1,0:T(8,128)}, f32[2,4,8,128]{3,2,1,0:T(8,128)}) custom-call(f32[8]{0:T(128)} %eps_hbm.1, f32[3,32,8,128]{3,2,1,0:T(8,128)} %elec_hbm.1, f32[3,32,8,128]{3,2,1,0:T(8,128)} %magn_hbm.1, s32[32,8,128]{2,1,0:T(8,128)} %mat_hbm.1), custom_call_target="tpu_custom_call" | custom-call | tf_op jit(solution)/shard_map/pack/pallas_call | solution.py:608
  5.3 4.9 %collective-permute-start.1 = (f32[2,4,8,128]{3,2,1,0:T(8,128)}, f32[2,4,8,128]{3,2,1,0:T(8,128)S(1)}, u32[]{:S(2)}, u32[]{:S(2)}) collective-permute-start(f32[2,4,8,128]{3,2,1,0:T(8,128)} %get-tuple-element.23), channel_id=1, source_target_pairs={{0,4},{4,8},{8,12},{1,5},{5,9},{9,13},{2,6},{6,10},{10,14},{3,7},{... | collective-permute-start | bytes 98312 | tf_op jit(solution)/shard_map/ppermute | solution.py:580
  10.2 1.3 %collective-permute-start.2 = (f32[2,4,8,128]{3,2,1,0:T(8,128)}, f32[2,4,8,128]{3,2,1,0:T(8,128)S(1)}, u32[]{:S(2)}, u32[]{:S(2)}) collective-permute-start(f32[2,4,8,128]{3,2,1,0:T(8,128)} %get-tuple-element.24), channel_id=1, source_target_pairs={{4,0},{8,4},{12,8},{5,1},{9,5},{13,9},{6,2},{10,6},{14,10},{7,3},{... | collective-permute-start | bytes 98312 | tf_op jit(solution)/shard_map/ppermute | solution.py:580
  11.5 0.6 %collective-permute-done.1.low_ref = f32[2,4,8,128]{3,2,1,0:T(8,128)S(1)} collective-permute-done((f32[2,4,8,128]{3,2,1,0:T(8,128)}, f32[2,4,8,128]{3,2,1,0:T(8,128)S(1)}, u32[]{:S(2)}, u32[]{:S(2)}) %collective-permute-start.1) | collective-permute-done | bytes 32800 | tf_op jit(solution)/shard_map/ppermute | solution.py:580
  12.1 4.1 %collective-permute-done.2.high_ref = f32[2,4,8,128]{3,2,1,0:T(8,128)S(1)} collective-permute-done((f32[2,4,8,128]{3,2,1,0:T(8,128)}, f32[2,4,8,128]{3,2,1,0:T(8,128)S(1)}, u32[]{:S(2)}, u32[]{:S(2)}) %collective-permute-start.2) | collective-permute-done | bytes 32800 | tf_op jit(solution)/shard_map/ppermute | solution.py:580
  16.2 1.2 %copy-done = f32[7,32,8,128]{3,2,1,0:T(8,128)S(1)} copy-done((f32[7,32,8,128]{3,2,1,0:T(8,128)S(1)}, f32[7,32,8,128]{3,2,1,0:T(8,128)}, u32[]{:S(2)}) %copy-start) | copy-done | bytes 917528
  17.4 0.1 planes.1
  17.5 0.0 copy-start.2
  17.5 1.5 %collective-permute-start.5 = (f32[26,32,128]{2,1,0:T(8,128)S(1)}, f32[26,32,128]{2,1,0:T(8,128)S(1)}, u32[]{:S(2)}, u32[]{:S(2)}) collective-permute-start(f32[26,32,128]{2,1,0:T(8,128)S(1)} %planes.1), channel_id=1, source_target_pairs={{0,2},{2,0},{1,3},{3,1},{4,6},{6,4},{5,7},{7,5},{8,10},{10,8},{9,1... | collective-permute-start | bytes 1277960 | tf_op jit(solution)/shard_map/ppermute | solution.py:584
  19.0 0.0 copy-done.8
  19.0 0.0 collective-permute-start
  19.0 0.5 %collective-permute-start.3 = (f32[2,4,8,128]{3,2,1,0:T(8,128)S(1)}, f32[2,4,8,128]{3,2,1,0:T(8,128)S(1)}, u32[]{:S(2)}, u32[]{:S(2)}) collective-permute-start(f32[2,4,8,128]{3,2,1,0:T(8,128)S(1)} %collective-permute-done.1.low_ref), channel_id=1, source_target_pairs={{0,1},{1,0},{2,3},{3,2},{4,5},{5,4},{6,7},{7,6},{8,9},{9,8},{10,11... | collective-permute-start | bytes 98312 | tf_op jit(solution)/shard_map/ppermute | solution.py:584
  19.6 0.0 collective-permute-start.4
  19.6 0.9 %collective-permute-done.3.low_z_ref = f32[2,4,8,128]{3,2,1,0:T(8,128)S(1)} collective-permute-done((f32[2,4,8,128]{3,2,1,0:T(8,128)S(1)}, f32[2,4,8,128]{3,2,1,0:T(8,128)S(1)}, u32[]{:S(2)}, u32[]{:S(2)}) %collective-permute-start.3) | collective-permute-done | bytes 32800 | tf_op jit(solution)/shard_map/ppermute | solution.py:584
  20.4 0.3 collective-permute-done.4.high_z_ref
  20.8 0.0 collective-permute-done.z_ref
  20.8 0.0 copy-start.4
  20.8 0.0 copy-start.5
  20.8 0.0 copy-start.6
  20.9 0.8 %collective-permute-start.6 = (f32[23,8,128]{2,1,0:T(8,128)S(1)}, f32[23,8,128]{2,1,0:T(8,128)S(1)}, u32[]{:S(2)}, u32[]{:S(2)}) collective-permute-start(f32[23,8,128]{2,1,0:T(8,128)S(1)} %corners.1), channel_id=1, source_target_pairs={{0,2},{2,0},{1,3},{3,1},{4,6},{6,4},{5,7},{7,5},{8,10},{10,8},{9,1... | collective-permute-start | bytes 282632 | tf_op jit(solution)/shard_map/ppermute | solution.py:584
  21.7 0.0 copy-done.1
  21.7 0.0 copy-done.3
  21.7 0.0 copy-done.2
  21.7 0.0 copy-done.5
  21.7 0.0 copy-done.6
  21.7 3.7 %inner.1 = (f32[3,8,5,8,128]{4,3,2,1,0:T(8,128)S(1)}, f32[3,8,5,8,128]{4,3,2,1,0:T(8,128)S(1)}, f32[8,5,8,128]{3,2,1,0:T(8,128)S(1)}, f32[3,2,5,8,128]{4,3,2,1,0...) custom-call(f32[7,32,8,128]{3,2,1,0:T(8,128)S(1)} %copy-done.1, ...), custom_call_target="tpu_custom_call" | custom-call | tf_op jit(solution)/shard_map/inner/pallas_call | solution.py:650
  25.4 4.3 %collective-permute-done.6.rest_1_ = f32[23,8,128]{2,1,0:T(8,128)S(1)} collective-permute-done((f32[23,8,128]{2,1,0:T(8,128)S(1)}, f32[23,8,128]{2,1,0:T(8,128)S(1)}, u32[]{:S(2)}, u32[]{:S(2)}) %collective-permute-start.6) | collective-permute-done | bytes 94240 | tf_op jit(solution)/shard_map/ppermute | solution.py:584
  29.7 0.0 collective-permute-done.5.rest_0_
  29.7 0.7 %copy-done.7 = s32[1,1,4]{2,1,0:T(1,128)S(1)} copy-done((s32[1,1,4]{2,1,0:T(1,128)S(1)}, s32[1,1,4]{2,1,0:T(1,128)}, u32[]{:S(2)}) %copy-start.7) | copy-done | bytes 40
  30.4 5.2 %outer.1 = (f32[3,256,128]{2,1,0:T(8,128)}, f32[3,256,128]{2,1,0:T(8,128)}, f32[16,2,16]{2,1,0:T(2,128)S(1)}) custom-call(s32[1,1,4]{2,1,0:T(1,128)S(1)} %copy-done.4, s32[1,1,4]{2,1,0:T(1,128)S(1)} %copy-done.7, f32[3,8,5,8,128]{4,3,2,1,0:T(8,128)S(1)} %get-tuple-element.25.e_in, f32[3,8,5,8,128]{4,3,2,1,0:T(8,128)S(1)} %get-tuple-element.26.h_in, ...), custom_call_target="tpu_custom_call" | custom-call | tf_op jit(solution)/shard_map/outer/pallas_call | solution.py:676
  35.6 11.2 %all_to_all.5 = f32[16,2,16]{2,1,0:T(2,128)S(1)} all-to-all(f32[16,2,16]{2,1,0:T(2,128)S(1)} %get-tuple-element.36), channel_id=1, replica_groups=mesh['grp'=2,'col'=4,'row'=2,'gz'=2] {'col','row','gz'}, dimensions={0} | all-to-all | bytes 4096 | tf_op jit(solution)/shard_map/all_to_all | solution.py:691
  46.8 0.6 %reduce_sum.9 = f32[2,16]{1,0:T(2,128)} reduce(f32[16,2,16]{2,1,0:T(2,128)S(1)} %all_to_all.5, f32[]{:T(128)} %constant.0.clone.1), dimensions={0}, to_apply=%region_0.0 | reduce | flops 480 | bytes 2180 | tf_op jit(solution)/shard_map/reduce_sum | solution.py:695
  (7 shorter events, 0.1 us)
Async XLA Ops:
  5.3 6.8 %collective-permute-start.1 = (f32[2,4,8,128]{3,2,1,0:T(8,128)}, f32[2,4,8,128]{3,2,1,0:T(8,128)S(1)}, u32[]{:S(2)}, u32[]{:S(2)}) collective-permute-start(f32[2,4,8,128]{3,2,1,0:T(8,128)} %get-tuple-element.23), channel_id=1, source_target_pairs={{0,4},{4,8},{8,12},{1,5},{5,9},{9,13},{2,6},{6,10},{10,14},{3,7},{... | collective-permute-start | bytes 98312 | tf_op jit(solution)/shard_map/ppermute | solution.py:580
  10.2 6.0 %collective-permute-start.2 = (f32[2,4,8,128]{3,2,1,0:T(8,128)}, f32[2,4,8,128]{3,2,1,0:T(8,128)S(1)}, u32[]{:S(2)}, u32[]{:S(2)}) collective-permute-start(f32[2,4,8,128]{3,2,1,0:T(8,128)} %get-tuple-element.24), channel_id=1, source_target_pairs={{4,0},{8,4},{12,8},{5,1},{9,5},{13,9},{6,2},{10,6},{14,10},{7,3},{... | collective-permute-start | bytes 98312 | tf_op jit(solution)/shard_map/ppermute | solution.py:580
  16.2 1.2 %copy-start = (f32[7,32,8,128]{3,2,1,0:T(8,128)S(1)}, f32[7,32,8,128]{3,2,1,0:T(8,128)}, u32[]{:S(2)}) copy-start(f32[7,32,8,128]{3,2,1,0:T(8,128)} %get-tuple-element.20.main_ref) | copy-start | bytes 2752516
  17.4 1.7 %copy-start.8 = (f32[7,4,8,128]{3,2,1,0:T(8,128)S(1)}, f32[7,4,8,128]{3,2,1,0:T(8,128)}, u32[]{:S(2)}) copy-start(f32[7,4,8,128]{3,2,1,0:T(8,128)} %get-tuple-element.21) | copy-start | bytes 344068
  17.4 4.3 %copy-start.1 = (f32[7,32,8,128]{3,2,1,0:T(8,128)S(1)}, f32[7,32,8,128]{3,2,1,0:T(8,128)}, u32[]{:S(2)}) copy-start(f32[7,32,8,128]{3,2,1,0:T(8,128)} %get-tuple-element.20.main_ref) | copy-start | bytes 2752516
  17.4 4.3 %copy-start.3 = (f32[8,32,64]{2,1,0:T(8,128)S(1)}, f32[8,32,64]{2,1,0:T(8,128)}, u32[]{:S(2)}) copy-start(f32[8,32,64]{2,1,0:T(8,128)} %mode_ref.1) | copy-start | bytes 196612
  17.5 4.2 %copy-start.2 = (f32[7,2,4,8,128]{4,3,2,1,0:T(8,128)S(1)}, f32[7,2,4,8,128]{4,3,2,1,0:T(8,128)}, u32[]{:S(2)}) copy-start(f32[7,2,4,8,128]{4,3,2,1,0:T(8,128)} %get-tuple-element.22.own_ref) | copy-start | bytes 688132
  17.5 12.2 %collective-permute-start.5 = (f32[26,32,128]{2,1,0:T(8,128)S(1)}, f32[26,32,128]{2,1,0:T(8,128)S(1)}, u32[]{:S(2)}, u32[]{:S(2)}) collective-permute-start(f32[26,32,128]{2,1,0:T(8,128)S(1)} %planes.1), channel_id=1, source_target_pairs={{0,2},{2,0},{1,3},{3,1},{4,6},{6,4},{5,7},{7,5},{8,10},{10,8},{9,1... | collective-permute-start | bytes 1277960 | tf_op jit(solution)/shard_map/ppermute | solution.py:584
  19.0 1.7 %collective-permute-start = (f32[7,4,8,128]{3,2,1,0:T(8,128)S(1)}, f32[7,4,8,128]{3,2,1,0:T(8,128)S(1)}, u32[]{:S(2)}, u32[]{:S(2)}) collective-permute-start(f32[7,4,8,128]{3,2,1,0:T(8,128)S(1)} %copy-done.8), channel_id=1, source_target_pairs={{0,1},{1,0},{2,3},{3,2},{4,5},{5,4},{6,7},{7,6},{8,9},{9,8},{10,11... | collective-permute-start | bytes 344072 | tf_op jit(solution)/shard_map/ppermute | solution.py:584
  19.0 1.4 %collective-permute-start.3 = (f32[2,4,8,128]{3,2,1,0:T(8,128)S(1)}, f32[2,4,8,128]{3,2,1,0:T(8,128)S(1)}, u32[]{:S(2)}, u32[]{:S(2)}) collective-permute-start(f32[2,4,8,128]{3,2,1,0:T(8,128)S(1)} %collective-permute-done.1.low_ref), channel_id=1, source_target_pairs={{0,1},{1,0},{2,3},{3,2},{4,5},{5,4},{6,7},{7,6},{8,9},{9,8},{10,11... | collective-permute-start | bytes 98312 | tf_op jit(solution)/shard_map/ppermute | solution.py:584
  19.6 1.2 %collective-permute-start.4 = (f32[2,4,8,128]{3,2,1,0:T(8,128)S(1)}, f32[2,4,8,128]{3,2,1,0:T(8,128)S(1)}, u32[]{:S(2)}, u32[]{:S(2)}) collective-permute-start(f32[2,4,8,128]{3,2,1,0:T(8,128)S(1)} %collective-permute-done.2.high_ref), channel_id=1, source_target_pairs={{0,1},{1,0},{2,3},{3,2},{4,5},{5,4},{6,7},{7,6},{8,9},{9,8},{10,11... | collective-permute-start | bytes 98312 | tf_op jit(solution)/shard_map/ppermute | solution.py:584
  20.8 0.8 %copy-start.4 = (s32[1,1,4]{2,1,0:T(1,128)S(1)}, s32[1,1,4]{2,1,0:T(1,128)}, u32[]{:S(2)}) copy-start(s32[1,1,4]{2,1,0:T(1,128)} %prow_ref.3) | copy-start | bytes 52
  20.8 0.8 %copy-start.5 = (s32[1,1,4]{2,1,0:T(1,128)S(1)}, s32[1,1,4]{2,1,0:T(1,128)}, u32[]{:S(2)}) copy-start(s32[1,1,4]{2,1,0:T(1,128)} %pcol_ref.1) | copy-start | bytes 52
  20.8 0.8 %copy-start.6 = (s32[1,1,4]{2,1,0:T(1,128)S(1)}, s32[1,1,4]{2,1,0:T(1,128)}, u32[]{:S(2)}) copy-start(s32[1,1,4]{2,1,0:T(1,128)} %pmode_ref.1) | copy-start | bytes 52
  20.9 8.9 %collective-permute-start.6 = (f32[23,8,128]{2,1,0:T(8,128)S(1)}, f32[23,8,128]{2,1,0:T(8,128)S(1)}, u32[]{:S(2)}, u32[]{:S(2)}) collective-permute-start(f32[23,8,128]{2,1,0:T(8,128)S(1)} %corners.1), channel_id=1, source_target_pairs={{0,2},{2,0},{1,3},{3,1},{4,6},{6,4},{5,7},{7,5},{8,10},{10,8},{9,1... | collective-permute-start | bytes 282632 | tf_op jit(solution)/shard_map/ppermute | solution.py:584
  29.7 0.7 %copy-start.7 = (s32[1,1,4]{2,1,0:T(1,128)S(1)}, s32[1,1,4]{2,1,0:T(1,128)}, u32[]{:S(2)}) copy-start(s32[1,1,4]{2,1,0:T(1,128)} %pid_ref.1) | copy-start | bytes 52

commit v8 on v7

--- a/solution.py
+++ b/solution.py
@@ -62,7 +62,8 @@
         body(False, 1)
 
 
-def pack_kernel(eps_hbm, elec_hbm, magn_hbm, mat_hbm, main_ref, z_ref, own_ref, up_ref, down_ref, eps_ref, mat_ref, sems):
+def pack_kernel(row_size, eps_hbm, elec_hbm, magn_hbm, mat_hbm, state_ref, z_ref, own_ref, even_ref, odd_ref, *rest):
+    x_refs, (main_ref, eps_ref, mat_ref, sems) = rest[:-4], rest[-4:]
     copies = [pltpu.make_async_copy(eps_hbm, eps_ref, sems.at[0]), pltpu.make_async_copy(mat_hbm, mat_ref, sems.at[1])]
     copies.append(pltpu.make_async_copy(elec_hbm, main_ref.at[pl.ds(0, 3)], sems.at[2]))
     copies.append(pltpu.make_async_copy(magn_hbm, main_ref.at[pl.ds(3, 3)], sems.at[3]))
@@ -81,7 +82,18 @@
     start = jnp.where(lax.axis_index("gz") == 0, LAYERS - DEPTH, 0)
     for f in range(FIELDS):
         z_ref[f] = main_ref[f, pl.ds(start, DEPTH)]
-    pack_edges(main_ref, own_ref, up_ref, down_ref)
+    block = LAYERS * ROWS
+    flat = main_ref.reshape(FIELDS * block, 128)
+    for f in range(FIELDS):
+        for x in range(ROWS):
+            state_ref[f, x] = flat[pl.ds(f * block + x, LAYERS, stride=ROWS), :].reshape(OWN, 8, 128)
+
+    def send(up, slot):
+        for i, (f, x) in enumerate(UP_PLANES if up else DOWN_PLANES):
+            x_refs[slot][i] = state_ref[f, x]
+
+    directions(row_size, send)
+    pack_edges(state_ref, own_ref, even_ref, odd_ref)
 
 
 def gather_edges(tiles, groups):
@@ -93,43 +105,40 @@
     return own
 
 
-def pack_edges(main_ref, own_ref, up_ref, down_ref):
+def pack_edges(state_ref, own_ref, even_ref, odd_ref):
     lane = iota(1)
     groups = [(lane >> 5) == r for r in range(4)]
     slots = [((lane & (GROUP - 1)) >> 2) == f for f in range(FIELDS)]
-    block = LAYERS * ROWS
-    flat = main_ref.reshape(FIELDS * block, 128)
-    values = []
+    even = (lax.axis_index("col") & 1) == 0
     for b in range(2):
         for zz in range(OWN):
             up = down = jnp.zeros((8, 128), jnp.float32)
+            owns = []
             for f in range(FIELDS):
-                at = f * block + zz * 8 * ROWS + 4 * b
-                own = gather_edges([flat[pl.ds(at + r, 8, stride=ROWS), :] for r in range(4)], groups)
+                own = gather_edges([state_ref[f, 4 * b + r, zz] for r in range(4)], groups)
                 up = jnp.where(slots[f], turn(own, DEPTH * f - 4, 1), up)
                 down = jnp.where(slots[f], turn(own, DEPTH * f - 8, 1), down)
-                values.append((own_ref, (f, b, zz), own))
-            values += [(up_ref, (b, zz), up), (down_ref, (b, zz), down)]
-    for ref, where, value in values:
-        ref[where] = value
-
-
-def plane_kernel(row_size, main_ref, low_ref, high_ref, *x_refs):
-    block = LAYERS * ROWS
-    flat = main_ref.reshape(FIELDS * block, 128)
-
-    def send(up, slot):
-        planes = UP_PLANES if up else DOWN_PLANES
-        for start in range(0, len(planes), 8):
-            part = [flat[pl.ds(f * block + x, LAYERS, stride=ROWS), :] for f, x in planes[start : start + 8]]
-            for i, plane in enumerate(part):
-                x_refs[slot][start + i] = plane
-
-    directions(row_size, send)
-
-
-def halo_layers(valid, gz, side_ref, b):
-    return jnp.where(valid, jnp.where(gz == 0, side_ref[b, 0], side_ref[b, OWN - 1]), 0.0)
+                owns.append(own)
+            for f in range(FIELDS):
+                own_ref[f, b, zz] = owns[f]
+            even_ref[b, zz] = jnp.where(even, up, down)
+            odd_ref[b, zz] = jnp.where(even, down, up)
+
+
+def low_and_high(even_ref, odd_ref):
+    even = (lax.axis_index("col") & 1) == 0
+
+    def low(*at):
+        return jnp.where(even, odd_ref[at], even_ref[at])
+
+    def high(*at):
+        return jnp.where(even, even_ref[at], odd_ref[at])
+
+    return low, high
+
+
+def halo_layers(valid, gz, side, b):
+    return jnp.where(valid, jnp.where(gz == 0, side(b, 0), side(b, OWN - 1)), 0.0)
 
 
 def spread_layers(gz, z_ref, ext_ref):
@@ -140,11 +149,13 @@
         ext_ref[f, DEPTH * ROWS :] = jnp.where(gz == 0, nothing, halo)
 
 
-def corner_kernel(row_size, z_ref, low_ref, high_ref, low_z_ref, high_z_ref, *rest):
+def corner_kernel(row_size, z_ref, even_ref, odd_ref, even_z_ref, odd_z_ref, *rest):
     x_refs, ext_ref = rest[:-1], rest[-1]
     gz = lax.axis_index("gz")
     valid = (iota(0) < 4) == (gz == 0)
     spread_layers(gz, z_ref, ext_ref)
+    low, high = low_and_high(even_ref, odd_ref)
+    low_z, high_z = low_and_high(even_z_ref, odd_z_ref)
 
     def send(up, slot):
         planes = UP_PLANES if up else DOWN_PLANES
@@ -160,10 +171,10 @@
             x_refs[slot][i] = pair
         b = 1 if up else 0
         for zz in range(OWN):
-            x_refs[slot][PAIRS + zz] = low_ref[b, zz]
-            x_refs[slot][PAIRS + CHUNK + zz] = high_ref[b, zz]
-        x_refs[slot][PAIRS + OWN] = halo_layers(valid, gz, low_z_ref, b)
-        x_refs[slot][PAIRS + CHUNK + OWN] = halo_layers(valid, gz, high_z_ref, b)
+            x_refs[slot][PAIRS + zz] = low(b, zz)
+            x_refs[slot][PAIRS + CHUNK + zz] = high(b, zz)
+        x_refs[slot][PAIRS + OWN] = halo_layers(valid, gz, low_z, b)
+        x_refs[slot][PAIRS + CHUNK + OWN] = halo_layers(valid, gz, high_z, b)
 
     directions(row_size, send)
 
@@ -395,31 +406,31 @@
 
 
 def inner_kernel(
-    row_size, main_ref, z_ref, own_ref, low_ref, high_ref, low_z_ref, high_z_ref, mode_ref, prow_ref, pcol_ref, pmode_ref,
-    e_ref, h_ref, c_ref, edge_e_ref, edge_h_ref, edge_c_ref, done_ref, weight_ref, sum_ref, ext_ref, strip_ref, ez_ref, edge_ez_ref,
+    row_size, state_ref, z_ref, own_ref, even_ref, odd_ref, even_z_ref, odd_z_ref, mode_ref, prow_ref, pcol_ref, pmode_ref, pid_ref,
+    e_ref, h_ref, c_ref, edge_e_ref, edge_h_ref, edge_c_ref, done_ref, weight_ref, sum_ref, ext_ref, halo_ref, strip_ref, ez_ref, edge_ez_ref,
 ):
     gz, row = lax.axis_index("gz"), lax.axis_index("row")
     lane, sub = iota(1), iota(0)
     place = lane & (GROUP - 1)
     groups = [(lane >> 5) == r for r in range(4)]
     valid = (sub < 4) == (gz == 0)
-    block = LAYERS * ROWS
-    flat = main_ref.reshape(FIELDS * block, 128)
     spread_layers(gz, z_ref, ext_ref)
+    low_of, high_of = low_and_high(even_ref, odd_ref)
+    low_z, high_z = low_and_high(even_z_ref, odd_z_ref)
+    for f in range(FIELDS):
+        for x in range(ROWS):
+            halo_ref[f, x] = ext_ref[f, pl.ds(x, 8, stride=ROWS), :]
 
     def first(f, i, zz):
-        x = i - DEPTH
-        if zz == OWN:
-            return ext_ref[f, pl.ds(x, 8, stride=ROWS), :]
-        return flat[pl.ds(f * block + zz * 8 * ROWS + x, 8, stride=ROWS), :]
+        return halo_ref[f, i - DEPTH] if zz == OWN else state_ref[f, i - DEPTH, zz]
 
     joined = {}
     for b in range(2):
         for zz in range(CHUNK):
             if zz < OWN:
-                low, high = low_ref[b, zz], high_ref[b, zz]
+                low, high = low_of(b, zz), high_of(b, zz)
             else:
-                low, high = (halo_layers(valid, gz, ref, b) for ref in (low_z_ref, high_z_ref))
+                low, high = (halo_layers(valid, gz, side, b) for side in (low_z, high_z))
             for f in range(FIELDS):
                 if zz < OWN:
                     own = own_ref[f, b, zz]
@@ -478,7 +489,7 @@
 ):
     n_x = 1 if row_size == 2 else 2
     x_refs, corner_refs = rest[:n_x], rest[n_x : 2 * n_x]
-    eout_hbm, hout_hbm, term_ref, ez_ref, edge_ez_ref, sum_ref, out_ref, sems = rest[2 * n_x :]
+    eout_hbm, hout_hbm, term_ref, ez_ref, edge_ez_ref, sum_ref, turned_ref, out_ref, sems = rest[2 * n_x :]
     gz, row = lax.axis_index("gz"), lax.axis_index("row")
     lane, sub = iota(1), iota(0)
     place = lane & (GROUP - 1)
@@ -506,7 +517,7 @@
                 packed = corner_refs[slot][i % PAIRS]
                 if i >= PAIRS:
                     packed = turn(packed, 4, 0)
-                tiles = [x_refs[slot][i, 8 * zz : 8 * zz + 8, :] for zz in range(OWN)]
+                tiles = [x_refs[slot][i, zz] for zz in range(OWN)]
                 tiles.append(jnp.where(valid, packed, 0.0))
                 for zz in range(CHUNK):
                     main.put(f, DEPTH + x + offset, zz, tiles[zz])
@@ -547,7 +558,7 @@
                 else:
                     tiles = {(r, zz): done_ref[f, r, zz] for r in range(4) for zz in range(OWN)}
                 for (r, zz), tile in tiles.items():
-                    out_ref[f, pl.ds(zz * 8 * ROWS + 4 * b + r, 8, stride=ROWS), :] = tile
+                    turned_ref[f, 4 * b + r, 8 * zz : 8 * zz + 8, :] = tile
 
     if row_size == 2:
         pl.when(row == 0)(functools.partial(run, False, True))
@@ -556,7 +567,11 @@
         run(True, True)
 
     copies = []
+    flat = turned_ref.reshape(6 * ROWS * LAYERS, 128)
     for part, dest in ((0, eout_hbm), (1, hout_hbm)):
+        for f in range(3 * part, 3 * part + 3):
+            for z in range(LAYERS):
+                out_ref[f, z] = flat[pl.ds(f * ROWS * LAYERS + z, ROWS, stride=LAYERS), :]
         copies.append(pltpu.make_async_copy(out_ref.at[pl.ds(3 * part, 3)], dest, sems.at[part]))
         copies[-1].start()
     basis = zeros
@@ -580,8 +595,9 @@
     return lax.ppermute(block, axis, route)
 
 
-def swapped(block, axis, size):
-    return lax.ppermute(block, axis, [(i, i ^ 1) for i in range(size)])
+def swapped(block, axis, size, start=0):
+    pairs = [(i, i + 1) for i in range(start, size - 1, 2)]
+    return lax.ppermute(block, axis, pairs + [(j, i) for i, j in pairs])
 
 
 def solution(mesh):
@@ -605,38 +621,32 @@
         def scratch(*shape):
             return pltpu.VMEM(shape, f32)
 
-        main, z_send, own, up_send, down_send = pl.pallas_call(
-            pack_kernel,
+        state, z_send, own, even_send, odd_send, *x_send = pl.pallas_call(
+            functools.partial(pack_kernel, row_size),
             out_shape=[
-                array(FIELDS, LAYERS, ROWS, 128),
+                array(FIELDS, ROWS, OWN, 8, 128),
                 array(FIELDS, DEPTH, ROWS, 128),
                 array(FIELDS, 2, OWN, 8, 128),
                 array(2, OWN, 8, 128),
                 array(2, OWN, 8, 128),
-            ],
+            ]
+            + [array(PLANES, OWN, 8, 128)] * n_x,
             in_specs=[HBM] * 4,
-            out_specs=[VMEM] * 5,
+            out_specs=[VMEM] * (5 + n_x),
             scratch_shapes=[
+                scratch(FIELDS, LAYERS, ROWS, 128),
                 pltpu.SMEM(eps_table.shape, f32),
                 pltpu.VMEM(material.shape, jnp.int32),
                 pltpu.SemaphoreType.DMA((4,)),
             ],
             name="pack",
         )(eps_table, electric, magnetic, material)
-        low = shifted(up_send, "col", col_size, 1)
-        high = shifted(down_send, "col", col_size, -1)
+        x_halo = across_rows(x_send)
+        even = swapped(even_send, "col", col_size)
+        odd = swapped(odd_send, "col", col_size, 1)
         z_halo = swapped(z_send, "gz", gz_size)
-        x_send = pl.pallas_call(
-            functools.partial(plane_kernel, row_size),
-            out_shape=[array(PLANES, LAYERS, 128)] * n_x,
-            in_specs=[VMEM] + [pl.BlockSpec(memory_space=pl.ANY)] * 2,
-            out_specs=[VMEM] * n_x,
-            compiler_params=PARAMS,
-            name="planes",
-        )(main, low, high)
-        x_halo = across_rows(x_send)
-        low_z = swapped(low, "gz", gz_size)
-        high_z = swapped(high, "gz", gz_size)
+        even_z = swapped(even, "gz", gz_size)
+        odd_z = swapped(odd, "gz", gz_size)
         corner_send = pl.pallas_call(
             functools.partial(corner_kernel, row_size),
             out_shape=[array(PAIRS + 2 * CHUNK, 8, 128)] * n_x,
@@ -645,7 +655,7 @@
             scratch_shapes=[scratch(FIELDS, 8 * ROWS, 128)],
             compiler_params=PARAMS,
             name="corners",
-        )(z_halo, low, high, low_z, high_z)
+        )(z_halo, even, odd, even_z, odd_z)
         corner = across_rows(corner_send)
         inner = pl.pallas_call(
             functools.partial(inner_kernel, row_size),
@@ -660,29 +670,31 @@
                 array(PORT_TILE, 2, OWN, 8, 128),
                 array(STEPS, 8, 128),
             ],
-            in_specs=[VMEM] * 8 + [SMEM] * 3,
+            in_specs=[VMEM] * 8 + [SMEM] * 4,
             out_specs=[VMEM] * 9,
             scratch_shapes=[
                 scratch(FIELDS, 8 * ROWS, 128),
+                scratch(FIELDS, ROWS, 8, 128),
                 scratch(PORT_TILE, LAYERS, 128),
                 scratch(ROWS, OWN, 8, 128),
                 scratch(2, OWN, 8, 128),
             ],
             compiler_params=PARAMS,
             name="inner",
-        )(main, z_halo, own, low, high, low_z, high_z, mode_table, port_row, port_col, port_mode)
+        )(state, z_halo, own, even, odd, even_z, odd_z, mode_table, port_row, port_col, port_mode, port_ids)
         devices = col_size * row_size * gz_size
         ports_each = PORT_TILE * col_size * row_size // devices
         electric_out, magnetic_out, term = pl.pallas_call(
             functools.partial(outer_kernel, row_size, ports_each),
-            out_shape=[array(3, LAYERS * ROWS, 128)] * 2 + [array(devices, ports_each, 2 * FREQ)],
+            out_shape=[array(3, LAYERS, ROWS, 128)] * 2 + [array(devices, ports_each, 2 * FREQ)],
             in_specs=[SMEM] * 2 + [VMEM] * (9 + 2 * n_x),
             out_specs=[HBM, HBM, VMEM],
             scratch_shapes=[
                 scratch(ROWS, OWN, 8, 128),
                 scratch(2, OWN, 8, 128),
                 scratch(STEPS, 8, 128),
-                scratch(6, LAYERS * ROWS, 128),
+                scratch(6, ROWS, LAYERS, 128),
+                scratch(6, LAYERS, ROWS, 128),
                 pltpu.SemaphoreType.DMA((2,)),
             ],
             compiler_params=PARAMS,
@@ -690,8 +702,8 @@
         )(port_row, port_ids, *inner, *x_halo, *corner)
         terms = lax.all_to_all(term, ("col", "row", "gz"), 0, 0, tiled=True)
         return (
-            electric_out.reshape(electric.shape),
-            magnetic_out.reshape(magnetic.shape),
+            electric_out,
+            magnetic_out,
             jnp.sum(terms, axis=0),
         )
 

time: 47.6 us -> 41.1 us (0.86)
  waiting for transfers between devices: 10.3 us -> 3.55 us
  starting transfers between devices: 9.08 us -> 6.06 us
  blocking collectives: 11.2 us -> 14 us
  Pallas kernels: 13.6 us -> 14.1 us
    ppermute x7, waiting for transfers between devices: 10.3 us -> 3.55 us  [swapped(): return lax.ppermute(block, axis, pairs + [(j, i) for i, j in pairs])]
    ppermute x7, starting transfers between devices: 9.08 us -> 6.06 us  [swapped(): return lax.ppermute(block, axis, pairs + [(j, i) for i, j in pairs])]
    all_to_all x1, blocking collectives: 11.2 us -> 14 us  [per_device(): terms = lax.all_to_all(term, ('col', 'row', 'gz'), 0, 0, tiled=True)]
    pallas_call x2 -> x1, Pallas kernels: 4.7 us -> 5.03 us  [per_device(): pl.pallas_call(functools.partial(pack_kernel, row_size), out_shape=[array...]
    unnamed x18 -> x14, local copies, waits for them, and re-layouts: 1.87 us -> 1.86 us
  transfers between devices with their start and end apart: 7 -> 7, of which waited for: 5 -> 4; matrix products, arithmetic and copies ran while one was open for 0% -> 0% of each run, Pallas kernels for 8% -> 9%
where the time goes in v8:
time: 41.1 us; the launch traced here: 40.9 us
  Pallas kernels  14.1 us (34%)
  blocking collectives  14 us (34%)
  starting transfers between devices  6.06 us (15%)
  waiting for transfers between devices  3.55 us (9%)
  local copies, waits for them, and re-layouts  1.86 us (5%)
  between operations  0.71 us (2%)
  other arithmetic  0.59 us (1%)
    all_to_all x1, blocking collectives, per_device(): terms = lax.all_to_all(term, ('col', 'row', 'gz'), 0, 0, tiled=True)  14 us
    ppermute x7, starting transfers between devices, swapped(): return lax.ppermute(block, axis, pairs + [(j, i) for i, j in pairs])  6.06 us
    pallas_call x1, Pallas kernels, per_device(): pl.pallas_call(functools.partial(outer_kernel, row_size, ports_each), out...  5.51 us
    pallas_call x1, Pallas kernels, per_device(): pl.pallas_call(functools.partial(pack_kernel, row_size), out_shape=[array...  5.03 us
    ppermute x7, waiting for transfers between devices, swapped(): return lax.ppermute(block, axis, pairs + [(j, i) for i, j in pairs])  3.55 us
    pallas_call x1, Pallas kernels, per_device(): pl.pallas_call(functools.partial(inner_kernel, row_size), out_shape=[arra...  3.49 us
    unnamed x14, local copies, waits for them, and re-layouts  1.86 us
  transfers between devices with their start and end apart: 7, of which 4 were waited for; matrix products, arithmetic and copies ran while one was open for 0% of the time, Pallas kernels for 9%

profile of v8, /device:TPU:0, one launch (start us, length us, event | category | flops | bytes accessed | tf_op | source)
XLA Modules:
  0.0 40.9 jit_solution(12517093171081944950)
XLA Ops:
  0.6 0.0 copy-start.2
  0.6 5.0 %pack.1 = (f32[7,8,4,8,128]{4,3,2,1,0:T(8,128)}, f32[7,4,8,128]{3,2,1,0:T(8,128)}, f32[7,2,4,8,128]{4,3,2,1,0:T(8,128)}, f32[2,4,8,128]{3,2,1,0:T(8,128)}, f32[2...) custom-call(f32[8]{0:T(128)} %eps_hbm.1, f32[3,32,8,128]{3,2,1,0:T(8,128)} %elec_hbm.1, f32[3,32,8,128]{3,2,1,0:T(8,128)} %magn_hbm.1, ...), custom_call_target="tpu_custom_call" | custom-call | tf_op jit(solution)/shard_map/pack/pallas_call | solution.py:624
  5.7 0.0 copy-start.1
  5.7 3.0 %collective-permute-start.5 = (f32[26,4,8,128]{3,2,1,0:T(8,128)}, f32[26,4,8,128]{3,2,1,0:T(8,128)S(1)}, u32[]{:S(2)}, u32[]{:S(2)}) collective-permute-start(f32[26,4,8,128]{3,2,1,0:T(8,128)} %get-tuple-element.35), channel_id=1, source_target_pairs={{0,2},{2,0},{1,3},{3,1},{4,6},{6,4},{5,7},{7,5},{8,10},{10,8},{9,1... | collective-permute-start | bytes 1277960 | tf_op jit(solution)/shard_map/ppermute | solution.py:600
  8.7 0.0 collective-permute-start
  8.7 1.6 %collective-permute-start.1 = (f32[2,4,8,128]{3,2,1,0:T(8,128)}, f32[2,4,8,128]{3,2,1,0:T(8,128)S(1)}, u32[]{:S(2)}, u32[]{:S(2)}) collective-permute-start(f32[2,4,8,128]{3,2,1,0:T(8,128)} %get-tuple-element.24), channel_id=1, source_target_pairs={{0,4},{8,12},{4,0},{12,8},{1,5},{9,13},{5,1},{13,9},{2,6},{10,14},... | collective-permute-start | bytes 98312 | tf_op jit(solution)/shard_map/ppermute | solution.py:600
  10.3 0.7 %collective-permute-start.2 = (f32[2,4,8,128]{3,2,1,0:T(8,128)}, f32[2,4,8,128]{3,2,1,0:T(8,128)S(1)}, u32[]{:S(2)}, u32[]{:S(2)}) collective-permute-start(f32[2,4,8,128]{3,2,1,0:T(8,128)} %get-tuple-element.25), channel_id=1, source_target_pairs={{4,8},{8,4},{5,9},{9,5},{6,10},{10,6},{7,11},{11,7},{20,24},{24,20... | collective-permute-start | bytes 98312 | tf_op jit(solution)/shard_map/ppermute | solution.py:600
  10.9 1.9 %collective-permute-done.1.even_ref = f32[2,4,8,128]{3,2,1,0:T(8,128)S(1)} collective-permute-done((f32[2,4,8,128]{3,2,1,0:T(8,128)}, f32[2,4,8,128]{3,2,1,0:T(8,128)S(1)}, u32[]{:S(2)}, u32[]{:S(2)}) %collective-permute-start.1) | collective-permute-done | bytes 32800 | tf_op jit(solution)/shard_map/ppermute | solution.py:600
  12.8 0.0 collective-permute-start.3
  12.8 0.0 collective-permute-done.2.odd_ref
  12.8 0.5 %collective-permute-start.4 = (f32[2,4,8,128]{3,2,1,0:T(8,128)S(1)}, f32[2,4,8,128]{3,2,1,0:T(8,128)S(1)}, u32[]{:S(2)}, u32[]{:S(2)}) collective-permute-start(f32[2,4,8,128]{3,2,1,0:T(8,128)S(1)} %collective-permute-done.2.odd_ref), channel_id=1, source_target_pairs={{0,1},{1,0},{2,3},{3,2},{4,5},{5,4},{6,7},{7,6},{8,9},{9,8},{10,11... | collective-permute-start | bytes 98312 | tf_op jit(solution)/shard_map/ppermute | solution.py:600
  13.3 0.7 %collective-permute-done.3.even_z_ref = f32[2,4,8,128]{3,2,1,0:T(8,128)S(1)} collective-permute-done((f32[2,4,8,128]{3,2,1,0:T(8,128)S(1)}, f32[2,4,8,128]{3,2,1,0:T(8,128)S(1)}, u32[]{:S(2)}, u32[]{:S(2)}) %collective-permute-start.3) | collective-permute-done | bytes 32800 | tf_op jit(solution)/shard_map/ppermute | solution.py:600
  14.0 0.2 collective-permute-done.4.odd_z_ref
  14.2 0.0 collective-permute-done.z_ref
  14.2 0.0 copy-start.6
  14.3 0.3 collective-permute-start.6
  14.6 0.0 copy-start.3
  14.6 0.0 copy-start.4
  14.6 0.0 copy-start.5
  14.6 0.0 copy-done.2
  14.6 0.0 copy-done.1
  14.6 0.3 copy-done.6
  14.9 0.4 copy-done.3
  15.2 0.0 copy-done.4
  15.2 0.0 copy-done.5
  15.3 1.2 %copy-done = f32[7,8,4,8,128]{4,3,2,1,0:T(8,128)S(1)} copy-done((f32[7,8,4,8,128]{4,3,2,1,0:T(8,128)S(1)}, f32[7,8,4,8,128]{4,3,2,1,0:T(8,128)}, u32[]{:S(2)}) %copy-start) | copy-done | bytes 917528
  16.4 3.5 %inner.1 = (f32[3,8,5,8,128]{4,3,2,1,0:T(8,128)S(1)}, f32[3,8,5,8,128]{4,3,2,1,0:T(8,128)S(1)}, f32[8,5,8,128]{3,2,1,0:T(8,128)S(1)}, f32[3,2,5,8,128]{4,3,2,1,0...) custom-call(f32[7,8,4,8,128]{4,3,2,1,0:T(8,128)S(1)} %copy-done, ...), custom_call_target="tpu_custom_call" | custom-call | tf_op jit(solution)/shard_map/inner/pallas_call | solution.py:660
  19.9 0.8 %collective-permute-done.6.rest_1_ = f32[23,8,128]{2,1,0:T(8,128)S(1)} collective-permute-done((f32[23,8,128]{2,1,0:T(8,128)S(1)}, f32[23,8,128]{2,1,0:T(8,128)S(1)}, u32[]{:S(2)}, u32[]{:S(2)}) %collective-permute-start.6) | collective-permute-done | bytes 94240 | tf_op jit(solution)/shard_map/ppermute | solution.py:600
  20.7 0.0 collective-permute-done.5.rest_0_
  20.7 5.5 %outer.1 = (f32[3,32,8,128]{3,2,1,0:T(8,128)}, f32[3,32,8,128]{3,2,1,0:T(8,128)}, f32[16,2,16]{2,1,0:T(2,128)S(1)}) custom-call(s32[1,1,4]{2,1,0:T(1,128)S(1)} %copy-done.3, s32[1,1,4]{2,1,0:T(1,128)S(1)} %copy-done.4, f32[3,8,5,8,128]{4,3,2,1,0:T(8,128)S(1)} %get-tuple-element.26.e_in, f32[3,8,5,8,128]{4,3,2,1,0:T(8,128)S(1)} %get-tuple-element.27.h_in, ...), custom_call_target="tpu_custom_call" | custom-call | tf_op jit(solution)/shard_map/outer/pallas_call | solution.py:687
  26.3 14.0 %all_to_all.5 = f32[16,2,16]{2,1,0:T(2,128)S(1)} all-to-all(f32[16,2,16]{2,1,0:T(2,128)S(1)} %get-tuple-element.38), channel_id=1, replica_groups=mesh['grp'=2,'col'=4,'row'=2,'gz'=2] {'col','row','gz'}, dimensions={0} | all-to-all | bytes 4096 | tf_op jit(solution)/shard_map/all_to_all | solution.py:703
  40.3 0.6 %reduce_sum.9 = f32[2,16]{1,0:T(2,128)} reduce(f32[16,2,16]{2,1,0:T(2,128)S(1)} %all_to_all.5, f32[]{:T(128)} %constant.0.clone.1), dimensions={0}, to_apply=%region_0.0 | reduce | flops 480 | bytes 2180 | tf_op jit(solution)/shard_map/reduce_sum | solution.py:707
  (2 shorter events, 0.0 us)
Async XLA Ops:
  0.6 14.0 %copy-start.2 = (f32[8,32,64]{2,1,0:T(8,128)S(1)}, f32[8,32,64]{2,1,0:T(8,128)}, u32[]{:S(2)}) copy-start(f32[8,32,64]{2,1,0:T(8,128)} %mode_ref.1) | copy-start | bytes 196612
  5.7 8.9 %copy-start.1 = (f32[7,2,4,8,128]{4,3,2,1,0:T(8,128)S(1)}, f32[7,2,4,8,128]{4,3,2,1,0:T(8,128)}, u32[]{:S(2)}) copy-start(f32[7,2,4,8,128]{4,3,2,1,0:T(8,128)} %get-tuple-element.23.own_ref) | copy-start | bytes 688132
  5.7 15.1 %collective-permute-start.5 = (f32[26,4,8,128]{3,2,1,0:T(8,128)}, f32[26,4,8,128]{3,2,1,0:T(8,128)S(1)}, u32[]{:S(2)}, u32[]{:S(2)}) collective-permute-start(f32[26,4,8,128]{3,2,1,0:T(8,128)} %get-tuple-element.35), channel_id=1, source_target_pairs={{0,2},{2,0},{1,3},{3,1},{4,6},{6,4},{5,7},{7,5},{8,10},{10,8},{9,1... | collective-permute-start | bytes 1277960 | tf_op jit(solution)/shard_map/ppermute | solution.py:600
  8.7 5.5 %collective-permute-start = (f32[7,4,8,128]{3,2,1,0:T(8,128)}, f32[7,4,8,128]{3,2,1,0:T(8,128)S(1)}, u32[]{:S(2)}, u32[]{:S(2)}) collective-permute-start(f32[7,4,8,128]{3,2,1,0:T(8,128)} %get-tuple-element.22), channel_id=1, source_target_pairs={{0,1},{1,0},{2,3},{3,2},{4,5},{5,4},{6,7},{7,6},{8,9},{9,8},{10,11... | collective-permute-start | bytes 344072 | tf_op jit(solution)/shard_map/ppermute | solution.py:600
  8.7 4.1 %collective-permute-start.1 = (f32[2,4,8,128]{3,2,1,0:T(8,128)}, f32[2,4,8,128]{3,2,1,0:T(8,128)S(1)}, u32[]{:S(2)}, u32[]{:S(2)}) collective-permute-start(f32[2,4,8,128]{3,2,1,0:T(8,128)} %get-tuple-element.24), channel_id=1, source_target_pairs={{0,4},{8,12},{4,0},{12,8},{1,5},{9,13},{5,1},{13,9},{2,6},{10,14},... | collective-permute-start | bytes 98312 | tf_op jit(solution)/shard_map/ppermute | solution.py:600
  10.3 2.6 %collective-permute-start.2 = (f32[2,4,8,128]{3,2,1,0:T(8,128)}, f32[2,4,8,128]{3,2,1,0:T(8,128)S(1)}, u32[]{:S(2)}, u32[]{:S(2)}) collective-permute-start(f32[2,4,8,128]{3,2,1,0:T(8,128)} %get-tuple-element.25), channel_id=1, source_target_pairs={{4,8},{8,4},{5,9},{9,5},{6,10},{10,6},{7,11},{11,7},{20,24},{24,20... | collective-permute-start | bytes 98312 | tf_op jit(solution)/shard_map/ppermute | solution.py:600
  12.8 1.2 %collective-permute-start.3 = (f32[2,4,8,128]{3,2,1,0:T(8,128)S(1)}, f32[2,4,8,128]{3,2,1,0:T(8,128)S(1)}, u32[]{:S(2)}, u32[]{:S(2)}) collective-permute-start(f32[2,4,8,128]{3,2,1,0:T(8,128)S(1)} %collective-permute-done.1.even_ref), channel_id=1, source_target_pairs={{0,1},{1,0},{2,3},{3,2},{4,5},{5,4},{6,7},{7,6},{8,9},{9,8},{10,11... | collective-permute-start | bytes 98312 | tf_op jit(solution)/shard_map/ppermute | solution.py:600
  12.8 1.4 %collective-permute-start.4 = (f32[2,4,8,128]{3,2,1,0:T(8,128)S(1)}, f32[2,4,8,128]{3,2,1,0:T(8,128)S(1)}, u32[]{:S(2)}, u32[]{:S(2)}) collective-permute-start(f32[2,4,8,128]{3,2,1,0:T(8,128)S(1)} %collective-permute-done.2.odd_ref), channel_id=1, source_target_pairs={{0,1},{1,0},{2,3},{3,2},{4,5},{5,4},{6,7},{7,6},{8,9},{9,8},{10,11... | collective-permute-start | bytes 98312 | tf_op jit(solution)/shard_map/ppermute | solution.py:600
  14.2 0.7 %copy-start.6 = (s32[1,1,4]{2,1,0:T(1,128)S(1)}, s32[1,1,4]{2,1,0:T(1,128)}, u32[]{:S(2)}) copy-start(s32[1,1,4]{2,1,0:T(1,128)} %pmode_ref.1) | copy-start | bytes 52
  14.3 6.5 %collective-permute-start.6 = (f32[23,8,128]{2,1,0:T(8,128)S(1)}, f32[23,8,128]{2,1,0:T(8,128)S(1)}, u32[]{:S(2)}, u32[]{:S(2)}) collective-permute-start(f32[23,8,128]{2,1,0:T(8,128)S(1)} %corners.1), channel_id=1, source_target_pairs={{0,2},{2,0},{1,3},{3,1},{4,6},{6,4},{5,7},{7,5},{8,10},{10,8},{9,1... | collective-permute-start | bytes 282632 | tf_op jit(solution)/shard_map/ppermute | solution.py:600
  14.6 0.7 %copy-start.3 = (s32[1,1,4]{2,1,0:T(1,128)S(1)}, s32[1,1,4]{2,1,0:T(1,128)}, u32[]{:S(2)}) copy-start(s32[1,1,4]{2,1,0:T(1,128)} %prow_ref.3) | copy-start | bytes 52
  14.6 0.7 %copy-start.4 = (s32[1,1,4]{2,1,0:T(1,128)S(1)}, s32[1,1,4]{2,1,0:T(1,128)}, u32[]{:S(2)}) copy-start(s32[1,1,4]{2,1,0:T(1,128)} %pid_ref.3) | copy-start | bytes 52
  14.6 0.7 %copy-start.5 = (s32[1,1,4]{2,1,0:T(1,128)S(1)}, s32[1,1,4]{2,1,0:T(1,128)}, u32[]{:S(2)}) copy-start(s32[1,1,4]{2,1,0:T(1,128)} %pcol_ref.1) | copy-start | bytes 52
  15.3 1.2 %copy-start = (f32[7,8,4,8,128]{4,3,2,1,0:T(8,128)S(1)}, f32[7,8,4,8,128]{4,3,2,1,0:T(8,128)}, u32[]{:S(2)}) copy-start(f32[7,8,4,8,128]{4,3,2,1,0:T(8,128)} %get-tuple-element.21.state_ref) | copy-start | bytes 2752516

commit v9 on v8

--- a/solution.py
+++ b/solution.py
@@ -96,19 +96,24 @@
     pack_edges(state_ref, own_ref, even_ref, odd_ref)
 
 
+def lane_groups():
+    group = iota(1) >> 5
+    return [jnp.where(group == r, 1.0, 0.0) for r in range(4)]
+
+
 def gather_edges(tiles, groups):
     own = None
     for r, tile in enumerate(tiles):
         if tile is not None:
-            moved = turn(tile, GROUP * r + 8, 1)
-            own = moved if own is None else jnp.where(groups[r], moved, own)
+            moved = turn(tile, GROUP * r + 8, 1) * groups[r]
+            own = moved if own is None else own + moved
     return own
 
 
 def pack_edges(state_ref, own_ref, even_ref, odd_ref):
     lane = iota(1)
-    groups = [(lane >> 5) == r for r in range(4)]
-    slots = [((lane & (GROUP - 1)) >> 2) == f for f in range(FIELDS)]
+    groups = lane_groups()
+    slots = [jnp.where(((lane & (GROUP - 1)) >> 2) == f, 1.0, 0.0) for f in range(FIELDS)]
     even = (lax.axis_index("col") & 1) == 0
     for b in range(2):
         for zz in range(OWN):
@@ -116,8 +121,8 @@
             owns = []
             for f in range(FIELDS):
                 own = gather_edges([state_ref[f, 4 * b + r, zz] for r in range(4)], groups)
-                up = jnp.where(slots[f], turn(own, DEPTH * f - 4, 1), up)
-                down = jnp.where(slots[f], turn(own, DEPTH * f - 8, 1), down)
+                up = up + turn(own, DEPTH * f - 4, 1) * slots[f]
+                down = down + turn(own, DEPTH * f - 8, 1) * slots[f]
                 owns.append(own)
             for f in range(FIELDS):
                 own_ref[f, b, zz] = owns[f]
@@ -149,7 +154,7 @@
         ext_ref[f, DEPTH * ROWS :] = jnp.where(gz == 0, nothing, halo)
 
 
-def corner_kernel(row_size, z_ref, even_ref, odd_ref, even_z_ref, odd_z_ref, *rest):
+def corner_kernel(row_size, prep_ref, z_ref, even_ref, odd_ref, even_z_ref, odd_z_ref, *rest):
     x_refs, ext_ref = rest[:-1], rest[-1]
     gz = lax.axis_index("gz")
     valid = (iota(0) < 4) == (gz == 0)
@@ -405,14 +410,34 @@
     return out
 
 
+def prep_kernel(state_hbm, even_ref, mode_ref, prow_ref, pcol_ref, pmode_ref, pid_ref, state_ref, weight_ref, strip_ref, sem):
+    copy = pltpu.make_async_copy(state_hbm, state_ref, sem)
+    copy.start()
+    lane = iota(1)
+    for k in range(PORT_TILE):
+        strip_ref[k] = jnp.zeros(strip_ref.shape[1:], jnp.float32)
+        strip_ref[k, :, 0:PLEN] = mode_ref[pmode_ref[0, 0, k]]
+    for k in range(PORT_TILE):
+        turned = GROUP * (prow_ref[0, 0, k] & 3)
+        at = lane - turned
+        for zz in range(OWN):
+            tile = pltpu.roll(strip_ref[k, 8 * zz : 8 * zz + 8, :], pcol_ref[0, 0, k], 1)
+            weight_ref[k, 0, zz] = jnp.where((lane >= DEPTH) & (lane < 128 - DEPTH), tile, 0.0)
+            own = pltpu.roll(tile, turned + 8, 1)
+            edge = jnp.where((at >= 4) & (at < 8), own, 0.0)
+            weight_ref[k, 1, zz] = jnp.where((at >= 16) & (at < 20), turn(own, 8, 1), edge)
+
+    copy.wait()
+
+
 def inner_kernel(
-    row_size, state_ref, z_ref, own_ref, even_ref, odd_ref, even_z_ref, odd_z_ref, mode_ref, prow_ref, pcol_ref, pmode_ref, pid_ref,
-    e_ref, h_ref, c_ref, edge_e_ref, edge_h_ref, edge_c_ref, done_ref, weight_ref, sum_ref, ext_ref, halo_ref, strip_ref, ez_ref, edge_ez_ref,
+    row_size, state_ref, z_ref, own_ref, even_ref, odd_ref, even_z_ref, odd_z_ref, weight_ref, prow_ref,
+    e_ref, h_ref, c_ref, edge_e_ref, edge_h_ref, edge_c_ref, done_ref, sum_ref, ext_ref, halo_ref, ez_ref, edge_ez_ref,
 ):
     gz, row = lax.axis_index("gz"), lax.axis_index("row")
     lane, sub = iota(1), iota(0)
     place = lane & (GROUP - 1)
-    groups = [(lane >> 5) == r for r in range(4)]
+    groups = lane_groups()
     valid = (sub < 4) == (gz == 0)
     spread_layers(gz, z_ref, ext_ref)
     low_of, high_of = low_and_high(even_ref, odd_ref)
@@ -437,19 +462,6 @@
                 else:
                     own = gather_edges([first(f, DEPTH + 4 * b + r, zz) for r in range(4)], groups)
                 joined[f, b + 1, zz] = edge_tile(own, low, high, f, place)
-    for k in range(PORT_TILE):
-        strip_ref[k] = jnp.zeros(strip_ref.shape[1:], jnp.float32)
-        strip_ref[k, :, 0:PLEN] = mode_ref[pmode_ref[0, 0, k]]
-    for k in range(PORT_TILE):
-        turned = GROUP * (prow_ref[0, 0, k] & 3)
-        at = lane - turned
-        for zz in range(OWN):
-            tile = pltpu.roll(strip_ref[k, 8 * zz : 8 * zz + 8, :], pcol_ref[0, 0, k], 1)
-            weight_ref[k, 0, zz] = jnp.where((lane >= DEPTH) & (lane < 128 - DEPTH), tile, 0.0)
-            own = pltpu.roll(tile, turned + 8, 1)
-            edge = jnp.where((at >= 4) & (at < 8), own, 0.0)
-            weight_ref[k, 1, zz] = jnp.where((at >= 16) & (at < 20), turn(own, 8, 1), edge)
-
     def run(has_below, has_above):
         main = Tiles(first, ez_ref, DEPTH)
         edge = Tiles(lambda f, i, zz: joined[f, i, zz], edge_ez_ref, 1)
@@ -484,8 +496,8 @@
 
 
 def outer_kernel(
-    row_size, ports_each, prow_ref, pid_ref, e_in, h_in, c_in, edge_e_in, edge_h_in, edge_c_in, done_ref, weight_ref,
-    sum_in, *rest,
+    row_size, ports_each, prow_ref, pid_ref, e_in, h_in, c_in, edge_e_in, edge_h_in, edge_c_in, done_ref, sum_in, weight_ref,
+    *rest,
 ):
     n_x = 1 if row_size == 2 else 2
     x_refs, corner_refs = rest[:n_x], rest[n_x : 2 * n_x]
@@ -493,7 +505,7 @@
     gz, row = lax.axis_index("gz"), lax.axis_index("row")
     lane, sub = iota(1), iota(0)
     place = lane & (GROUP - 1)
-    groups = [(lane >> 5) == r for r in range(4)]
+    groups = lane_groups()
     valid = (sub < 4) == (gz == 0)
     zeros = jnp.zeros((8, 128), jnp.float32)
 
@@ -647,15 +659,24 @@
         z_halo = swapped(z_send, "gz", gz_size)
         even_z = swapped(even, "gz", gz_size)
         odd_z = swapped(odd, "gz", gz_size)
+        state, weights = pl.pallas_call(
+            prep_kernel,
+            out_shape=[array(FIELDS, ROWS, OWN, 8, 128), array(PORT_TILE, 2, OWN, 8, 128)],
+            in_specs=[HBM, pl.BlockSpec(memory_space=pl.ANY), VMEM] + [SMEM] * 4,
+            out_specs=[VMEM] * 2,
+            scratch_shapes=[scratch(PORT_TILE, LAYERS, 128), pltpu.SemaphoreType.DMA],
+            compiler_params=PARAMS,
+            name="prep",
+        )(state, even, mode_table, port_row, port_col, port_mode, port_ids)
         corner_send = pl.pallas_call(
             functools.partial(corner_kernel, row_size),
             out_shape=[array(PAIRS + 2 * CHUNK, 8, 128)] * n_x,
-            in_specs=[VMEM] * 5,
+            in_specs=[pl.BlockSpec(memory_space=pl.ANY)] + [VMEM] * 5,
             out_specs=[VMEM] * n_x,
             scratch_shapes=[scratch(FIELDS, 8 * ROWS, 128)],
             compiler_params=PARAMS,
             name="corners",
-        )(z_halo, even, odd, even_z, odd_z)
+        )(weights, z_halo, even, odd, even_z, odd_z)
         corner = across_rows(corner_send)
         inner = pl.pallas_call(
             functools.partial(inner_kernel, row_size),
@@ -667,21 +688,19 @@
                 array(3, 2, CHUNK, 8, 128),
                 array(2, CHUNK, 8, 128),
                 array(6, 4, OWN, 8, 128),
-                array(PORT_TILE, 2, OWN, 8, 128),
                 array(STEPS, 8, 128),
             ],
-            in_specs=[VMEM] * 8 + [SMEM] * 4,
-            out_specs=[VMEM] * 9,
+            in_specs=[VMEM] * 8 + [SMEM],
+            out_specs=[VMEM] * 8,
             scratch_shapes=[
                 scratch(FIELDS, 8 * ROWS, 128),
                 scratch(FIELDS, ROWS, 8, 128),
-                scratch(PORT_TILE, LAYERS, 128),
                 scratch(ROWS, OWN, 8, 128),
                 scratch(2, OWN, 8, 128),
             ],
             compiler_params=PARAMS,
             name="inner",
-        )(state, z_halo, own, even, odd, even_z, odd_z, mode_table, port_row, port_col, port_mode, port_ids)
+        )(state, z_halo, own, even, odd, even_z, odd_z, weights, port_row)
         devices = col_size * row_size * gz_size
         ports_each = PORT_TILE * col_size * row_size // devices
         electric_out, magnetic_out, term = pl.pallas_call(
@@ -699,7 +718,7 @@
             ],
             compiler_params=PARAMS,
             name="outer",
-        )(port_row, port_ids, *inner, *x_halo, *corner)
+        )(port_row, port_ids, *inner, weights, *x_halo, *corner)
         terms = lax.all_to_all(term, ("col", "row", "gz"), 0, 0, tiled=True)
         return (
             electric_out,

time: 41.1 us -> 40.6 us (0.988)
  waiting for transfers between devices: 3.55 us -> 2.49 us
  Pallas kernels: 14.1 us -> 15 us
    ppermute x7, waiting for transfers between devices: 3.55 us -> 2.49 us  [swapped(): return lax.ppermute(block, axis, pairs + [(j, i) for i, j in pairs])]
    pallas_call x0 -> x1, Pallas kernels: none -> 1.04 us  [per_device(): pl.pallas_call(prep_kernel, out_shape=[array(FIELDS, ROWS, OWN, 8, 128),...]
    all_to_all x1, blocking collectives: 14 us -> 13.6 us  [per_device(): terms = lax.all_to_all(term, ('col', 'row', 'gz'), 0, 0, tiled=True)]
  transfers between devices with their start and end apart: 7 -> 7, of which waited for: 4 -> 2; matrix products, arithmetic and copies ran while one was open for 0% -> 0% of each run, Pallas kernels for 9% -> 11%
where the time goes in v9:
time: 40.6 us; the launch traced here: 40.4 us
  Pallas kernels  15 us (37%)
  blocking collectives  13.6 us (33%)
  starting transfers between devices  6.21 us (15%)
  waiting for transfers between devices  2.49 us (6%)
  local copies, waits for them, and re-layouts  1.74 us (4%)
  between operations  0.75 us (2%)
  other arithmetic  0.59 us (1%)
    all_to_all x1, blocking collectives, per_device(): terms = lax.all_to_all(term, ('col', 'row', 'gz'), 0, 0, tiled=True)  13.6 us
    ppermute x7, starting transfers between devices, swapped(): return lax.ppermute(block, axis, pairs + [(j, i) for i, j in pairs])  6.21 us
    pallas_call x1, Pallas kernels, per_device(): pl.pallas_call(functools.partial(outer_kernel, row_size, ports_each), out...  5.48 us
    pallas_call x1, Pallas kernels, per_device(): pl.pallas_call(functools.partial(pack_kernel, row_size), out_shape=[array...  5.01 us
    pallas_call x1, Pallas kernels, per_device(): pl.pallas_call(functools.partial(inner_kernel, row_size), out_shape=[arra...  3.43 us
    ppermute x7, waiting for transfers between devices, swapped(): return lax.ppermute(block, axis, pairs + [(j, i) for i, j in pairs])  2.49 us
    unnamed x14, local copies, waits for them, and re-layouts  1.74 us
    pallas_call x1, Pallas kernels, per_device(): pl.pallas_call(prep_kernel, out_shape=[array(FIELDS, ROWS, OWN, 8, 128),...  1.04 us
  transfers between devices with their start and end apart: 7, of which 2 were waited for; matrix products, arithmetic and copies ran while one was open for 0% of the time, Pallas kernels for 11%

profile of v9, /device:TPU:0, one launch (start us, length us, event | category | flops | bytes accessed | tf_op | source)
XLA Modules:
  0.0 40.4 jit_solution(10891576685381432704)
XLA Ops:
  0.6 0.0 copy-start.2
  0.6 5.0 %pack.1 = (f32[7,8,4,8,128]{4,3,2,1,0:T(8,128)}, f32[7,4,8,128]{3,2,1,0:T(8,128)}, f32[7,2,4,8,128]{4,3,2,1,0:T(8,128)}, f32[2,4,8,128]{3,2,1,0:T(8,128)}, f32[2...) custom-call(f32[8]{0:T(128)} %eps_hbm.1, f32[3,32,8,128]{3,2,1,0:T(8,128)} %elec_hbm.1, f32[3,32,8,128]{3,2,1,0:T(8,128)} %magn_hbm.1, ...), custom_call_target="tpu_custom_call" | custom-call | tf_op jit(solution)/shard_map/pack/pallas_call | solution.py:636
  5.7 3.0 %collective-permute-start.5 = (f32[26,4,8,128]{3,2,1,0:T(8,128)}, f32[26,4,8,128]{3,2,1,0:T(8,128)S(1)}, u32[]{:S(2)}, u32[]{:S(2)}) collective-permute-start(f32[26,4,8,128]{3,2,1,0:T(8,128)} %get-tuple-element.37), channel_id=1, source_target_pairs={{0,2},{2,0},{1,3},{3,1},{4,6},{6,4},{5,7},{7,5},{8,10},{10,8},{9,1... | collective-permute-start | bytes 1277960 | tf_op jit(solution)/shard_map/ppermute | solution.py:612
  8.7 0.0 collective-permute-start.1
  8.7 1.6 %collective-permute-start = (f32[2,4,8,128]{3,2,1,0:T(8,128)}, f32[2,4,8,128]{3,2,1,0:T(8,128)S(1)}, u32[]{:S(2)}, u32[]{:S(2)}) collective-permute-start(f32[2,4,8,128]{3,2,1,0:T(8,128)} %get-tuple-element.23), channel_id=1, source_target_pairs={{0,4},{8,12},{4,0},{12,8},{1,5},{9,13},{5,1},{13,9},{2,6},{10,14},... | collective-permute-start | bytes 98312 | tf_op jit(solution)/shard_map/ppermute | solution.py:612
  10.2 0.0 copy-start.6
  10.3 0.8 %collective-permute-start.2 = (f32[2,4,8,128]{3,2,1,0:T(8,128)}, f32[2,4,8,128]{3,2,1,0:T(8,128)S(1)}, u32[]{:S(2)}, u32[]{:S(2)}) collective-permute-start(f32[2,4,8,128]{3,2,1,0:T(8,128)} %get-tuple-element.27), channel_id=1, source_target_pairs={{4,8},{8,4},{5,9},{9,5},{6,10},{10,6},{7,11},{11,7},{20,24},{24,20... | collective-permute-start | bytes 98312 | tf_op jit(solution)/shard_map/ppermute | solution.py:612
  11.1 1.7 %collective-permute-done.even_ref = f32[2,4,8,128]{3,2,1,0:T(8,128)S(1)} collective-permute-done((f32[2,4,8,128]{3,2,1,0:T(8,128)}, f32[2,4,8,128]{3,2,1,0:T(8,128)S(1)}, u32[]{:S(2)}, u32[]{:S(2)}) %collective-permute-start) | collective-permute-done | bytes 32800 | tf_op jit(solution)/shard_map/ppermute | solution.py:612
  12.8 0.0 collective-permute-start.3
  12.8 0.0 collective-permute-done.2.odd_ref
  12.8 0.5 %collective-permute-start.4 = (f32[2,4,8,128]{3,2,1,0:T(8,128)S(1)}, f32[2,4,8,128]{3,2,1,0:T(8,128)S(1)}, u32[]{:S(2)}, u32[]{:S(2)}) collective-permute-start(f32[2,4,8,128]{3,2,1,0:T(8,128)S(1)} %collective-permute-done.2.odd_ref), channel_id=1, source_target_pairs={{0,1},{1,0},{2,3},{3,2},{4,5},{5,4},{6,7},{7,6},{8,9},{9,8},{10,11... | collective-permute-start | bytes 98312 | tf_op jit(solution)/shard_map/ppermute | solution.py:612
  13.3 0.0 copy-done.2
  13.3 0.0 copy-done.6
  13.3 0.0 copy-done.3
  13.3 0.0 copy-done.4
  13.3 0.0 copy-done.5
  13.3 0.0 copy-start
  13.3 1.2 %copy-done = f32[7,8,4,8,128]{4,3,2,1,0:T(8,128)S(1)} copy-done((f32[7,8,4,8,128]{4,3,2,1,0:T(8,128)S(1)}, f32[7,8,4,8,128]{4,3,2,1,0:T(8,128)}, u32[]{:S(2)}) %copy-start) | copy-done | bytes 917528
  14.5 1.0 %prep.1 = (f32[7,8,4,8,128]{4,3,2,1,0:T(8,128)S(1)}, f32[4,2,4,8,128]{4,3,2,1,0:T(8,128)S(1)}) custom-call(f32[7,8,4,8,128]{4,3,2,1,0:T(8,128)S(1)} %copy-done, f32[2,4,8,128]{3,2,1,0:T(8,128)S(1)} %collective-permute-done.even_ref, f32[8,32,64]{2,1,0:T(8,128)S(1)} %copy-done.2, s32[1,1,4]{2,1,0:T(1,128)S(1)} %copy-done.3, s32[1,1,4]{2,1,0:T(1,128)S(1)} %copy-done.5, ...), custom_call_target="tpu_custom_call" | custom-call | tf_op jit(solution)/shard_map/prep/pallas_call | solution.py:662
  15.6 0.0 collective-permute-done.3.even_z_ref
  15.6 0.0 collective-permute-done.4.odd_z_ref
  15.6 0.0 collective-permute-done.1.z_ref
  15.6 0.0 copy-start.1
  15.6 0.1 corners.1
  15.7 0.3 collective-permute-start.6
  16.0 0.5 %copy-done.1 = f32[7,2,4,8,128]{4,3,2,1,0:T(8,128)S(1)} copy-done((f32[7,2,4,8,128]{4,3,2,1,0:T(8,128)S(1)}, f32[7,2,4,8,128]{4,3,2,1,0:T(8,128)}, u32[]{:S(2)}) %copy-start.1) | copy-done | bytes 229400
  16.5 3.4 %inner.1 = (f32[3,8,5,8,128]{4,3,2,1,0:T(8,128)S(1)}, f32[3,8,5,8,128]{4,3,2,1,0:T(8,128)S(1)}, f32[8,5,8,128]{3,2,1,0:T(8,128)S(1)}, f32[3,2,5,8,128]{4,3,2,1,0...) custom-call(f32[7,8,4,8,128]{4,3,2,1,0:T(8,128)S(1)} %get-tuple-elem, ...), custom_call_target="tpu_custom_call" | custom-call | tf_op jit(solution)/shard_map/inner/pallas_call | solution.py:681
  20.0 0.7 %collective-permute-done.6.rest_1_ = f32[23,8,128]{2,1,0:T(8,128)S(1)} collective-permute-done((f32[23,8,128]{2,1,0:T(8,128)S(1)}, f32[23,8,128]{2,1,0:T(8,128)S(1)}, u32[]{:S(2)}, u32[]{:S(2)}) %collective-permute-start.6) | collective-permute-done | bytes 94240 | tf_op jit(solution)/shard_map/ppermute | solution.py:612
  20.7 0.0 collective-permute-done.5.rest_0_
  20.7 5.5 %outer.1 = (f32[3,32,8,128]{3,2,1,0:T(8,128)}, f32[3,32,8,128]{3,2,1,0:T(8,128)}, f32[16,2,16]{2,1,0:T(2,128)S(1)}) custom-call(s32[1,1,4]{2,1,0:T(1,128)S(1)} %copy-done.3, s32[1,1,4]{2,1,0:T(1,128)S(1)} %copy-done.4, f32[3,8,5,8,128]{4,3,2,1,0:T(8,128)S(1)} %get-tuple-element.29.e_in, f32[3,8,5,8,128]{4,3,2,1,0:T(8,128)S(1)} %get-tuple-element.30.h_in, ...), custom_call_target="tpu_custom_call" | custom-call | tf_op jit(solution)/shard_map/outer/pallas_call | solution.py:706
  26.2 13.6 %all_to_all.5 = f32[16,2,16]{2,1,0:T(2,128)S(1)} all-to-all(f32[16,2,16]{2,1,0:T(2,128)S(1)} %get-tuple-element.40), channel_id=1, replica_groups=mesh['grp'=2,'col'=4,'row'=2,'gz'=2] {'col','row','gz'}, dimensions={0} | all-to-all | bytes 4096 | tf_op jit(solution)/shard_map/all_to_all | solution.py:722
  39.8 0.6 %reduce_sum.9 = f32[2,16]{1,0:T(2,128)} reduce(f32[16,2,16]{2,1,0:T(2,128)S(1)} %all_to_all.5, f32[]{:T(128)} %constant.0.clone.1), dimensions={0}, to_apply=%region_0.0 | reduce | flops 480 | bytes 2180 | tf_op jit(solution)/shard_map/reduce_sum | solution.py:726
  (3 shorter events, 0.0 us)
Async XLA Ops:
  0.6 12.7 %copy-start.2 = (f32[8,32,64]{2,1,0:T(8,128)S(1)}, f32[8,32,64]{2,1,0:T(8,128)}, u32[]{:S(2)}) copy-start(f32[8,32,64]{2,1,0:T(8,128)} %mode_ref.1) | copy-start | bytes 196612
  5.7 15.1 %collective-permute-start.5 = (f32[26,4,8,128]{3,2,1,0:T(8,128)}, f32[26,4,8,128]{3,2,1,0:T(8,128)S(1)}, u32[]{:S(2)}, u32[]{:S(2)}) collective-permute-start(f32[26,4,8,128]{3,2,1,0:T(8,128)} %get-tuple-element.37), channel_id=1, source_target_pairs={{0,2},{2,0},{1,3},{3,1},{4,6},{6,4},{5,7},{7,5},{8,10},{10,8},{9,1... | collective-permute-start | bytes 1277960 | tf_op jit(solution)/shard_map/ppermute | solution.py:612
  8.7 6.9 %collective-permute-start.1 = (f32[7,4,8,128]{3,2,1,0:T(8,128)}, f32[7,4,8,128]{3,2,1,0:T(8,128)S(1)}, u32[]{:S(2)}, u32[]{:S(2)}) collective-permute-start(f32[7,4,8,128]{3,2,1,0:T(8,128)} %get-tuple-element.25), channel_id=1, source_target_pairs={{0,1},{1,0},{2,3},{3,2},{4,5},{5,4},{6,7},{7,6},{8,9},{9,8},{10,11... | collective-permute-start | bytes 344072 | tf_op jit(solution)/shard_map/ppermute | solution.py:612
  8.7 4.1 %collective-permute-start = (f32[2,4,8,128]{3,2,1,0:T(8,128)}, f32[2,4,8,128]{3,2,1,0:T(8,128)S(1)}, u32[]{:S(2)}, u32[]{:S(2)}) collective-permute-start(f32[2,4,8,128]{3,2,1,0:T(8,128)} %get-tuple-element.23), channel_id=1, source_target_pairs={{0,4},{8,12},{4,0},{12,8},{1,5},{9,13},{5,1},{13,9},{2,6},{10,14},... | collective-permute-start | bytes 98312 | tf_op jit(solution)/shard_map/ppermute | solution.py:612
  10.2 3.1 %copy-start.6 = (s32[1,1,4]{2,1,0:T(1,128)S(1)}, s32[1,1,4]{2,1,0:T(1,128)}, u32[]{:S(2)}) copy-start(s32[1,1,4]{2,1,0:T(1,128)} %pmode_ref.1) | copy-start | bytes 52
  10.2 3.1 %copy-start.3 = (s32[1,1,4]{2,1,0:T(1,128)S(1)}, s32[1,1,4]{2,1,0:T(1,128)}, u32[]{:S(2)}) copy-start(s32[1,1,4]{2,1,0:T(1,128)} %prow_ref.5) | copy-start | bytes 52
  10.2 3.1 %copy-start.4 = (s32[1,1,4]{2,1,0:T(1,128)S(1)}, s32[1,1,4]{2,1,0:T(1,128)}, u32[]{:S(2)}) copy-start(s32[1,1,4]{2,1,0:T(1,128)} %pid_ref.3) | copy-start | bytes 52
  10.2 3.1 %copy-start.5 = (s32[1,1,4]{2,1,0:T(1,128)S(1)}, s32[1,1,4]{2,1,0:T(1,128)}, u32[]{:S(2)}) copy-start(s32[1,1,4]{2,1,0:T(1,128)} %pcol_ref.1) | copy-start | bytes 52
  10.3 2.5 %collective-permute-start.2 = (f32[2,4,8,128]{3,2,1,0:T(8,128)}, f32[2,4,8,128]{3,2,1,0:T(8,128)S(1)}, u32[]{:S(2)}, u32[]{:S(2)}) collective-permute-start(f32[2,4,8,128]{3,2,1,0:T(8,128)} %get-tuple-element.27), channel_id=1, source_target_pairs={{4,8},{8,4},{5,9},{9,5},{6,10},{10,6},{7,11},{11,7},{20,24},{24,20... | collective-permute-start | bytes 98312 | tf_op jit(solution)/shard_map/ppermute | solution.py:612
  12.8 2.8 %collective-permute-start.3 = (f32[2,4,8,128]{3,2,1,0:T(8,128)S(1)}, f32[2,4,8,128]{3,2,1,0:T(8,128)S(1)}, u32[]{:S(2)}, u32[]{:S(2)}) collective-permute-start(f32[2,4,8,128]{3,2,1,0:T(8,128)S(1)} %collective-permute-done.even_ref), channel_id=1, source_target_pairs={{0,1},{1,0},{2,3},{3,2},{4,5},{5,4},{6,7},{7,6},{8,9},{9,8},{10,11... | collective-permute-start | bytes 98312 | tf_op jit(solution)/shard_map/ppermute | solution.py:612
  12.8 2.8 %collective-permute-start.4 = (f32[2,4,8,128]{3,2,1,0:T(8,128)S(1)}, f32[2,4,8,128]{3,2,1,0:T(8,128)S(1)}, u32[]{:S(2)}, u32[]{:S(2)}) collective-permute-start(f32[2,4,8,128]{3,2,1,0:T(8,128)S(1)} %collective-permute-done.2.odd_ref), channel_id=1, source_target_pairs={{0,1},{1,0},{2,3},{3,2},{4,5},{5,4},{6,7},{7,6},{8,9},{9,8},{10,11... | collective-permute-start | bytes 98312 | tf_op jit(solution)/shard_map/ppermute | solution.py:612
  13.3 1.2 %copy-start = (f32[7,8,4,8,128]{4,3,2,1,0:T(8,128)S(1)}, f32[7,8,4,8,128]{4,3,2,1,0:T(8,128)}, u32[]{:S(2)}) copy-start(f32[7,8,4,8,128]{4,3,2,1,0:T(8,128)} %get-tuple-element.22.state_hbm) | copy-start | bytes 2752516
  15.6 0.9 %copy-start.1 = (f32[7,2,4,8,128]{4,3,2,1,0:T(8,128)S(1)}, f32[7,2,4,8,128]{4,3,2,1,0:T(8,128)}, u32[]{:S(2)}) copy-start(f32[7,2,4,8,128]{4,3,2,1,0:T(8,128)} %get-tuple-element.26.own_ref) | copy-start | bytes 688132
  15.7 5.0 %collective-permute-start.6 = (f32[23,8,128]{2,1,0:T(8,128)S(1)}, f32[23,8,128]{2,1,0:T(8,128)S(1)}, u32[]{:S(2)}, u32[]{:S(2)}) collective-permute-start(f32[23,8,128]{2,1,0:T(8,128)S(1)} %corners.1), channel_id=1, source_target_pairs={{0,2},{2,0},{1,3},{3,1},{4,6},{6,4},{5,7},{7,5},{8,10},{10,8},{9,1... | collective-permute-start | bytes 282632 | tf_op jit(solution)/shard_map/ppermute | solution.py:612

commit v10 on v9

--- a/solution.py
+++ b/solution.py
@@ -101,13 +101,23 @@
     return [jnp.where(group == r, 1.0, 0.0) for r in range(4)]
 
 
-def gather_edges(tiles, groups):
-    own = None
-    for r, tile in enumerate(tiles):
-        if tile is not None:
-            moved = turn(tile, GROUP * r + 8, 1) * groups[r]
-            own = moved if own is None else own + moved
-    return own
+def gather_edges(rows_of, groups):
+    moved = [[tile if tile is None else turn(tile, GROUP * r + 8, 1) for r, tile in enumerate(rows)] for rows in rows_of]
+    out = []
+    for rows in moved:
+        parts = [tile * groups[r] for r, tile in enumerate(rows) if tile is not None]
+        out.append(functools.reduce(lambda a, b: a + b, parts) if parts else jnp.zeros((8, 128), jnp.float32))
+    return out
+
+
+def staged(items, first, second):
+    waiting = None
+    for item in items:
+        made = first(item)
+        if waiting is not None:
+            second(*waiting)
+        waiting = (item, made)
+    second(*waiting)
 
 
 def pack_edges(state_ref, own_ref, even_ref, odd_ref):
@@ -115,19 +125,23 @@
     groups = lane_groups()
     slots = [jnp.where(((lane & (GROUP - 1)) >> 2) == f, 1.0, 0.0) for f in range(FIELDS)]
     even = (lax.axis_index("col") & 1) == 0
-    for b in range(2):
-        for zz in range(OWN):
-            up = down = jnp.zeros((8, 128), jnp.float32)
-            owns = []
-            for f in range(FIELDS):
-                own = gather_edges([state_ref[f, 4 * b + r, zz] for r in range(4)], groups)
-                up = up + turn(own, DEPTH * f - 4, 1) * slots[f]
-                down = down + turn(own, DEPTH * f - 8, 1) * slots[f]
-                owns.append(own)
-            for f in range(FIELDS):
-                own_ref[f, b, zz] = owns[f]
-            even_ref[b, zz] = jnp.where(even, up, down)
-            odd_ref[b, zz] = jnp.where(even, down, up)
+
+    def first(at):
+        b, zz = at
+        return gather_edges([[state_ref[f, 4 * b + r, zz] for r in range(4)] for f in range(FIELDS)], groups)
+
+    def second(at, owns):
+        b, zz = at
+        ups = [turn(own, DEPTH * f - 4, 1) for f, own in enumerate(owns)]
+        downs = [turn(own, DEPTH * f - 8, 1) for f, own in enumerate(owns)]
+        up = functools.reduce(lambda a, b: a + b, [v * m for v, m in zip(ups, slots)])
+        down = functools.reduce(lambda a, b: a + b, [v * m for v, m in zip(downs, slots)])
+        for f in range(FIELDS):
+            own_ref[f, b, zz] = owns[f]
+        even_ref[b, zz] = jnp.where(even, up, down)
+        odd_ref[b, zz] = jnp.where(even, down, up)
+
+    staged([(b, zz) for b in range(2) for zz in range(OWN)], first, second)
 
 
 def low_and_high(even_ref, odd_ref):
@@ -142,8 +156,11 @@
     return low, high
 
 
-def halo_layers(valid, gz, side, b):
-    return jnp.where(valid, jnp.where(gz == 0, side(b, 0), side(b, OWN - 1)), 0.0)
+def layer_edge_kernel(even_ref, odd_ref, inner_ref, out_ref):
+    gz = lax.axis_index("gz")
+    for i, ref in enumerate((even_ref, odd_ref)):
+        for b in range(2):
+            out_ref[i, b] = jnp.where(gz == 0, ref[b, OWN - 1], ref[b, 0])
 
 
 def spread_layers(gz, z_ref, ext_ref):
@@ -154,13 +171,13 @@
         ext_ref[f, DEPTH * ROWS :] = jnp.where(gz == 0, nothing, halo)
 
 
-def corner_kernel(row_size, prep_ref, z_ref, even_ref, odd_ref, even_z_ref, odd_z_ref, *rest):
+def corner_kernel(row_size, z_ref, even_ref, odd_ref, layer_ref, *rest):
     x_refs, ext_ref = rest[:-1], rest[-1]
     gz = lax.axis_index("gz")
     valid = (iota(0) < 4) == (gz == 0)
     spread_layers(gz, z_ref, ext_ref)
     low, high = low_and_high(even_ref, odd_ref)
-    low_z, high_z = low_and_high(even_z_ref, odd_z_ref)
+    low_z, high_z = low_and_high(layer_ref.at[0], layer_ref.at[1])
 
     def send(up, slot):
         planes = UP_PLANES if up else DOWN_PLANES
@@ -178,16 +195,25 @@
         for zz in range(OWN):
             x_refs[slot][PAIRS + zz] = low(b, zz)
             x_refs[slot][PAIRS + CHUNK + zz] = high(b, zz)
-        x_refs[slot][PAIRS + OWN] = halo_layers(valid, gz, low_z, b)
-        x_refs[slot][PAIRS + CHUNK + OWN] = halo_layers(valid, gz, high_z, b)
+        x_refs[slot][PAIRS + OWN] = jnp.where(valid, low_z(b), 0.0)
+        x_refs[slot][PAIRS + CHUNK + OWN] = jnp.where(valid, high_z(b), 0.0)
 
     directions(row_size, send)
 
 
-def edge_tile(own, low, high, f, place):
-    out = jnp.where(place < 16, turn(low, 12 - DEPTH * f, 1), turn(own, 8, 1))
-    out = jnp.where(place < 12, turn(high, 8 - DEPTH * f, 1), out)
-    return jnp.where(place < 8, own, out)
+def turn_sides(low, high):
+    lows = [turn(low, 12 - DEPTH * f, 1) for f in range(FIELDS)]
+    return lows, [turn(high, 8 - DEPTH * f, 1) for f in range(FIELDS)]
+
+
+def edge_tiles(owns, sides, place):
+    turned = [turn(own, 8, 1) for own in owns]
+    out = []
+    for own, own_turned, low, high in zip(owns, turned, *sides):
+        tile = jnp.where(place < 16, low, own_turned)
+        tile = jnp.where(place < 12, high, tile)
+        out.append(jnp.where(place < 8, own, tile))
+    return out
 
 
 class Tiles:
@@ -368,9 +394,12 @@
             h_rows = list(range(DEPTH + h_span[0], DEPTH + h_span[1] + 1))
             e_rows = list(range(DEPTH + e_span[0], DEPTH + e_span[1] + 1))
             skip = h_rows[:1] if self.skip_hx and h_span[0] < e_span[0] else []
-            parts.append(
-                leapfrog(self.main, self.main_exists, h_rows, e_rows, Rows(), self.main_h, self.main_c, layers, last, skip)
-            )
+            if self.main is not None:
+                parts.append(
+                    leapfrog(self.main, self.main_exists, h_rows, e_rows, Rows(), self.main_h, self.main_c, layers, last, skip)
+                )
+            if self.edge is None:
+                continue
             h_of, c_of = functools.partial(self.edge_h, span=h_span), functools.partial(self.edge_c, span=e_span)
             parts.append(
                 leapfrog(
@@ -383,36 +412,49 @@
             next(part, None)
 
 
+def rows_cases(row_size, row, run):
+    if row_size == 2:
+        pl.when(row == 0)(functools.partial(run, False, True))
+        pl.when(row == 1)(functools.partial(run, True, False))
+    else:
+        run(True, True)
+
+
 def port_sums(n, reached, prow_ref, weight_ref, ez_ref, edge_ref, sum_ref, add_ref):
     for k in range(PORT_TILE):
         at = prow_ref[0, 0, k]
         total = jnp.zeros((8, 128), jnp.float32)
         for zz in range(OWN):
-            total = total + ez_ref[at, zz] * weight_ref[k, 0, zz]
-            total = total + edge_ref[at >> 2, zz] * weight_ref[k, 1, zz]
+            if ez_ref is not None:
+                total = total + ez_ref[at, zz] * weight_ref[k, 0, zz]
+            if edge_ref is not None:
+                total = total + edge_ref[at >> 2, zz] * weight_ref[k, 1, zz]
         total = jnp.sum(jnp.where(reached(n, at), total, 0.0), axis=0, keepdims=True)
         if add_ref is not None:
             total = total + add_ref[n - 1, k : k + 1, :]
         sum_ref[n - 1, k : k + 1, :] = total
 
 
-def finished(f, b, main, edge):
+def finish(fields, b, main, edge, write):
     lane = iota(1)
     place = lane & (GROUP - 1)
     sides = (lane < DEPTH) | (lane >= 128 - DEPTH)
-    out = {}
-    for zz in range(OWN):
-        tile = edge.get(f, b + 1, zz)
-        near = jnp.where(place < 8, tile, turn(tile, -8, 1))
-        for r in range(4):
-            own = main.get(f, DEPTH + 4 * b + r, zz)
-            out[r, zz] = jnp.where(sides, turn(near, -(GROUP * r + 8), 1), own)
-    return out
-
-
-def prep_kernel(state_hbm, even_ref, mode_ref, prow_ref, pcol_ref, pmode_ref, pid_ref, state_ref, weight_ref, strip_ref, sem):
-    copy = pltpu.make_async_copy(state_hbm, state_ref, sem)
-    copy.start()
+
+    def first(f):
+        tiles = [edge.get(f, b + 1, zz) for zz in range(OWN)]
+        turned = [turn(tile, -8, 1) for tile in tiles]
+        return [jnp.where(place < 8, tile, other) for tile, other in zip(tiles, turned)]
+
+    def second(f, near):
+        turned = {(r, zz): turn(near[zz], -(GROUP * r + 8), 1) for r in range(4) for zz in range(OWN)}
+        made = {(r, zz): jnp.where(sides, tile, main.get(f, DEPTH + 4 * b + r, zz)) for (r, zz), tile in turned.items()}
+        for (r, zz), tile in made.items():
+            write(f, r, zz, tile)
+
+    staged(fields, first, second)
+
+
+def port_weights(mode_ref, prow_ref, pcol_ref, pmode_ref, weight_ref, strip_ref):
     lane = iota(1)
     for k in range(PORT_TILE):
         strip_ref[k] = jnp.zeros(strip_ref.shape[1:], jnp.float32)
@@ -427,45 +469,24 @@
             edge = jnp.where((at >= 4) & (at < 8), own, 0.0)
             weight_ref[k, 1, zz] = jnp.where((at >= 16) & (at < 20), turn(own, 8, 1), edge)
 
-    copy.wait()
-
 
 def inner_kernel(
-    row_size, state_ref, z_ref, own_ref, even_ref, odd_ref, even_z_ref, odd_z_ref, weight_ref, prow_ref,
-    e_ref, h_ref, c_ref, edge_e_ref, edge_h_ref, edge_c_ref, done_ref, sum_ref, ext_ref, halo_ref, ez_ref, edge_ez_ref,
+    row_size, state_ref, z_ref, mode_ref, prow_ref, pcol_ref, pmode_ref, pid_ref,
+    e_ref, h_ref, c_ref, sum_ref, weight_ref, ext_ref, halo_ref, ez_ref, strip_ref,
 ):
     gz, row = lax.axis_index("gz"), lax.axis_index("row")
-    lane, sub = iota(1), iota(0)
-    place = lane & (GROUP - 1)
-    groups = lane_groups()
-    valid = (sub < 4) == (gz == 0)
     spread_layers(gz, z_ref, ext_ref)
-    low_of, high_of = low_and_high(even_ref, odd_ref)
-    low_z, high_z = low_and_high(even_z_ref, odd_z_ref)
     for f in range(FIELDS):
         for x in range(ROWS):
             halo_ref[f, x] = ext_ref[f, pl.ds(x, 8, stride=ROWS), :]
+    port_weights(mode_ref, prow_ref, pcol_ref, pmode_ref, weight_ref, strip_ref)
 
     def first(f, i, zz):
         return halo_ref[f, i - DEPTH] if zz == OWN else state_ref[f, i - DEPTH, zz]
 
-    joined = {}
-    for b in range(2):
-        for zz in range(CHUNK):
-            if zz < OWN:
-                low, high = low_of(b, zz), high_of(b, zz)
-            else:
-                low, high = (halo_layers(valid, gz, side, b) for side in (low_z, high_z))
-            for f in range(FIELDS):
-                if zz < OWN:
-                    own = own_ref[f, b, zz]
-                else:
-                    own = gather_edges([first(f, DEPTH + 4 * b + r, zz) for r in range(4)], groups)
-                joined[f, b + 1, zz] = edge_tile(own, low, high, f, place)
     def run(has_below, has_above):
         main = Tiles(first, ez_ref, DEPTH)
-        edge = Tiles(lambda f, i, zz: joined[f, i, zz], edge_ez_ref, 1)
-        stepper = Stepper(row_size, main, edge, range(4, 12), (1, 2), False)
+        stepper = Stepper(row_size, main, None, range(4, 12), (), False)
 
         def reached(n, at):
             low, high = spans_inner(n, has_below, has_above)[1]
@@ -473,30 +494,72 @@
 
         for n in range(1, STEPS + 1):
             stepper.step(n, [spans_inner(n, has_below, has_above)])
-            port_sums(n, reached, prow_ref, weight_ref, ez_ref, edge_ez_ref, sum_ref, None)
-        for tiles, base, count, refs in (
-            (main, DEPTH, ROWS, (e_ref, h_ref, c_ref)),
-            (edge, 1, 2, (edge_e_ref, edge_h_ref, edge_c_ref)),
-        ):
-            for i in range(count):
-                for zz in range(CHUNK):
-                    for f in range(6):
-                        refs[f // 3][f % 3, i, zz] = tiles.get(f, base + i, zz)
-                    refs[2][i, zz] = tiles.get(6, base + i, zz)
+            port_sums(n, reached, prow_ref, weight_ref, ez_ref, None, sum_ref, None)
+        for i in range(ROWS):
+            for zz in range(CHUNK):
+                for f in range(6):
+                    (e_ref, h_ref)[f // 3][f % 3, i, zz] = main.get(f, DEPTH + i, zz)
+                c_ref[i, zz] = main.get(6, DEPTH + i, zz)
+
+    rows_cases(row_size, row, run)
+
+
+def rim_kernel(
+    row_size, z_ref, own_ref, even_ref, odd_ref, layer_ref, e_in, h_in, sum_in, weight_ref, prow_ref,
+    edge_e_ref, edge_h_ref, edge_c_ref, done_ref, sum_ref, ext_ref, ez_ref,
+):
+    gz, row = lax.axis_index("gz"), lax.axis_index("row")
+    place = iota(1) & (GROUP - 1)
+    groups = lane_groups()
+    valid = (iota(0) < 4) == (gz == 0)
+    spread_layers(gz, z_ref, ext_ref)
+    low_of, high_of = low_and_high(even_ref, odd_ref)
+    low_z, high_z = low_and_high(layer_ref.at[0], layer_ref.at[1])
+    joined = {}
+
+    def first(at):
+        b, zz = at
+        if zz < OWN:
+            return [own_ref[f, b, zz] for f in range(FIELDS)], turn_sides(low_of(b, zz), high_of(b, zz))
+        rows = [[ext_ref[f, pl.ds(4 * b + r, 8, stride=ROWS), :] for r in range(4)] for f in range(FIELDS)]
+        sides = turn_sides(*(jnp.where(valid, side(b), 0.0) for side in (low_z, high_z)))
+        return gather_edges(rows, groups), sides
+
+    def second(at, made):
+        for f, tile in enumerate(edge_tiles(*made, place)):
+            joined[f, at[0] + 1, at[1]] = tile
+
+    staged([(b, zz) for b in range(2) for zz in range(CHUNK)], first, second)
+
+    def run(has_below, has_above):
+        main = Tiles(lambda f, i, zz: (e_in, h_in)[f // 3][f % 3, i - DEPTH, zz], None, DEPTH)
+        edge = Tiles(lambda f, i, zz: joined[f, i, zz], ez_ref, 1)
+        stepper = Stepper(row_size, None, edge, (), (1, 2), False)
+
+        def reached(n, at):
+            low, high = spans_inner(n, has_below, has_above)[1]
+            return (at >= low) & (at <= high)
+
+        for n in range(1, STEPS + 1):
+            stepper.step(n, [spans_inner(n, has_below, has_above)])
+            port_sums(n, reached, prow_ref, weight_ref, None, ez_ref, sum_ref, sum_in)
+        for i in range(2):
+            for zz in range(CHUNK):
+                for f in range(6):
+                    (edge_e_ref, edge_h_ref)[f // 3][f % 3, i, zz] = edge.get(f, 1 + i, zz)
+                edge_c_ref[i, zz] = edge.get(6, 1 + i, zz)
         if has_below != has_above:
-            for f in range(6):
-                for (r, zz), tile in finished(f, 0 if has_above else 1, main, edge).items():
-                    done_ref[f, r, zz] = tile
-
-    if row_size == 2:
-        pl.when(row == 0)(functools.partial(run, False, True))
-        pl.when(row == 1)(functools.partial(run, True, False))
-    else:
-        run(True, True)
+
+            def write(f, r, zz, tile):
+                done_ref[f, r, zz] = tile
+
+            finish(range(6), 0 if has_above else 1, main, edge, write)
+
+    rows_cases(row_size, row, run)
 
 
 def outer_kernel(
-    row_size, ports_each, prow_ref, pid_ref, e_in, h_in, c_in, edge_e_in, edge_h_in, edge_c_in, done_ref, sum_in, weight_ref,
+    row_size, ports_each, prow_ref, pid_ref, e_in, h_in, c_in, weight_ref, edge_e_in, edge_h_in, edge_c_in, done_ref, sum_in,
     *rest,
 ):
     n_x = 1 if row_size == 2 else 2
@@ -534,14 +597,17 @@
                 for zz in range(CHUNK):
                     main.put(f, DEPTH + x + offset, zz, tiles[zz])
                     got[f, x + offset - 4 * b, zz] = tiles[zz]
-            for zz in range(CHUNK):
-                low = corner_refs[slot][PAIRS + zz]
-                high = corner_refs[slot][PAIRS + CHUNK + zz]
-                for f in range(FIELDS):
-                    tiles = [got.get((f, r, zz)) for r in range(4)]
-                    own = gather_edges(tiles, groups)
-                    tile = edge_tile(zeros if own is None else own, low, high, f, place)
+
+            def first(zz):
+                rows = [[got.get((f, r, zz)) for r in range(4)] for f in range(FIELDS)]
+                sides = turn_sides(corner_refs[slot][PAIRS + zz], corner_refs[slot][PAIRS + CHUNK + zz])
+                return gather_edges(rows, groups), sides
+
+            def second(zz, made):
+                for f, tile in enumerate(edge_tiles(*made, place)):
                     edge.put(f, 1 + b, zz, tile)
+
+            staged(range(CHUNK), first, second)
 
         if has_below:
             halo_rows(UP_PLANES, 0, -ROWS, -1)
@@ -563,20 +629,20 @@
             spans = ([spans_below(n)] if has_below else []) + ([spans_above(n)] if has_above else [])
             stepper.step(n, spans)
             port_sums(n, reached, prow_ref, weight_ref, ez_ref, edge_ez_ref, sum_ref, sum_in)
-        for f in range(6):
-            for b in range(2):
-                if has_below and has_above or b == (1 if has_above else 0):
-                    tiles = finished(f, b, main, edge)
-                else:
-                    tiles = {(r, zz): done_ref[f, r, zz] for r in range(4) for zz in range(OWN)}
-                for (r, zz), tile in tiles.items():
-                    turned_ref[f, 4 * b + r, 8 * zz : 8 * zz + 8, :] = tile
-
-    if row_size == 2:
-        pl.when(row == 0)(functools.partial(run, False, True))
-        pl.when(row == 1)(functools.partial(run, True, False))
-    else:
-        run(True, True)
+        def write(f, r, zz, tile, b):
+            turned_ref[f, 4 * b + r, 8 * zz : 8 * zz + 8, :] = tile
+
+        for b in range(2):
+            put = functools.partial(write, b=b)
+            if has_below and has_above or b == (1 if has_above else 0):
+                finish(range(6), b, main, edge, put)
+            else:
+                for f in range(6):
+                    for r in range(4):
+                        for zz in range(OWN):
+                            put(f, r, zz, done_ref[f, r, zz])
+
+    rows_cases(row_size, row, run)
 
     copies = []
     flat = turned_ref.reshape(6 * ROWS * LAYERS, 128)
@@ -657,50 +723,61 @@
         even = swapped(even_send, "col", col_size)
         odd = swapped(odd_send, "col", col_size, 1)
         z_halo = swapped(z_send, "gz", gz_size)
-        even_z = swapped(even, "gz", gz_size)
-        odd_z = swapped(odd, "gz", gz_size)
-        state, weights = pl.pallas_call(
-            prep_kernel,
-            out_shape=[array(FIELDS, ROWS, OWN, 8, 128), array(PORT_TILE, 2, OWN, 8, 128)],
-            in_specs=[HBM, pl.BlockSpec(memory_space=pl.ANY), VMEM] + [SMEM] * 4,
-            out_specs=[VMEM] * 2,
-            scratch_shapes=[scratch(PORT_TILE, LAYERS, 128), pltpu.SemaphoreType.DMA],
-            compiler_params=PARAMS,
-            name="prep",
-        )(state, even, mode_table, port_row, port_col, port_mode, port_ids)
-        corner_send = pl.pallas_call(
-            functools.partial(corner_kernel, row_size),
-            out_shape=[array(PAIRS + 2 * CHUNK, 8, 128)] * n_x,
-            in_specs=[pl.BlockSpec(memory_space=pl.ANY)] + [VMEM] * 5,
-            out_specs=[VMEM] * n_x,
-            scratch_shapes=[scratch(FIELDS, 8 * ROWS, 128)],
-            compiler_params=PARAMS,
-            name="corners",
-        )(weights, z_halo, even, odd, even_z, odd_z)
-        corner = across_rows(corner_send)
-        inner = pl.pallas_call(
+        e_now, h_now, c_now, sums, weights = pl.pallas_call(
             functools.partial(inner_kernel, row_size),
             out_shape=[
                 array(3, ROWS, CHUNK, 8, 128),
                 array(3, ROWS, CHUNK, 8, 128),
                 array(ROWS, CHUNK, 8, 128),
+                array(STEPS, 8, 128),
+                array(PORT_TILE, 2, OWN, 8, 128),
+            ],
+            in_specs=[VMEM] * 3 + [SMEM] * 4,
+            out_specs=[VMEM] * 5,
+            scratch_shapes=[
+                scratch(FIELDS, 8 * ROWS, 128),
+                scratch(FIELDS, ROWS, 8, 128),
+                scratch(ROWS, OWN, 8, 128),
+                scratch(PORT_TILE, LAYERS, 128),
+            ],
+            compiler_params=PARAMS,
+            cost_estimate=pl.CostEstimate(flops=5_000_000, bytes_accessed=10_000_000, transcendentals=0),
+            name="inner",
+        )(state, z_halo, mode_table, port_row, port_col, port_mode, port_ids)
+        layer_send = pl.pallas_call(
+            layer_edge_kernel,
+            out_shape=array(2, 2, 8, 128),
+            in_specs=[VMEM] * 2 + [pl.BlockSpec(memory_space=pl.ANY)],
+            out_specs=VMEM,
+            compiler_params=PARAMS,
+            name="layer_edges",
+        )(even, odd, sums)
+        layer_halo = swapped(layer_send, "gz", gz_size)
+        corner_send = pl.pallas_call(
+            functools.partial(corner_kernel, row_size),
+            out_shape=[array(PAIRS + 2 * CHUNK, 8, 128)] * n_x,
+            in_specs=[VMEM] * 4,
+            out_specs=[VMEM] * n_x,
+            scratch_shapes=[scratch(FIELDS, 8 * ROWS, 128)],
+            compiler_params=PARAMS,
+            name="corners",
+        )(z_halo, even, odd, layer_halo)
+        corner = across_rows(corner_send)
+        edges = pl.pallas_call(
+            functools.partial(rim_kernel, row_size),
+            out_shape=[
                 array(3, 2, CHUNK, 8, 128),
                 array(3, 2, CHUNK, 8, 128),
                 array(2, CHUNK, 8, 128),
                 array(6, 4, OWN, 8, 128),
                 array(STEPS, 8, 128),
             ],
-            in_specs=[VMEM] * 8 + [SMEM],
-            out_specs=[VMEM] * 8,
-            scratch_shapes=[
-                scratch(FIELDS, 8 * ROWS, 128),
-                scratch(FIELDS, ROWS, 8, 128),
-                scratch(ROWS, OWN, 8, 128),
-                scratch(2, OWN, 8, 128),
-            ],
+            in_specs=[VMEM] * 9 + [SMEM],
+            out_specs=[VMEM] * 5,
+            scratch_shapes=[scratch(FIELDS, 8 * ROWS, 128), scratch(2, OWN, 8, 128)],
             compiler_params=PARAMS,
-            name="inner",
-        )(state, z_halo, own, even, odd, even_z, odd_z, weights, port_row)
+            name="rim",
+        )(z_halo, own, even, odd, layer_halo, e_now, h_now, sums, weights, port_row)
         devices = col_size * row_size * gz_size
         ports_each = PORT_TILE * col_size * row_size // devices
         electric_out, magnetic_out, term = pl.pallas_call(
@@ -718,7 +795,7 @@
             ],
             compiler_params=PARAMS,
             name="outer",
-        )(port_row, port_ids, *inner, weights, *x_halo, *corner)
+        )(port_row, port_ids, e_now, h_now, c_now, weights, *edges, *x_halo, *corner)
         terms = lax.all_to_all(term, ("col", "row", "gz"), 0, 0, tiled=True)
         return (
             electric_out,

time: 40.6 us -> 35.3 us (0.87)
  Pallas kernels: 15 us -> 9.81 us
  waiting for transfers between devices: 2.49 us -> 3.88 us
  blocking collectives: 13.6 us -> 12.5 us
  local copies, waits for them, and re-layouts: 1.74 us -> 1.2 us
    pallas_call x1, Pallas kernels: 5.48 us -> 3.31 us  [per_device(): pl.pallas_call(functools.partial(outer_kernel, row_size, ports_each), out...]
    pallas_call x1, Pallas kernels: 5.01 us -> 2.96 us  [per_device(): pl.pallas_call(functools.partial(pack_kernel, row_size), out_shape=[array...]
    pallas_call x1, Pallas kernels: 3.43 us -> 1.52 us  [per_device(): pl.pallas_call(functools.partial(inner_kernel, row_size), out_shape=[arra...]
    ppermute x7 -> x6, waiting for transfers between devices: 2.49 us -> 3.88 us  [swapped(): return lax.ppermute(block, axis, pairs + [(j, i) for i, j in pairs])]
    all_to_all x1, blocking collectives: 13.6 us -> 12.5 us  [per_device(): terms = lax.all_to_all(term, ('col', 'row', 'gz'), 0, 0, tiled=True)]
    pallas_call x1 -> x2, Pallas kernels: 1.04 us -> 1.99 us  [the longest x1 1.98 us: per_device(): pl.pallas_call(functools.partial(rim_kernel, row_size), out_shape=[array(...]
    unnamed x14, local copies, waits for them, and re-layouts: 1.74 us -> 1.2 us
    ppermute x7 -> x6, starting transfers between devices: 6.21 us -> 6.3 us  [swapped(): return lax.ppermute(block, axis, pairs + [(j, i) for i, j in pairs])]
  transfers between devices with their start and end apart: 7 -> 6, of which waited for: 2 -> 2; matrix products, arithmetic and copies ran while one was open for 0% -> 0% of each run, Pallas kernels for 11% -> 10%
where the time goes in v10:
time: 35.3 us; the launch traced here: 35 us
  blocking collectives  12.5 us (35%)
  Pallas kernels  9.81 us (28%)
  starting transfers between devices  6.3 us (18%)
  waiting for transfers between devices  3.88 us (11%)
  local copies, waits for them, and re-layouts  1.2 us (3%)
  between operations  0.78 us (2%)
  other arithmetic  0.59 us (2%)
    all_to_all x1, blocking collectives, per_device(): terms = lax.all_to_all(term, ('col', 'row', 'gz'), 0, 0, tiled=True)  12.5 us
    ppermute x6, starting transfers between devices, swapped(): return lax.ppermute(block, axis, pairs + [(j, i) for i, j in pairs])  6.3 us
    ppermute x6, waiting for transfers between devices, swapped(): return lax.ppermute(block, axis, pairs + [(j, i) for i, j in pairs])  3.88 us
    pallas_call x1, Pallas kernels, per_device(): pl.pallas_call(functools.partial(outer_kernel, row_size, ports_each), out...  3.31 us
    pallas_call x1, Pallas kernels, per_device(): pl.pallas_call(functools.partial(pack_kernel, row_size), out_shape=[array...  2.96 us
    pallas_call x1, Pallas kernels, per_device(): pl.pallas_call(functools.partial(rim_kernel, row_size), out_shape=[array(...  1.98 us
    pallas_call x1, Pallas kernels, per_device(): pl.pallas_call(functools.partial(inner_kernel, row_size), out_shape=[arra...  1.52 us
    unnamed x14, local copies, waits for them, and re-layouts  1.2 us
  transfers between devices with their start and end apart: 6, of which 2 were waited for; matrix products, arithmetic and copies ran while one was open for 0% of the time, Pallas kernels for 10%

profile of v10, /device:TPU:0, one launch (start us, length us, event | category | flops | bytes accessed | tf_op | source)
XLA Modules:
  0.0 35.0 jit_solution(11450682060211538647)
XLA Ops:
  0.6 0.0 copy-start.2
  0.6 3.0 %pack.1 = (f32[7,8,4,8,128]{4,3,2,1,0:T(8,128)}, f32[7,4,8,128]{3,2,1,0:T(8,128)}, f32[7,2,4,8,128]{4,3,2,1,0:T(8,128)}, f32[2,4,8,128]{3,2,1,0:T(8,128)}, f32[2...) custom-call(f32[8]{0:T(128)} %eps_hbm.1, f32[3,32,8,128]{3,2,1,0:T(8,128)} %elec_hbm.1, f32[3,32,8,128]{3,2,1,0:T(8,128)} %magn_hbm.1, ...), custom_call_target="tpu_custom_call" | custom-call | tf_op jit(solution)/shard_map/pack/pallas_call | solution.py:702
  3.6 3.0 %collective-permute-start.4 = (f32[26,4,8,128]{3,2,1,0:T(8,128)}, f32[26,4,8,128]{3,2,1,0:T(8,128)S(1)}, u32[]{:S(2)}, u32[]{:S(2)}) collective-permute-start(f32[26,4,8,128]{3,2,1,0:T(8,128)} %get-tuple-element.37), channel_id=1, source_target_pairs={{0,2},{2,0},{1,3},{3,1},{4,6},{6,4},{5,7},{7,5},{8,10},{10,8},{9,1... | collective-permute-start | bytes 1277960 | tf_op jit(solution)/shard_map/ppermute | solution.py:678
  6.6 0.0 collective-permute-start
  6.6 1.6 %collective-permute-start.1 = (f32[2,4,8,128]{3,2,1,0:T(8,128)}, f32[2,4,8,128]{3,2,1,0:T(8,128)S(1)}, u32[]{:S(2)}, u32[]{:S(2)}) collective-permute-start(f32[2,4,8,128]{3,2,1,0:T(8,128)} %get-tuple-element.29), channel_id=1, source_target_pairs={{0,4},{8,12},{4,0},{12,8},{1,5},{9,13},{5,1},{13,9},{2,6},{10,14},... | collective-permute-start | bytes 98312 | tf_op jit(solution)/shard_map/ppermute | solution.py:678
  8.2 0.0 copy-start.6
  8.2 0.0 copy-start.3
  8.2 0.0 copy-start.4
  8.2 0.0 copy-start.5
  8.2 0.8 %collective-permute-start.2 = (f32[2,4,8,128]{3,2,1,0:T(8,128)}, f32[2,4,8,128]{3,2,1,0:T(8,128)S(1)}, u32[]{:S(2)}, u32[]{:S(2)}) collective-permute-start(f32[2,4,8,128]{3,2,1,0:T(8,128)} %get-tuple-element.30), channel_id=1, source_target_pairs={{4,8},{8,4},{5,9},{9,5},{6,10},{10,6},{7,11},{11,7},{20,24},{24,20... | collective-permute-start | bytes 98312 | tf_op jit(solution)/shard_map/ppermute | solution.py:678
  9.0 0.0 collective-permute-done.z_ref
  9.0 0.0 copy-done.2
  9.0 0.0 copy-done.6
  9.0 0.0 copy-done.3
  9.0 0.0 copy-done.4
  9.1 0.0 copy-done.5
  9.1 0.0 copy-start
  9.1 1.2 %copy-done = f32[7,8,4,8,128]{4,3,2,1,0:T(8,128)S(1)} copy-done((f32[7,8,4,8,128]{4,3,2,1,0:T(8,128)S(1)}, f32[7,8,4,8,128]{4,3,2,1,0:T(8,128)}, u32[]{:S(2)}) %copy-start) | copy-done | bytes 917528
  10.2 1.5 %inner.1 = (f32[3,8,5,8,128]{4,3,2,1,0:T(8,128)S(1)}, f32[3,8,5,8,128]{4,3,2,1,0:T(8,128)S(1)}, f32[8,5,8,128]{3,2,1,0:T(8,128)S(1)}, f32[4,8,128]{2,1,0:T(8,128)S(1)}, f32[4,2,4,8,128]{4,3,2,1,0:T(8,128)S(1)}) custom-call(f32[7,8,4,8,128]{4,3,2,1,0:T(8,128)S(1)} %copy-done, f32[7,4,8,128]{3,2,1,0:T(8,128)S(1)} %collective-permute-done.z_ref, ...), custom_call_target="tpu_custom_call" | custom-call | flops 5000000 | bytes 10000000 | tf_op jit(solution)/shard_map/inner/pallas_call | solution.py:726
  11.8 0.0 copy-start.1
  11.8 0.0 collective-permute-done.1.even_ref
  11.8 0.0 collective-permute-done.2.odd_ref
  11.8 0.3 collective-permute-start.3
  12.1 1.0 %collective-permute-done.3.layer_ref = f32[2,2,8,128]{3,2,1,0:T(8,128)S(1)} collective-permute-done((f32[2,2,8,128]{3,2,1,0:T(8,128)S(1)}, f32[2,2,8,128]{3,2,1,0:T(8,128)S(1)}, u32[]{:S(2)}, u32[]{:S(2)}) %collective-permute-start.3) | collective-permute-done | bytes 16416 | tf_op jit(solution)/shard_map/ppermute | solution.py:678
  13.1 0.6 %collective-permute-start.5 = (f32[23,8,128]{2,1,0:T(8,128)S(1)}, f32[23,8,128]{2,1,0:T(8,128)S(1)}, u32[]{:S(2)}, u32[]{:S(2)}) collective-permute-start(f32[23,8,128]{2,1,0:T(8,128)S(1)} %corners.1), channel_id=1, source_target_pairs={{0,2},{2,0},{1,3},{3,1},{4,6},{6,4},{5,7},{7,5},{8,10},{10,8},{9,1... | collective-permute-start | bytes 282632 | tf_op jit(solution)/shard_map/ppermute | solution.py:678
  13.8 0.0 copy-done.1
  13.8 2.0 %rim.1 = (f32[3,2,5,8,128]{4,3,2,1,0:T(8,128)S(1)}, f32[3,2,5,8,128]{4,3,2,1,0:T(8,128)S(1)}, f32[2,5,8,128]{3,2,1,0:T(8,128)S(1)}, f32[6,4,4,8,128]{4,3,2,1,0:T(8,128)S(1)}, f32[4,8,128]{2,1,0:T(8,128)S(1)}) custom-call(f32[7,4,8,128]{3,2,1,0:T(8,128)S(1)} %collective-permute-done.z_ref, f32[7,2,4,8,128]{4,3,2,1,0:T(8,128)S(1)} %copy-done.1, ...), custom_call_target="tpu_custom_call" | custom-call | tf_op jit(solution)/shard_map/rim/pallas_call | solution.py:766
  15.7 2.9 %collective-permute-done.5.rest_1_ = f32[23,8,128]{2,1,0:T(8,128)S(1)} collective-permute-done((f32[23,8,128]{2,1,0:T(8,128)S(1)}, f32[23,8,128]{2,1,0:T(8,128)S(1)}, u32[]{:S(2)}, u32[]{:S(2)}) %collective-permute-start.5) | collective-permute-done | bytes 94240 | tf_op jit(solution)/shard_map/ppermute | solution.py:678
  18.7 0.0 collective-permute-done.4.rest_0_
  18.7 3.3 %outer.1 = (f32[3,32,8,128]{3,2,1,0:T(8,128)}, f32[3,32,8,128]{3,2,1,0:T(8,128)}, f32[16,2,16]{2,1,0:T(2,128)S(1)}) custom-call(s32[1,1,4]{2,1,0:T(1,128)S(1)} %copy-done.3, s32[1,1,4]{2,1,0:T(1,128)S(1)} %copy-done.4, f32[3,8,5,8,128]{4,3,2,1,0:T(8,128)S(1)} %get-tuple-element.24.e_in, f32[3,8,5,8,128]{4,3,2,1,0:T(8,128)S(1)} %get-tuple-element.25.h_in, ...), custom_call_target="tpu_custom_call" | custom-call | tf_op jit(solution)/shard_map/outer/pallas_call | solution.py:783
  22.0 12.5 %all_to_all.5 = f32[16,2,16]{2,1,0:T(2,128)S(1)} all-to-all(f32[16,2,16]{2,1,0:T(2,128)S(1)} %get-tuple-element.40), channel_id=1, replica_groups=mesh['grp'=2,'col'=4,'row'=2,'gz'=2] {'col','row','gz'}, dimensions={0} | all-to-all | bytes 4096 | tf_op jit(solution)/shard_map/all_to_all | solution.py:799
  34.4 0.6 %reduce_sum.9 = f32[2,16]{1,0:T(2,128)} reduce(f32[16,2,16]{2,1,0:T(2,128)S(1)} %all_to_all.5, f32[]{:T(128)} %constant.0.clone.1), dimensions={0}, to_apply=%region_0.0 | reduce | flops 480 | bytes 2180 | tf_op jit(solution)/shard_map/reduce_sum | solution.py:803
  (2 shorter events, 0.1 us)
Async XLA Ops:
  0.6 8.4 %copy-start.2 = (f32[8,32,64]{2,1,0:T(8,128)S(1)}, f32[8,32,64]{2,1,0:T(8,128)}, u32[]{:S(2)}) copy-start(f32[8,32,64]{2,1,0:T(8,128)} %mode_ref.1) | copy-start | bytes 196612
  3.6 15.1 %collective-permute-start.4 = (f32[26,4,8,128]{3,2,1,0:T(8,128)}, f32[26,4,8,128]{3,2,1,0:T(8,128)S(1)}, u32[]{:S(2)}, u32[]{:S(2)}) collective-permute-start(f32[26,4,8,128]{3,2,1,0:T(8,128)} %get-tuple-element.37), channel_id=1, source_target_pairs={{0,2},{2,0},{1,3},{3,1},{4,6},{6,4},{5,7},{7,5},{8,10},{10,8},{9,1... | collective-permute-start | bytes 1277960 | tf_op jit(solution)/shard_map/ppermute | solution.py:678
  6.6 2.4 %collective-permute-start = (f32[7,4,8,128]{3,2,1,0:T(8,128)}, f32[7,4,8,128]{3,2,1,0:T(8,128)S(1)}, u32[]{:S(2)}, u32[]{:S(2)}) collective-permute-start(f32[7,4,8,128]{3,2,1,0:T(8,128)} %get-tuple-element.23), channel_id=1, source_target_pairs={{0,1},{1,0},{2,3},{3,2},{4,5},{5,4},{6,7},{7,6},{8,9},{9,8},{10,11... | collective-permute-start | bytes 344072 | tf_op jit(solution)/shard_map/ppermute | solution.py:678
  6.6 5.2 %collective-permute-start.1 = (f32[2,4,8,128]{3,2,1,0:T(8,128)}, f32[2,4,8,128]{3,2,1,0:T(8,128)S(1)}, u32[]{:S(2)}, u32[]{:S(2)}) collective-permute-start(f32[2,4,8,128]{3,2,1,0:T(8,128)} %get-tuple-element.29), channel_id=1, source_target_pairs={{0,4},{8,12},{4,0},{12,8},{1,5},{9,13},{5,1},{13,9},{2,6},{10,14},... | collective-permute-start | bytes 98312 | tf_op jit(solution)/shard_map/ppermute | solution.py:678
  8.2 0.8 %copy-start.6 = (s32[1,1,4]{2,1,0:T(1,128)S(1)}, s32[1,1,4]{2,1,0:T(1,128)}, u32[]{:S(2)}) copy-start(s32[1,1,4]{2,1,0:T(1,128)} %pmode_ref.1) | copy-start | bytes 52
  8.2 0.8 %copy-start.3 = (s32[1,1,4]{2,1,0:T(1,128)S(1)}, s32[1,1,4]{2,1,0:T(1,128)}, u32[]{:S(2)}) copy-start(s32[1,1,4]{2,1,0:T(1,128)} %prow_ref.5) | copy-start | bytes 52
  8.2 0.9 %copy-start.4 = (s32[1,1,4]{2,1,0:T(1,128)S(1)}, s32[1,1,4]{2,1,0:T(1,128)}, u32[]{:S(2)}) copy-start(s32[1,1,4]{2,1,0:T(1,128)} %pid_ref.3) | copy-start | bytes 52
  8.2 0.9 %copy-start.5 = (s32[1,1,4]{2,1,0:T(1,128)S(1)}, s32[1,1,4]{2,1,0:T(1,128)}, u32[]{:S(2)}) copy-start(s32[1,1,4]{2,1,0:T(1,128)} %pcol_ref.1) | copy-start | bytes 52
  8.2 3.6 %collective-permute-start.2 = (f32[2,4,8,128]{3,2,1,0:T(8,128)}, f32[2,4,8,128]{3,2,1,0:T(8,128)S(1)}, u32[]{:S(2)}, u32[]{:S(2)}) collective-permute-start(f32[2,4,8,128]{3,2,1,0:T(8,128)} %get-tuple-element.30), channel_id=1, source_target_pairs={{4,8},{8,4},{5,9},{9,5},{6,10},{10,6},{7,11},{11,7},{20,24},{24,20... | collective-permute-start | bytes 98312 | tf_op jit(solution)/shard_map/ppermute | solution.py:678
  9.1 1.2 %copy-start = (f32[7,8,4,8,128]{4,3,2,1,0:T(8,128)S(1)}, f32[7,8,4,8,128]{4,3,2,1,0:T(8,128)}, u32[]{:S(2)}) copy-start(f32[7,8,4,8,128]{4,3,2,1,0:T(8,128)} %get-tuple-element.22.state_ref) | copy-start | bytes 2752516
  11.8 2.0 %copy-start.1 = (f32[7,2,4,8,128]{4,3,2,1,0:T(8,128)S(1)}, f32[7,2,4,8,128]{4,3,2,1,0:T(8,128)}, u32[]{:S(2)}) copy-start(f32[7,2,4,8,128]{4,3,2,1,0:T(8,128)} %get-tuple-element.28.own_ref) | copy-start | bytes 688132
  11.8 1.2 %collective-permute-start.3 = (f32[2,2,8,128]{3,2,1,0:T(8,128)S(1)}, f32[2,2,8,128]{3,2,1,0:T(8,128)S(1)}, u32[]{:S(2)}, u32[]{:S(2)}) collective-permute-start(f32[2,2,8,128]{3,2,1,0:T(8,128)S(1)} %layer_edges.1), channel_id=1, source_target_pairs={{0,1},{1,0},{2,3},{3,2},{4,5},{5,4},{6,7},{7,6},{8,9},{9,8},{10,11... | collective-permute-start | bytes 49160 | tf_op jit(solution)/shard_map/ppermute | solution.py:678
  13.1 5.5 %collective-permute-start.5 = (f32[23,8,128]{2,1,0:T(8,128)S(1)}, f32[23,8,128]{2,1,0:T(8,128)S(1)}, u32[]{:S(2)}, u32[]{:S(2)}) collective-permute-start(f32[23,8,128]{2,1,0:T(8,128)S(1)} %corners.1), channel_id=1, source_target_pairs={{0,2},{2,0},{1,3},{3,1},{4,6},{6,4},{5,7},{7,5},{8,10},{10,8},{9,1... | collective-permute-start | bytes 282632 | tf_op jit(solution)/shard_map/ppermute | solution.py:678

commit v11 on v10

--- a/solution.py
+++ b/solution.py
@@ -62,8 +62,20 @@
         body(False, 1)
 
 
-def pack_kernel(row_size, eps_hbm, elec_hbm, magn_hbm, mat_hbm, state_ref, z_ref, own_ref, even_ref, odd_ref, *rest):
-    x_refs, (main_ref, eps_ref, mat_ref, sems) = rest[:-4], rest[-4:]
+def coefficient(material, eps_ref):
+    eps = jnp.full((8, 128), eps_ref[0], jnp.float32)
+    for which in range(1, MATS):
+        eps = jnp.where(material == which, eps_ref[which], eps)
+    return time_step * (1.0 / eps)
+
+
+def rows_outside(flat, f, state_ref, at):
+    for x in range(ROWS):
+        state_ref[at, x] = flat[pl.ds(f * LAYERS * ROWS + x, LAYERS, stride=ROWS), :].reshape(OWN, 8, 128)
+
+
+def pack_kernel(row_size, eps_hbm, elec_hbm, magn_hbm, mat_hbm, z_ref, own_ref, even_ref, odd_ref, *rest):
+    x_refs, (state_ref, main_ref, eps_ref, mat_ref, sems) = rest[:-5], rest[-5:]
     copies = [pltpu.make_async_copy(eps_hbm, eps_ref, sems.at[0]), pltpu.make_async_copy(mat_hbm, mat_ref, sems.at[1])]
     copies.append(pltpu.make_async_copy(elec_hbm, main_ref.at[pl.ds(0, 3)], sems.at[2]))
     copies.append(pltpu.make_async_copy(magn_hbm, main_ref.at[pl.ds(3, 3)], sems.at[3]))
@@ -72,21 +84,15 @@
     copies[0].wait()
     copies[1].wait()
     for z in range(LAYERS):
-        material = mat_ref[z]
-        eps = jnp.full((8, 128), eps_ref[0], jnp.float32)
-        for which in range(1, MATS):
-            eps = jnp.where(material == which, eps_ref[which], eps)
-        main_ref[6, z] = time_step * (1.0 / eps)
+        main_ref[6, z] = coefficient(mat_ref[z], eps_ref)
     copies[2].wait()
     copies[3].wait()
     start = jnp.where(lax.axis_index("gz") == 0, LAYERS - DEPTH, 0)
     for f in range(FIELDS):
         z_ref[f] = main_ref[f, pl.ds(start, DEPTH)]
-    block = LAYERS * ROWS
-    flat = main_ref.reshape(FIELDS * block, 128)
+    flat = main_ref.reshape(FIELDS * LAYERS * ROWS, 128)
     for f in range(FIELDS):
-        for x in range(ROWS):
-            state_ref[f, x] = flat[pl.ds(f * block + x, LAYERS, stride=ROWS), :].reshape(OWN, 8, 128)
+        rows_outside(flat, f, state_ref, f)
 
     def send(up, slot):
         for i, (f, x) in enumerate(UP_PLANES if up else DOWN_PLANES):
@@ -171,32 +177,32 @@
         ext_ref[f, DEPTH * ROWS :] = jnp.where(gz == 0, nothing, halo)
 
 
-def corner_kernel(row_size, z_ref, even_ref, odd_ref, layer_ref, *rest):
+def layer_kernel(row_size, z_ref, *rest):
     x_refs, ext_ref = rest[:-1], rest[-1]
-    gz = lax.axis_index("gz")
-    valid = (iota(0) < 4) == (gz == 0)
-    spread_layers(gz, z_ref, ext_ref)
+    spread_layers(lax.axis_index("gz"), z_ref, ext_ref)
+
+    def send(up, slot):
+        planes = UP_PLANES if up else DOWN_PLANES
+        tiles = [ext_ref[f, pl.ds(x, 8, stride=ROWS), :] for f, x in planes]
+        turned = [turn(tile, 4, 0) for tile in tiles[PAIRS:]]
+        for i in range(PAIRS):
+            x_refs[slot][i] = tiles[i] + turned[i] if i < len(turned) else tiles[i]
+
+    directions(row_size, send)
+
+
+def corner_kernel(row_size, even_ref, odd_ref, layer_ref, *x_refs):
+    valid = (iota(0) < 4) == (lax.axis_index("gz") == 0)
     low, high = low_and_high(even_ref, odd_ref)
     low_z, high_z = low_and_high(layer_ref.at[0], layer_ref.at[1])
 
     def send(up, slot):
-        planes = UP_PLANES if up else DOWN_PLANES
-
-        def tile(i):
-            f, x = planes[i]
-            return ext_ref[f, pl.ds(x, 8, stride=ROWS), :]
-
-        for i in range(PAIRS):
-            pair = tile(i)
-            if i + PAIRS < len(planes):
-                pair = pair + turn(tile(i + PAIRS), 4, 0)
-            x_refs[slot][i] = pair
         b = 1 if up else 0
         for zz in range(OWN):
-            x_refs[slot][PAIRS + zz] = low(b, zz)
-            x_refs[slot][PAIRS + CHUNK + zz] = high(b, zz)
-        x_refs[slot][PAIRS + OWN] = jnp.where(valid, low_z(b), 0.0)
-        x_refs[slot][PAIRS + CHUNK + OWN] = jnp.where(valid, high_z(b), 0.0)
+            x_refs[slot][zz] = low(b, zz)
+            x_refs[slot][CHUNK + zz] = high(b, zz)
+        x_refs[slot][OWN] = jnp.where(valid, low_z(b), 0.0)
+        x_refs[slot][CHUNK + OWN] = jnp.where(valid, high_z(b), 0.0)
 
     directions(row_size, send)
 
@@ -228,7 +234,7 @@
     def put(self, f, i, zz, tile):
         self.values[f, i, zz] = tile
         at = i - self.shift
-        if f == 2 and zz < OWN and 0 <= at < self.ez_ref.shape[0]:
+        if f == 2 and zz < OWN and self.ez_ref is not None and 0 <= at < self.ez_ref.shape[0]:
             self.ez_ref[at, zz] = tile
 
 
@@ -471,8 +477,8 @@
 
 
 def inner_kernel(
-    row_size, state_ref, z_ref, mode_ref, prow_ref, pcol_ref, pmode_ref, pid_ref,
-    e_ref, h_ref, c_ref, sum_ref, weight_ref, ext_ref, halo_ref, ez_ref, strip_ref,
+    row_size, elec_ref, magn_ref, mat_ref, z_ref, mode_ref, eps_ref, prow_ref, pcol_ref, pmode_ref, pid_ref,
+    e_ref, h_ref, c_ref, sum_ref, weight_ref, state_ref, plain_ref, ext_ref, halo_ref, ez_ref, strip_ref,
 ):
     gz, row = lax.axis_index("gz"), lax.axis_index("row")
     spread_layers(gz, z_ref, ext_ref)
@@ -480,6 +486,12 @@
         for x in range(ROWS):
             halo_ref[f, x] = ext_ref[f, pl.ds(x, 8, stride=ROWS), :]
     port_weights(mode_ref, prow_ref, pcol_ref, pmode_ref, weight_ref, strip_ref)
+    for z in range(LAYERS):
+        plain_ref[z] = coefficient(mat_ref[z], eps_ref)
+    for f in range(3):
+        rows_outside(elec_ref.reshape(3 * LAYERS * ROWS, 128), f, state_ref, f)
+        rows_outside(magn_ref.reshape(3 * LAYERS * ROWS, 128), f, state_ref, f + 3)
+    rows_outside(plain_ref.reshape(LAYERS * ROWS, 128), 0, state_ref, 6)
 
     def first(f, i, zz):
         return halo_ref[f, i - DEPTH] if zz == OWN else state_ref[f, i - DEPTH, zz]
@@ -558,50 +570,97 @@
     rows_cases(row_size, row, run)
 
 
-def outer_kernel(
-    row_size, ports_each, prow_ref, pid_ref, e_in, h_in, c_in, weight_ref, edge_e_in, edge_h_in, edge_c_in, done_ref, sum_in,
-    *rest,
-):
+def outer_spans(n, has_below, has_above):
+    return ([spans_below(n)] if has_below else []) + ([spans_above(n)] if has_above else [])
+
+
+def outer_reached(has_below, has_above):
+    def reached(n, at):
+        parts = [(at >= span[0]) & (at <= span[1]) for _, span in outer_spans(n, has_below, has_above)]
+        return functools.reduce(lambda a, b: a | b, parts)
+
+    return reached
+
+
+def outer_main_kernel(row_size, prow_ref, e_in, h_in, c_in, weight_ref, sum_in, *rest):
     n_x = 1 if row_size == 2 else 2
-    x_refs, corner_refs = rest[:n_x], rest[n_x : 2 * n_x]
-    eout_hbm, hout_hbm, term_ref, ez_ref, edge_ez_ref, sum_ref, turned_ref, out_ref, sems = rest[2 * n_x :]
+    x_refs, ext_refs = rest[:n_x], rest[n_x : 2 * n_x]
+    fixed_ref, own_ref, sum_ref, ez_ref = rest[2 * n_x :]
     gz, row = lax.axis_index("gz"), lax.axis_index("row")
-    lane, sub = iota(1), iota(0)
-    place = lane & (GROUP - 1)
     groups = lane_groups()
-    valid = (sub < 4) == (gz == 0)
-    zeros = jnp.zeros((8, 128), jnp.float32)
+    valid = (iota(0) < 4) == (gz == 0)
 
     def first_main(f, i, zz):
         if f == 6:
             return c_in[i - DEPTH, zz]
         return e_in[f, i - DEPTH, zz] if f < 3 else h_in[f - 3, i - DEPTH, zz]
 
+    def run(has_below, has_above):
+        main = Tiles(first_main, ez_ref, DEPTH)
+
+        def halo_rows(planes, slot, offset, b):
+            got = {}
+            packed = [ext_refs[slot][i] for i in range(PAIRS)]
+            packed += [turn(tile, 4, 0) for tile in packed[: len(planes) - PAIRS]]
+            for i, (f, x) in enumerate(planes):
+                tiles = [x_refs[slot][i, zz] for zz in range(OWN)] + [jnp.where(valid, packed[i], 0.0)]
+                for zz in range(CHUNK):
+                    main.put(f, DEPTH + x + offset, zz, tiles[zz])
+                    got[f, x + offset - 4 * b, zz] = tiles[zz]
+
+            def first(zz):
+                return gather_edges([[got.get((f, r, zz)) for r in range(4)] for f in range(FIELDS)], groups)
+
+            def second(zz, owns):
+                for f, tile in enumerate(owns):
+                    own_ref[slot, f, zz] = tile
+
+            staged(range(CHUNK), first, second)
+
+        if has_below:
+            halo_rows(UP_PLANES, 0, -ROWS, -1)
+        if has_above:
+            halo_rows(DOWN_PLANES, n_x - 1, ROWS, 2)
+        rows = range(0 if has_below else 4, 16 if has_above else 12)
+        stepper = Stepper(row_size, main, None, rows, (), True)
+        for n in range(1, STEPS + 1):
+            stepper.step(n, outer_spans(n, has_below, has_above))
+            port_sums(n, outer_reached(has_below, has_above), prow_ref, weight_ref, ez_ref, None, sum_ref, sum_in)
+        for b in range(2):
+            if has_below and has_above or b == (1 if has_above else 0):
+                for f in range(6):
+                    for x in range(4 * b, 4 * b + 4):
+                        for zz in range(OWN):
+                            fixed_ref[f, x, zz] = main.get(f, DEPTH + x, zz)
+
+    rows_cases(row_size, row, run)
+
+
+def outer_edge_kernel(
+    row_size, ports_each, prow_ref, pid_ref, edge_e_in, edge_h_in, edge_c_in, done_ref, weight_ref, fixed_ref, own_ref, sum_in,
+    *rest,
+):
+    n_x = 1 if row_size == 2 else 2
+    corner_refs = rest[:n_x]
+    eout_hbm, hout_hbm, term_ref, ez_ref, sum_ref, turned_ref, out_ref, sems = rest[n_x:]
+    row = lax.axis_index("row")
+    lane, sub = iota(1), iota(0)
+    place = lane & (GROUP - 1)
+    zeros = jnp.zeros((8, 128), jnp.float32)
+
     def first_edge(f, i, zz):
         if f == 6:
             return edge_c_in[i - 1, zz]
         return edge_e_in[f, i - 1, zz] if f < 3 else edge_h_in[f - 3, i - 1, zz]
 
     def run(has_below, has_above):
-        main = Tiles(first_main, ez_ref, DEPTH)
-        edge = Tiles(first_edge, edge_ez_ref, 1)
-
-        def halo_rows(planes, slot, offset, b):
-            got = {}
-            for i, (f, x) in enumerate(planes):
-                packed = corner_refs[slot][i % PAIRS]
-                if i >= PAIRS:
-                    packed = turn(packed, 4, 0)
-                tiles = [x_refs[slot][i, zz] for zz in range(OWN)]
-                tiles.append(jnp.where(valid, packed, 0.0))
-                for zz in range(CHUNK):
-                    main.put(f, DEPTH + x + offset, zz, tiles[zz])
-                    got[f, x + offset - 4 * b, zz] = tiles[zz]
-
+        main = Tiles(lambda f, i, zz: fixed_ref[f, i - DEPTH, zz], None, DEPTH)
+        edge = Tiles(first_edge, ez_ref, 1)
+
+        def halo_block(slot, b):
             def first(zz):
-                rows = [[got.get((f, r, zz)) for r in range(4)] for f in range(FIELDS)]
-                sides = turn_sides(corner_refs[slot][PAIRS + zz], corner_refs[slot][PAIRS + CHUNK + zz])
-                return gather_edges(rows, groups), sides
+                owns = [own_ref[slot, f, zz] for f in range(FIELDS)]
+                return owns, turn_sides(corner_refs[slot][zz], corner_refs[slot][CHUNK + zz])
 
             def second(zz, made):
                 for f, tile in enumerate(edge_tiles(*made, place)):
@@ -610,25 +669,15 @@
             staged(range(CHUNK), first, second)
 
         if has_below:
-            halo_rows(UP_PLANES, 0, -ROWS, -1)
+            halo_block(0, -1)
         if has_above:
-            halo_rows(DOWN_PLANES, n_x - 1, ROWS, 2)
-
-        def reached(n, at):
-            out = None
-            for wanted, span in ((has_below, spans_below(n)[1]), (has_above, spans_above(n)[1])):
-                if wanted:
-                    part = (at >= span[0]) & (at <= span[1])
-                    out = part if out is None else out | part
-            return out
-
-        rows = range(0 if has_below else 4, 16 if has_above else 12)
+            halo_block(n_x - 1, 2)
         blocks = range(0 if has_below else 1, 4 if has_above else 3)
-        stepper = Stepper(row_size, main, edge, rows, blocks, True)
+        stepper = Stepper(row_size, None, edge, (), blocks, True)
         for n in range(1, STEPS + 1):
-            spans = ([spans_below(n)] if has_below else []) + ([spans_above(n)] if has_above else [])
-            stepper.step(n, spans)
-            port_sums(n, reached, prow_ref, weight_ref, ez_ref, edge_ez_ref, sum_ref, sum_in)
+            stepper.step(n, outer_spans(n, has_below, has_above))
+            port_sums(n, outer_reached(has_below, has_above), prow_ref, weight_ref, None, ez_ref, sum_ref, sum_in)
+
         def write(f, r, zz, tile, b):
             turned_ref[f, 4 * b + r, 8 * zz : 8 * zz + 8, :] = tile
 
@@ -699,10 +748,9 @@
         def scratch(*shape):
             return pltpu.VMEM(shape, f32)
 
-        state, z_send, own, even_send, odd_send, *x_send = pl.pallas_call(
+        z_send, own, even_send, odd_send, *x_send = pl.pallas_call(
             functools.partial(pack_kernel, row_size),
             out_shape=[
-                array(FIELDS, ROWS, OWN, 8, 128),
                 array(FIELDS, DEPTH, ROWS, 128),
                 array(FIELDS, 2, OWN, 8, 128),
                 array(2, OWN, 8, 128),
@@ -710,8 +758,9 @@
             ]
             + [array(PLANES, OWN, 8, 128)] * n_x,
             in_specs=[HBM] * 4,
-            out_specs=[VMEM] * (5 + n_x),
+            out_specs=[VMEM] * (4 + n_x),
             scratch_shapes=[
+                scratch(FIELDS, ROWS, OWN, 8, 128),
                 scratch(FIELDS, LAYERS, ROWS, 128),
                 pltpu.SMEM(eps_table.shape, f32),
                 pltpu.VMEM(material.shape, jnp.int32),
@@ -723,6 +772,16 @@
         even = swapped(even_send, "col", col_size)
         odd = swapped(odd_send, "col", col_size, 1)
         z_halo = swapped(z_send, "gz", gz_size)
+        ext_send = pl.pallas_call(
+            functools.partial(layer_kernel, row_size),
+            out_shape=[array(PAIRS, 8, 128)] * n_x,
+            in_specs=[VMEM],
+            out_specs=[VMEM] * n_x,
+            scratch_shapes=[scratch(FIELDS, 8 * ROWS, 128)],
+            compiler_params=PARAMS,
+            name="layers",
+        )(z_halo)
+        ext_halo = across_rows(ext_send)
         e_now, h_now, c_now, sums, weights = pl.pallas_call(
             functools.partial(inner_kernel, row_size),
             out_shape=[
@@ -732,9 +791,11 @@
                 array(STEPS, 8, 128),
                 array(PORT_TILE, 2, OWN, 8, 128),
             ],
-            in_specs=[VMEM] * 3 + [SMEM] * 4,
+            in_specs=[VMEM] * 5 + [SMEM] * 5,
             out_specs=[VMEM] * 5,
             scratch_shapes=[
+                scratch(FIELDS, ROWS, OWN, 8, 128),
+                scratch(LAYERS, ROWS, 128),
                 scratch(FIELDS, 8 * ROWS, 128),
                 scratch(FIELDS, ROWS, 8, 128),
                 scratch(ROWS, OWN, 8, 128),
@@ -743,7 +804,7 @@
             compiler_params=PARAMS,
             cost_estimate=pl.CostEstimate(flops=5_000_000, bytes_accessed=10_000_000, transcendentals=0),
             name="inner",
-        )(state, z_halo, mode_table, port_row, port_col, port_mode, port_ids)
+        )(electric, magnetic, material, z_halo, mode_table, eps_table, port_row, port_col, port_mode, port_ids)
         layer_send = pl.pallas_call(
             layer_edge_kernel,
             out_shape=array(2, 2, 8, 128),
@@ -755,13 +816,12 @@
         layer_halo = swapped(layer_send, "gz", gz_size)
         corner_send = pl.pallas_call(
             functools.partial(corner_kernel, row_size),
-            out_shape=[array(PAIRS + 2 * CHUNK, 8, 128)] * n_x,
-            in_specs=[VMEM] * 4,
+            out_shape=[array(2 * CHUNK, 8, 128)] * n_x,
+            in_specs=[VMEM] * 3,
             out_specs=[VMEM] * n_x,
-            scratch_shapes=[scratch(FIELDS, 8 * ROWS, 128)],
             compiler_params=PARAMS,
             name="corners",
-        )(z_halo, even, odd, layer_halo)
+        )(even, odd, layer_halo)
         corner = across_rows(corner_send)
         edges = pl.pallas_call(
             functools.partial(rim_kernel, row_size),
@@ -780,13 +840,26 @@
         )(z_halo, own, even, odd, layer_halo, e_now, h_now, sums, weights, port_row)
         devices = col_size * row_size * gz_size
         ports_each = PORT_TILE * col_size * row_size // devices
+        edge_e, edge_h, edge_c, done, sums = edges
+        fixed, halo_own, sums = pl.pallas_call(
+            functools.partial(outer_main_kernel, row_size),
+            out_shape=[
+                array(6, ROWS, OWN, 8, 128),
+                array(n_x, FIELDS, CHUNK, 8, 128),
+                array(STEPS, 8, 128),
+            ],
+            in_specs=[SMEM] + [VMEM] * (5 + 2 * n_x),
+            out_specs=[VMEM] * 3,
+            scratch_shapes=[scratch(ROWS, OWN, 8, 128)],
+            compiler_params=PARAMS,
+            name="outer_main",
+        )(port_row, e_now, h_now, c_now, weights, sums, *x_halo, *ext_halo)
         electric_out, magnetic_out, term = pl.pallas_call(
-            functools.partial(outer_kernel, row_size, ports_each),
+            functools.partial(outer_edge_kernel, row_size, ports_each),
             out_shape=[array(3, LAYERS, ROWS, 128)] * 2 + [array(devices, ports_each, 2 * FREQ)],
-            in_specs=[SMEM] * 2 + [VMEM] * (9 + 2 * n_x),
+            in_specs=[SMEM] * 2 + [VMEM] * (8 + n_x),
             out_specs=[HBM, HBM, VMEM],
             scratch_shapes=[
-                scratch(ROWS, OWN, 8, 128),
                 scratch(2, OWN, 8, 128),
                 scratch(STEPS, 8, 128),
                 scratch(6, ROWS, LAYERS, 128),
@@ -794,8 +867,8 @@
                 pltpu.SemaphoreType.DMA((2,)),
             ],
             compiler_params=PARAMS,
-            name="outer",
-        )(port_row, port_ids, e_now, h_now, c_now, weights, *edges, *x_halo, *corner)
+            name="outer_edge",
+        )(port_row, port_ids, edge_e, edge_h, edge_c, done, weights, fixed, halo_own, sums, *corner)
         terms = lax.all_to_all(term, ("col", "row", "gz"), 0, 0, tiled=True)
         return (
             electric_out,

time: 35.3 us -> 35.7 us (1.011)
  waiting for transfers between devices: 3.88 us -> 2.3 us
  starting transfers between devices: 6.3 us -> 7.45 us
  Pallas kernels: 9.81 us -> 10.8 us
    ppermute x6 -> x7, waiting for transfers between devices: 3.88 us -> 2.3 us  [swapped(): return lax.ppermute(block, axis, pairs + [(j, i) for i, j in pairs])]
    ppermute x6 -> x7, starting transfers between devices: 6.3 us -> 7.45 us  [swapped(): return lax.ppermute(block, axis, pairs + [(j, i) for i, j in pairs])]
    pallas_call x1 -> x3, Pallas kernels: 3.31 us -> 4.33 us  [the longest x1 2.93 us: per_device(): pl.pallas_call(functools.partial(outer_edge_kernel, row_size, ports_each)...]
    unnamed x14 -> x20, local copies, waits for them, and re-layouts: 1.2 us -> 0.94 us
  transfers between devices with their start and end apart: 6 -> 7, of which waited for: 2 -> 2; matrix products, arithmetic and copies ran while one was open for 0% -> 0% of each run, Pallas kernels for 10% -> 14%
where the time goes in v11:
time: 35.7 us; the launch traced here: 35.5 us
  blocking collectives  12.5 us (35%)
  Pallas kernels  10.8 us (30%)
  starting transfers between devices  7.45 us (21%)
  waiting for transfers between devices  2.3 us (6%)
  local copies, waits for them, and re-layouts  0.94 us (3%)
  between operations  0.86 us (2%)
  other arithmetic  0.59 us (2%)
    all_to_all x1, blocking collectives, per_device(): terms = lax.all_to_all(term, ('col', 'row', 'gz'), 0, 0, tiled=True)  12.5 us
    ppermute x7, starting transfers between devices, swapped(): return lax.ppermute(block, axis, pairs + [(j, i) for i, j in pairs])  7.45 us
    pallas_call x1, Pallas kernels, per_device(): pl.pallas_call(functools.partial(outer_edge_kernel, row_size, ports_each)...  2.93 us
    pallas_call x1, Pallas kernels, per_device(): pl.pallas_call(functools.partial(pack_kernel, row_size), out_shape=[array...  2.8 us
    ppermute x7, waiting for transfers between devices, swapped(): return lax.ppermute(block, axis, pairs + [(j, i) for i, j in pairs])  2.3 us
    pallas_call x1, Pallas kernels, per_device(): pl.pallas_call(functools.partial(rim_kernel, row_size), out_shape=[array(...  1.98 us
    pallas_call x1, Pallas kernels, per_device(): pl.pallas_call(functools.partial(inner_kernel, row_size), out_shape=[arra...  1.7 us
    pallas_call x1, Pallas kernels, per_device(): pl.pallas_call(functools.partial(outer_main_kernel, row_size), out_shape=...  1.37 us
  transfers between devices with their start and end apart: 7, of which 2 were waited for; matrix products, arithmetic and copies ran while one was open for 0% of the time, Pallas kernels for 14%

profile of v11, /device:TPU:0, one launch (start us, length us, event | category | flops | bytes accessed | tf_op | source)
XLA Modules:
  0.0 35.5 jit_solution(2467363730600296062)
XLA Ops:
  0.7 2.8 %pack.1 = (f32[7,4,8,128]{3,2,1,0:T(8,128)}, f32[7,2,4,8,128]{4,3,2,1,0:T(8,128)}, f32[2,4,8,128]{3,2,1,0:T(8,128)}, f32[2,4,8,128]{3,2,1,0:T(8,128)}, f32[26,4,8,128]{3,2,1,0:T(8,128)}) custom-call(f32[8]{0:T(128)} %eps_ref.1, f32[3,32,8,128]{3,2,1,0:T(8,128)} %elec_ref.1, f32[3,32,8,128]{3,2,1,0:T(8,128)} %magn_ref.1, s32[32,8,128]{2,1,0:T(8,128)} %mat_ref.1), custom_call_target="tpu_custom_call" | custom-call | tf_op jit(solution)/shard_map/pack/pallas_call | solution.py:751
  3.5 3.0 %collective-permute-start.4 = (f32[26,4,8,128]{3,2,1,0:T(8,128)}, f32[26,4,8,128]{3,2,1,0:T(8,128)S(1)}, u32[]{:S(2)}, u32[]{:S(2)}) collective-permute-start(f32[26,4,8,128]{3,2,1,0:T(8,128)} %get-tuple-element.38), channel_id=1, source_target_pairs={{0,2},{2,0},{1,3},{3,1},{4,6},{6,4},{5,7},{7,5},{8,10},{10,8},{9,1... | collective-permute-start | bytes 1277960 | tf_op jit(solution)/shard_map/ppermute | solution.py:727
  6.5 0.0 collective-permute-start
  6.5 0.0 copy-start.6
  6.5 0.0 copy-start.7
  6.5 1.6 %collective-permute-start.1 = (f32[2,4,8,128]{3,2,1,0:T(8,128)}, f32[2,4,8,128]{3,2,1,0:T(8,128)S(1)}, u32[]{:S(2)}, u32[]{:S(2)}) collective-permute-start(f32[2,4,8,128]{3,2,1,0:T(8,128)} %get-tuple-element.26), channel_id=1, source_target_pairs={{0,4},{8,12},{4,0},{12,8},{1,5},{9,13},{5,1},{13,9},{2,6},{10,14},... | collective-permute-start | bytes 98312 | tf_op jit(solution)/shard_map/ppermute | solution.py:727
  8.1 0.7 %collective-permute-start.2 = (f32[2,4,8,128]{3,2,1,0:T(8,128)}, f32[2,4,8,128]{3,2,1,0:T(8,128)S(1)}, u32[]{:S(2)}, u32[]{:S(2)}) collective-permute-start(f32[2,4,8,128]{3,2,1,0:T(8,128)} %get-tuple-element.27), channel_id=1, source_target_pairs={{4,8},{8,4},{5,9},{9,5},{6,10},{10,6},{7,11},{11,7},{20,24},{24,20... | collective-permute-start | bytes 98312 | tf_op jit(solution)/shard_map/ppermute | solution.py:727
  8.8 0.0 collective-permute-done.z_ref
  8.8 0.0 copy-done.2
  8.8 0.0 copy-done.1
  8.8 0.0 copy-done
  8.8 0.0 copy-done.8
  8.9 0.0 copy-done.9
  8.9 0.0 copy-done.5
  8.9 0.0 copy-start.4
  8.9 0.9 %copy-done.4 = f32[8,32,64]{2,1,0:T(8,128)S(1)} copy-done((f32[8,32,64]{2,1,0:T(8,128)S(1)}, f32[8,32,64]{2,1,0:T(8,128)}, u32[]{:S(2)}) %copy-start.4) | copy-done | bytes 65560
  9.8 1.7 %inner.1 = (f32[3,8,5,8,128]{4,3,2,1,0:T(8,128)S(1)}, f32[3,8,5,8,128]{4,3,2,1,0:T(8,128)S(1)}, f32[8,5,8,128]{3,2,1,0:T(8,128)S(1)}, f32[4,8,128]{2,1,0:T(8,128)S(1)}, f32[4,2,4,8,128]{4,3,2,1,0:T(8,128)S(1)}) custom-call(f32[3,32,8,128]{3,2,1,0:T(8,128)S(1)} %copy-done, f32[3,32,8,128]{3,2,1,0:T(8,128)S(1)} %copy-done.1, s32[32,8,128]{2,1,0:T(8,128)S(1)} %copy-done.2, ...), custom_call_target="tpu_custom_call" | custom-call | flops 5000000 | bytes 10000000 | tf_op jit(solution)/shard_map/inner/pallas_call | solution.py:785
  11.5 0.0 copy-start.3
  11.5 0.0 collective-permute-done.1.even_ref
  11.5 0.0 collective-permute-done.2.odd_ref
  11.6 0.3 collective-permute-start.3
  11.9 0.6 %collective-permute-start.5 = (f32[13,8,128]{2,1,0:T(8,128)S(1)}, f32[13,8,128]{2,1,0:T(8,128)S(1)}, u32[]{:S(2)}, u32[]{:S(2)}) collective-permute-start(f32[13,8,128]{2,1,0:T(8,128)S(1)} %layers.1), channel_id=1, source_target_pairs={{0,2},{2,0},{1,3},{3,1},{4,6},{6,4},{5,7},{7,5},{8,10},{10,8},{9,1... | collective-permute-start | bytes 159752 | tf_op jit(solution)/shard_map/ppermute | solution.py:727
  12.5 0.3 collective-permute-done.3.layer_ref
  12.8 1.2 %collective-permute-start.6 = (f32[10,8,128]{2,1,0:T(8,128)S(1)}, f32[10,8,128]{2,1,0:T(8,128)S(1)}, u32[]{:S(2)}, u32[]{:S(2)}) collective-permute-start(f32[10,8,128]{2,1,0:T(8,128)S(1)} %corners.1), channel_id=1, source_target_pairs={{0,2},{2,0},{1,3},{3,1},{4,6},{6,4},{5,7},{7,5},{8,10},{10,8},{9,1... | collective-permute-start | bytes 122888 | tf_op jit(solution)/shard_map/ppermute | solution.py:727
  14.1 2.0 %rim.1 = (f32[3,2,5,8,128]{4,3,2,1,0:T(8,128)S(1)}, f32[3,2,5,8,128]{4,3,2,1,0:T(8,128)S(1)}, f32[2,5,8,128]{3,2,1,0:T(8,128)S(1)}, f32[6,4,4,8,128]{4,3,2,1,0:T(8,128)S(1)}, f32[4,8,128]{2,1,0:T(8,128)S(1)}) custom-call(f32[7,4,8,128]{3,2,1,0:T(8,128)S(1)} %collective-permute-done.z_ref, f32[7,2,4,8,128]{4,3,2,1,0:T(8,128)S(1)} %copy-done.3, ...), custom_call_target="tpu_custom_call" | custom-call | tf_op jit(solution)/shard_map/rim/pallas_call | solution.py:826
  16.1 2.0 %collective-permute-done.5.rest_1_ = f32[13,8,128]{2,1,0:T(8,128)S(1)} collective-permute-done((f32[13,8,128]{2,1,0:T(8,128)S(1)}, f32[13,8,128]{2,1,0:T(8,128)S(1)}, u32[]{:S(2)}, u32[]{:S(2)}) %collective-permute-start.5) | collective-permute-done | bytes 53280 | tf_op jit(solution)/shard_map/ppermute | solution.py:727
  18.1 0.0 collective-permute-done.4.rest_0_
  18.1 1.4 %outer_main.1 = (f32[6,8,4,8,128]{4,3,2,1,0:T(8,128)S(1)}, f32[1,7,5,8,128]{4,3,2,1,0:T(8,128)S(1)}, f32[4,8,128]{2,1,0:T(8,128)S(1)}) custom-call(s32[1,1,4]{2,1,0:T(1,128)S(1)} %copy-done.5, f32[3,8,5,8,128]{4,3,2,1,0:T(8,128)S(1)} %get-tuple-element.29.e_in, f32[3,8,5,8,128]{4,3,2,1,0:T(8,128)S(1)} %get-tuple-element.30.h_in, ...), custom_call_target="tpu_custom_call" | custom-call | tf_op jit(solution)/shard_map/outer_main/pallas_call | solution.py:844
  19.4 0.0 collective-permute-done.6.rest_0_
  19.5 2.9 %outer_edge.1 = (f32[3,32,8,128]{3,2,1,0:T(8,128)}, f32[3,32,8,128]{3,2,1,0:T(8,128)}, f32[16,2,16]{2,1,0:T(2,128)S(1)}) custom-call(s32[1,1,4]{2,1,0:T(1,128)S(1)} %copy-done.5, s32[1,1,4]{2,1,0:T(1,128)S(1)} %copy-done.7, f32[3,2,5,8,128]{4,3,2,1,0:T(8,128)S(1)} %get-tuple-element.32.edge_e_in, f32[3,2,5,8,128]{4,3,2,1,0:T(8,128)S(1)} %get-tuple-element.33.edge_h_in, ...), custom_call_target="tpu_custom_call" | custom-call | tf_op jit(solution)/shard_map/outer_edge/pallas_call | solution.py:857
  22.4 12.5 %all_to_all.5 = f32[16,2,16]{2,1,0:T(2,128)S(1)} all-to-all(f32[16,2,16]{2,1,0:T(2,128)S(1)} %get-tuple-element.44), channel_id=1, replica_groups=mesh['grp'=2,'col'=4,'row'=2,'gz'=2] {'col','row','gz'}, dimensions={0} | all-to-all | bytes 4096 | tf_op jit(solution)/shard_map/all_to_all | solution.py:872
  34.9 0.6 %reduce_sum.9 = f32[2,16]{1,0:T(2,128)} reduce(f32[16,2,16]{2,1,0:T(2,128)S(1)} %all_to_all.5, f32[]{:T(128)} %constant.0.clone.1), dimensions={0}, to_apply=%region_0.0 | reduce | flops 480 | bytes 2180 | tf_op jit(solution)/shard_map/reduce_sum | solution.py:876
  (12 shorter events, 0.1 us)
Async XLA Ops:
  0.6 8.2 %copy-start.2 = (s32[32,8,128]{2,1,0:T(8,128)S(1)}, s32[32,8,128]{2,1,0:T(8,128)}, u32[]{:S(2)}) copy-start(s32[32,8,128]{2,1,0:T(8,128)} %mat_ref.1) | copy-start | bytes 393220
  0.6 8.2 %copy-start.1 = (f32[3,32,8,128]{3,2,1,0:T(8,128)S(1)}, f32[3,32,8,128]{3,2,1,0:T(8,128)}, u32[]{:S(2)}) copy-start(f32[3,32,8,128]{3,2,1,0:T(8,128)} %magn_ref.1) | copy-start | bytes 1179652
  0.7 8.2 %copy-start = (f32[3,32,8,128]{3,2,1,0:T(8,128)S(1)}, f32[3,32,8,128]{3,2,1,0:T(8,128)}, u32[]{:S(2)}) copy-start(f32[3,32,8,128]{3,2,1,0:T(8,128)} %elec_ref.1) | copy-start | bytes 1179652
  3.5 14.6 %collective-permute-start.4 = (f32[26,4,8,128]{3,2,1,0:T(8,128)}, f32[26,4,8,128]{3,2,1,0:T(8,128)S(1)}, u32[]{:S(2)}, u32[]{:S(2)}) collective-permute-start(f32[26,4,8,128]{3,2,1,0:T(8,128)} %get-tuple-element.38), channel_id=1, source_target_pairs={{0,2},{2,0},{1,3},{3,1},{4,6},{6,4},{5,7},{7,5},{8,10},{10,8},{9,1... | collective-permute-start | bytes 1277960 | tf_op jit(solution)/shard_map/ppermute | solution.py:727
  6.5 2.3 %collective-permute-start = (f32[7,4,8,128]{3,2,1,0:T(8,128)}, f32[7,4,8,128]{3,2,1,0:T(8,128)S(1)}, u32[]{:S(2)}, u32[]{:S(2)}) collective-permute-start(f32[7,4,8,128]{3,2,1,0:T(8,128)} %get-tuple-element.24), channel_id=1, source_target_pairs={{0,1},{1,0},{2,3},{3,2},{4,5},{5,4},{6,7},{7,6},{8,9},{9,8},{10,11... | collective-permute-start | bytes 344072 | tf_op jit(solution)/shard_map/ppermute | solution.py:727
  6.5 2.4 %copy-start.8 = (s32[1,1,4]{2,1,0:T(1,128)S(1)}, s32[1,1,4]{2,1,0:T(1,128)}, u32[]{:S(2)}) copy-start(s32[1,1,4]{2,1,0:T(1,128)} %pcol_ref.1) | copy-start | bytes 52
  6.5 2.4 %copy-start.9 = (s32[1,1,4]{2,1,0:T(1,128)S(1)}, s32[1,1,4]{2,1,0:T(1,128)}, u32[]{:S(2)}) copy-start(s32[1,1,4]{2,1,0:T(1,128)} %pmode_ref.1) | copy-start | bytes 52
  6.5 2.4 %copy-start.5 = (s32[1,1,4]{2,1,0:T(1,128)S(1)}, s32[1,1,4]{2,1,0:T(1,128)}, u32[]{:S(2)}) copy-start(s32[1,1,4]{2,1,0:T(1,128)} %prow_ref.7) | copy-start | bytes 52
  6.5 2.4 %copy-start.6 = (f32[8]{0:T(128)S(1)}, f32[8]{0:T(128)}, u32[]{:S(2)}) copy-start(f32[8]{0:T(128)} %eps_ref.1) | copy-start | bytes 100
  6.5 2.4 %copy-start.7 = (s32[1,1,4]{2,1,0:T(1,128)S(1)}, s32[1,1,4]{2,1,0:T(1,128)}, u32[]{:S(2)}) copy-start(s32[1,1,4]{2,1,0:T(1,128)} %pid_ref.3) | copy-start | bytes 52
  6.5 5.0 %collective-permute-start.1 = (f32[2,4,8,128]{3,2,1,0:T(8,128)}, f32[2,4,8,128]{3,2,1,0:T(8,128)S(1)}, u32[]{:S(2)}, u32[]{:S(2)}) collective-permute-start(f32[2,4,8,128]{3,2,1,0:T(8,128)} %get-tuple-element.26), channel_id=1, source_target_pairs={{0,4},{8,12},{4,0},{12,8},{1,5},{9,13},{5,1},{13,9},{2,6},{10,14},... | collective-permute-start | bytes 98312 | tf_op jit(solution)/shard_map/ppermute | solution.py:727
  8.1 3.4 %collective-permute-start.2 = (f32[2,4,8,128]{3,2,1,0:T(8,128)}, f32[2,4,8,128]{3,2,1,0:T(8,128)S(1)}, u32[]{:S(2)}, u32[]{:S(2)}) collective-permute-start(f32[2,4,8,128]{3,2,1,0:T(8,128)} %get-tuple-element.27), channel_id=1, source_target_pairs={{4,8},{8,4},{5,9},{9,5},{6,10},{10,6},{7,11},{11,7},{20,24},{24,20... | collective-permute-start | bytes 98312 | tf_op jit(solution)/shard_map/ppermute | solution.py:727
  8.9 0.9 %copy-start.4 = (f32[8,32,64]{2,1,0:T(8,128)S(1)}, f32[8,32,64]{2,1,0:T(8,128)}, u32[]{:S(2)}) copy-start(f32[8,32,64]{2,1,0:T(8,128)} %mode_ref.1) | copy-start | bytes 196612
  11.5 2.6 %copy-start.3 = (f32[7,2,4,8,128]{4,3,2,1,0:T(8,128)S(1)}, f32[7,2,4,8,128]{4,3,2,1,0:T(8,128)}, u32[]{:S(2)}) copy-start(f32[7,2,4,8,128]{4,3,2,1,0:T(8,128)} %get-tuple-element.25.own_ref) | copy-start | bytes 688132
  11.6 1.2 %collective-permute-start.3 = (f32[2,2,8,128]{3,2,1,0:T(8,128)S(1)}, f32[2,2,8,128]{3,2,1,0:T(8,128)S(1)}, u32[]{:S(2)}, u32[]{:S(2)}) collective-permute-start(f32[2,2,8,128]{3,2,1,0:T(8,128)S(1)} %layer_edges.1), channel_id=1, source_target_pairs={{0,1},{1,0},{2,3},{3,2},{4,5},{5,4},{6,7},{7,6},{8,9},{9,8},{10,11... | collective-permute-start | bytes 49160 | tf_op jit(solution)/shard_map/ppermute | solution.py:727
  11.9 6.2 %collective-permute-start.5 = (f32[13,8,128]{2,1,0:T(8,128)S(1)}, f32[13,8,128]{2,1,0:T(8,128)S(1)}, u32[]{:S(2)}, u32[]{:S(2)}) collective-permute-start(f32[13,8,128]{2,1,0:T(8,128)S(1)} %layers.1), channel_id=1, source_target_pairs={{0,2},{2,0},{1,3},{3,1},{4,6},{6,4},{5,7},{7,5},{8,10},{10,8},{9,1... | collective-permute-start | bytes 159752 | tf_op jit(solution)/shard_map/ppermute | solution.py:727
  12.8 6.6 %collective-permute-start.6 = (f32[10,8,128]{2,1,0:T(8,128)S(1)}, f32[10,8,128]{2,1,0:T(8,128)S(1)}, u32[]{:S(2)}, u32[]{:S(2)}) collective-permute-start(f32[10,8,128]{2,1,0:T(8,128)S(1)} %corners.1), channel_id=1, source_target_pairs={{0,2},{2,0},{1,3},{3,1},{4,6},{6,4},{5,7},{7,5},{8,10},{10,8},{9,1... | collective-permute-start | bytes 122888 | tf_op jit(solution)/shard_map/ppermute | solution.py:727

commit v12 on v10

--- a/solution.py
+++ b/solution.py
@@ -31,6 +31,7 @@
 VMEM = pl.BlockSpec(memory_space=pltpu.VMEM)
 SMEM = pl.BlockSpec(memory_space=pltpu.SMEM)
 HBM = pl.BlockSpec(memory_space=pltpu.HBM)
+ANY = pl.BlockSpec(memory_space=pl.ANY)
 PARAMS = pltpu.CompilerParams(vmem_limit_bytes=16 * 1024 * 1024)
 
 
@@ -62,8 +63,20 @@
         body(False, 1)
 
 
-def pack_kernel(row_size, eps_hbm, elec_hbm, magn_hbm, mat_hbm, state_ref, z_ref, own_ref, even_ref, odd_ref, *rest):
-    x_refs, (main_ref, eps_ref, mat_ref, sems) = rest[:-4], rest[-4:]
+def coefficient(material, eps_ref):
+    eps = jnp.full((8, 128), eps_ref[0], jnp.float32)
+    for which in range(1, MATS):
+        eps = jnp.where(material == which, eps_ref[which], eps)
+    return time_step * (1.0 / eps)
+
+
+def rows_outside(flat, f, state_ref, at):
+    for x in range(ROWS):
+        state_ref[at, x] = flat[pl.ds(f * LAYERS * ROWS + x, LAYERS, stride=ROWS), :].reshape(OWN, 8, 128)
+
+
+def pack_kernel(row_size, eps_hbm, elec_hbm, magn_hbm, mat_hbm, z_ref, own_ref, even_ref, odd_ref, *rest):
+    x_refs, (state_ref, main_ref, eps_ref, mat_ref, sems) = rest[:-5], rest[-5:]
     copies = [pltpu.make_async_copy(eps_hbm, eps_ref, sems.at[0]), pltpu.make_async_copy(mat_hbm, mat_ref, sems.at[1])]
     copies.append(pltpu.make_async_copy(elec_hbm, main_ref.at[pl.ds(0, 3)], sems.at[2]))
     copies.append(pltpu.make_async_copy(magn_hbm, main_ref.at[pl.ds(3, 3)], sems.at[3]))
@@ -72,21 +85,15 @@
     copies[0].wait()
     copies[1].wait()
     for z in range(LAYERS):
-        material = mat_ref[z]
-        eps = jnp.full((8, 128), eps_ref[0], jnp.float32)
-        for which in range(1, MATS):
-            eps = jnp.where(material == which, eps_ref[which], eps)
-        main_ref[6, z] = time_step * (1.0 / eps)
+        main_ref[6, z] = coefficient(mat_ref[z], eps_ref)
     copies[2].wait()
     copies[3].wait()
     start = jnp.where(lax.axis_index("gz") == 0, LAYERS - DEPTH, 0)
     for f in range(FIELDS):
         z_ref[f] = main_ref[f, pl.ds(start, DEPTH)]
-    block = LAYERS * ROWS
-    flat = main_ref.reshape(FIELDS * block, 128)
+    flat = main_ref.reshape(FIELDS * LAYERS * ROWS, 128)
     for f in range(FIELDS):
-        for x in range(ROWS):
-            state_ref[f, x] = flat[pl.ds(f * block + x, LAYERS, stride=ROWS), :].reshape(OWN, 8, 128)
+        rows_outside(flat, f, state_ref, f)
 
     def send(up, slot):
         for i, (f, x) in enumerate(UP_PLANES if up else DOWN_PLANES):
@@ -171,7 +178,7 @@
         ext_ref[f, DEPTH * ROWS :] = jnp.where(gz == 0, nothing, halo)
 
 
-def corner_kernel(row_size, z_ref, even_ref, odd_ref, layer_ref, *rest):
+def corner_kernel(row_size, weight_ref, z_ref, even_ref, odd_ref, layer_ref, *rest):
     x_refs, ext_ref = rest[:-1], rest[-1]
     gz = lax.axis_index("gz")
     valid = (iota(0) < 4) == (gz == 0)
@@ -228,7 +235,7 @@
     def put(self, f, i, zz, tile):
         self.values[f, i, zz] = tile
         at = i - self.shift
-        if f == 2 and zz < OWN and 0 <= at < self.ez_ref.shape[0]:
+        if f == 2 and zz < OWN and self.ez_ref is not None and 0 <= at < self.ez_ref.shape[0]:
             self.ez_ref[at, zz] = tile
 
 
@@ -454,7 +461,7 @@
     staged(fields, first, second)
 
 
-def port_weights(mode_ref, prow_ref, pcol_ref, pmode_ref, weight_ref, strip_ref):
+def weight_kernel(mode_ref, prow_ref, pcol_ref, pmode_ref, pid_ref, order_ref, weight_ref, strip_ref):
     lane = iota(1)
     for k in range(PORT_TILE):
         strip_ref[k] = jnp.zeros(strip_ref.shape[1:], jnp.float32)
@@ -470,31 +477,35 @@
             weight_ref[k, 1, zz] = jnp.where((at >= 16) & (at < 20), turn(own, 8, 1), edge)
 
 
+def after_kernel(order_ref, value_ref, out_ref):
+    out_ref[...] = value_ref[...]
+
+
 def inner_kernel(
-    row_size, state_ref, z_ref, mode_ref, prow_ref, pcol_ref, pmode_ref, pid_ref,
-    e_ref, h_ref, c_ref, sum_ref, weight_ref, ext_ref, halo_ref, ez_ref, strip_ref,
+    row_size, elec_ref, magn_ref, mat_ref, z_ref, eps_ref,
+    e_ref, h_ref, c_ref, ez_ref, state_ref, plain_ref, ext_ref, halo_ref,
 ):
     gz, row = lax.axis_index("gz"), lax.axis_index("row")
     spread_layers(gz, z_ref, ext_ref)
     for f in range(FIELDS):
         for x in range(ROWS):
             halo_ref[f, x] = ext_ref[f, pl.ds(x, 8, stride=ROWS), :]
-    port_weights(mode_ref, prow_ref, pcol_ref, pmode_ref, weight_ref, strip_ref)
+    for z in range(LAYERS):
+        plain_ref[z] = coefficient(mat_ref[z], eps_ref)
+    for f in range(3):
+        rows_outside(elec_ref.reshape(3 * LAYERS * ROWS, 128), f, state_ref, f)
+        rows_outside(magn_ref.reshape(3 * LAYERS * ROWS, 128), f, state_ref, f + 3)
+    rows_outside(plain_ref.reshape(LAYERS * ROWS, 128), 0, state_ref, 6)
 
     def first(f, i, zz):
         return halo_ref[f, i - DEPTH] if zz == OWN else state_ref[f, i - DEPTH, zz]
 
     def run(has_below, has_above):
-        main = Tiles(first, ez_ref, DEPTH)
+        main = Tiles(first, None, DEPTH)
         stepper = Stepper(row_size, main, None, range(4, 12), (), False)
-
-        def reached(n, at):
-            low, high = spans_inner(n, has_below, has_above)[1]
-            return (at >= low) & (at <= high)
-
         for n in range(1, STEPS + 1):
+            main.ez_ref = ez_ref.at[n - 1]
             stepper.step(n, [spans_inner(n, has_below, has_above)])
-            port_sums(n, reached, prow_ref, weight_ref, ez_ref, None, sum_ref, None)
         for i in range(ROWS):
             for zz in range(CHUNK):
                 for f in range(6):
@@ -505,7 +516,7 @@
 
 
 def rim_kernel(
-    row_size, z_ref, own_ref, even_ref, odd_ref, layer_ref, e_in, h_in, sum_in, weight_ref, prow_ref,
+    row_size, z_ref, own_ref, even_ref, odd_ref, layer_ref, e_in, h_in, ez_in, weight_ref, prow_ref,
     edge_e_ref, edge_h_ref, edge_c_ref, done_ref, sum_ref, ext_ref, ez_ref,
 ):
     gz, row = lax.axis_index("gz"), lax.axis_index("row")
@@ -542,7 +553,7 @@
 
         for n in range(1, STEPS + 1):
             stepper.step(n, [spans_inner(n, has_below, has_above)])
-            port_sums(n, reached, prow_ref, weight_ref, None, ez_ref, sum_ref, sum_in)
+            port_sums(n, reached, prow_ref, weight_ref, ez_in.at[n - 1], ez_ref, sum_ref, None)
         for i in range(2):
             for zz in range(CHUNK):
                 for f in range(6):
@@ -699,10 +710,9 @@
         def scratch(*shape):
             return pltpu.VMEM(shape, f32)
 
-        state, z_send, own, even_send, odd_send, *x_send = pl.pallas_call(
+        z_send, own, even_send, odd_send, *x_send = pl.pallas_call(
             functools.partial(pack_kernel, row_size),
             out_shape=[
-                array(FIELDS, ROWS, OWN, 8, 128),
                 array(FIELDS, DEPTH, ROWS, 128),
                 array(FIELDS, 2, OWN, 8, 128),
                 array(2, OWN, 8, 128),
@@ -710,8 +720,9 @@
             ]
             + [array(PLANES, OWN, 8, 128)] * n_x,
             in_specs=[HBM] * 4,
-            out_specs=[VMEM] * (5 + n_x),
+            out_specs=[VMEM] * (4 + n_x),
             scratch_shapes=[
+                scratch(FIELDS, ROWS, OWN, 8, 128),
                 scratch(FIELDS, LAYERS, ROWS, 128),
                 pltpu.SMEM(eps_table.shape, f32),
                 pltpu.VMEM(material.shape, jnp.int32),
@@ -721,29 +732,36 @@
         )(eps_table, electric, magnetic, material)
         x_halo = across_rows(x_send)
         even = swapped(even_send, "col", col_size)
-        odd = swapped(odd_send, "col", col_size, 1)
         z_halo = swapped(z_send, "gz", gz_size)
-        e_now, h_now, c_now, sums, weights = pl.pallas_call(
+        e_now, h_now, c_now, ez_now = pl.pallas_call(
             functools.partial(inner_kernel, row_size),
             out_shape=[
                 array(3, ROWS, CHUNK, 8, 128),
                 array(3, ROWS, CHUNK, 8, 128),
                 array(ROWS, CHUNK, 8, 128),
-                array(STEPS, 8, 128),
-                array(PORT_TILE, 2, OWN, 8, 128),
+                array(STEPS, ROWS, OWN, 8, 128),
             ],
-            in_specs=[VMEM] * 3 + [SMEM] * 4,
-            out_specs=[VMEM] * 5,
+            in_specs=[VMEM] * 4 + [SMEM],
+            out_specs=[VMEM] * 4,
             scratch_shapes=[
+                scratch(FIELDS, ROWS, OWN, 8, 128),
+                scratch(LAYERS, ROWS, 128),
                 scratch(FIELDS, 8 * ROWS, 128),
                 scratch(FIELDS, ROWS, 8, 128),
-                scratch(ROWS, OWN, 8, 128),
-                scratch(PORT_TILE, LAYERS, 128),
             ],
             compiler_params=PARAMS,
             cost_estimate=pl.CostEstimate(flops=5_000_000, bytes_accessed=10_000_000, transcendentals=0),
             name="inner",
-        )(state, z_halo, mode_table, port_row, port_col, port_mode, port_ids)
+        )(electric, magnetic, material, z_halo, eps_table)
+        odd_send = pl.pallas_call(
+            after_kernel,
+            out_shape=array(2, OWN, 8, 128),
+            in_specs=[ANY, VMEM],
+            out_specs=VMEM,
+            compiler_params=PARAMS,
+            name="after_inner",
+        )(c_now, odd_send)
+        odd = swapped(odd_send, "col", col_size, 1)
         layer_send = pl.pallas_call(
             layer_edge_kernel,
             out_shape=array(2, 2, 8, 128),
@@ -751,17 +769,26 @@
             out_specs=VMEM,
             compiler_params=PARAMS,
             name="layer_edges",
-        )(even, odd, sums)
+        )(even, odd, c_now)
         layer_halo = swapped(layer_send, "gz", gz_size)
+        weights = pl.pallas_call(
+            weight_kernel,
+            out_shape=array(PORT_TILE, 2, OWN, 8, 128),
+            in_specs=[VMEM] + [SMEM] * 4 + [ANY],
+            out_specs=VMEM,
+            scratch_shapes=[scratch(PORT_TILE, LAYERS, 128)],
+            compiler_params=PARAMS,
+            name="weights",
+        )(mode_table, port_row, port_col, port_mode, port_ids, layer_send)
         corner_send = pl.pallas_call(
             functools.partial(corner_kernel, row_size),
             out_shape=[array(PAIRS + 2 * CHUNK, 8, 128)] * n_x,
-            in_specs=[VMEM] * 4,
+            in_specs=[ANY] + [VMEM] * 4,
             out_specs=[VMEM] * n_x,
             scratch_shapes=[scratch(FIELDS, 8 * ROWS, 128)],
             compiler_params=PARAMS,
             name="corners",
-        )(z_halo, even, odd, layer_halo)
+        )(weights, z_halo, even, odd, layer_halo)
         corner = across_rows(corner_send)
         edges = pl.pallas_call(
             functools.partial(rim_kernel, row_size),
@@ -777,7 +804,7 @@
             scratch_shapes=[scratch(FIELDS, 8 * ROWS, 128), scratch(2, OWN, 8, 128)],
             compiler_params=PARAMS,
             name="rim",
-        )(z_halo, own, even, odd, layer_halo, e_now, h_now, sums, weights, port_row)
+        )(z_halo, own, even, odd, layer_halo, e_now, h_now, ez_now, weights, port_row)
         devices = col_size * row_size * gz_size
         ports_each = PORT_TILE * col_size * row_size // devices
         electric_out, magnetic_out, term = pl.pallas_call(

time: 35.3 us -> 36.2 us (1.025)
  local copies, waits for them, and re-layouts: 1.2 us -> 0.17 us
  blocking collectives: 12.5 us -> 13.5 us
  Pallas kernels: 9.81 us -> 10.5 us
    all_to_all x1, blocking collectives: 12.5 us -> 13.5 us  [per_device(): terms = lax.all_to_all(term, ('col', 'row', 'gz'), 0, 0, tiled=True)]
    unnamed x14 -> x22, local copies, waits for them, and re-layouts: 1.2 us -> 0.17 us
    pallas_call x0 -> x2, Pallas kernels: none -> 0.79 us  [the longest x1 0.79 us: per_device(): pl.pallas_call(weight_kernel, out_shape=array(PORT_TILE, 2, OWN, 8, 128),...]
  transfers between devices with their start and end apart: 6 -> 6, of which waited for: 2 -> 3; matrix products, arithmetic and copies ran while one was open for 0% -> 0% of each run, Pallas kernels for 10% -> 12%
where the time goes in v12:
time: 36.2 us; the launch traced here: 36 us
  blocking collectives  13.5 us (37%)
  Pallas kernels  10.5 us (29%)
  starting transfers between devices  6.19 us (17%)
  waiting for transfers between devices  4.16 us (11%)
  between operations  0.82 us (2%)
  other arithmetic  0.59 us (2%)
    all_to_all x1, blocking collectives, per_device(): terms = lax.all_to_all(term, ('col', 'row', 'gz'), 0, 0, tiled=True)  13.5 us
    ppermute x6, starting transfers between devices, swapped(): return lax.ppermute(block, axis, pairs + [(j, i) for i, j in pairs])  6.19 us
    ppermute x6, waiting for transfers between devices, swapped(): return lax.ppermute(block, axis, pairs + [(j, i) for i, j in pairs])  4.16 us
    pallas_call x1, Pallas kernels, per_device(): pl.pallas_call(functools.partial(outer_kernel, row_size, ports_each), out...  3.31 us
    pallas_call x1, Pallas kernels, per_device(): pl.pallas_call(functools.partial(pack_kernel, row_size), out_shape=[array...  2.8 us
    pallas_call x1, Pallas kernels, per_device(): pl.pallas_call(functools.partial(rim_kernel, row_size), out_shape=[array(...  2.01 us
    pallas_call x1, Pallas kernels, per_device(): pl.pallas_call(functools.partial(inner_kernel, row_size), out_shape=[arra...  1.54 us
    pallas_call x1, Pallas kernels, per_device(): pl.pallas_call(weight_kernel, out_shape=array(PORT_TILE, 2, OWN, 8, 128),...  0.79 us
  transfers between devices with their start and end apart: 6, of which 3 were waited for; matrix products, arithmetic and copies ran while one was open for 0% of the time, Pallas kernels for 12%

profile of v12, /device:TPU:0, one launch (start us, length us, event | category | flops | bytes accessed | tf_op | source)
XLA Modules:
  0.0 36.0 jit_solution(5033818719329416039)
XLA Ops:
  0.6 0.0 copy-start.2
  0.6 0.0 copy-start.1
  0.7 0.0 copy-start
  0.7 2.8 %pack.1 = (f32[7,4,8,128]{3,2,1,0:T(8,128)}, f32[7,2,4,8,128]{4,3,2,1,0:T(8,128)}, f32[2,4,8,128]{3,2,1,0:T(8,128)}, f32[2,4,8,128]{3,2,1,0:T(8,128)}, f32[26,4,8,128]{3,2,1,0:T(8,128)}) custom-call(f32[8]{0:T(128)} %eps_ref.1, f32[3,32,8,128]{3,2,1,0:T(8,128)} %elec_ref.1, f32[3,32,8,128]{3,2,1,0:T(8,128)} %magn_ref.1, s32[32,8,128]{2,1,0:T(8,128)} %mat_ref.1), custom_call_target="tpu_custom_call" | custom-call | tf_op jit(solution)/shard_map/pack/pallas_call | solution.py:713
  3.5 3.0 %collective-permute-start.4 = (f32[26,4,8,128]{3,2,1,0:T(8,128)}, f32[26,4,8,128]{3,2,1,0:T(8,128)S(1)}, u32[]{:S(2)}, u32[]{:S(2)}) collective-permute-start(f32[26,4,8,128]{3,2,1,0:T(8,128)} %get-tuple-element.33), channel_id=1, source_target_pairs={{0,2},{2,0},{1,3},{3,1},{4,6},{6,4},{5,7},{7,5},{8,10},{10,8},{9,1... | collective-permute-start | bytes 1277960 | tf_op jit(solution)/shard_map/ppermute | solution.py:689
  6.5 0.0 collective-permute-start
  6.5 1.6 %collective-permute-start.1 = (f32[2,4,8,128]{3,2,1,0:T(8,128)}, f32[2,4,8,128]{3,2,1,0:T(8,128)S(1)}, u32[]{:S(2)}, u32[]{:S(2)}) collective-permute-start(f32[2,4,8,128]{3,2,1,0:T(8,128)} %get-tuple-element.24), channel_id=1, source_target_pairs={{0,4},{8,12},{4,0},{12,8},{1,5},{9,13},{5,1},{13,9},{2,6},{10,14},... | collective-permute-start | bytes 98312 | tf_op jit(solution)/shard_map/ppermute | solution.py:689
  8.1 0.0 collective-permute-done.z_ref
  8.1 0.0 copy-done
  8.1 0.0 copy-done.7
  8.1 1.5 %inner.1 = (f32[3,8,5,8,128]{4,3,2,1,0:T(8,128)S(1)}, f32[3,8,5,8,128]{4,3,2,1,0:T(8,128)S(1)}, f32[8,5,8,128]{3,2,1,0:T(8,128)S(1)}, f32[4,8,4,8,128]{4,3,2,1,0:T(8,128)S(1)}) custom-call(f32[3,32,8,128]{3,2,1,0:T(8,128)S(1)} %copy-done, f32[3,32,8,128]{3,2,1,0:T(8,128)S(1)} %copy-done.1, s32[32,8,128]{2,1,0:T(8,128)S(1)} %copy-done.2, ...), custom_call_target="tpu_custom_call" | custom-call | flops 5000000 | bytes 10000000 | tf_op jit(solution)/shard_map/inner/pallas_call | solution.py:736
  9.7 0.0 copy-start.4
  9.7 0.0 copy-start.6
  9.7 0.0 copy-start.8
  9.7 0.0 copy-start.9
  9.7 0.0 copy-start.10
  9.7 0.8 %collective-permute-start.2 = (f32[2,4,8,128]{3,2,1,0:T(8,128)S(1)}, f32[2,4,8,128]{3,2,1,0:T(8,128)S(1)}, u32[]{:S(2)}, u32[]{:S(2)}) collective-permute-start(f32[2,4,8,128]{3,2,1,0:T(8,128)S(1)} %after_inner.1), channel_id=1, source_target_pairs={{4,8},{8,4},{5,9},{9,5},{6,10},{10,6},{7,11},{11,7},{20,24},{24,20... | collective-permute-start | bytes 98312 | tf_op jit(solution)/shard_map/ppermute | solution.py:689
  10.5 0.1 collective-permute-done.1.even_ref
  10.6 0.0 collective-permute-done.2.odd_ref
  10.6 0.2 collective-permute-start.3
  10.9 0.0 copy-done.8
  10.9 0.8 %weights.1.weight_ref = f32[4,2,4,8,128]{4,3,2,1,0:T(8,128)S(1)} custom-call(f32[8,32,64]{2,1,0:T(8,128)S(1)} %copy-done.4, s32[1,1,4]{2,1,0:T(1,128)S(1)} %copy-done.6, s32[1,1,4]{2,1,0:T(1,128)S(1)} %copy-done.9, s32[1,1,4]{2,1,0:T(1,128)S(1)} %copy-done.10, s32[1,1,4]{2,1,0:T(1,128)S(1)} %copy-done.8, f32[2,2,8,128]{3,2,1,0:T(8,128)S(1)} %layer_edges.1.order_ref), custom_call_target="tpu_custom_call" | custom-call | tf_op jit(solution)/shard_map/weights/pallas_call | solution.py:774
  11.7 0.0 copy-start.3
  11.7 0.2 collective-permute-done.3.layer_ref
  11.9 0.6 %collective-permute-start.5 = (f32[23,8,128]{2,1,0:T(8,128)S(1)}, f32[23,8,128]{2,1,0:T(8,128)S(1)}, u32[]{:S(2)}, u32[]{:S(2)}) collective-permute-start(f32[23,8,128]{2,1,0:T(8,128)S(1)} %corners.1), channel_id=1, source_target_pairs={{0,2},{2,0},{1,3},{3,1},{4,6},{6,4},{5,7},{7,5},{8,10},{10,8},{9,1... | collective-permute-start | bytes 282632 | tf_op jit(solution)/shard_map/ppermute | solution.py:689
  12.5 0.1 copy-done.3
  12.6 2.0 %rim.1 = (f32[3,2,5,8,128]{4,3,2,1,0:T(8,128)S(1)}, f32[3,2,5,8,128]{4,3,2,1,0:T(8,128)S(1)}, f32[2,5,8,128]{3,2,1,0:T(8,128)S(1)}, f32[6,4,4,8,128]{4,3,2,1,0:T(8,128)S(1)}, f32[4,8,128]{2,1,0:T(8,128)S(1)}) custom-call(f32[7,4,8,128]{3,2,1,0:T(8,128)S(1)} %collective-permute-done.z_ref, f32[7,2,4,8,128]{4,3,2,1,0:T(8,128)S(1)} %copy-done.3, ...), custom_call_target="tpu_custom_call" | custom-call | tf_op jit(solution)/shard_map/rim/pallas_call | solution.py:793
  14.6 3.9 %collective-permute-done.5.rest_1_ = f32[23,8,128]{2,1,0:T(8,128)S(1)} collective-permute-done((f32[23,8,128]{2,1,0:T(8,128)S(1)}, f32[23,8,128]{2,1,0:T(8,128)S(1)}, u32[]{:S(2)}, u32[]{:S(2)}) %collective-permute-start.5) | collective-permute-done | bytes 94240 | tf_op jit(solution)/shard_map/ppermute | solution.py:689
  18.5 0.0 collective-permute-done.4.rest_0_
  18.5 3.3 %outer.1 = (f32[3,32,8,128]{3,2,1,0:T(8,128)}, f32[3,32,8,128]{3,2,1,0:T(8,128)}, f32[16,2,16]{2,1,0:T(2,128)S(1)}) custom-call(s32[1,1,4]{2,1,0:T(1,128)S(1)} %copy-done.6, s32[1,1,4]{2,1,0:T(1,128)S(1)} %copy-done.8, f32[3,8,5,8,128]{4,3,2,1,0:T(8,128)S(1)} %get-tuple-element.21.e_in, f32[3,8,5,8,128]{4,3,2,1,0:T(8,128)S(1)} %get-tuple-element.22.h_in, ...), custom_call_target="tpu_custom_call" | custom-call | tf_op jit(solution)/shard_map/outer/pallas_call | solution.py:810
  21.8 13.5 %all_to_all.5 = f32[16,2,16]{2,1,0:T(2,128)S(1)} all-to-all(f32[16,2,16]{2,1,0:T(2,128)S(1)} %get-tuple-element.36), channel_id=1, replica_groups=mesh['grp'=2,'col'=4,'row'=2,'gz'=2] {'col','row','gz'}, dimensions={0} | all-to-all | bytes 4096 | tf_op jit(solution)/shard_map/all_to_all | solution.py:826
  35.4 0.6 %reduce_sum.9 = f32[2,16]{1,0:T(2,128)} reduce(f32[16,2,16]{2,1,0:T(2,128)S(1)} %all_to_all.5, f32[]{:T(128)} %constant.0.clone.1), dimensions={0}, to_apply=%region_0.0 | reduce | flops 480 | bytes 2180 | tf_op jit(solution)/shard_map/reduce_sum | solution.py:830
  (12 shorter events, 0.1 us)
Async XLA Ops:
  0.6 7.4 %copy-start.2 = (s32[32,8,128]{2,1,0:T(8,128)S(1)}, s32[32,8,128]{2,1,0:T(8,128)}, u32[]{:S(2)}) copy-start(s32[32,8,128]{2,1,0:T(8,128)} %mat_ref.1) | copy-start | bytes 393220
  0.6 7.4 %copy-start.1 = (f32[3,32,8,128]{3,2,1,0:T(8,128)S(1)}, f32[3,32,8,128]{3,2,1,0:T(8,128)}, u32[]{:S(2)}) copy-start(f32[3,32,8,128]{3,2,1,0:T(8,128)} %magn_ref.1) | copy-start | bytes 1179652
  0.7 7.4 %copy-start = (f32[3,32,8,128]{3,2,1,0:T(8,128)S(1)}, f32[3,32,8,128]{3,2,1,0:T(8,128)}, u32[]{:S(2)}) copy-start(f32[3,32,8,128]{3,2,1,0:T(8,128)} %elec_ref.1) | copy-start | bytes 1179652
  3.5 15.1 %collective-permute-start.4 = (f32[26,4,8,128]{3,2,1,0:T(8,128)}, f32[26,4,8,128]{3,2,1,0:T(8,128)S(1)}, u32[]{:S(2)}, u32[]{:S(2)}) collective-permute-start(f32[26,4,8,128]{3,2,1,0:T(8,128)} %get-tuple-element.33), channel_id=1, source_target_pairs={{0,2},{2,0},{1,3},{3,1},{4,6},{6,4},{5,7},{7,5},{8,10},{10,8},{9,1... | collective-permute-start | bytes 1277960 | tf_op jit(solution)/shard_map/ppermute | solution.py:689
  6.5 1.6 %copy-start.7 = (f32[8]{0:T(128)S(1)}, f32[8]{0:T(128)}, u32[]{:S(2)}) copy-start(f32[8]{0:T(128)} %eps_ref.1) | copy-start | bytes 100
  6.5 1.6 %collective-permute-start = (f32[7,4,8,128]{3,2,1,0:T(8,128)}, f32[7,4,8,128]{3,2,1,0:T(8,128)S(1)}, u32[]{:S(2)}, u32[]{:S(2)}) collective-permute-start(f32[7,4,8,128]{3,2,1,0:T(8,128)} %get-tuple-element.20), channel_id=1, source_target_pairs={{0,1},{1,0},{2,3},{3,2},{4,5},{5,4},{6,7},{7,6},{8,9},{9,8},{10,11... | collective-permute-start | bytes 344072 | tf_op jit(solution)/shard_map/ppermute | solution.py:689
  6.5 3.2 %copy-start.5 = (f32[2,4,8,128]{3,2,1,0:T(8,128)S(1)}, f32[2,4,8,128]{3,2,1,0:T(8,128)}, u32[]{:S(2)}) copy-start(f32[2,4,8,128]{3,2,1,0:T(8,128)} %get-tuple-element.25.value_ref) | copy-start | bytes 98308
  6.5 4.1 %collective-permute-start.1 = (f32[2,4,8,128]{3,2,1,0:T(8,128)}, f32[2,4,8,128]{3,2,1,0:T(8,128)S(1)}, u32[]{:S(2)}, u32[]{:S(2)}) collective-permute-start(f32[2,4,8,128]{3,2,1,0:T(8,128)} %get-tuple-element.24), channel_id=1, source_target_pairs={{0,4},{8,12},{4,0},{12,8},{1,5},{9,13},{5,1},{13,9},{2,6},{10,14},... | collective-permute-start | bytes 98312 | tf_op jit(solution)/shard_map/ppermute | solution.py:689
  9.7 1.2 %copy-start.4 = (f32[8,32,64]{2,1,0:T(8,128)S(1)}, f32[8,32,64]{2,1,0:T(8,128)}, u32[]{:S(2)}) copy-start(f32[8,32,64]{2,1,0:T(8,128)} %mode_ref.1) | copy-start | bytes 196612
  9.7 1.2 %copy-start.6 = (s32[1,1,4]{2,1,0:T(1,128)S(1)}, s32[1,1,4]{2,1,0:T(1,128)}, u32[]{:S(2)}) copy-start(s32[1,1,4]{2,1,0:T(1,128)} %prow_ref.5) | copy-start | bytes 52
  9.7 1.2 %copy-start.8 = (s32[1,1,4]{2,1,0:T(1,128)S(1)}, s32[1,1,4]{2,1,0:T(1,128)}, u32[]{:S(2)}) copy-start(s32[1,1,4]{2,1,0:T(1,128)} %pid_ref.3) | copy-start | bytes 52
  9.7 1.2 %copy-start.9 = (s32[1,1,4]{2,1,0:T(1,128)S(1)}, s32[1,1,4]{2,1,0:T(1,128)}, u32[]{:S(2)}) copy-start(s32[1,1,4]{2,1,0:T(1,128)} %pcol_ref.1) | copy-start | bytes 52
  9.7 1.2 %copy-start.10 = (s32[1,1,4]{2,1,0:T(1,128)S(1)}, s32[1,1,4]{2,1,0:T(1,128)}, u32[]{:S(2)}) copy-start(s32[1,1,4]{2,1,0:T(1,128)} %pmode_ref.1) | copy-start | bytes 52
  9.7 0.9 %collective-permute-start.2 = (f32[2,4,8,128]{3,2,1,0:T(8,128)S(1)}, f32[2,4,8,128]{3,2,1,0:T(8,128)S(1)}, u32[]{:S(2)}, u32[]{:S(2)}) collective-permute-start(f32[2,4,8,128]{3,2,1,0:T(8,128)S(1)} %after_inner.1), channel_id=1, source_target_pairs={{4,8},{8,4},{5,9},{9,5},{6,10},{10,6},{7,11},{11,7},{20,24},{24,20... | collective-permute-start | bytes 98312 | tf_op jit(solution)/shard_map/ppermute | solution.py:689
  10.6 1.2 %collective-permute-start.3 = (f32[2,2,8,128]{3,2,1,0:T(8,128)S(1)}, f32[2,2,8,128]{3,2,1,0:T(8,128)S(1)}, u32[]{:S(2)}, u32[]{:S(2)}) collective-permute-start(f32[2,2,8,128]{3,2,1,0:T(8,128)S(1)} %layer_edges.1.order_ref), channel_id=1, source_target_pairs={{0,1},{1,0},{2,3},{3,2},{4,5},{5,4},{6,7},{7,6},{8,9},{9,8},{10,11... | collective-permute-start | bytes 49160 | tf_op jit(solution)/shard_map/ppermute | solution.py:689
  11.7 0.9 %copy-start.3 = (f32[7,2,4,8,128]{4,3,2,1,0:T(8,128)S(1)}, f32[7,2,4,8,128]{4,3,2,1,0:T(8,128)}, u32[]{:S(2)}) copy-start(f32[7,2,4,8,128]{4,3,2,1,0:T(8,128)} %get-tuple-element.26.own_ref) | copy-start | bytes 688132
  11.9 6.6 %collective-permute-start.5 = (f32[23,8,128]{2,1,0:T(8,128)S(1)}, f32[23,8,128]{2,1,0:T(8,128)S(1)}, u32[]{:S(2)}, u32[]{:S(2)}) collective-permute-start(f32[23,8,128]{2,1,0:T(8,128)S(1)} %corners.1), channel_id=1, source_target_pairs={{0,2},{2,0},{1,3},{3,1},{4,6},{6,4},{5,7},{7,5},{8,10},{10,8},{9,1... | collective-permute-start | bytes 282632 | tf_op jit(solution)/shard_map/ppermute | solution.py:689

commit v13 on v12

--- a/solution.py
+++ b/solution.py
@@ -390,7 +390,7 @@
     def edge_c(self, i, span):
         return self.masked([self.edge.get(6, i, zz) for zz in range(CHUNK)], i - 1, span)
 
-    def step(self, n, spans):
+    def step(self, n, spans, between=None):
         def blocks_of(span):
             return [b + 1 for b in range(-1, 3) if span[0] <= 4 * b + 3 and span[1] >= 4 * b]
 
@@ -415,6 +415,8 @@
             )
         for part in parts:
             next(part)
+        if between is not None:
+            between()
         for part in parts:
             next(part, None)
 
@@ -475,10 +477,6 @@
             own = pltpu.roll(tile, turned + 8, 1)
             edge = jnp.where((at >= 4) & (at < 8), own, 0.0)
             weight_ref[k, 1, zz] = jnp.where((at >= 16) & (at < 20), turn(own, 8, 1), edge)
-
-
-def after_kernel(order_ref, value_ref, out_ref):
-    out_ref[...] = value_ref[...]
 
 
 def inner_kernel(
@@ -593,6 +591,20 @@
             return edge_c_in[i - 1, zz]
         return edge_e_in[f, i - 1, zz] if f < 3 else edge_h_in[f - 3, i - 1, zz]
 
+    def write_terms():
+        basis = zeros
+        for n in range(STEPS):
+            for f in range(2 * FREQ):
+                basis = jnp.where((sub == n) & (lane == f), float(BASIS[n, f]), basis)
+        transform = zeros
+        for n in range(STEPS):
+            sampled = jnp.sum(sum_ref[n], axis=1, keepdims=True)
+            transform = transform + sampled * basis[n : n + 1, :]
+        term_ref[...] = jnp.zeros(term_ref.shape, jnp.float32)
+        for k in range(PORT_TILE):
+            port = pid_ref[0, 0, k]
+            term_ref[port // ports_each, pl.ds(port % ports_each, 1), :] = transform[k : k + 1, : 2 * FREQ]
+
     def run(has_below, has_above):
         main = Tiles(first_main, ez_ref, DEPTH)
         edge = Tiles(first_edge, edge_ez_ref, 1)
@@ -635,48 +647,42 @@
 
         rows = range(0 if has_below else 4, 16 if has_above else 12)
         blocks = range(0 if has_below else 1, 4 if has_above else 3)
+        copies = []
+
+        def hand_out(part):
+            fields = range(3 * part, 3 * part + 3)
+
+            def write(f, r, zz, tile, b):
+                turned_ref[f, 4 * b + r, 8 * zz : 8 * zz + 8, :] = tile
+
+            for b in range(2):
+                put = functools.partial(write, b=b)
+                if has_below and has_above or b == (1 if has_above else 0):
+                    finish(fields, b, main, edge, put)
+                else:
+                    for f in fields:
+                        for r in range(4):
+                            for zz in range(OWN):
+                                put(f, r, zz, done_ref[f, r, zz])
+            flat = turned_ref.reshape(6 * ROWS * LAYERS, 128)
+            for f in fields:
+                for z in range(LAYERS):
+                    out_ref[f, z] = flat[pl.ds(f * ROWS * LAYERS + z, ROWS, stride=LAYERS), :]
+            dest = hout_hbm if part else eout_hbm
+            copies.append(pltpu.make_async_copy(out_ref.at[pl.ds(3 * part, 3)], dest, sems.at[part]))
+            copies[-1].start()
+
         stepper = Stepper(row_size, main, edge, rows, blocks, True)
         for n in range(1, STEPS + 1):
             spans = ([spans_below(n)] if has_below else []) + ([spans_above(n)] if has_above else [])
-            stepper.step(n, spans)
+            stepper.step(n, spans, functools.partial(hand_out, 1) if n == STEPS else None)
             port_sums(n, reached, prow_ref, weight_ref, ez_ref, edge_ez_ref, sum_ref, sum_in)
-        def write(f, r, zz, tile, b):
-            turned_ref[f, 4 * b + r, 8 * zz : 8 * zz + 8, :] = tile
-
-        for b in range(2):
-            put = functools.partial(write, b=b)
-            if has_below and has_above or b == (1 if has_above else 0):
-                finish(range(6), b, main, edge, put)
-            else:
-                for f in range(6):
-                    for r in range(4):
-                        for zz in range(OWN):
-                            put(f, r, zz, done_ref[f, r, zz])
+        hand_out(0)
+        write_terms()
+        for copy in copies:
+            copy.wait()
 
     rows_cases(row_size, row, run)
-
-    copies = []
-    flat = turned_ref.reshape(6 * ROWS * LAYERS, 128)
-    for part, dest in ((0, eout_hbm), (1, hout_hbm)):
-        for f in range(3 * part, 3 * part + 3):
-            for z in range(LAYERS):
-                out_ref[f, z] = flat[pl.ds(f * ROWS * LAYERS + z, ROWS, stride=LAYERS), :]
-        copies.append(pltpu.make_async_copy(out_ref.at[pl.ds(3 * part, 3)], dest, sems.at[part]))
-        copies[-1].start()
-    basis = zeros
-    for n in range(STEPS):
-        for f in range(2 * FREQ):
-            basis = jnp.where((sub == n) & (lane == f), float(BASIS[n, f]), basis)
-    transform = zeros
-    for n in range(STEPS):
-        sampled = jnp.sum(sum_ref[n], axis=1, keepdims=True)
-        transform = transform + sampled * basis[n : n + 1, :]
-    term_ref[...] = jnp.zeros(term_ref.shape, jnp.float32)
-    for k in range(PORT_TILE):
-        port = pid_ref[0, 0, k]
-        term_ref[port // ports_each, pl.ds(port % ports_each, 1), :] = transform[k : k + 1, : 2 * FREQ]
-    for copy in copies:
-        copy.wait()
 
 
 def shifted(block, axis, size, distance):
@@ -732,6 +738,7 @@
         )(eps_table, electric, magnetic, material)
         x_halo = across_rows(x_send)
         even = swapped(even_send, "col", col_size)
+        odd = swapped(odd_send, "col", col_size, 1)
         z_halo = swapped(z_send, "gz", gz_size)
         e_now, h_now, c_now, ez_now = pl.pallas_call(
             functools.partial(inner_kernel, row_size),
@@ -753,15 +760,6 @@
             cost_estimate=pl.CostEstimate(flops=5_000_000, bytes_accessed=10_000_000, transcendentals=0),
             name="inner",
         )(electric, magnetic, material, z_halo, eps_table)
-        odd_send = pl.pallas_call(
-            after_kernel,
-            out_shape=array(2, OWN, 8, 128),
-            in_specs=[ANY, VMEM],
-            out_specs=VMEM,
-            compiler_params=PARAMS,
-            name="after_inner",
-        )(c_now, odd_send)
-        odd = swapped(odd_send, "col", col_size, 1)
         layer_send = pl.pallas_call(
             layer_edge_kernel,
             out_shape=array(2, 2, 8, 128),

time: 36.2 us -> 35.1 us (0.970)
  blocking collectives: 13.5 us -> 12.5 us
  local copies, waits for them, and re-layouts: 0.17 us -> 0.94 us
  waiting for transfers between devices: 4.16 us -> 3.73 us
    all_to_all x1, blocking collectives: 13.5 us -> 12.5 us  [per_device(): terms = lax.all_to_all(term, ('col', 'row', 'gz'), 0, 0, tiled=True)]
    unnamed x22 -> x20, local copies, waits for them, and re-layouts: 0.17 us -> 0.94 us
    ppermute x6, waiting for transfers between devices: 4.16 us -> 3.73 us  [swapped(): return lax.ppermute(block, axis, pairs + [(j, i) for i, j in pairs])]
  transfers between devices with their start and end apart: 6 -> 6, of which waited for: 3 -> 2; matrix products, arithmetic and copies ran while one was open for 0% -> 0% of each run, Pallas kernels for 12% -> 13%
where the time goes in v13:
time: 35.1 us; the launch traced here: 34.8 us
  blocking collectives  12.5 us (36%)
  Pallas kernels  10.5 us (30%)
  starting transfers between devices  5.84 us (17%)
  waiting for transfers between devices  3.73 us (11%)
  local copies, waits for them, and re-layouts  0.94 us (3%)
  between operations  0.81 us (2%)
  other arithmetic  0.59 us (2%)
    all_to_all x1, blocking collectives, per_device(): terms = lax.all_to_all(term, ('col', 'row', 'gz'), 0, 0, tiled=True)  12.5 us
    ppermute x6, starting transfers between devices, swapped(): return lax.ppermute(block, axis, pairs + [(j, i) for i, j in pairs])  5.84 us
    ppermute x6, waiting for transfers between devices, swapped(): return lax.ppermute(block, axis, pairs + [(j, i) for i, j in pairs])  3.73 us
    pallas_call x1, Pallas kernels, per_device(): pl.pallas_call(functools.partial(outer_kernel, row_size, ports_each), out...  3.27 us
    pallas_call x1, Pallas kernels, per_device(): pl.pallas_call(functools.partial(pack_kernel, row_size), out_shape=[array...  2.79 us
    pallas_call x1, Pallas kernels, per_device(): pl.pallas_call(functools.partial(rim_kernel, row_size), out_shape=[array(...  2.01 us
    pallas_call x1, Pallas kernels, per_device(): pl.pallas_call(functools.partial(inner_kernel, row_size), out_shape=[arra...  1.54 us
    unnamed x20, local copies, waits for them, and re-layouts  0.94 us
  transfers between devices with their start and end apart: 6, of which 2 were waited for; matrix products, arithmetic and copies ran while one was open for 0% of the time, Pallas kernels for 13%

profile of v13, /device:TPU:0, one launch (start us, length us, event | category | flops | bytes accessed | tf_op | source)
XLA Modules:
  0.0 34.8 jit_solution(733673043234890515)
XLA Ops:
  0.6 0.0 copy-start.2
  0.6 0.0 copy-start.1
  0.7 0.0 copy-start
  0.7 2.8 %pack.1 = (f32[7,4,8,128]{3,2,1,0:T(8,128)}, f32[7,2,4,8,128]{4,3,2,1,0:T(8,128)}, f32[2,4,8,128]{3,2,1,0:T(8,128)}, f32[2,4,8,128]{3,2,1,0:T(8,128)}, f32[26,4,8,128]{3,2,1,0:T(8,128)}) custom-call(f32[8]{0:T(128)} %eps_ref.1, f32[3,32,8,128]{3,2,1,0:T(8,128)} %elec_ref.1, f32[3,32,8,128]{3,2,1,0:T(8,128)} %magn_ref.1, s32[32,8,128]{2,1,0:T(8,128)} %mat_ref.1), custom_call_target="tpu_custom_call" | custom-call | tf_op jit(solution)/shard_map/pack/pallas_call | solution.py:719
  3.5 3.0 %collective-permute-start.4 = (f32[26,4,8,128]{3,2,1,0:T(8,128)}, f32[26,4,8,128]{3,2,1,0:T(8,128)S(1)}, u32[]{:S(2)}, u32[]{:S(2)}) collective-permute-start(f32[26,4,8,128]{3,2,1,0:T(8,128)} %get-tuple-element.33), channel_id=1, source_target_pairs={{0,2},{2,0},{1,3},{3,1},{4,6},{6,4},{5,7},{7,5},{8,10},{10,8},{9,1... | collective-permute-start | bytes 1277960 | tf_op jit(solution)/shard_map/ppermute | solution.py:695
  6.5 0.0 collective-permute-start
  6.5 1.6 %collective-permute-start.1 = (f32[2,4,8,128]{3,2,1,0:T(8,128)}, f32[2,4,8,128]{3,2,1,0:T(8,128)S(1)}, u32[]{:S(2)}, u32[]{:S(2)}) collective-permute-start(f32[2,4,8,128]{3,2,1,0:T(8,128)} %get-tuple-element.24), channel_id=1, source_target_pairs={{0,4},{8,12},{4,0},{12,8},{1,5},{9,13},{5,1},{13,9},{2,6},{10,14},... | collective-permute-start | bytes 98312 | tf_op jit(solution)/shard_map/ppermute | solution.py:695
  8.0 0.7 %collective-permute-start.2 = (f32[2,4,8,128]{3,2,1,0:T(8,128)}, f32[2,4,8,128]{3,2,1,0:T(8,128)S(1)}, u32[]{:S(2)}, u32[]{:S(2)}) collective-permute-start(f32[2,4,8,128]{3,2,1,0:T(8,128)} %get-tuple-element.25), channel_id=1, source_target_pairs={{4,8},{8,4},{5,9},{9,5},{6,10},{10,6},{7,11},{11,7},{20,24},{24,20... | collective-permute-start | bytes 98312 | tf_op jit(solution)/shard_map/ppermute | solution.py:695
  8.7 0.0 collective-permute-done.z_ref
  8.7 1.5 %inner.1 = (f32[3,8,5,8,128]{4,3,2,1,0:T(8,128)S(1)}, f32[3,8,5,8,128]{4,3,2,1,0:T(8,128)S(1)}, f32[8,5,8,128]{3,2,1,0:T(8,128)S(1)}, f32[4,8,4,8,128]{4,3,2,1,0:T(8,128)S(1)}) custom-call(f32[3,32,8,128]{3,2,1,0:T(8,128)S(1)} %copy-done, f32[3,32,8,128]{3,2,1,0:T(8,128)S(1)} %copy-done.1, s32[32,8,128]{2,1,0:T(8,128)S(1)} %copy-done.2, ...), custom_call_target="tpu_custom_call" | custom-call | flops 5000000 | bytes 10000000 | tf_op jit(solution)/shard_map/inner/pallas_call | solution.py:743
  10.3 0.0 copy-start.4
  10.3 0.3 collective-permute-done.1.even_ref
  10.6 0.0 collective-permute-done.2.odd_ref
  10.6 0.0 copy-start.9
  10.6 0.1 collective-permute-start.3
  10.7 0.5 %copy-done.4 = f32[8,32,64]{2,1,0:T(8,128)S(1)} copy-done((f32[8,32,64]{2,1,0:T(8,128)S(1)}, f32[8,32,64]{2,1,0:T(8,128)}, u32[]{:S(2)}) %copy-start.4) | copy-done | bytes 65560
  11.2 0.1 copy-done.5
  11.3 0.0 copy-done.7
  11.3 0.0 copy-done.8
  11.3 0.0 copy-done.9
  11.3 0.8 %weights.1.weight_ref = f32[4,2,4,8,128]{4,3,2,1,0:T(8,128)S(1)} custom-call(f32[8,32,64]{2,1,0:T(8,128)S(1)} %copy-done.4, s32[1,1,4]{2,1,0:T(1,128)S(1)} %copy-done.5, s32[1,1,4]{2,1,0:T(1,128)S(1)} %copy-done.8, s32[1,1,4]{2,1,0:T(1,128)S(1)} %copy-done.9, s32[1,1,4]{2,1,0:T(1,128)S(1)} %copy-done.7, f32[2,2,8,128]{3,2,1,0:T(8,128)S(1)} %layer_edges.1.order_ref), custom_call_target="tpu_custom_call" | custom-call | tf_op jit(solution)/shard_map/weights/pallas_call | solution.py:772
  12.1 0.0 copy-start.3
  12.1 0.0 collective-permute-done.3.layer_ref
  12.1 0.1 corners.1
  12.2 0.5 %collective-permute-start.5 = (f32[23,8,128]{2,1,0:T(8,128)S(1)}, f32[23,8,128]{2,1,0:T(8,128)S(1)}, u32[]{:S(2)}, u32[]{:S(2)}) collective-permute-start(f32[23,8,128]{2,1,0:T(8,128)S(1)} %corners.1), channel_id=1, source_target_pairs={{0,2},{2,0},{1,3},{3,1},{4,6},{6,4},{5,7},{7,5},{8,10},{10,8},{9,1... | collective-permute-start | bytes 282632 | tf_op jit(solution)/shard_map/ppermute | solution.py:695
  12.7 0.3 copy-done.3
  13.0 2.0 %rim.1 = (f32[3,2,5,8,128]{4,3,2,1,0:T(8,128)S(1)}, f32[3,2,5,8,128]{4,3,2,1,0:T(8,128)S(1)}, f32[2,5,8,128]{3,2,1,0:T(8,128)S(1)}, f32[6,4,4,8,128]{4,3,2,1,0:T(8,128)S(1)}, f32[4,8,128]{2,1,0:T(8,128)S(1)}) custom-call(f32[7,4,8,128]{3,2,1,0:T(8,128)S(1)} %collective-permute-done.z_ref, f32[7,2,4,8,128]{4,3,2,1,0:T(8,128)S(1)} %copy-done.3, ...), custom_call_target="tpu_custom_call" | custom-call | tf_op jit(solution)/shard_map/rim/pallas_call | solution.py:791
  15.1 3.4 %collective-permute-done.5.rest_1_ = f32[23,8,128]{2,1,0:T(8,128)S(1)} collective-permute-done((f32[23,8,128]{2,1,0:T(8,128)S(1)}, f32[23,8,128]{2,1,0:T(8,128)S(1)}, u32[]{:S(2)}, u32[]{:S(2)}) %collective-permute-start.5) | collective-permute-done | bytes 94240 | tf_op jit(solution)/shard_map/ppermute | solution.py:695
  18.5 0.0 collective-permute-done.4.rest_0_
  18.5 3.3 %outer.1 = (f32[3,32,8,128]{3,2,1,0:T(8,128)}, f32[3,32,8,128]{3,2,1,0:T(8,128)}, f32[16,2,16]{2,1,0:T(2,128)S(1)}) custom-call(s32[1,1,4]{2,1,0:T(1,128)S(1)} %copy-done.5, s32[1,1,4]{2,1,0:T(1,128)S(1)} %copy-done.7, f32[3,8,5,8,128]{4,3,2,1,0:T(8,128)S(1)} %get-tuple-element.21.e_in, f32[3,8,5,8,128]{4,3,2,1,0:T(8,128)S(1)} %get-tuple-element.22.h_in, ...), custom_call_target="tpu_custom_call" | custom-call | tf_op jit(solution)/shard_map/outer/pallas_call | solution.py:808
  21.8 12.5 %all_to_all.5 = f32[16,2,16]{2,1,0:T(2,128)S(1)} all-to-all(f32[16,2,16]{2,1,0:T(2,128)S(1)} %get-tuple-element.36), channel_id=1, replica_groups=mesh['grp'=2,'col'=4,'row'=2,'gz'=2] {'col','row','gz'}, dimensions={0} | all-to-all | bytes 4096 | tf_op jit(solution)/shard_map/all_to_all | solution.py:824
  34.3 0.6 %reduce_sum.9 = f32[2,16]{1,0:T(2,128)} reduce(f32[16,2,16]{2,1,0:T(2,128)S(1)} %all_to_all.5, f32[]{:T(128)} %constant.0.clone.1), dimensions={0}, to_apply=%region_0.0 | reduce | flops 480 | bytes 2180 | tf_op jit(solution)/shard_map/reduce_sum | solution.py:828
  (9 shorter events, 0.0 us)
Async XLA Ops:
  0.6 8.1 %copy-start.2 = (s32[32,8,128]{2,1,0:T(8,128)S(1)}, s32[32,8,128]{2,1,0:T(8,128)}, u32[]{:S(2)}) copy-start(s32[32,8,128]{2,1,0:T(8,128)} %mat_ref.1) | copy-start | bytes 393220
  0.6 8.1 %copy-start.1 = (f32[3,32,8,128]{3,2,1,0:T(8,128)S(1)}, f32[3,32,8,128]{3,2,1,0:T(8,128)}, u32[]{:S(2)}) copy-start(f32[3,32,8,128]{3,2,1,0:T(8,128)} %magn_ref.1) | copy-start | bytes 1179652
  0.7 8.1 %copy-start = (f32[3,32,8,128]{3,2,1,0:T(8,128)S(1)}, f32[3,32,8,128]{3,2,1,0:T(8,128)}, u32[]{:S(2)}) copy-start(f32[3,32,8,128]{3,2,1,0:T(8,128)} %elec_ref.1) | copy-start | bytes 1179652
  3.5 15.1 %collective-permute-start.4 = (f32[26,4,8,128]{3,2,1,0:T(8,128)}, f32[26,4,8,128]{3,2,1,0:T(8,128)S(1)}, u32[]{:S(2)}, u32[]{:S(2)}) collective-permute-start(f32[26,4,8,128]{3,2,1,0:T(8,128)} %get-tuple-element.33), channel_id=1, source_target_pairs={{0,2},{2,0},{1,3},{3,1},{4,6},{6,4},{5,7},{7,5},{8,10},{10,8},{9,1... | collective-permute-start | bytes 1277960 | tf_op jit(solution)/shard_map/ppermute | solution.py:695
  6.5 2.2 %collective-permute-start = (f32[7,4,8,128]{3,2,1,0:T(8,128)}, f32[7,4,8,128]{3,2,1,0:T(8,128)S(1)}, u32[]{:S(2)}, u32[]{:S(2)}) collective-permute-start(f32[7,4,8,128]{3,2,1,0:T(8,128)} %get-tuple-element.20), channel_id=1, source_target_pairs={{0,1},{1,0},{2,3},{3,2},{4,5},{5,4},{6,7},{7,6},{8,9},{9,8},{10,11... | collective-permute-start | bytes 344072 | tf_op jit(solution)/shard_map/ppermute | solution.py:695
  6.5 2.3 %copy-start.6 = (f32[8]{0:T(128)S(1)}, f32[8]{0:T(128)}, u32[]{:S(2)}) copy-start(f32[8]{0:T(128)} %eps_ref.1) | copy-start | bytes 100
  6.5 4.1 %collective-permute-start.1 = (f32[2,4,8,128]{3,2,1,0:T(8,128)}, f32[2,4,8,128]{3,2,1,0:T(8,128)S(1)}, u32[]{:S(2)}, u32[]{:S(2)}) collective-permute-start(f32[2,4,8,128]{3,2,1,0:T(8,128)} %get-tuple-element.24), channel_id=1, source_target_pairs={{0,4},{8,12},{4,0},{12,8},{1,5},{9,13},{5,1},{13,9},{2,6},{10,14},... | collective-permute-start | bytes 98312 | tf_op jit(solution)/shard_map/ppermute | solution.py:695
  8.0 2.6 %collective-permute-start.2 = (f32[2,4,8,128]{3,2,1,0:T(8,128)}, f32[2,4,8,128]{3,2,1,0:T(8,128)S(1)}, u32[]{:S(2)}, u32[]{:S(2)}) collective-permute-start(f32[2,4,8,128]{3,2,1,0:T(8,128)} %get-tuple-element.25), channel_id=1, source_target_pairs={{4,8},{8,4},{5,9},{9,5},{6,10},{10,6},{7,11},{11,7},{20,24},{24,20... | collective-permute-start | bytes 98312 | tf_op jit(solution)/shard_map/ppermute | solution.py:695
  10.3 0.9 %copy-start.4 = (f32[8,32,64]{2,1,0:T(8,128)S(1)}, f32[8,32,64]{2,1,0:T(8,128)}, u32[]{:S(2)}) copy-start(f32[8,32,64]{2,1,0:T(8,128)} %mode_ref.1) | copy-start | bytes 196612
  10.6 0.7 %copy-start.5 = (s32[1,1,4]{2,1,0:T(1,128)S(1)}, s32[1,1,4]{2,1,0:T(1,128)}, u32[]{:S(2)}) copy-start(s32[1,1,4]{2,1,0:T(1,128)} %prow_ref.5) | copy-start | bytes 52
  10.6 0.7 %copy-start.7 = (s32[1,1,4]{2,1,0:T(1,128)S(1)}, s32[1,1,4]{2,1,0:T(1,128)}, u32[]{:S(2)}) copy-start(s32[1,1,4]{2,1,0:T(1,128)} %pid_ref.3) | copy-start | bytes 52
  10.6 0.7 %copy-start.8 = (s32[1,1,4]{2,1,0:T(1,128)S(1)}, s32[1,1,4]{2,1,0:T(1,128)}, u32[]{:S(2)}) copy-start(s32[1,1,4]{2,1,0:T(1,128)} %pcol_ref.1) | copy-start | bytes 52
  10.6 0.7 %copy-start.9 = (s32[1,1,4]{2,1,0:T(1,128)S(1)}, s32[1,1,4]{2,1,0:T(1,128)}, u32[]{:S(2)}) copy-start(s32[1,1,4]{2,1,0:T(1,128)} %pmode_ref.1) | copy-start | bytes 52
  10.6 1.5 %collective-permute-start.3 = (f32[2,2,8,128]{3,2,1,0:T(8,128)S(1)}, f32[2,2,8,128]{3,2,1,0:T(8,128)S(1)}, u32[]{:S(2)}, u32[]{:S(2)}) collective-permute-start(f32[2,2,8,128]{3,2,1,0:T(8,128)S(1)} %layer_edges.1.order_ref), channel_id=1, source_target_pairs={{0,1},{1,0},{2,3},{3,2},{4,5},{5,4},{6,7},{7,6},{8,9},{9,8},{10,11... | collective-permute-start | bytes 49160 | tf_op jit(solution)/shard_map/ppermute | solution.py:695
  12.1 0.9 %copy-start.3 = (f32[7,2,4,8,128]{4,3,2,1,0:T(8,128)S(1)}, f32[7,2,4,8,128]{4,3,2,1,0:T(8,128)}, u32[]{:S(2)}) copy-start(f32[7,2,4,8,128]{4,3,2,1,0:T(8,128)} %get-tuple-element.26.own_ref) | copy-start | bytes 688132
  12.2 6.3 %collective-permute-start.5 = (f32[23,8,128]{2,1,0:T(8,128)S(1)}, f32[23,8,128]{2,1,0:T(8,128)S(1)}, u32[]{:S(2)}, u32[]{:S(2)}) collective-permute-start(f32[23,8,128]{2,1,0:T(8,128)S(1)} %corners.1), channel_id=1, source_target_pairs={{0,2},{2,0},{1,3},{3,1},{4,6},{6,4},{5,7},{7,5},{8,10},{10,8},{9,1... | collective-permute-start | bytes 282632 | tf_op jit(solution)/shard_map/ppermute | solution.py:695

commit v14 on v13

--- a/solution.py
+++ b/solution.py
@@ -75,8 +75,7 @@
         state_ref[at, x] = flat[pl.ds(f * LAYERS * ROWS + x, LAYERS, stride=ROWS), :].reshape(OWN, 8, 128)
 
 
-def pack_kernel(row_size, eps_hbm, elec_hbm, magn_hbm, mat_hbm, z_ref, own_ref, even_ref, odd_ref, *rest):
-    x_refs, (state_ref, main_ref, eps_ref, mat_ref, sems) = rest[:-5], rest[-5:]
+def fetch(eps_hbm, elec_hbm, magn_hbm, mat_hbm, main_ref, eps_ref, mat_ref, sems):
     copies = [pltpu.make_async_copy(eps_hbm, eps_ref, sems.at[0]), pltpu.make_async_copy(mat_hbm, mat_ref, sems.at[1])]
     copies.append(pltpu.make_async_copy(elec_hbm, main_ref.at[pl.ds(0, 3)], sems.at[2]))
     copies.append(pltpu.make_async_copy(magn_hbm, main_ref.at[pl.ds(3, 3)], sems.at[3]))
@@ -88,18 +87,31 @@
         main_ref[6, z] = coefficient(mat_ref[z], eps_ref)
     copies[2].wait()
     copies[3].wait()
+
+
+def plane_kernel(row_size, eps_hbm, elec_hbm, magn_hbm, mat_hbm, *rest):
+    x_refs, (main_ref, eps_ref, mat_ref, sems) = rest[:-4], rest[-4:]
+    fetch(eps_hbm, elec_hbm, magn_hbm, mat_hbm, main_ref, eps_ref, mat_ref, sems)
+    flat = main_ref.reshape(FIELDS * LAYERS * ROWS, 128)
+
+    def send(up, slot):
+        for i, (f, x) in enumerate(UP_PLANES if up else DOWN_PLANES):
+            plane = flat[pl.ds(f * LAYERS * ROWS + x, LAYERS, stride=ROWS), :]
+            x_refs[slot][i] = plane.reshape(OWN, 8, 128)
+
+    directions(row_size, send)
+
+
+def pack_kernel(
+    order_ref, eps_hbm, elec_hbm, magn_hbm, mat_hbm, z_ref, own_ref, even_ref, odd_ref, state_ref, main_ref, eps_ref, mat_ref, sems
+):
+    fetch(eps_hbm, elec_hbm, magn_hbm, mat_hbm, main_ref, eps_ref, mat_ref, sems)
     start = jnp.where(lax.axis_index("gz") == 0, LAYERS - DEPTH, 0)
     for f in range(FIELDS):
         z_ref[f] = main_ref[f, pl.ds(start, DEPTH)]
     flat = main_ref.reshape(FIELDS * LAYERS * ROWS, 128)
     for f in range(FIELDS):
         rows_outside(flat, f, state_ref, f)
-
-    def send(up, slot):
-        for i, (f, x) in enumerate(UP_PLANES if up else DOWN_PLANES):
-            x_refs[slot][i] = state_ref[f, x]
-
-    directions(row_size, send)
     pack_edges(state_ref, own_ref, even_ref, odd_ref)
 
 
@@ -716,27 +728,34 @@
         def scratch(*shape):
             return pltpu.VMEM(shape, f32)
 
-        z_send, own, even_send, odd_send, *x_send = pl.pallas_call(
-            functools.partial(pack_kernel, row_size),
+        fetched = [
+            scratch(FIELDS, LAYERS, ROWS, 128),
+            pltpu.SMEM(eps_table.shape, f32),
+            pltpu.VMEM(material.shape, jnp.int32),
+            pltpu.SemaphoreType.DMA((4,)),
+        ]
+        x_send = pl.pallas_call(
+            functools.partial(plane_kernel, row_size),
+            out_shape=[array(PLANES, OWN, 8, 128)] * n_x,
+            in_specs=[HBM] * 4,
+            out_specs=[VMEM] * n_x,
+            scratch_shapes=fetched,
+            name="planes",
+        )(eps_table, electric, magnetic, material)
+        x_halo = across_rows(x_send)
+        z_send, own, even_send, odd_send = pl.pallas_call(
+            pack_kernel,
             out_shape=[
                 array(FIELDS, DEPTH, ROWS, 128),
                 array(FIELDS, 2, OWN, 8, 128),
                 array(2, OWN, 8, 128),
                 array(2, OWN, 8, 128),
-            ]
-            + [array(PLANES, OWN, 8, 128)] * n_x,
-            in_specs=[HBM] * 4,
-            out_specs=[VMEM] * (4 + n_x),
-            scratch_shapes=[
-                scratch(FIELDS, ROWS, OWN, 8, 128),
-                scratch(FIELDS, LAYERS, ROWS, 128),
-                pltpu.SMEM(eps_table.shape, f32),
-                pltpu.VMEM(material.shape, jnp.int32),
-                pltpu.SemaphoreType.DMA((4,)),
             ],
+            in_specs=[ANY] + [HBM] * 4,
+            out_specs=[VMEM] * 4,
+            scratch_shapes=[scratch(FIELDS, ROWS, OWN, 8, 128)] + fetched,
             name="pack",
-        )(eps_table, electric, magnetic, material)
-        x_halo = across_rows(x_send)
+        )(x_send[0], eps_table, electric, magnetic, material)
         even = swapped(even_send, "col", col_size)
         odd = swapped(odd_send, "col", col_size, 1)
         z_halo = swapped(z_send, "gz", gz_size)

time: 35.1 us -> 36.4 us (1.037)
  waiting for transfers between devices: 3.73 us -> 2.17 us
  Pallas kernels: 10.5 us -> 12 us
  blocking collectives: 12.5 us -> 13.6 us
    pallas_call x1 -> x2, Pallas kernels: 2.79 us -> 4.45 us  [the longest x1 2.38 us: per_device(): pl.pallas_call(pack_kernel, out_shape=[array(FIELDS, DEPTH, ROWS, 128), a...]
    ppermute x6, waiting for transfers between devices: 3.73 us -> 2.17 us  [swapped(): return lax.ppermute(block, axis, pairs + [(j, i) for i, j in pairs])]
    all_to_all x1, blocking collectives: 12.5 us -> 13.6 us  [per_device(): terms = lax.all_to_all(term, ('col', 'row', 'gz'), 0, 0, tiled=True)]
  transfers between devices with their start and end apart: 6 -> 6, of which waited for: 2 -> 2; matrix products, arithmetic and copies ran while one was open for 0% -> 0% of each run, Pallas kernels for 13% -> 19%
where the time goes in v14:
time: 36.4 us; the launch traced here: 36.2 us
  blocking collectives  13.6 us (37%)
  Pallas kernels  12 us (33%)
  starting transfers between devices  5.97 us (16%)
  waiting for transfers between devices  2.17 us (6%)
  local copies, waits for them, and re-layouts  0.95 us (3%)
  between operations  0.83 us (2%)
  other arithmetic  0.59 us (2%)
    all_to_all x1, blocking collectives, per_device(): terms = lax.all_to_all(term, ('col', 'row', 'gz'), 0, 0, tiled=True)  13.6 us
    ppermute x6, starting transfers between devices, swapped(): return lax.ppermute(block, axis, pairs + [(j, i) for i, j in pairs])  5.97 us
    pallas_call x1, Pallas kernels, per_device(): pl.pallas_call(functools.partial(outer_kernel, row_size, ports_each), out...  3.23 us
    pallas_call x1, Pallas kernels, per_device(): pl.pallas_call(pack_kernel, out_shape=[array(FIELDS, DEPTH, ROWS, 128), a...  2.38 us
    ppermute x6, waiting for transfers between devices, swapped(): return lax.ppermute(block, axis, pairs + [(j, i) for i, j in pairs])  2.17 us
    pallas_call x1, Pallas kernels, per_device(): pl.pallas_call(functools.partial(plane_kernel, row_size), out_shape=[arra...  2.06 us
    pallas_call x1, Pallas kernels, per_device(): pl.pallas_call(functools.partial(rim_kernel, row_size), out_shape=[array(...  1.99 us
    pallas_call x1, Pallas kernels, per_device(): pl.pallas_call(functools.partial(inner_kernel, row_size), out_shape=[arra...  1.53 us
  transfers between devices with their start and end apart: 6, of which 2 were waited for; matrix products, arithmetic and copies ran while one was open for 0% of the time, Pallas kernels for 19%

profile of v14, /device:TPU:0, one launch (start us, length us, event | category | flops | bytes accessed | tf_op | source)
XLA Modules:
  0.0 36.2 jit_solution(3975809442786784403)
XLA Ops:
  0.6 2.1 %planes.1.order_ref = f32[26,4,8,128]{3,2,1,0:T(8,128)} custom-call(f32[8]{0:T(128)} %eps_ref.1, f32[3,32,8,128]{3,2,1,0:T(8,128)} %elec_ref.1, f32[3,32,8,128]{3,2,1,0:T(8,128)} %magn_ref.1, s32[32,8,128]{2,1,0:T(8,128)} %mat_ref.1), custom_call_target="tpu_custom_call" | custom-call | tf_op jit(solution)/shard_map/planes/pallas_call | solution.py:737
  2.7 0.0 copy-start
  2.7 0.0 copy-start.1
  2.7 0.0 copy-start.2
  2.7 3.0 %collective-permute-start.4 = (f32[26,4,8,128]{3,2,1,0:T(8,128)}, f32[26,4,8,128]{3,2,1,0:T(8,128)S(1)}, u32[]{:S(2)}, u32[]{:S(2)}) collective-permute-start(f32[26,4,8,128]{3,2,1,0:T(8,128)} %planes.1.order_ref), channel_id=1, source_target_pairs={{0,2},{2,0},{1,3},{3,1},{4,6},{6,4},{5,7},{7,5},{8,10},{10,8},{9,1... | collective-permute-start | bytes 1277960 | tf_op jit(solution)/shard_map/ppermute | solution.py:707
  5.7 2.4 %pack.1 = (f32[7,4,8,128]{3,2,1,0:T(8,128)}, f32[7,2,4,8,128]{4,3,2,1,0:T(8,128)}, f32[2,4,8,128]{3,2,1,0:T(8,128)}, f32[2,4,8,128]{3,2,1,0:T(8,128)}) custom-call(f32[26,4,8,128]{3,2,1,0:T(8,128)} %planes.1.order_ref, f32[8]{0:T(128)} %eps_ref.1, f32[3,32,8,128]{3,2,1,0:T(8,128)} %elec_ref.1, f32[3,32,8,128]{3,2,1,0:T(8,128)} %magn_ref.1, s32[32,8,128]{2,1,0:T(8,128)} %mat_ref.1), custom_call_target="tpu_custom_call" | custom-call | tf_op jit(solution)/shard_map/pack/pallas_call | solution.py:746
  8.1 0.1 collective-permute-start
  8.2 0.0 copy-start.5
  8.2 1.6 %collective-permute-start.1 = (f32[2,4,8,128]{3,2,1,0:T(8,128)}, f32[2,4,8,128]{3,2,1,0:T(8,128)S(1)}, u32[]{:S(2)}, u32[]{:S(2)}) collective-permute-start(f32[2,4,8,128]{3,2,1,0:T(8,128)} %get-tuple-element.23), channel_id=1, source_target_pairs={{0,4},{8,12},{4,0},{12,8},{1,5},{9,13},{5,1},{13,9},{2,6},{10,14},... | collective-permute-start | bytes 98312 | tf_op jit(solution)/shard_map/ppermute | solution.py:707
  9.9 0.7 %collective-permute-start.2 = (f32[2,4,8,128]{3,2,1,0:T(8,128)}, f32[2,4,8,128]{3,2,1,0:T(8,128)S(1)}, u32[]{:S(2)}, u32[]{:S(2)}) collective-permute-start(f32[2,4,8,128]{3,2,1,0:T(8,128)} %get-tuple-element.24), channel_id=1, source_target_pairs={{4,8},{8,4},{5,9},{9,5},{6,10},{10,6},{7,11},{11,7},{20,24},{24,20... | collective-permute-start | bytes 98312 | tf_op jit(solution)/shard_map/ppermute | solution.py:707
  10.5 0.0 collective-permute-done.z_ref
  10.6 1.5 %inner.1 = (f32[3,8,5,8,128]{4,3,2,1,0:T(8,128)S(1)}, f32[3,8,5,8,128]{4,3,2,1,0:T(8,128)S(1)}, f32[8,5,8,128]{3,2,1,0:T(8,128)S(1)}, f32[4,8,4,8,128]{4,3,2,1,0:T(8,128)S(1)}) custom-call(f32[3,32,8,128]{3,2,1,0:T(8,128)S(1)} %copy-done, f32[3,32,8,128]{3,2,1,0:T(8,128)S(1)} %copy-done.1, s32[32,8,128]{2,1,0:T(8,128)S(1)} %copy-done.2, ...), custom_call_target="tpu_custom_call" | custom-call | flops 5000000 | bytes 10000000 | tf_op jit(solution)/shard_map/inner/pallas_call | solution.py:762
  12.1 0.0 copy-start.4
  12.1 0.3 collective-permute-done.1.even_ref
  12.4 0.0 collective-permute-done.2.odd_ref
  12.4 0.0 copy-start.9
  12.4 0.1 collective-permute-start.3
  12.5 0.5 %copy-done.4 = f32[8,32,64]{2,1,0:T(8,128)S(1)} copy-done((f32[8,32,64]{2,1,0:T(8,128)S(1)}, f32[8,32,64]{2,1,0:T(8,128)}, u32[]{:S(2)}) %copy-start.4) | copy-done | bytes 65560
  13.0 0.1 copy-done.6
  13.1 0.0 copy-done.7
  13.1 0.0 copy-done.8
  13.1 0.0 copy-done.9
  13.1 0.8 %weights.1.weight_ref = f32[4,2,4,8,128]{4,3,2,1,0:T(8,128)S(1)} custom-call(f32[8,32,64]{2,1,0:T(8,128)S(1)} %copy-done.4, s32[1,1,4]{2,1,0:T(1,128)S(1)} %copy-done.6, s32[1,1,4]{2,1,0:T(1,128)S(1)} %copy-done.8, s32[1,1,4]{2,1,0:T(1,128)S(1)} %copy-done.9, s32[1,1,4]{2,1,0:T(1,128)S(1)} %copy-done.7, f32[2,2,8,128]{3,2,1,0:T(8,128)S(1)} %layer_edges.1.order_ref), custom_call_target="tpu_custom_call" | custom-call | tf_op jit(solution)/shard_map/weights/pallas_call | solution.py:791
  13.9 0.0 copy-start.3
  13.9 0.1 corners.1
  14.0 0.5 %collective-permute-start.5 = (f32[23,8,128]{2,1,0:T(8,128)S(1)}, f32[23,8,128]{2,1,0:T(8,128)S(1)}, u32[]{:S(2)}, u32[]{:S(2)}) collective-permute-start(f32[23,8,128]{2,1,0:T(8,128)S(1)} %corners.1), channel_id=1, source_target_pairs={{0,2},{2,0},{1,3},{3,1},{4,6},{6,4},{5,7},{7,5},{8,10},{10,8},{9,1... | collective-permute-start | bytes 282632 | tf_op jit(solution)/shard_map/ppermute | solution.py:707
  14.5 0.3 copy-done.3
  14.9 2.0 %rim.1 = (f32[3,2,5,8,128]{4,3,2,1,0:T(8,128)S(1)}, f32[3,2,5,8,128]{4,3,2,1,0:T(8,128)S(1)}, f32[2,5,8,128]{3,2,1,0:T(8,128)S(1)}, f32[6,4,4,8,128]{4,3,2,1,0:T(8,128)S(1)}, f32[4,8,128]{2,1,0:T(8,128)S(1)}) custom-call(f32[7,4,8,128]{3,2,1,0:T(8,128)S(1)} %collective-permute-done.z_ref, f32[7,2,4,8,128]{4,3,2,1,0:T(8,128)S(1)} %copy-done.3, ...), custom_call_target="tpu_custom_call" | custom-call | tf_op jit(solution)/shard_map/rim/pallas_call | solution.py:810
  16.9 1.9 %collective-permute-done.5.rest_1_ = f32[23,8,128]{2,1,0:T(8,128)S(1)} collective-permute-done((f32[23,8,128]{2,1,0:T(8,128)S(1)}, f32[23,8,128]{2,1,0:T(8,128)S(1)}, u32[]{:S(2)}, u32[]{:S(2)}) %collective-permute-start.5) | collective-permute-done | bytes 94240 | tf_op jit(solution)/shard_map/ppermute | solution.py:707
  18.7 3.2 %outer.1 = (f32[3,32,8,128]{3,2,1,0:T(8,128)}, f32[3,32,8,128]{3,2,1,0:T(8,128)}, f32[16,2,16]{2,1,0:T(2,128)S(1)}) custom-call(s32[1,1,4]{2,1,0:T(1,128)S(1)} %copy-done.6, s32[1,1,4]{2,1,0:T(1,128)S(1)} %copy-done.7, f32[3,8,5,8,128]{4,3,2,1,0:T(8,128)S(1)} %get-tuple-element.20.e_in, f32[3,8,5,8,128]{4,3,2,1,0:T(8,128)S(1)} %get-tuple-element.21.h_in, ...), custom_call_target="tpu_custom_call" | custom-call | tf_op jit(solution)/shard_map/outer/pallas_call | solution.py:827
  22.0 13.6 %all_to_all.5 = f32[16,2,16]{2,1,0:T(2,128)S(1)} all-to-all(f32[16,2,16]{2,1,0:T(2,128)S(1)} %get-tuple-element.34), channel_id=1, replica_groups=mesh['grp'=2,'col'=4,'row'=2,'gz'=2] {'col','row','gz'}, dimensions={0} | all-to-all | bytes 4096 | tf_op jit(solution)/shard_map/all_to_all | solution.py:843
  35.6 0.6 %reduce_sum.9 = f32[2,16]{1,0:T(2,128)} reduce(f32[16,2,16]{2,1,0:T(2,128)S(1)} %all_to_all.5, f32[]{:T(128)} %constant.0.clone.1), dimensions={0}, to_apply=%region_0.0 | reduce | flops 480 | bytes 2180 | tf_op jit(solution)/shard_map/reduce_sum | solution.py:847
  (10 shorter events, 0.0 us)
Async XLA Ops:
  2.7 7.8 %copy-start = (f32[3,32,8,128]{3,2,1,0:T(8,128)S(1)}, f32[3,32,8,128]{3,2,1,0:T(8,128)}, u32[]{:S(2)}) copy-start(f32[3,32,8,128]{3,2,1,0:T(8,128)} %elec_ref.1) | copy-start | bytes 1179652
  2.7 7.8 %copy-start.1 = (f32[3,32,8,128]{3,2,1,0:T(8,128)S(1)}, f32[3,32,8,128]{3,2,1,0:T(8,128)}, u32[]{:S(2)}) copy-start(f32[3,32,8,128]{3,2,1,0:T(8,128)} %magn_ref.1) | copy-start | bytes 1179652
  2.7 7.8 %copy-start.2 = (s32[32,8,128]{2,1,0:T(8,128)S(1)}, s32[32,8,128]{2,1,0:T(8,128)}, u32[]{:S(2)}) copy-start(s32[32,8,128]{2,1,0:T(8,128)} %mat_ref.1) | copy-start | bytes 393220
  2.7 16.0 %collective-permute-start.4 = (f32[26,4,8,128]{3,2,1,0:T(8,128)}, f32[26,4,8,128]{3,2,1,0:T(8,128)S(1)}, u32[]{:S(2)}, u32[]{:S(2)}) collective-permute-start(f32[26,4,8,128]{3,2,1,0:T(8,128)} %planes.1.order_ref), channel_id=1, source_target_pairs={{0,2},{2,0},{1,3},{3,1},{4,6},{6,4},{5,7},{7,5},{8,10},{10,8},{9,1... | collective-permute-start | bytes 1277960 | tf_op jit(solution)/shard_map/ppermute | solution.py:707
  8.1 2.4 %collective-permute-start = (f32[7,4,8,128]{3,2,1,0:T(8,128)}, f32[7,4,8,128]{3,2,1,0:T(8,128)S(1)}, u32[]{:S(2)}, u32[]{:S(2)}) collective-permute-start(f32[7,4,8,128]{3,2,1,0:T(8,128)} %get-tuple-element.19), channel_id=1, source_target_pairs={{0,1},{1,0},{2,3},{3,2},{4,5},{5,4},{6,7},{7,6},{8,9},{9,8},{10,11... | collective-permute-start | bytes 344072 | tf_op jit(solution)/shard_map/ppermute | solution.py:707
  8.2 2.4 %copy-start.5 = (f32[8]{0:T(128)S(1)}, f32[8]{0:T(128)}, u32[]{:S(2)}) copy-start(f32[8]{0:T(128)} %eps_ref.1) | copy-start | bytes 100
  8.2 4.2 %collective-permute-start.1 = (f32[2,4,8,128]{3,2,1,0:T(8,128)}, f32[2,4,8,128]{3,2,1,0:T(8,128)S(1)}, u32[]{:S(2)}, u32[]{:S(2)}) collective-permute-start(f32[2,4,8,128]{3,2,1,0:T(8,128)} %get-tuple-element.23), channel_id=1, source_target_pairs={{0,4},{8,12},{4,0},{12,8},{1,5},{9,13},{5,1},{13,9},{2,6},{10,14},... | collective-permute-start | bytes 98312 | tf_op jit(solution)/shard_map/ppermute | solution.py:707
  9.9 2.6 %collective-permute-start.2 = (f32[2,4,8,128]{3,2,1,0:T(8,128)}, f32[2,4,8,128]{3,2,1,0:T(8,128)S(1)}, u32[]{:S(2)}, u32[]{:S(2)}) collective-permute-start(f32[2,4,8,128]{3,2,1,0:T(8,128)} %get-tuple-element.24), channel_id=1, source_target_pairs={{4,8},{8,4},{5,9},{9,5},{6,10},{10,6},{7,11},{11,7},{20,24},{24,20... | collective-permute-start | bytes 98312 | tf_op jit(solution)/shard_map/ppermute | solution.py:707
  12.1 0.9 %copy-start.4 = (f32[8,32,64]{2,1,0:T(8,128)S(1)}, f32[8,32,64]{2,1,0:T(8,128)}, u32[]{:S(2)}) copy-start(f32[8,32,64]{2,1,0:T(8,128)} %mode_ref.1) | copy-start | bytes 196612
  12.4 0.7 %copy-start.6 = (s32[1,1,4]{2,1,0:T(1,128)S(1)}, s32[1,1,4]{2,1,0:T(1,128)}, u32[]{:S(2)}) copy-start(s32[1,1,4]{2,1,0:T(1,128)} %prow_ref.5) | copy-start | bytes 52
  12.4 0.7 %copy-start.7 = (s32[1,1,4]{2,1,0:T(1,128)S(1)}, s32[1,1,4]{2,1,0:T(1,128)}, u32[]{:S(2)}) copy-start(s32[1,1,4]{2,1,0:T(1,128)} %pid_ref.3) | copy-start | bytes 52
  12.4 0.7 %copy-start.8 = (s32[1,1,4]{2,1,0:T(1,128)S(1)}, s32[1,1,4]{2,1,0:T(1,128)}, u32[]{:S(2)}) copy-start(s32[1,1,4]{2,1,0:T(1,128)} %pcol_ref.1) | copy-start | bytes 52
  12.4 0.7 %copy-start.9 = (s32[1,1,4]{2,1,0:T(1,128)S(1)}, s32[1,1,4]{2,1,0:T(1,128)}, u32[]{:S(2)}) copy-start(s32[1,1,4]{2,1,0:T(1,128)} %pmode_ref.1) | copy-start | bytes 52
  12.4 1.5 %collective-permute-start.3 = (f32[2,2,8,128]{3,2,1,0:T(8,128)S(1)}, f32[2,2,8,128]{3,2,1,0:T(8,128)S(1)}, u32[]{:S(2)}, u32[]{:S(2)}) collective-permute-start(f32[2,2,8,128]{3,2,1,0:T(8,128)S(1)} %layer_edges.1.order_ref), channel_id=1, source_target_pairs={{0,1},{1,0},{2,3},{3,2},{4,5},{5,4},{6,7},{7,6},{8,9},{9,8},{10,11... | collective-permute-start | bytes 49160 | tf_op jit(solution)/shard_map/ppermute | solution.py:707
  13.9 0.9 %copy-start.3 = (f32[7,2,4,8,128]{4,3,2,1,0:T(8,128)S(1)}, f32[7,2,4,8,128]{4,3,2,1,0:T(8,128)}, u32[]{:S(2)}) copy-start(f32[7,2,4,8,128]{4,3,2,1,0:T(8,128)} %get-tuple-element.25.own_ref) | copy-start | bytes 688132
  14.0 4.7 %collective-permute-start.5 = (f32[23,8,128]{2,1,0:T(8,128)S(1)}, f32[23,8,128]{2,1,0:T(8,128)S(1)}, u32[]{:S(2)}, u32[]{:S(2)}) collective-permute-start(f32[23,8,128]{2,1,0:T(8,128)S(1)} %corners.1), channel_id=1, source_target_pairs={{0,2},{2,0},{1,3},{3,1},{4,6},{6,4},{5,7},{7,5},{8,10},{10,8},{9,1... | collective-permute-start | bytes 282632 | tf_op jit(solution)/shard_map/ppermute | solution.py:707

commit v15 on v13

--- a/solution.py
+++ b/solution.py
@@ -305,22 +305,34 @@
         for (f, zz), tile in new.items():
             tiles.put(f, i, zz, tile)
 
-    def sweep(rows, load, work):
+    def items(rows, load, work):
         loaded = {}
 
         def want(i):
             if i not in loaded and i in exists:
                 loaded[i] = load(i)
 
-        for i in rows:
+        def ahead(i):
             for j in (i - 1, i, i + 1):
-                if j in rows or j == i + (1 if load is load_e else -1):
+                if j in rows and j <= i or j == i + (1 if load is load_e else -1):
                     want(j)
-            work(i, loaded)
-
-    sweep(h_rows, load_e, work_h)
-    yield
-    sweep(e_rows, load_h, work_e)
+
+        return [(functools.partial(ahead, i), functools.partial(work, i, loaded)) for i in rows]
+
+    return items(h_rows, load_e, work_h), items(e_rows, load_h, work_e)
+
+
+def pipeline(items):
+    if items:
+        items[0][0]()
+    for at, (_, work) in enumerate(items):
+        if at + 1 < len(items):
+            items[at + 1][0]()
+        work()
+
+
+def aside(work):
+    return lambda: None, work
 
 
 class Rows:
@@ -413,12 +425,11 @@
                     self.edge, self.edge_exists, blocks_of(h_span), blocks_of(e_span), self.blocks, h_of, c_of, layers, last, []
                 )
             )
-        for part in parts:
-            next(part)
-        if between is not None:
-            between()
-        for part in parts:
-            next(part, None)
+        hs = [item for part in parts for item in part[0]]
+        es = [item for part in parts for item in part[1]]
+        if between is None and len(hs) < 4:
+            between = lambda: None
+        return hs + ([aside(between)] if between is not None else []) + es
 
 
 def rows_cases(row_size, row, run):
@@ -501,9 +512,11 @@
     def run(has_below, has_above):
         main = Tiles(first, None, DEPTH)
         stepper = Stepper(row_size, main, None, range(4, 12), (), False)
+        items = []
         for n in range(1, STEPS + 1):
-            main.ez_ref = ez_ref.at[n - 1]
-            stepper.step(n, [spans_inner(n, has_below, has_above)])
+            items.append(aside(functools.partial(setattr, main, "ez_ref", ez_ref.at[n - 1])))
+            items += stepper.step(n, [spans_inner(n, has_below, has_above)])
+        pipeline(items)
         for i in range(ROWS):
             for zz in range(CHUNK):
                 for f in range(6):
@@ -549,9 +562,12 @@
             low, high = spans_inner(n, has_below, has_above)[1]
             return (at >= low) & (at <= high)
 
+        items = []
         for n in range(1, STEPS + 1):
-            stepper.step(n, [spans_inner(n, has_below, has_above)])
-            port_sums(n, reached, prow_ref, weight_ref, ez_in.at[n - 1], ez_ref, sum_ref, None)
+            items += stepper.step(n, [spans_inner(n, has_below, has_above)])
+            sums = functools.partial(port_sums, n, reached, prow_ref, weight_ref, ez_in.at[n - 1], ez_ref, sum_ref, None)
+            items.append(aside(sums))
+        pipeline(items)
         for i in range(2):
             for zz in range(CHUNK):
                 for f in range(6):
@@ -673,10 +689,13 @@
             copies[-1].start()
 
         stepper = Stepper(row_size, main, edge, rows, blocks, True)
+        items = []
         for n in range(1, STEPS + 1):
             spans = ([spans_below(n)] if has_below else []) + ([spans_above(n)] if has_above else [])
-            stepper.step(n, spans, functools.partial(hand_out, 1) if n == STEPS else None)
-            port_sums(n, reached, prow_ref, weight_ref, ez_ref, edge_ez_ref, sum_ref, sum_in)
+            items += stepper.step(n, spans, functools.partial(hand_out, 1) if n == STEPS else None)
+            sums = functools.partial(port_sums, n, reached, prow_ref, weight_ref, ez_ref, edge_ez_ref, sum_ref, sum_in)
+            items.append(aside(sums))
+        pipeline(items)
         hand_out(0)
         write_terms()
         for copy in copies:

time: 35.1 us -> 35.1 us (level)
  no operation moved by 1% of the time
where the time goes in v15:
time: 35.1 us; the launch traced here: 34.8 us
  blocking collectives  12.5 us (36%)
  Pallas kernels  10.4 us (30%)
  starting transfers between devices  5.84 us (17%)
  waiting for transfers between devices  3.73 us (11%)
  local copies, waits for them, and re-layouts  0.94 us (3%)
  between operations  0.81 us (2%)
  other arithmetic  0.59 us (2%)
    all_to_all x1, blocking collectives, per_device(): terms = lax.all_to_all(term, ('col', 'row', 'gz'), 0, 0, tiled=True)  12.5 us
    ppermute x6, starting transfers between devices, swapped(): return lax.ppermute(block, axis, pairs + [(j, i) for i, j in pairs])  5.84 us
    ppermute x6, waiting for transfers between devices, swapped(): return lax.ppermute(block, axis, pairs + [(j, i) for i, j in pairs])  3.73 us
    pallas_call x1, Pallas kernels, per_device(): pl.pallas_call(functools.partial(outer_kernel, row_size, ports_each), out...  3.25 us
    pallas_call x1, Pallas kernels, per_device(): pl.pallas_call(functools.partial(pack_kernel, row_size), out_shape=[array...  2.79 us
    pallas_call x1, Pallas kernels, per_device(): pl.pallas_call(functools.partial(rim_kernel, row_size), out_shape=[array(...  2.01 us
    pallas_call x1, Pallas kernels, per_device(): pl.pallas_call(functools.partial(inner_kernel, row_size), out_shape=[arra...  1.54 us
    unnamed x20, local copies, waits for them, and re-layouts  0.94 us
  transfers between devices with their start and end apart: 6, of which 2 were waited for; matrix products, arithmetic and copies ran while one was open for 0% of the time, Pallas kernels for 13%

profile of v15, /device:TPU:0, one launch (start us, length us, event | category | flops | bytes accessed | tf_op | source)
XLA Modules:
  0.0 34.8 jit_solution(17223659580875788309)
XLA Ops:
  0.6 0.0 copy-start.2
  0.6 0.0 copy-start.1
  0.7 0.0 copy-start
  0.7 2.8 %pack.1 = (f32[7,4,8,128]{3,2,1,0:T(8,128)}, f32[7,2,4,8,128]{4,3,2,1,0:T(8,128)}, f32[2,4,8,128]{3,2,1,0:T(8,128)}, f32[2,4,8,128]{3,2,1,0:T(8,128)}, f32[26,4,8,128]{3,2,1,0:T(8,128)}) custom-call(f32[8]{0:T(128)} %eps_ref.1, f32[3,32,8,128]{3,2,1,0:T(8,128)} %elec_ref.1, f32[3,32,8,128]{3,2,1,0:T(8,128)} %magn_ref.1, s32[32,8,128]{2,1,0:T(8,128)} %mat_ref.1), custom_call_target="tpu_custom_call" | custom-call | tf_op jit(solution)/shard_map/pack/pallas_call | solution.py:738
  3.5 3.0 %collective-permute-start.4 = (f32[26,4,8,128]{3,2,1,0:T(8,128)}, f32[26,4,8,128]{3,2,1,0:T(8,128)S(1)}, u32[]{:S(2)}, u32[]{:S(2)}) collective-permute-start(f32[26,4,8,128]{3,2,1,0:T(8,128)} %get-tuple-element.33), channel_id=1, source_target_pairs={{0,2},{2,0},{1,3},{3,1},{4,6},{6,4},{5,7},{7,5},{8,10},{10,8},{9,1... | collective-permute-start | bytes 1277960 | tf_op jit(solution)/shard_map/ppermute | solution.py:714
  6.5 0.0 collective-permute-start
  6.5 1.6 %collective-permute-start.1 = (f32[2,4,8,128]{3,2,1,0:T(8,128)}, f32[2,4,8,128]{3,2,1,0:T(8,128)S(1)}, u32[]{:S(2)}, u32[]{:S(2)}) collective-permute-start(f32[2,4,8,128]{3,2,1,0:T(8,128)} %get-tuple-element.24), channel_id=1, source_target_pairs={{0,4},{8,12},{4,0},{12,8},{1,5},{9,13},{5,1},{13,9},{2,6},{10,14},... | collective-permute-start | bytes 98312 | tf_op jit(solution)/shard_map/ppermute | solution.py:714
  8.0 0.7 %collective-permute-start.2 = (f32[2,4,8,128]{3,2,1,0:T(8,128)}, f32[2,4,8,128]{3,2,1,0:T(8,128)S(1)}, u32[]{:S(2)}, u32[]{:S(2)}) collective-permute-start(f32[2,4,8,128]{3,2,1,0:T(8,128)} %get-tuple-element.25), channel_id=1, source_target_pairs={{4,8},{8,4},{5,9},{9,5},{6,10},{10,6},{7,11},{11,7},{20,24},{24,20... | collective-permute-start | bytes 98312 | tf_op jit(solution)/shard_map/ppermute | solution.py:714
  8.7 0.0 collective-permute-done.z_ref
  8.7 1.5 %inner.1 = (f32[3,8,5,8,128]{4,3,2,1,0:T(8,128)S(1)}, f32[3,8,5,8,128]{4,3,2,1,0:T(8,128)S(1)}, f32[8,5,8,128]{3,2,1,0:T(8,128)S(1)}, f32[4,8,4,8,128]{4,3,2,1,0:T(8,128)S(1)}) custom-call(f32[3,32,8,128]{3,2,1,0:T(8,128)S(1)} %copy-done, f32[3,32,8,128]{3,2,1,0:T(8,128)S(1)} %copy-done.1, s32[32,8,128]{2,1,0:T(8,128)S(1)} %copy-done.2, ...), custom_call_target="tpu_custom_call" | custom-call | flops 5000000 | bytes 10000000 | tf_op jit(solution)/shard_map/inner/pallas_call | solution.py:762
  10.3 0.0 copy-start.4
  10.3 0.3 collective-permute-done.1.even_ref
  10.6 0.0 collective-permute-done.2.odd_ref
  10.6 0.0 copy-start.9
  10.6 0.1 collective-permute-start.3
  10.7 0.5 %copy-done.4 = f32[8,32,64]{2,1,0:T(8,128)S(1)} copy-done((f32[8,32,64]{2,1,0:T(8,128)S(1)}, f32[8,32,64]{2,1,0:T(8,128)}, u32[]{:S(2)}) %copy-start.4) | copy-done | bytes 65560
  11.2 0.1 copy-done.5
  11.3 0.0 copy-done.7
  11.3 0.0 copy-done.8
  11.3 0.0 copy-done.9
  11.3 0.8 %weights.1.weight_ref = f32[4,2,4,8,128]{4,3,2,1,0:T(8,128)S(1)} custom-call(f32[8,32,64]{2,1,0:T(8,128)S(1)} %copy-done.4, s32[1,1,4]{2,1,0:T(1,128)S(1)} %copy-done.5, s32[1,1,4]{2,1,0:T(1,128)S(1)} %copy-done.8, s32[1,1,4]{2,1,0:T(1,128)S(1)} %copy-done.9, s32[1,1,4]{2,1,0:T(1,128)S(1)} %copy-done.7, f32[2,2,8,128]{3,2,1,0:T(8,128)S(1)} %layer_edges.1.order_ref), custom_call_target="tpu_custom_call" | custom-call | tf_op jit(solution)/shard_map/weights/pallas_call | solution.py:791
  12.1 0.0 copy-start.3
  12.1 0.0 collective-permute-done.3.layer_ref
  12.1 0.1 corners.1
  12.2 0.5 %collective-permute-start.5 = (f32[23,8,128]{2,1,0:T(8,128)S(1)}, f32[23,8,128]{2,1,0:T(8,128)S(1)}, u32[]{:S(2)}, u32[]{:S(2)}) collective-permute-start(f32[23,8,128]{2,1,0:T(8,128)S(1)} %corners.1), channel_id=1, source_target_pairs={{0,2},{2,0},{1,3},{3,1},{4,6},{6,4},{5,7},{7,5},{8,10},{10,8},{9,1... | collective-permute-start | bytes 282632 | tf_op jit(solution)/shard_map/ppermute | solution.py:714
  12.7 0.3 copy-done.3
  13.0 2.0 %rim.1 = (f32[3,2,5,8,128]{4,3,2,1,0:T(8,128)S(1)}, f32[3,2,5,8,128]{4,3,2,1,0:T(8,128)S(1)}, f32[2,5,8,128]{3,2,1,0:T(8,128)S(1)}, f32[6,4,4,8,128]{4,3,2,1,0:T(8,128)S(1)}, f32[4,8,128]{2,1,0:T(8,128)S(1)}) custom-call(f32[7,4,8,128]{3,2,1,0:T(8,128)S(1)} %collective-permute-done.z_ref, f32[7,2,4,8,128]{4,3,2,1,0:T(8,128)S(1)} %copy-done.3, ...), custom_call_target="tpu_custom_call" | custom-call | tf_op jit(solution)/shard_map/rim/pallas_call | solution.py:810
  15.1 3.4 %collective-permute-done.5.rest_1_ = f32[23,8,128]{2,1,0:T(8,128)S(1)} collective-permute-done((f32[23,8,128]{2,1,0:T(8,128)S(1)}, f32[23,8,128]{2,1,0:T(8,128)S(1)}, u32[]{:S(2)}, u32[]{:S(2)}) %collective-permute-start.5) | collective-permute-done | bytes 94240 | tf_op jit(solution)/shard_map/ppermute | solution.py:714
  18.5 0.0 collective-permute-done.4.rest_0_
  18.5 3.2 %outer.1 = (f32[3,32,8,128]{3,2,1,0:T(8,128)}, f32[3,32,8,128]{3,2,1,0:T(8,128)}, f32[16,2,16]{2,1,0:T(2,128)S(1)}) custom-call(s32[1,1,4]{2,1,0:T(1,128)S(1)} %copy-done.5, s32[1,1,4]{2,1,0:T(1,128)S(1)} %copy-done.7, f32[3,8,5,8,128]{4,3,2,1,0:T(8,128)S(1)} %get-tuple-element.21.e_in, f32[3,8,5,8,128]{4,3,2,1,0:T(8,128)S(1)} %get-tuple-element.22.h_in, ...), custom_call_target="tpu_custom_call" | custom-call | tf_op jit(solution)/shard_map/outer/pallas_call | solution.py:827
  21.8 12.5 %all_to_all.5 = f32[16,2,16]{2,1,0:T(2,128)S(1)} all-to-all(f32[16,2,16]{2,1,0:T(2,128)S(1)} %get-tuple-element.36), channel_id=1, replica_groups=mesh['grp'=2,'col'=4,'row'=2,'gz'=2] {'col','row','gz'}, dimensions={0} | all-to-all | bytes 4096 | tf_op jit(solution)/shard_map/all_to_all | solution.py:843
  34.2 0.6 %reduce_sum.9 = f32[2,16]{1,0:T(2,128)} reduce(f32[16,2,16]{2,1,0:T(2,128)S(1)} %all_to_all.5, f32[]{:T(128)} %constant.0.clone.1), dimensions={0}, to_apply=%region_0.0 | reduce | flops 480 | bytes 2180 | tf_op jit(solution)/shard_map/reduce_sum | solution.py:847
  (9 shorter events, 0.0 us)
Async XLA Ops:
  0.6 8.1 %copy-start.2 = (s32[32,8,128]{2,1,0:T(8,128)S(1)}, s32[32,8,128]{2,1,0:T(8,128)}, u32[]{:S(2)}) copy-start(s32[32,8,128]{2,1,0:T(8,128)} %mat_ref.1) | copy-start | bytes 393220
  0.6 8.1 %copy-start.1 = (f32[3,32,8,128]{3,2,1,0:T(8,128)S(1)}, f32[3,32,8,128]{3,2,1,0:T(8,128)}, u32[]{:S(2)}) copy-start(f32[3,32,8,128]{3,2,1,0:T(8,128)} %magn_ref.1) | copy-start | bytes 1179652
  0.7 8.1 %copy-start = (f32[3,32,8,128]{3,2,1,0:T(8,128)S(1)}, f32[3,32,8,128]{3,2,1,0:T(8,128)}, u32[]{:S(2)}) copy-start(f32[3,32,8,128]{3,2,1,0:T(8,128)} %elec_ref.1) | copy-start | bytes 1179652
  3.5 15.1 %collective-permute-start.4 = (f32[26,4,8,128]{3,2,1,0:T(8,128)}, f32[26,4,8,128]{3,2,1,0:T(8,128)S(1)}, u32[]{:S(2)}, u32[]{:S(2)}) collective-permute-start(f32[26,4,8,128]{3,2,1,0:T(8,128)} %get-tuple-element.33), channel_id=1, source_target_pairs={{0,2},{2,0},{1,3},{3,1},{4,6},{6,4},{5,7},{7,5},{8,10},{10,8},{9,1... | collective-permute-start | bytes 1277960 | tf_op jit(solution)/shard_map/ppermute | solution.py:714
  6.5 2.2 %collective-permute-start = (f32[7,4,8,128]{3,2,1,0:T(8,128)}, f32[7,4,8,128]{3,2,1,0:T(8,128)S(1)}, u32[]{:S(2)}, u32[]{:S(2)}) collective-permute-start(f32[7,4,8,128]{3,2,1,0:T(8,128)} %get-tuple-element.20), channel_id=1, source_target_pairs={{0,1},{1,0},{2,3},{3,2},{4,5},{5,4},{6,7},{7,6},{8,9},{9,8},{10,11... | collective-permute-start | bytes 344072 | tf_op jit(solution)/shard_map/ppermute | solution.py:714
  6.5 2.3 %copy-start.6 = (f32[8]{0:T(128)S(1)}, f32[8]{0:T(128)}, u32[]{:S(2)}) copy-start(f32[8]{0:T(128)} %eps_ref.1) | copy-start | bytes 100
  6.5 4.1 %collective-permute-start.1 = (f32[2,4,8,128]{3,2,1,0:T(8,128)}, f32[2,4,8,128]{3,2,1,0:T(8,128)S(1)}, u32[]{:S(2)}, u32[]{:S(2)}) collective-permute-start(f32[2,4,8,128]{3,2,1,0:T(8,128)} %get-tuple-element.24), channel_id=1, source_target_pairs={{0,4},{8,12},{4,0},{12,8},{1,5},{9,13},{5,1},{13,9},{2,6},{10,14},... | collective-permute-start | bytes 98312 | tf_op jit(solution)/shard_map/ppermute | solution.py:714
  8.0 2.6 %collective-permute-start.2 = (f32[2,4,8,128]{3,2,1,0:T(8,128)}, f32[2,4,8,128]{3,2,1,0:T(8,128)S(1)}, u32[]{:S(2)}, u32[]{:S(2)}) collective-permute-start(f32[2,4,8,128]{3,2,1,0:T(8,128)} %get-tuple-element.25), channel_id=1, source_target_pairs={{4,8},{8,4},{5,9},{9,5},{6,10},{10,6},{7,11},{11,7},{20,24},{24,20... | collective-permute-start | bytes 98312 | tf_op jit(solution)/shard_map/ppermute | solution.py:714
  10.3 0.9 %copy-start.4 = (f32[8,32,64]{2,1,0:T(8,128)S(1)}, f32[8,32,64]{2,1,0:T(8,128)}, u32[]{:S(2)}) copy-start(f32[8,32,64]{2,1,0:T(8,128)} %mode_ref.1) | copy-start | bytes 196612
  10.6 0.7 %copy-start.5 = (s32[1,1,4]{2,1,0:T(1,128)S(1)}, s32[1,1,4]{2,1,0:T(1,128)}, u32[]{:S(2)}) copy-start(s32[1,1,4]{2,1,0:T(1,128)} %prow_ref.5) | copy-start | bytes 52
  10.6 0.7 %copy-start.7 = (s32[1,1,4]{2,1,0:T(1,128)S(1)}, s32[1,1,4]{2,1,0:T(1,128)}, u32[]{:S(2)}) copy-start(s32[1,1,4]{2,1,0:T(1,128)} %pid_ref.3) | copy-start | bytes 52
  10.6 0.7 %copy-start.8 = (s32[1,1,4]{2,1,0:T(1,128)S(1)}, s32[1,1,4]{2,1,0:T(1,128)}, u32[]{:S(2)}) copy-start(s32[1,1,4]{2,1,0:T(1,128)} %pcol_ref.1) | copy-start | bytes 52
  10.6 0.7 %copy-start.9 = (s32[1,1,4]{2,1,0:T(1,128)S(1)}, s32[1,1,4]{2,1,0:T(1,128)}, u32[]{:S(2)}) copy-start(s32[1,1,4]{2,1,0:T(1,128)} %pmode_ref.1) | copy-start | bytes 52
  10.6 1.5 %collective-permute-start.3 = (f32[2,2,8,128]{3,2,1,0:T(8,128)S(1)}, f32[2,2,8,128]{3,2,1,0:T(8,128)S(1)}, u32[]{:S(2)}, u32[]{:S(2)}) collective-permute-start(f32[2,2,8,128]{3,2,1,0:T(8,128)S(1)} %layer_edges.1.order_ref), channel_id=1, source_target_pairs={{0,1},{1,0},{2,3},{3,2},{4,5},{5,4},{6,7},{7,6},{8,9},{9,8},{10,11... | collective-permute-start | bytes 49160 | tf_op jit(solution)/shard_map/ppermute | solution.py:714
  12.1 0.9 %copy-start.3 = (f32[7,2,4,8,128]{4,3,2,1,0:T(8,128)S(1)}, f32[7,2,4,8,128]{4,3,2,1,0:T(8,128)}, u32[]{:S(2)}) copy-start(f32[7,2,4,8,128]{4,3,2,1,0:T(8,128)} %get-tuple-element.26.own_ref) | copy-start | bytes 688132
  12.2 6.3 %collective-permute-start.5 = (f32[23,8,128]{2,1,0:T(8,128)S(1)}, f32[23,8,128]{2,1,0:T(8,128)S(1)}, u32[]{:S(2)}, u32[]{:S(2)}) collective-permute-start(f32[23,8,128]{2,1,0:T(8,128)S(1)} %corners.1), channel_id=1, source_target_pairs={{0,2},{2,0},{1,3},{3,1},{4,6},{6,4},{5,7},{7,5},{8,10},{10,8},{9,1... | collective-permute-start | bytes 282632 | tf_op jit(solution)/shard_map/ppermute | solution.py:714

commit v16 on v13

--- a/solution.py
+++ b/solution.py
@@ -76,31 +76,39 @@
 
 
 def pack_kernel(row_size, eps_hbm, elec_hbm, magn_hbm, mat_hbm, z_ref, own_ref, even_ref, odd_ref, *rest):
-    x_refs, (state_ref, main_ref, eps_ref, mat_ref, sems) = rest[:-5], rest[-5:]
-    copies = [pltpu.make_async_copy(eps_hbm, eps_ref, sems.at[0]), pltpu.make_async_copy(mat_hbm, mat_ref, sems.at[1])]
-    copies.append(pltpu.make_async_copy(elec_hbm, main_ref.at[pl.ds(0, 3)], sems.at[2]))
-    copies.append(pltpu.make_async_copy(magn_hbm, main_ref.at[pl.ds(3, 3)], sems.at[3]))
+    n_x = 1 if row_size == 2 else 2
+    x_hbms, x_refs, (state_ref, main_ref, eps_ref, mat_ref, sems) = rest[:n_x], rest[n_x : 2 * n_x], rest[2 * n_x :]
+    copies = [pltpu.make_async_copy(eps_hbm, eps_ref, sems.at[6]), pltpu.make_async_copy(mat_hbm, mat_ref, sems.at[7])]
+    for f in range(3):
+        copies.append(pltpu.make_async_copy(elec_hbm.at[f], main_ref.at[f], sems.at[f]))
+    for f in range(3):
+        copies.append(pltpu.make_async_copy(magn_hbm.at[f], main_ref.at[3 + f], sems.at[3 + f]))
     for copy in copies:
         copy.start()
+    flat = main_ref.reshape(FIELDS * LAYERS * ROWS, 128)
     copies[0].wait()
     copies[1].wait()
     for z in range(LAYERS):
         main_ref[6, z] = coefficient(mat_ref[z], eps_ref)
-    copies[2].wait()
-    copies[3].wait()
+    rows_outside(flat, 6, state_ref, 6)
+    for f in range(6):
+        copies[2 + f].wait()
+        rows_outside(flat, f, state_ref, f)
+
+    def send(up, slot):
+        for i, (f, x) in enumerate(UP_PLANES if up else DOWN_PLANES):
+            x_refs[slot][i] = state_ref[f, x]
+
+    directions(row_size, send)
+    outs = [pltpu.make_async_copy(ref, hbm, sems.at[8 + i]) for i, (ref, hbm) in enumerate(zip(x_refs, x_hbms))]
+    for out in outs:
+        out.start()
     start = jnp.where(lax.axis_index("gz") == 0, LAYERS - DEPTH, 0)
     for f in range(FIELDS):
         z_ref[f] = main_ref[f, pl.ds(start, DEPTH)]
-    flat = main_ref.reshape(FIELDS * LAYERS * ROWS, 128)
-    for f in range(FIELDS):
-        rows_outside(flat, f, state_ref, f)
-
-    def send(up, slot):
-        for i, (f, x) in enumerate(UP_PLANES if up else DOWN_PLANES):
-            x_refs[slot][i] = state_ref[f, x]
-
-    directions(row_size, send)
     pack_edges(state_ref, own_ref, even_ref, odd_ref)
+    for out in outs:
+        out.wait()
 
 
 def lane_groups():
@@ -726,13 +734,14 @@
             ]
             + [array(PLANES, OWN, 8, 128)] * n_x,
             in_specs=[HBM] * 4,
-            out_specs=[VMEM] * (4 + n_x),
-            scratch_shapes=[
+            out_specs=[VMEM] * 4 + [HBM] * n_x,
+            scratch_shapes=[scratch(PLANES, OWN, 8, 128)] * n_x
+            + [
                 scratch(FIELDS, ROWS, OWN, 8, 128),
                 scratch(FIELDS, LAYERS, ROWS, 128),
                 pltpu.SMEM(eps_table.shape, f32),
                 pltpu.VMEM(material.shape, jnp.int32),
-                pltpu.SemaphoreType.DMA((4,)),
+                pltpu.SemaphoreType.DMA((10,)),
             ],
             name="pack",
         )(eps_table, electric, magnetic, material)
@@ -777,7 +786,7 @@
             scratch_shapes=[scratch(PORT_TILE, LAYERS, 128)],
             compiler_params=PARAMS,
             name="weights",
-        )(mode_table, port_row, port_col, port_mode, port_ids, layer_send)
+        )(mode_table, port_row, port_col, port_mode, port_ids, c_now)
         corner_send = pl.pallas_call(
             functools.partial(corner_kernel, row_size),
             out_shape=[array(PAIRS + 2 * CHUNK, 8, 128)] * n_x,

time: 35.1 us -> 35.2 us (level)
  no operation moved by 1% of the time
where the time goes in v16:
time: 35.2 us; the launch traced here: 35 us
  blocking collectives  12.5 us (36%)
  Pallas kernels  10.6 us (30%)
  starting transfers between devices  5.84 us (17%)
  waiting for transfers between devices  3.73 us (11%)
  local copies, waits for them, and re-layouts  0.94 us (3%)
  between operations  0.81 us (2%)
  other arithmetic  0.59 us (2%)
    all_to_all x1, blocking collectives, per_device(): terms = lax.all_to_all(term, ('col', 'row', 'gz'), 0, 0, tiled=True)  12.5 us
    ppermute x6, starting transfers between devices, swapped(): return lax.ppermute(block, axis, pairs + [(j, i) for i, j in pairs])  5.84 us
    ppermute x6, waiting for transfers between devices, swapped(): return lax.ppermute(block, axis, pairs + [(j, i) for i, j in pairs])  3.73 us
    pallas_call x1, Pallas kernels, per_device(): pl.pallas_call(functools.partial(outer_kernel, row_size, ports_each), out...  3.27 us
    pallas_call x1, Pallas kernels, per_device(): pl.pallas_call(functools.partial(pack_kernel, row_size), out_shape=[array...  2.94 us
    pallas_call x1, Pallas kernels, per_device(): pl.pallas_call(functools.partial(rim_kernel, row_size), out_shape=[array(...  2.01 us
    pallas_call x1, Pallas kernels, per_device(): pl.pallas_call(functools.partial(inner_kernel, row_size), out_shape=[arra...  1.54 us
    unnamed x20, local copies, waits for them, and re-layouts  0.94 us
  transfers between devices with their start and end apart: 6, of which 2 were waited for; matrix products, arithmetic and copies ran while one was open for 0% of the time, Pallas kernels for 13%

profile of v16, /device:TPU:0, one launch (start us, length us, event | category | flops | bytes accessed | tf_op | source)
XLA Modules:
  0.0 35.0 jit_solution(5472065632332260189)
XLA Ops:
  0.6 0.0 copy-start.2
  0.6 0.0 copy-start.1
  0.7 0.0 copy-start
  0.7 2.9 %pack.1 = (f32[7,4,8,128]{3,2,1,0:T(8,128)}, f32[7,2,4,8,128]{4,3,2,1,0:T(8,128)}, f32[2,4,8,128]{3,2,1,0:T(8,128)}, f32[2,4,8,128]{3,2,1,0:T(8,128)}, f32[26,4,8,128]{3,2,1,0:T(8,128)}) custom-call(f32[8]{0:T(128)} %eps_ref.1, f32[3,32,8,128]{3,2,1,0:T(8,128)} %elec_ref.1, f32[3,32,8,128]{3,2,1,0:T(8,128)} %magn_ref.1, s32[32,8,128]{2,1,0:T(8,128)} %mat_ref.1), custom_call_target="tpu_custom_call" | custom-call | tf_op jit(solution)/shard_map/pack/pallas_call | solution.py:727
  3.6 3.0 %collective-permute-start.4 = (f32[26,4,8,128]{3,2,1,0:T(8,128)}, f32[26,4,8,128]{3,2,1,0:T(8,128)S(1)}, u32[]{:S(2)}, u32[]{:S(2)}) collective-permute-start(f32[26,4,8,128]{3,2,1,0:T(8,128)} %get-tuple-element.33), channel_id=1, source_target_pairs={{0,2},{2,0},{1,3},{3,1},{4,6},{6,4},{5,7},{7,5},{8,10},{10,8},{9,1... | collective-permute-start | bytes 1277960 | tf_op jit(solution)/shard_map/ppermute | solution.py:703
  6.6 0.0 collective-permute-start
  6.6 1.6 %collective-permute-start.1 = (f32[2,4,8,128]{3,2,1,0:T(8,128)}, f32[2,4,8,128]{3,2,1,0:T(8,128)S(1)}, u32[]{:S(2)}, u32[]{:S(2)}) collective-permute-start(f32[2,4,8,128]{3,2,1,0:T(8,128)} %get-tuple-element.25), channel_id=1, source_target_pairs={{0,4},{8,12},{4,0},{12,8},{1,5},{9,13},{5,1},{13,9},{2,6},{10,14},... | collective-permute-start | bytes 98312 | tf_op jit(solution)/shard_map/ppermute | solution.py:703
  8.2 0.7 %collective-permute-start.2 = (f32[2,4,8,128]{3,2,1,0:T(8,128)}, f32[2,4,8,128]{3,2,1,0:T(8,128)S(1)}, u32[]{:S(2)}, u32[]{:S(2)}) collective-permute-start(f32[2,4,8,128]{3,2,1,0:T(8,128)} %get-tuple-element.26), channel_id=1, source_target_pairs={{4,8},{8,4},{5,9},{9,5},{6,10},{10,6},{7,11},{11,7},{20,24},{24,20... | collective-permute-start | bytes 98312 | tf_op jit(solution)/shard_map/ppermute | solution.py:703
  8.9 0.0 collective-permute-done.z_ref
  8.9 1.5 %inner.1 = (f32[3,8,5,8,128]{4,3,2,1,0:T(8,128)S(1)}, f32[3,8,5,8,128]{4,3,2,1,0:T(8,128)S(1)}, f32[8,5,8,128]{3,2,1,0:T(8,128)S(1)}, f32[4,8,4,8,128]{4,3,2,1,0:T(8,128)S(1)}) custom-call(f32[3,32,8,128]{3,2,1,0:T(8,128)S(1)} %copy-done, f32[3,32,8,128]{3,2,1,0:T(8,128)S(1)} %copy-done.1, s32[32,8,128]{2,1,0:T(8,128)S(1)} %copy-done.2, ...), custom_call_target="tpu_custom_call" | custom-call | flops 5000000 | bytes 10000000 | tf_op jit(solution)/shard_map/inner/pallas_call | solution.py:752
  10.5 0.0 copy-start.4
  10.5 0.3 collective-permute-done.1.even_ref
  10.7 0.0 collective-permute-done.2.odd_ref
  10.8 0.0 copy-start.9
  10.8 0.1 collective-permute-start.3
  10.9 0.5 %copy-done.4 = f32[8,32,64]{2,1,0:T(8,128)S(1)} copy-done((f32[8,32,64]{2,1,0:T(8,128)S(1)}, f32[8,32,64]{2,1,0:T(8,128)}, u32[]{:S(2)}) %copy-start.4) | copy-done | bytes 65560
  11.4 0.1 copy-done.5
  11.4 0.0 copy-done.7
  11.4 0.0 copy-done.8
  11.5 0.0 copy-done.9
  11.5 0.8 %weights.1.weight_ref = f32[4,2,4,8,128]{4,3,2,1,0:T(8,128)S(1)} custom-call(f32[8,32,64]{2,1,0:T(8,128)S(1)} %copy-done.4, s32[1,1,4]{2,1,0:T(1,128)S(1)} %copy-done.5, s32[1,1,4]{2,1,0:T(1,128)S(1)} %copy-done.8, s32[1,1,4]{2,1,0:T(1,128)S(1)} %copy-done.9, s32[1,1,4]{2,1,0:T(1,128)S(1)} %copy-done.7, ...), custom_call_target="tpu_custom_call" | custom-call | tf_op jit(solution)/shard_map/weights/pallas_call | solution.py:781
  12.3 0.0 copy-start.3
  12.3 0.0 collective-permute-done.3.layer_ref
  12.3 0.1 corners.1
  12.3 0.5 %collective-permute-start.5 = (f32[23,8,128]{2,1,0:T(8,128)S(1)}, f32[23,8,128]{2,1,0:T(8,128)S(1)}, u32[]{:S(2)}, u32[]{:S(2)}) collective-permute-start(f32[23,8,128]{2,1,0:T(8,128)S(1)} %corners.1), channel_id=1, source_target_pairs={{0,2},{2,0},{1,3},{3,1},{4,6},{6,4},{5,7},{7,5},{8,10},{10,8},{9,1... | collective-permute-start | bytes 282632 | tf_op jit(solution)/shard_map/ppermute | solution.py:703
  12.9 0.3 copy-done.3
  13.2 2.0 %rim.1 = (f32[3,2,5,8,128]{4,3,2,1,0:T(8,128)S(1)}, f32[3,2,5,8,128]{4,3,2,1,0:T(8,128)S(1)}, f32[2,5,8,128]{3,2,1,0:T(8,128)S(1)}, f32[6,4,4,8,128]{4,3,2,1,0:T(8,128)S(1)}, f32[4,8,128]{2,1,0:T(8,128)S(1)}) custom-call(f32[7,4,8,128]{3,2,1,0:T(8,128)S(1)} %collective-permute-done.z_ref, f32[7,2,4,8,128]{4,3,2,1,0:T(8,128)S(1)} %copy-done.3, ...), custom_call_target="tpu_custom_call" | custom-call | tf_op jit(solution)/shard_map/rim/pallas_call | solution.py:800
  15.2 3.4 %collective-permute-done.5.rest_1_ = f32[23,8,128]{2,1,0:T(8,128)S(1)} collective-permute-done((f32[23,8,128]{2,1,0:T(8,128)S(1)}, f32[23,8,128]{2,1,0:T(8,128)S(1)}, u32[]{:S(2)}, u32[]{:S(2)}) %collective-permute-start.5) | collective-permute-done | bytes 94240 | tf_op jit(solution)/shard_map/ppermute | solution.py:703
  18.7 0.0 collective-permute-done.4.rest_0_
  18.7 3.3 %outer.1 = (f32[3,32,8,128]{3,2,1,0:T(8,128)}, f32[3,32,8,128]{3,2,1,0:T(8,128)}, f32[16,2,16]{2,1,0:T(2,128)S(1)}) custom-call(s32[1,1,4]{2,1,0:T(1,128)S(1)} %copy-done.5, s32[1,1,4]{2,1,0:T(1,128)S(1)} %copy-done.7, f32[3,8,5,8,128]{4,3,2,1,0:T(8,128)S(1)} %get-tuple-element.21.e_in, f32[3,8,5,8,128]{4,3,2,1,0:T(8,128)S(1)} %get-tuple-element.22.h_in, ...), custom_call_target="tpu_custom_call" | custom-call | tf_op jit(solution)/shard_map/outer/pallas_call | solution.py:817
  21.9 12.5 %all_to_all.5 = f32[16,2,16]{2,1,0:T(2,128)S(1)} all-to-all(f32[16,2,16]{2,1,0:T(2,128)S(1)} %get-tuple-element.36), channel_id=1, replica_groups=mesh['grp'=2,'col'=4,'row'=2,'gz'=2] {'col','row','gz'}, dimensions={0} | all-to-all | bytes 4096 | tf_op jit(solution)/shard_map/all_to_all | solution.py:833
  34.4 0.6 %reduce_sum.9 = f32[2,16]{1,0:T(2,128)} reduce(f32[16,2,16]{2,1,0:T(2,128)S(1)} %all_to_all.5, f32[]{:T(128)} %constant.0.clone.1), dimensions={0}, to_apply=%region_0.0 | reduce | flops 480 | bytes 2180 | tf_op jit(solution)/shard_map/reduce_sum | solution.py:837
  (9 shorter events, 0.0 us)
Async XLA Ops:
  0.6 8.2 %copy-start.2 = (s32[32,8,128]{2,1,0:T(8,128)S(1)}, s32[32,8,128]{2,1,0:T(8,128)}, u32[]{:S(2)}) copy-start(s32[32,8,128]{2,1,0:T(8,128)} %mat_ref.1) | copy-start | bytes 393220
  0.6 8.2 %copy-start.1 = (f32[3,32,8,128]{3,2,1,0:T(8,128)S(1)}, f32[3,32,8,128]{3,2,1,0:T(8,128)}, u32[]{:S(2)}) copy-start(f32[3,32,8,128]{3,2,1,0:T(8,128)} %magn_ref.1) | copy-start | bytes 1179652
  0.7 8.2 %copy-start = (f32[3,32,8,128]{3,2,1,0:T(8,128)S(1)}, f32[3,32,8,128]{3,2,1,0:T(8,128)}, u32[]{:S(2)}) copy-start(f32[3,32,8,128]{3,2,1,0:T(8,128)} %elec_ref.1) | copy-start | bytes 1179652
  3.6 15.1 %collective-permute-start.4 = (f32[26,4,8,128]{3,2,1,0:T(8,128)}, f32[26,4,8,128]{3,2,1,0:T(8,128)S(1)}, u32[]{:S(2)}, u32[]{:S(2)}) collective-permute-start(f32[26,4,8,128]{3,2,1,0:T(8,128)} %get-tuple-element.33), channel_id=1, source_target_pairs={{0,2},{2,0},{1,3},{3,1},{4,6},{6,4},{5,7},{7,5},{8,10},{10,8},{9,1... | collective-permute-start | bytes 1277960 | tf_op jit(solution)/shard_map/ppermute | solution.py:703
  6.6 2.2 %collective-permute-start = (f32[7,4,8,128]{3,2,1,0:T(8,128)}, f32[7,4,8,128]{3,2,1,0:T(8,128)S(1)}, u32[]{:S(2)}, u32[]{:S(2)}) collective-permute-start(f32[7,4,8,128]{3,2,1,0:T(8,128)} %get-tuple-element.20), channel_id=1, source_target_pairs={{0,1},{1,0},{2,3},{3,2},{4,5},{5,4},{6,7},{7,6},{8,9},{9,8},{10,11... | collective-permute-start | bytes 344072 | tf_op jit(solution)/shard_map/ppermute | solution.py:703
  6.6 2.3 %copy-start.6 = (f32[8]{0:T(128)S(1)}, f32[8]{0:T(128)}, u32[]{:S(2)}) copy-start(f32[8]{0:T(128)} %eps_ref.1) | copy-start | bytes 100
  6.6 4.1 %collective-permute-start.1 = (f32[2,4,8,128]{3,2,1,0:T(8,128)}, f32[2,4,8,128]{3,2,1,0:T(8,128)S(1)}, u32[]{:S(2)}, u32[]{:S(2)}) collective-permute-start(f32[2,4,8,128]{3,2,1,0:T(8,128)} %get-tuple-element.25), channel_id=1, source_target_pairs={{0,4},{8,12},{4,0},{12,8},{1,5},{9,13},{5,1},{13,9},{2,6},{10,14},... | collective-permute-start | bytes 98312 | tf_op jit(solution)/shard_map/ppermute | solution.py:703
  8.2 2.6 %collective-permute-start.2 = (f32[2,4,8,128]{3,2,1,0:T(8,128)}, f32[2,4,8,128]{3,2,1,0:T(8,128)S(1)}, u32[]{:S(2)}, u32[]{:S(2)}) collective-permute-start(f32[2,4,8,128]{3,2,1,0:T(8,128)} %get-tuple-element.26), channel_id=1, source_target_pairs={{4,8},{8,4},{5,9},{9,5},{6,10},{10,6},{7,11},{11,7},{20,24},{24,20... | collective-permute-start | bytes 98312 | tf_op jit(solution)/shard_map/ppermute | solution.py:703
  10.5 0.9 %copy-start.4 = (f32[8,32,64]{2,1,0:T(8,128)S(1)}, f32[8,32,64]{2,1,0:T(8,128)}, u32[]{:S(2)}) copy-start(f32[8,32,64]{2,1,0:T(8,128)} %mode_ref.1) | copy-start | bytes 196612
  10.7 0.7 %copy-start.5 = (s32[1,1,4]{2,1,0:T(1,128)S(1)}, s32[1,1,4]{2,1,0:T(1,128)}, u32[]{:S(2)}) copy-start(s32[1,1,4]{2,1,0:T(1,128)} %prow_ref.5) | copy-start | bytes 52
  10.7 0.7 %copy-start.7 = (s32[1,1,4]{2,1,0:T(1,128)S(1)}, s32[1,1,4]{2,1,0:T(1,128)}, u32[]{:S(2)}) copy-start(s32[1,1,4]{2,1,0:T(1,128)} %pid_ref.3) | copy-start | bytes 52
  10.8 0.7 %copy-start.8 = (s32[1,1,4]{2,1,0:T(1,128)S(1)}, s32[1,1,4]{2,1,0:T(1,128)}, u32[]{:S(2)}) copy-start(s32[1,1,4]{2,1,0:T(1,128)} %pcol_ref.1) | copy-start | bytes 52
  10.8 0.7 %copy-start.9 = (s32[1,1,4]{2,1,0:T(1,128)S(1)}, s32[1,1,4]{2,1,0:T(1,128)}, u32[]{:S(2)}) copy-start(s32[1,1,4]{2,1,0:T(1,128)} %pmode_ref.1) | copy-start | bytes 52
  10.8 1.5 %collective-permute-start.3 = (f32[2,2,8,128]{3,2,1,0:T(8,128)S(1)}, f32[2,2,8,128]{3,2,1,0:T(8,128)S(1)}, u32[]{:S(2)}, u32[]{:S(2)}) collective-permute-start(f32[2,2,8,128]{3,2,1,0:T(8,128)S(1)} %layer_edges.1), channel_id=1, source_target_pairs={{0,1},{1,0},{2,3},{3,2},{4,5},{5,4},{6,7},{7,6},{8,9},{9,8},{10,11... | collective-permute-start | bytes 49160 | tf_op jit(solution)/shard_map/ppermute | solution.py:703
  12.3 0.9 %copy-start.3 = (f32[7,2,4,8,128]{4,3,2,1,0:T(8,128)S(1)}, f32[7,2,4,8,128]{4,3,2,1,0:T(8,128)}, u32[]{:S(2)}) copy-start(f32[7,2,4,8,128]{4,3,2,1,0:T(8,128)} %get-tuple-element.24.own_ref) | copy-start | bytes 688132
  12.3 6.3 %collective-permute-start.5 = (f32[23,8,128]{2,1,0:T(8,128)S(1)}, f32[23,8,128]{2,1,0:T(8,128)S(1)}, u32[]{:S(2)}, u32[]{:S(2)}) collective-permute-start(f32[23,8,128]{2,1,0:T(8,128)S(1)} %corners.1), channel_id=1, source_target_pairs={{0,2},{2,0},{1,3},{3,1},{4,6},{6,4},{5,7},{7,5},{8,10},{10,8},{9,1... | collective-permute-start | bytes 282632 | tf_op jit(solution)/shard_map/ppermute | solution.py:703

commit v17 on v13

--- a/solution.py
+++ b/solution.py
@@ -734,6 +734,7 @@
                 pltpu.VMEM(material.shape, jnp.int32),
                 pltpu.SemaphoreType.DMA((4,)),
             ],
+            compiler_params=pltpu.CompilerParams(vmem_limit_bytes=62_500_000),
             name="pack",
         )(eps_table, electric, magnetic, material)
         x_halo = across_rows(x_send)

time: 35.1 us -> 35.1 us (level)
  no operation moved by 1% of the time
where the time goes in v17:
time: 35.1 us; the launch traced here: 34.8 us
  blocking collectives  12.5 us (36%)
  Pallas kernels  10.5 us (30%)
  starting transfers between devices  5.84 us (17%)
  waiting for transfers between devices  3.73 us (11%)
  local copies, waits for them, and re-layouts  0.94 us (3%)
  between operations  0.81 us (2%)
  other arithmetic  0.59 us (2%)
    all_to_all x1, blocking collectives, per_device(): terms = lax.all_to_all(term, ('col', 'row', 'gz'), 0, 0, tiled=True)  12.5 us
    ppermute x6, starting transfers between devices, swapped(): return lax.ppermute(block, axis, pairs + [(j, i) for i, j in pairs])  5.84 us
    ppermute x6, waiting for transfers between devices, swapped(): return lax.ppermute(block, axis, pairs + [(j, i) for i, j in pairs])  3.73 us
    pallas_call x1, Pallas kernels, per_device(): pl.pallas_call(functools.partial(outer_kernel, row_size, ports_each), out...  3.27 us
    pallas_call x1, Pallas kernels, per_device(): pl.pallas_call(functools.partial(pack_kernel, row_size), out_shape=[array...  2.79 us
    pallas_call x1, Pallas kernels, per_device(): pl.pallas_call(functools.partial(rim_kernel, row_size), out_shape=[array(...  2.01 us
    pallas_call x1, Pallas kernels, per_device(): pl.pallas_call(functools.partial(inner_kernel, row_size), out_shape=[arra...  1.54 us
    unnamed x20, local copies, waits for them, and re-layouts  0.94 us
  transfers between devices with their start and end apart: 6, of which 2 were waited for; matrix products, arithmetic and copies ran while one was open for 0% of the time, Pallas kernels for 13%

profile of v17, /device:TPU:0, one launch (start us, length us, event | category | flops | bytes accessed | tf_op | source)
XLA Modules:
  0.0 34.8 jit_solution(10646421445080276762)
XLA Ops:
  0.6 0.0 copy-start.2
  0.6 0.0 copy-start.1
  0.7 0.0 copy-start
  0.7 2.8 %pack.1 = (f32[7,4,8,128]{3,2,1,0:T(8,128)}, f32[7,2,4,8,128]{4,3,2,1,0:T(8,128)}, f32[2,4,8,128]{3,2,1,0:T(8,128)}, f32[2,4,8,128]{3,2,1,0:T(8,128)}, f32[26,4,8,128]{3,2,1,0:T(8,128)}) custom-call(f32[8]{0:T(128)} %eps_ref.1, f32[3,32,8,128]{3,2,1,0:T(8,128)} %elec_ref.1, f32[3,32,8,128]{3,2,1,0:T(8,128)} %magn_ref.1, s32[32,8,128]{2,1,0:T(8,128)} %mat_ref.1), custom_call_target="tpu_custom_call" | custom-call | tf_op jit(solution)/shard_map/pack/pallas_call | solution.py:719
  3.5 3.0 %collective-permute-start.4 = (f32[26,4,8,128]{3,2,1,0:T(8,128)}, f32[26,4,8,128]{3,2,1,0:T(8,128)S(1)}, u32[]{:S(2)}, u32[]{:S(2)}) collective-permute-start(f32[26,4,8,128]{3,2,1,0:T(8,128)} %get-tuple-element.33), channel_id=1, source_target_pairs={{0,2},{2,0},{1,3},{3,1},{4,6},{6,4},{5,7},{7,5},{8,10},{10,8},{9,1... | collective-permute-start | bytes 1277960 | tf_op jit(solution)/shard_map/ppermute | solution.py:695
  6.5 0.0 collective-permute-start
  6.5 1.6 %collective-permute-start.1 = (f32[2,4,8,128]{3,2,1,0:T(8,128)}, f32[2,4,8,128]{3,2,1,0:T(8,128)S(1)}, u32[]{:S(2)}, u32[]{:S(2)}) collective-permute-start(f32[2,4,8,128]{3,2,1,0:T(8,128)} %get-tuple-element.24), channel_id=1, source_target_pairs={{0,4},{8,12},{4,0},{12,8},{1,5},{9,13},{5,1},{13,9},{2,6},{10,14},... | collective-permute-start | bytes 98312 | tf_op jit(solution)/shard_map/ppermute | solution.py:695
  8.0 0.7 %collective-permute-start.2 = (f32[2,4,8,128]{3,2,1,0:T(8,128)}, f32[2,4,8,128]{3,2,1,0:T(8,128)S(1)}, u32[]{:S(2)}, u32[]{:S(2)}) collective-permute-start(f32[2,4,8,128]{3,2,1,0:T(8,128)} %get-tuple-element.25), channel_id=1, source_target_pairs={{4,8},{8,4},{5,9},{9,5},{6,10},{10,6},{7,11},{11,7},{20,24},{24,20... | collective-permute-start | bytes 98312 | tf_op jit(solution)/shard_map/ppermute | solution.py:695
  8.7 0.0 collective-permute-done.z_ref
  8.7 1.5 %inner.1 = (f32[3,8,5,8,128]{4,3,2,1,0:T(8,128)S(1)}, f32[3,8,5,8,128]{4,3,2,1,0:T(8,128)S(1)}, f32[8,5,8,128]{3,2,1,0:T(8,128)S(1)}, f32[4,8,4,8,128]{4,3,2,1,0:T(8,128)S(1)}) custom-call(f32[3,32,8,128]{3,2,1,0:T(8,128)S(1)} %copy-done, f32[3,32,8,128]{3,2,1,0:T(8,128)S(1)} %copy-done.1, s32[32,8,128]{2,1,0:T(8,128)S(1)} %copy-done.2, ...), custom_call_target="tpu_custom_call" | custom-call | flops 5000000 | bytes 10000000 | tf_op jit(solution)/shard_map/inner/pallas_call | solution.py:744
  10.3 0.0 copy-start.4
  10.3 0.3 collective-permute-done.1.even_ref
  10.6 0.0 collective-permute-done.2.odd_ref
  10.6 0.0 copy-start.9
  10.6 0.1 collective-permute-start.3
  10.7 0.5 %copy-done.4 = f32[8,32,64]{2,1,0:T(8,128)S(1)} copy-done((f32[8,32,64]{2,1,0:T(8,128)S(1)}, f32[8,32,64]{2,1,0:T(8,128)}, u32[]{:S(2)}) %copy-start.4) | copy-done | bytes 65560
  11.2 0.1 copy-done.5
  11.3 0.0 copy-done.7
  11.3 0.0 copy-done.8
  11.3 0.0 copy-done.9
  11.3 0.8 %weights.1.weight_ref = f32[4,2,4,8,128]{4,3,2,1,0:T(8,128)S(1)} custom-call(f32[8,32,64]{2,1,0:T(8,128)S(1)} %copy-done.4, s32[1,1,4]{2,1,0:T(1,128)S(1)} %copy-done.5, s32[1,1,4]{2,1,0:T(1,128)S(1)} %copy-done.8, s32[1,1,4]{2,1,0:T(1,128)S(1)} %copy-done.9, s32[1,1,4]{2,1,0:T(1,128)S(1)} %copy-done.7, f32[2,2,8,128]{3,2,1,0:T(8,128)S(1)} %layer_edges.1.order_ref), custom_call_target="tpu_custom_call" | custom-call | tf_op jit(solution)/shard_map/weights/pallas_call | solution.py:773
  12.1 0.0 copy-start.3
  12.1 0.0 collective-permute-done.3.layer_ref
  12.1 0.1 corners.1
  12.2 0.5 %collective-permute-start.5 = (f32[23,8,128]{2,1,0:T(8,128)S(1)}, f32[23,8,128]{2,1,0:T(8,128)S(1)}, u32[]{:S(2)}, u32[]{:S(2)}) collective-permute-start(f32[23,8,128]{2,1,0:T(8,128)S(1)} %corners.1), channel_id=1, source_target_pairs={{0,2},{2,0},{1,3},{3,1},{4,6},{6,4},{5,7},{7,5},{8,10},{10,8},{9,1... | collective-permute-start | bytes 282632 | tf_op jit(solution)/shard_map/ppermute | solution.py:695
  12.7 0.3 copy-done.3
  13.0 2.0 %rim.1 = (f32[3,2,5,8,128]{4,3,2,1,0:T(8,128)S(1)}, f32[3,2,5,8,128]{4,3,2,1,0:T(8,128)S(1)}, f32[2,5,8,128]{3,2,1,0:T(8,128)S(1)}, f32[6,4,4,8,128]{4,3,2,1,0:T(8,128)S(1)}, f32[4,8,128]{2,1,0:T(8,128)S(1)}) custom-call(f32[7,4,8,128]{3,2,1,0:T(8,128)S(1)} %collective-permute-done.z_ref, f32[7,2,4,8,128]{4,3,2,1,0:T(8,128)S(1)} %copy-done.3, ...), custom_call_target="tpu_custom_call" | custom-call | tf_op jit(solution)/shard_map/rim/pallas_call | solution.py:792
  15.1 3.4 %collective-permute-done.5.rest_1_ = f32[23,8,128]{2,1,0:T(8,128)S(1)} collective-permute-done((f32[23,8,128]{2,1,0:T(8,128)S(1)}, f32[23,8,128]{2,1,0:T(8,128)S(1)}, u32[]{:S(2)}, u32[]{:S(2)}) %collective-permute-start.5) | collective-permute-done | bytes 94240 | tf_op jit(solution)/shard_map/ppermute | solution.py:695
  18.5 0.0 collective-permute-done.4.rest_0_
  18.5 3.3 %outer.1 = (f32[3,32,8,128]{3,2,1,0:T(8,128)}, f32[3,32,8,128]{3,2,1,0:T(8,128)}, f32[16,2,16]{2,1,0:T(2,128)S(1)}) custom-call(s32[1,1,4]{2,1,0:T(1,128)S(1)} %copy-done.5, s32[1,1,4]{2,1,0:T(1,128)S(1)} %copy-done.7, f32[3,8,5,8,128]{4,3,2,1,0:T(8,128)S(1)} %get-tuple-element.21.e_in, f32[3,8,5,8,128]{4,3,2,1,0:T(8,128)S(1)} %get-tuple-element.22.h_in, ...), custom_call_target="tpu_custom_call" | custom-call | tf_op jit(solution)/shard_map/outer/pallas_call | solution.py:809
  21.8 12.5 %all_to_all.5 = f32[16,2,16]{2,1,0:T(2,128)S(1)} all-to-all(f32[16,2,16]{2,1,0:T(2,128)S(1)} %get-tuple-element.36), channel_id=1, replica_groups=mesh['grp'=2,'col'=4,'row'=2,'gz'=2] {'col','row','gz'}, dimensions={0} | all-to-all | bytes 4096 | tf_op jit(solution)/shard_map/all_to_all | solution.py:825
  34.3 0.6 %reduce_sum.9 = f32[2,16]{1,0:T(2,128)} reduce(f32[16,2,16]{2,1,0:T(2,128)S(1)} %all_to_all.5, f32[]{:T(128)} %constant.0.clone.1), dimensions={0}, to_apply=%region_0.0 | reduce | flops 480 | bytes 2180 | tf_op jit(solution)/shard_map/reduce_sum | solution.py:829
  (9 shorter events, 0.0 us)
Async XLA Ops:
  0.6 8.1 %copy-start.2 = (s32[32,8,128]{2,1,0:T(8,128)S(1)}, s32[32,8,128]{2,1,0:T(8,128)}, u32[]{:S(2)}) copy-start(s32[32,8,128]{2,1,0:T(8,128)} %mat_ref.1) | copy-start | bytes 393220
  0.6 8.1 %copy-start.1 = (f32[3,32,8,128]{3,2,1,0:T(8,128)S(1)}, f32[3,32,8,128]{3,2,1,0:T(8,128)}, u32[]{:S(2)}) copy-start(f32[3,32,8,128]{3,2,1,0:T(8,128)} %magn_ref.1) | copy-start | bytes 1179652
  0.7 8.1 %copy-start = (f32[3,32,8,128]{3,2,1,0:T(8,128)S(1)}, f32[3,32,8,128]{3,2,1,0:T(8,128)}, u32[]{:S(2)}) copy-start(f32[3,32,8,128]{3,2,1,0:T(8,128)} %elec_ref.1) | copy-start | bytes 1179652
  3.5 15.1 %collective-permute-start.4 = (f32[26,4,8,128]{3,2,1,0:T(8,128)}, f32[26,4,8,128]{3,2,1,0:T(8,128)S(1)}, u32[]{:S(2)}, u32[]{:S(2)}) collective-permute-start(f32[26,4,8,128]{3,2,1,0:T(8,128)} %get-tuple-element.33), channel_id=1, source_target_pairs={{0,2},{2,0},{1,3},{3,1},{4,6},{6,4},{5,7},{7,5},{8,10},{10,8},{9,1... | collective-permute-start | bytes 1277960 | tf_op jit(solution)/shard_map/ppermute | solution.py:695
  6.5 2.2 %collective-permute-start = (f32[7,4,8,128]{3,2,1,0:T(8,128)}, f32[7,4,8,128]{3,2,1,0:T(8,128)S(1)}, u32[]{:S(2)}, u32[]{:S(2)}) collective-permute-start(f32[7,4,8,128]{3,2,1,0:T(8,128)} %get-tuple-element.20), channel_id=1, source_target_pairs={{0,1},{1,0},{2,3},{3,2},{4,5},{5,4},{6,7},{7,6},{8,9},{9,8},{10,11... | collective-permute-start | bytes 344072 | tf_op jit(solution)/shard_map/ppermute | solution.py:695
  6.5 2.3 %copy-start.6 = (f32[8]{0:T(128)S(1)}, f32[8]{0:T(128)}, u32[]{:S(2)}) copy-start(f32[8]{0:T(128)} %eps_ref.1) | copy-start | bytes 100
  6.5 4.1 %collective-permute-start.1 = (f32[2,4,8,128]{3,2,1,0:T(8,128)}, f32[2,4,8,128]{3,2,1,0:T(8,128)S(1)}, u32[]{:S(2)}, u32[]{:S(2)}) collective-permute-start(f32[2,4,8,128]{3,2,1,0:T(8,128)} %get-tuple-element.24), channel_id=1, source_target_pairs={{0,4},{8,12},{4,0},{12,8},{1,5},{9,13},{5,1},{13,9},{2,6},{10,14},... | collective-permute-start | bytes 98312 | tf_op jit(solution)/shard_map/ppermute | solution.py:695
  8.0 2.6 %collective-permute-start.2 = (f32[2,4,8,128]{3,2,1,0:T(8,128)}, f32[2,4,8,128]{3,2,1,0:T(8,128)S(1)}, u32[]{:S(2)}, u32[]{:S(2)}) collective-permute-start(f32[2,4,8,128]{3,2,1,0:T(8,128)} %get-tuple-element.25), channel_id=1, source_target_pairs={{4,8},{8,4},{5,9},{9,5},{6,10},{10,6},{7,11},{11,7},{20,24},{24,20... | collective-permute-start | bytes 98312 | tf_op jit(solution)/shard_map/ppermute | solution.py:695
  10.3 0.9 %copy-start.4 = (f32[8,32,64]{2,1,0:T(8,128)S(1)}, f32[8,32,64]{2,1,0:T(8,128)}, u32[]{:S(2)}) copy-start(f32[8,32,64]{2,1,0:T(8,128)} %mode_ref.1) | copy-start | bytes 196612
  10.6 0.7 %copy-start.5 = (s32[1,1,4]{2,1,0:T(1,128)S(1)}, s32[1,1,4]{2,1,0:T(1,128)}, u32[]{:S(2)}) copy-start(s32[1,1,4]{2,1,0:T(1,128)} %prow_ref.5) | copy-start | bytes 52
  10.6 0.7 %copy-start.7 = (s32[1,1,4]{2,1,0:T(1,128)S(1)}, s32[1,1,4]{2,1,0:T(1,128)}, u32[]{:S(2)}) copy-start(s32[1,1,4]{2,1,0:T(1,128)} %pid_ref.3) | copy-start | bytes 52
  10.6 0.7 %copy-start.8 = (s32[1,1,4]{2,1,0:T(1,128)S(1)}, s32[1,1,4]{2,1,0:T(1,128)}, u32[]{:S(2)}) copy-start(s32[1,1,4]{2,1,0:T(1,128)} %pcol_ref.1) | copy-start | bytes 52
  10.6 0.7 %copy-start.9 = (s32[1,1,4]{2,1,0:T(1,128)S(1)}, s32[1,1,4]{2,1,0:T(1,128)}, u32[]{:S(2)}) copy-start(s32[1,1,4]{2,1,0:T(1,128)} %pmode_ref.1) | copy-start | bytes 52
  10.6 1.5 %collective-permute-start.3 = (f32[2,2,8,128]{3,2,1,0:T(8,128)S(1)}, f32[2,2,8,128]{3,2,1,0:T(8,128)S(1)}, u32[]{:S(2)}, u32[]{:S(2)}) collective-permute-start(f32[2,2,8,128]{3,2,1,0:T(8,128)S(1)} %layer_edges.1.order_ref), channel_id=1, source_target_pairs={{0,1},{1,0},{2,3},{3,2},{4,5},{5,4},{6,7},{7,6},{8,9},{9,8},{10,11... | collective-permute-start | bytes 49160 | tf_op jit(solution)/shard_map/ppermute | solution.py:695
  12.1 0.9 %copy-start.3 = (f32[7,2,4,8,128]{4,3,2,1,0:T(8,128)S(1)}, f32[7,2,4,8,128]{4,3,2,1,0:T(8,128)}, u32[]{:S(2)}) copy-start(f32[7,2,4,8,128]{4,3,2,1,0:T(8,128)} %get-tuple-element.26.own_ref) | copy-start | bytes 688132
  12.2 6.3 %collective-permute-start.5 = (f32[23,8,128]{2,1,0:T(8,128)S(1)}, f32[23,8,128]{2,1,0:T(8,128)S(1)}, u32[]{:S(2)}, u32[]{:S(2)}) collective-permute-start(f32[23,8,128]{2,1,0:T(8,128)S(1)} %corners.1), channel_id=1, source_target_pairs={{0,2},{2,0},{1,3},{3,1},{4,6},{6,4},{5,7},{7,5},{8,10},{10,8},{9,1... | collective-permute-start | bytes 282632 | tf_op jit(solution)/shard_map/ppermute | solution.py:695

commit v18 on v13

--- a/solution.py
+++ b/solution.py
@@ -650,7 +650,11 @@
         copies = []
 
         def hand_out(part):
-            fields = range(3 * part, 3 * part + 3)
+            for f in range(3 * part, 3 * part + 3):
+                hand_out_field(part, f)
+
+        def hand_out_field(part, field):
+            fields = range(field, field + 1)
 
             def write(f, r, zz, tile, b):
                 turned_ref[f, 4 * b + r, 8 * zz : 8 * zz + 8, :] = tile
@@ -669,7 +673,7 @@
                 for z in range(LAYERS):
                     out_ref[f, z] = flat[pl.ds(f * ROWS * LAYERS + z, ROWS, stride=LAYERS), :]
             dest = hout_hbm if part else eout_hbm
-            copies.append(pltpu.make_async_copy(out_ref.at[pl.ds(3 * part, 3)], dest, sems.at[part]))
+            copies.append(pltpu.make_async_copy(out_ref.at[field], dest.at[field % 3], sems.at[field]))
             copies[-1].start()
 
         stepper = Stepper(row_size, main, edge, rows, blocks, True)
@@ -816,7 +820,7 @@
                 scratch(STEPS, 8, 128),
                 scratch(6, ROWS, LAYERS, 128),
                 scratch(6, LAYERS, ROWS, 128),
-                pltpu.SemaphoreType.DMA((2,)),
+                pltpu.SemaphoreType.DMA((6,)),
             ],
             compiler_params=PARAMS,
             name="outer",

time: 35.1 us -> 35.1 us (level)
  no operation moved by 1% of the time
where the time goes in v18:
time: 35.1 us; the launch traced here: 34.8 us
  blocking collectives  12.5 us (36%)
  Pallas kernels  10.4 us (30%)
  starting transfers between devices  5.84 us (17%)
  waiting for transfers between devices  3.73 us (11%)
  local copies, waits for them, and re-layouts  0.94 us (3%)
  between operations  0.81 us (2%)
  other arithmetic  0.59 us (2%)
    all_to_all x1, blocking collectives, per_device(): terms = lax.all_to_all(term, ('col', 'row', 'gz'), 0, 0, tiled=True)  12.5 us
    ppermute x6, starting transfers between devices, swapped(): return lax.ppermute(block, axis, pairs + [(j, i) for i, j in pairs])  5.84 us
    ppermute x6, waiting for transfers between devices, swapped(): return lax.ppermute(block, axis, pairs + [(j, i) for i, j in pairs])  3.73 us
    pallas_call x1, Pallas kernels, per_device(): pl.pallas_call(functools.partial(outer_kernel, row_size, ports_each), out...  3.26 us
    pallas_call x1, Pallas kernels, per_device(): pl.pallas_call(functools.partial(pack_kernel, row_size), out_shape=[array...  2.79 us
    pallas_call x1, Pallas kernels, per_device(): pl.pallas_call(functools.partial(rim_kernel, row_size), out_shape=[array(...  2.01 us
    pallas_call x1, Pallas kernels, per_device(): pl.pallas_call(functools.partial(inner_kernel, row_size), out_shape=[arra...  1.54 us
    unnamed x20, local copies, waits for them, and re-layouts  0.94 us
  transfers between devices with their start and end apart: 6, of which 2 were waited for; matrix products, arithmetic and copies ran while one was open for 0% of the time, Pallas kernels for 13%

profile of v18, /device:TPU:0, one launch (start us, length us, event | category | flops | bytes accessed | tf_op | source)
XLA Modules:
  0.0 34.8 jit_solution(8773003085368747214)
XLA Ops:
  0.6 0.0 copy-start.2
  0.6 0.0 copy-start.1
  0.7 0.0 copy-start
  0.7 2.8 %pack.1 = (f32[7,4,8,128]{3,2,1,0:T(8,128)}, f32[7,2,4,8,128]{4,3,2,1,0:T(8,128)}, f32[2,4,8,128]{3,2,1,0:T(8,128)}, f32[2,4,8,128]{3,2,1,0:T(8,128)}, f32[26,4,8,128]{3,2,1,0:T(8,128)}) custom-call(f32[8]{0:T(128)} %eps_ref.1, f32[3,32,8,128]{3,2,1,0:T(8,128)} %elec_ref.1, f32[3,32,8,128]{3,2,1,0:T(8,128)} %magn_ref.1, s32[32,8,128]{2,1,0:T(8,128)} %mat_ref.1), custom_call_target="tpu_custom_call" | custom-call | tf_op jit(solution)/shard_map/pack/pallas_call | solution.py:723
  3.5 3.0 %collective-permute-start.4 = (f32[26,4,8,128]{3,2,1,0:T(8,128)}, f32[26,4,8,128]{3,2,1,0:T(8,128)S(1)}, u32[]{:S(2)}, u32[]{:S(2)}) collective-permute-start(f32[26,4,8,128]{3,2,1,0:T(8,128)} %get-tuple-element.33), channel_id=1, source_target_pairs={{0,2},{2,0},{1,3},{3,1},{4,6},{6,4},{5,7},{7,5},{8,10},{10,8},{9,1... | collective-permute-start | bytes 1277960 | tf_op jit(solution)/shard_map/ppermute | solution.py:699
  6.5 0.0 collective-permute-start
  6.5 1.6 %collective-permute-start.1 = (f32[2,4,8,128]{3,2,1,0:T(8,128)}, f32[2,4,8,128]{3,2,1,0:T(8,128)S(1)}, u32[]{:S(2)}, u32[]{:S(2)}) collective-permute-start(f32[2,4,8,128]{3,2,1,0:T(8,128)} %get-tuple-element.24), channel_id=1, source_target_pairs={{0,4},{8,12},{4,0},{12,8},{1,5},{9,13},{5,1},{13,9},{2,6},{10,14},... | collective-permute-start | bytes 98312 | tf_op jit(solution)/shard_map/ppermute | solution.py:699
  8.0 0.7 %collective-permute-start.2 = (f32[2,4,8,128]{3,2,1,0:T(8,128)}, f32[2,4,8,128]{3,2,1,0:T(8,128)S(1)}, u32[]{:S(2)}, u32[]{:S(2)}) collective-permute-start(f32[2,4,8,128]{3,2,1,0:T(8,128)} %get-tuple-element.25), channel_id=1, source_target_pairs={{4,8},{8,4},{5,9},{9,5},{6,10},{10,6},{7,11},{11,7},{20,24},{24,20... | collective-permute-start | bytes 98312 | tf_op jit(solution)/shard_map/ppermute | solution.py:699
  8.7 0.0 collective-permute-done.z_ref
  8.7 1.5 %inner.1 = (f32[3,8,5,8,128]{4,3,2,1,0:T(8,128)S(1)}, f32[3,8,5,8,128]{4,3,2,1,0:T(8,128)S(1)}, f32[8,5,8,128]{3,2,1,0:T(8,128)S(1)}, f32[4,8,4,8,128]{4,3,2,1,0:T(8,128)S(1)}) custom-call(f32[3,32,8,128]{3,2,1,0:T(8,128)S(1)} %copy-done, f32[3,32,8,128]{3,2,1,0:T(8,128)S(1)} %copy-done.1, s32[32,8,128]{2,1,0:T(8,128)S(1)} %copy-done.2, ...), custom_call_target="tpu_custom_call" | custom-call | flops 5000000 | bytes 10000000 | tf_op jit(solution)/shard_map/inner/pallas_call | solution.py:747
  10.3 0.0 copy-start.4
  10.3 0.3 collective-permute-done.1.even_ref
  10.6 0.0 collective-permute-done.2.odd_ref
  10.6 0.0 copy-start.9
  10.6 0.1 collective-permute-start.3
  10.7 0.5 %copy-done.4 = f32[8,32,64]{2,1,0:T(8,128)S(1)} copy-done((f32[8,32,64]{2,1,0:T(8,128)S(1)}, f32[8,32,64]{2,1,0:T(8,128)}, u32[]{:S(2)}) %copy-start.4) | copy-done | bytes 65560
  11.2 0.1 copy-done.5
  11.3 0.0 copy-done.7
  11.3 0.0 copy-done.8
  11.3 0.0 copy-done.9
  11.3 0.8 %weights.1.weight_ref = f32[4,2,4,8,128]{4,3,2,1,0:T(8,128)S(1)} custom-call(f32[8,32,64]{2,1,0:T(8,128)S(1)} %copy-done.4, s32[1,1,4]{2,1,0:T(1,128)S(1)} %copy-done.5, s32[1,1,4]{2,1,0:T(1,128)S(1)} %copy-done.8, s32[1,1,4]{2,1,0:T(1,128)S(1)} %copy-done.9, s32[1,1,4]{2,1,0:T(1,128)S(1)} %copy-done.7, f32[2,2,8,128]{3,2,1,0:T(8,128)S(1)} %layer_edges.1.order_ref), custom_call_target="tpu_custom_call" | custom-call | tf_op jit(solution)/shard_map/weights/pallas_call | solution.py:776
  12.1 0.0 copy-start.3
  12.1 0.0 collective-permute-done.3.layer_ref
  12.1 0.1 corners.1
  12.2 0.5 %collective-permute-start.5 = (f32[23,8,128]{2,1,0:T(8,128)S(1)}, f32[23,8,128]{2,1,0:T(8,128)S(1)}, u32[]{:S(2)}, u32[]{:S(2)}) collective-permute-start(f32[23,8,128]{2,1,0:T(8,128)S(1)} %corners.1), channel_id=1, source_target_pairs={{0,2},{2,0},{1,3},{3,1},{4,6},{6,4},{5,7},{7,5},{8,10},{10,8},{9,1... | collective-permute-start | bytes 282632 | tf_op jit(solution)/shard_map/ppermute | solution.py:699
  12.7 0.3 copy-done.3
  13.0 2.0 %rim.1 = (f32[3,2,5,8,128]{4,3,2,1,0:T(8,128)S(1)}, f32[3,2,5,8,128]{4,3,2,1,0:T(8,128)S(1)}, f32[2,5,8,128]{3,2,1,0:T(8,128)S(1)}, f32[6,4,4,8,128]{4,3,2,1,0:T(8,128)S(1)}, f32[4,8,128]{2,1,0:T(8,128)S(1)}) custom-call(f32[7,4,8,128]{3,2,1,0:T(8,128)S(1)} %collective-permute-done.z_ref, f32[7,2,4,8,128]{4,3,2,1,0:T(8,128)S(1)} %copy-done.3, ...), custom_call_target="tpu_custom_call" | custom-call | tf_op jit(solution)/shard_map/rim/pallas_call | solution.py:795
  15.1 3.4 %collective-permute-done.5.rest_1_ = f32[23,8,128]{2,1,0:T(8,128)S(1)} collective-permute-done((f32[23,8,128]{2,1,0:T(8,128)S(1)}, f32[23,8,128]{2,1,0:T(8,128)S(1)}, u32[]{:S(2)}, u32[]{:S(2)}) %collective-permute-start.5) | collective-permute-done | bytes 94240 | tf_op jit(solution)/shard_map/ppermute | solution.py:699
  18.5 0.0 collective-permute-done.4.rest_0_
  18.5 3.3 %outer.1 = (f32[3,32,8,128]{3,2,1,0:T(8,128)}, f32[3,32,8,128]{3,2,1,0:T(8,128)}, f32[16,2,16]{2,1,0:T(2,128)S(1)}) custom-call(s32[1,1,4]{2,1,0:T(1,128)S(1)} %copy-done.5, s32[1,1,4]{2,1,0:T(1,128)S(1)} %copy-done.7, f32[3,8,5,8,128]{4,3,2,1,0:T(8,128)S(1)} %get-tuple-element.21.e_in, f32[3,8,5,8,128]{4,3,2,1,0:T(8,128)S(1)} %get-tuple-element.22.h_in, ...), custom_call_target="tpu_custom_call" | custom-call | tf_op jit(solution)/shard_map/outer/pallas_call | solution.py:812
  21.8 12.5 %all_to_all.5 = f32[16,2,16]{2,1,0:T(2,128)S(1)} all-to-all(f32[16,2,16]{2,1,0:T(2,128)S(1)} %get-tuple-element.36), channel_id=1, replica_groups=mesh['grp'=2,'col'=4,'row'=2,'gz'=2] {'col','row','gz'}, dimensions={0} | all-to-all | bytes 4096 | tf_op jit(solution)/shard_map/all_to_all | solution.py:828
  34.2 0.6 %reduce_sum.9 = f32[2,16]{1,0:T(2,128)} reduce(f32[16,2,16]{2,1,0:T(2,128)S(1)} %all_to_all.5, f32[]{:T(128)} %constant.0.clone.1), dimensions={0}, to_apply=%region_0.0 | reduce | flops 480 | bytes 2180 | tf_op jit(solution)/shard_map/reduce_sum | solution.py:832
  (9 shorter events, 0.0 us)
Async XLA Ops:
  0.6 8.1 %copy-start.2 = (s32[32,8,128]{2,1,0:T(8,128)S(1)}, s32[32,8,128]{2,1,0:T(8,128)}, u32[]{:S(2)}) copy-start(s32[32,8,128]{2,1,0:T(8,128)} %mat_ref.1) | copy-start | bytes 393220
  0.6 8.1 %copy-start.1 = (f32[3,32,8,128]{3,2,1,0:T(8,128)S(1)}, f32[3,32,8,128]{3,2,1,0:T(8,128)}, u32[]{:S(2)}) copy-start(f32[3,32,8,128]{3,2,1,0:T(8,128)} %magn_ref.1) | copy-start | bytes 1179652
  0.7 8.1 %copy-start = (f32[3,32,8,128]{3,2,1,0:T(8,128)S(1)}, f32[3,32,8,128]{3,2,1,0:T(8,128)}, u32[]{:S(2)}) copy-start(f32[3,32,8,128]{3,2,1,0:T(8,128)} %elec_ref.1) | copy-start | bytes 1179652
  3.5 15.1 %collective-permute-start.4 = (f32[26,4,8,128]{3,2,1,0:T(8,128)}, f32[26,4,8,128]{3,2,1,0:T(8,128)S(1)}, u32[]{:S(2)}, u32[]{:S(2)}) collective-permute-start(f32[26,4,8,128]{3,2,1,0:T(8,128)} %get-tuple-element.33), channel_id=1, source_target_pairs={{0,2},{2,0},{1,3},{3,1},{4,6},{6,4},{5,7},{7,5},{8,10},{10,8},{9,1... | collective-permute-start | bytes 1277960 | tf_op jit(solution)/shard_map/ppermute | solution.py:699
  6.5 2.2 %collective-permute-start = (f32[7,4,8,128]{3,2,1,0:T(8,128)}, f32[7,4,8,128]{3,2,1,0:T(8,128)S(1)}, u32[]{:S(2)}, u32[]{:S(2)}) collective-permute-start(f32[7,4,8,128]{3,2,1,0:T(8,128)} %get-tuple-element.20), channel_id=1, source_target_pairs={{0,1},{1,0},{2,3},{3,2},{4,5},{5,4},{6,7},{7,6},{8,9},{9,8},{10,11... | collective-permute-start | bytes 344072 | tf_op jit(solution)/shard_map/ppermute | solution.py:699
  6.5 2.3 %copy-start.6 = (f32[8]{0:T(128)S(1)}, f32[8]{0:T(128)}, u32[]{:S(2)}) copy-start(f32[8]{0:T(128)} %eps_ref.1) | copy-start | bytes 100
  6.5 4.1 %collective-permute-start.1 = (f32[2,4,8,128]{3,2,1,0:T(8,128)}, f32[2,4,8,128]{3,2,1,0:T(8,128)S(1)}, u32[]{:S(2)}, u32[]{:S(2)}) collective-permute-start(f32[2,4,8,128]{3,2,1,0:T(8,128)} %get-tuple-element.24), channel_id=1, source_target_pairs={{0,4},{8,12},{4,0},{12,8},{1,5},{9,13},{5,1},{13,9},{2,6},{10,14},... | collective-permute-start | bytes 98312 | tf_op jit(solution)/shard_map/ppermute | solution.py:699
  8.0 2.6 %collective-permute-start.2 = (f32[2,4,8,128]{3,2,1,0:T(8,128)}, f32[2,4,8,128]{3,2,1,0:T(8,128)S(1)}, u32[]{:S(2)}, u32[]{:S(2)}) collective-permute-start(f32[2,4,8,128]{3,2,1,0:T(8,128)} %get-tuple-element.25), channel_id=1, source_target_pairs={{4,8},{8,4},{5,9},{9,5},{6,10},{10,6},{7,11},{11,7},{20,24},{24,20... | collective-permute-start | bytes 98312 | tf_op jit(solution)/shard_map/ppermute | solution.py:699
  10.3 0.9 %copy-start.4 = (f32[8,32,64]{2,1,0:T(8,128)S(1)}, f32[8,32,64]{2,1,0:T(8,128)}, u32[]{:S(2)}) copy-start(f32[8,32,64]{2,1,0:T(8,128)} %mode_ref.1) | copy-start | bytes 196612
  10.6 0.7 %copy-start.5 = (s32[1,1,4]{2,1,0:T(1,128)S(1)}, s32[1,1,4]{2,1,0:T(1,128)}, u32[]{:S(2)}) copy-start(s32[1,1,4]{2,1,0:T(1,128)} %prow_ref.5) | copy-start | bytes 52
  10.6 0.7 %copy-start.7 = (s32[1,1,4]{2,1,0:T(1,128)S(1)}, s32[1,1,4]{2,1,0:T(1,128)}, u32[]{:S(2)}) copy-start(s32[1,1,4]{2,1,0:T(1,128)} %pid_ref.3) | copy-start | bytes 52
  10.6 0.7 %copy-start.8 = (s32[1,1,4]{2,1,0:T(1,128)S(1)}, s32[1,1,4]{2,1,0:T(1,128)}, u32[]{:S(2)}) copy-start(s32[1,1,4]{2,1,0:T(1,128)} %pcol_ref.1) | copy-start | bytes 52
  10.6 0.7 %copy-start.9 = (s32[1,1,4]{2,1,0:T(1,128)S(1)}, s32[1,1,4]{2,1,0:T(1,128)}, u32[]{:S(2)}) copy-start(s32[1,1,4]{2,1,0:T(1,128)} %pmode_ref.1) | copy-start | bytes 52
  10.6 1.5 %collective-permute-start.3 = (f32[2,2,8,128]{3,2,1,0:T(8,128)S(1)}, f32[2,2,8,128]{3,2,1,0:T(8,128)S(1)}, u32[]{:S(2)}, u32[]{:S(2)}) collective-permute-start(f32[2,2,8,128]{3,2,1,0:T(8,128)S(1)} %layer_edges.1.order_ref), channel_id=1, source_target_pairs={{0,1},{1,0},{2,3},{3,2},{4,5},{5,4},{6,7},{7,6},{8,9},{9,8},{10,11... | collective-permute-start | bytes 49160 | tf_op jit(solution)/shard_map/ppermute | solution.py:699
  12.1 0.9 %copy-start.3 = (f32[7,2,4,8,128]{4,3,2,1,0:T(8,128)S(1)}, f32[7,2,4,8,128]{4,3,2,1,0:T(8,128)}, u32[]{:S(2)}) copy-start(f32[7,2,4,8,128]{4,3,2,1,0:T(8,128)} %get-tuple-element.26.own_ref) | copy-start | bytes 688132
  12.2 6.3 %collective-permute-start.5 = (f32[23,8,128]{2,1,0:T(8,128)S(1)}, f32[23,8,128]{2,1,0:T(8,128)S(1)}, u32[]{:S(2)}, u32[]{:S(2)}) collective-permute-start(f32[23,8,128]{2,1,0:T(8,128)S(1)} %corners.1), channel_id=1, source_target_pairs={{0,2},{2,0},{1,3},{3,1},{4,6},{6,4},{5,7},{7,5},{8,10},{10,8},{9,1... | collective-permute-start | bytes 282632 | tf_op jit(solution)/shard_map/ppermute | solution.py:699
